TPU v7x, 32 devices: a whole 2x2x4 slice. The times are simulated.
32 devices in a mesh: batch: 16 (over z, y, x), tm: 2 (over core).
Axes of the slice: x: 2, y: 2, z: 4, core: 2. Of those that a mesh axis runs over, the one named last changes fastest.
Arguments:
- tokens: bfloat16 [16, 2048, 384], P('batch', 'tm'), may hold values from -6 to 6
- cotangent: bfloat16 [16, 2048, 384], P('batch', 'tm'), may hold values from -6 to 6
- sample_ids: int32 [16, 2048], P('batch'), may hold values from 0 to 3, as said below
- pad_flags: int32 [16, 2048], P('batch'), may hold values from 0 to 1, as said below
- offsets: int32 [16, 2048], P('batch'), may hold values from 0 to 63
- w_qkv: float32 [384, 1152], P('batch'), may hold values from -0.3125 to 0.3125
- w_out: float32 [384, 384], P('batch'), may hold values from -1.25 to 1.25
- w_gate_up: float32 [384, 2048], P('batch'), may hold values from -0.3125 to 0.3125
- w_down: float32 [1024, 384], P('batch'), may hold values from -0.1875 to 0.1875
- gains: float32 [2, 384], P(None, 'batch'), may hold values from 0.25 to 2.6, as said below
- m_qkv: float32 [384, 1152], P('batch'), may hold values from -0.0048828125 to 0.0048828125
- m_out: float32 [384, 384], P('batch'), may hold values from -0.0048828125 to 0.0048828125
- m_gate_up: float32 [384, 2048], P('batch'), may hold values from -0.0048828125 to 0.0048828125
- m_down: float32 [1024, 384], P('batch'), may hold values from -0.0048828125 to 0.0048828125
- m_gains: float32 [2, 384], P(None, 'batch'), may hold values from -0.01953125 to 0.01953125
- v_qkv: float32 [384, 1152], P('batch'), may hold values from 5.648952e-07 to 2.2595807e-06
- v_out: float32 [384, 384], P('batch'), may hold values from 5.648952e-07 to 2.2595807e-06
- v_gate_up: float32 [384, 2048], P('batch'), may hold values from 5.648952e-07 to 2.2595807e-06
- v_down: float32 [1024, 384], P('batch'), may hold values from 5.648952e-07 to 2.2595807e-06
- v_gains: float32 [2, 384], P(None, 'batch'), may hold values from 9.038323e-06 to 3.615329e-05
Outputs:
- result: bfloat16 [16, 2048, 384], P('batch', 'tm')
- grad_tokens: bfloat16 [16, 2048, 384], P('batch', 'tm')
- grad_norm: float32 [], replicated
- new_m_qkv: float32 [384, 1152], P('batch')
- new_m_out: float32 [384, 384], P('batch')
- new_m_gate_up: float32 [384, 2048], P('batch')
- new_m_down: float32 [1024, 384], P('batch')
- new_m_gains: float32 [2, 384], P(None, 'batch')
- new_v_qkv: float32 [384, 1152], P('batch')
- new_v_out: float32 [384, 384], P('batch')
- new_v_gate_up: float32 [384, 2048], P('batch')
- new_v_down: float32 [1024, 384], P('batch')
- new_v_gains: float32 [2, 384], P(None, 'batch')
- new_w_qkv: float32 [384, 1152], P('batch')
- new_w_out: float32 [384, 384], P('batch')
- new_w_gate_up: float32 [384, 2048], P('batch')
- new_w_down: float32 [1024, 384], P('batch')
- new_gains: float32 [2, 384], P(None, 'batch')
- copy_qkv: bfloat16 [384, 1152], P('batch')
- copy_out: bfloat16 [384, 384], P('batch')
- copy_gate_up: bfloat16 [384, 2048], P('batch')
- copy_down: bfloat16 [1024, 384], P('batch')
- copy_gains: bfloat16 [2, 384], P(None, 'batch')
Inputs may be any that keep to these rules, and one draw needn't show every extreme that they name: `sample_ids`: along each row the numbers never fall and start at 0; the series numbered 1 covers at least positions 512 to 1535. `pad_flags`: each row ends in 1 to 256 padded slots, and no other slot is padded. Positive gains.
All inputs are finite; a program needn't handle non-finite values.
Results may differ from a plain program's by a relative error of at most 0.013.
The roundings to bfloat16 on the way count: a program that leaves them out, or rounds other values in their place, can miss the bound.
Values may be sent and summed in bfloat16 or wider, within the bound.
No kernel may reach another device: no remote copies, remote signals or barrier semaphores. Data moves between devices by JAX's collectives and lax.ppermute only.
A program may use at most 320 MiB of HBM per device.

v0:
```python
import math

import jax
import jax.numpy as jnp
from jax import lax
from jax.sharding import PartitionSpec as P

D = 384
FF = 1024
HEADS = 6
HD = 64
STEP = 3


norm_eps = 1e-06
beta_one = 0.5
beta_two = 0.5
adam_eps = 1e-08
decay_rate = 0.1
clip_limit = 1.0
masked_score = -1e30


def rms_scale(values):
    return lax.rsqrt(jnp.mean(values * values, axis=-1, keepdims=True) + norm_eps)


def norm_back(grad_normed, values, scale):
    return scale * grad_normed - values * scale * scale * scale * jnp.mean(
        grad_normed * values, axis=-1, keepdims=True
    )


def rotary_tables(positions):
    frequency = jnp.exp(jnp.arange(HD // 2, dtype=jnp.float32) * (-2.0 * math.log(10000.0) / HD))
    angles = positions.astype(jnp.float32)[..., None] * frequency
    return (jnp.cos(angles)[:, :, None, :], jnp.sin(angles)[:, :, None, :])


def rotary(field, cosine, sine, direction):
    half_size = field.shape[-1] // 2
    first_half = field[..., :half_size]
    second_half = field[..., half_size:]
    return jnp.concatenate(
        [
            first_half * cosine - direction * second_half * sine,
            second_half * cosine + direction * first_half * sine,
        ],
        axis=-1,
    )


def adam_update(master, grad, first, second, rate, decay):
    first_new = beta_one * first + (1.0 - beta_one) * grad
    second_new = beta_two * second + (1.0 - beta_two) * grad * grad
    direction = (
        first_new
        / (1.0 - beta_one**STEP)
        / (jnp.sqrt(second_new / (1.0 - beta_two**STEP)) + adam_eps)
    )
    return (first_new, second_new, master - rate * (direction + decay * master))


def square_total(arrays):
    total = jnp.sum(arrays[0] * arrays[0])
    for item in arrays[1:]:
        total = total + jnp.sum(item * item)
    return total


def per_device(
    tokens,
    cotangent,
    sample_ids,
    pad_flags,
    offsets,
    w_qkv,
    w_out,
    w_gate_up,
    w_down,
    gains,
    m_qkv,
    m_out,
    m_gate_up,
    m_down,
    m_gains,
    v_qkv,
    v_out,
    v_gate_up,
    v_down,
    v_gains,
):
    bf16 = jnp.bfloat16
    f32 = jnp.float32
    attn_in, attn_out, ffn_in, ffn_out, gain_pair = (
        lax.all_gather(w_qkv.astype(bf16), "batch", axis=0, tiled=True),
        lax.all_gather(w_out.astype(bf16), "batch", axis=0, tiled=True),
        lax.all_gather(w_gate_up.astype(bf16), "batch", axis=0, tiled=True),
        lax.all_gather(w_down.astype(bf16), "batch", axis=0, tiled=True),
        lax.all_gather(gains.astype(bf16), "batch", axis=1, tiled=True),
    )
    gain_one = gain_pair[0].astype(f32)
    gain_two = gain_pair[1].astype(f32)
    rows_dev, local_len, width = tokens.shape
    seq_len = sample_ids.shape[1]
    start = lax.axis_index("tm") * local_len
    local_ids = lax.dynamic_slice_in_dim(sample_ids, start, local_len, 1)
    local_pads = lax.dynamic_slice_in_dim(pad_flags, start, local_len, 1)
    local_offsets = lax.dynamic_slice_in_dim(offsets, start, local_len, 1)
    positions = start + jnp.arange(local_len, dtype=jnp.int32)[None, :] + local_offsets
    cosine, sine = rotary_tables(positions)
    score_scale = HD ** (-0.5)
    allowed = (
        (local_ids[:, :, None] == sample_ids[:, None, :])
        & (local_pads[:, :, None] == pad_flags[:, None, :])
    )[:, None]
    inputs = tokens.astype(f32)
    scale_one = rms_scale(inputs)
    normed = (inputs * scale_one * gain_one).astype(bf16)
    projected = jnp.einsum("rtd,de->rte", normed, attn_in, preferred_element_type=f32)
    split_heads = projected.reshape(rows_dev, local_len, 3, HEADS, HD)
    queries = rotary(split_heads[:, :, 0], cosine, sine, 1.0).astype(bf16)
    keys_here = (
        rotary(split_heads[:, :, 1], cosine, sine, 1.0).astype(bf16).reshape(rows_dev, local_len, D)
    )
    values_here = split_heads[:, :, 2].astype(bf16).reshape(rows_dev, local_len, D)
    keys_flat, values_flat = (
        lax.all_gather(keys_here, "tm", axis=1, tiled=True),
        lax.all_gather(values_here, "tm", axis=1, tiled=True),
    )
    keys_all = keys_flat.reshape(rows_dev, seq_len, HEADS, HD)
    values_all = values_flat.reshape(rows_dev, seq_len, HEADS, HD)

    def scores_of():
        raw_scores = (
            jnp.einsum("rqhd,rkhd->rhqk", queries, keys_all, preferred_element_type=f32)
            * score_scale
        )
        return jnp.where(allowed, raw_scores, masked_score)

    scores = scores_of()
    top_score = jnp.max(scores, axis=-1, keepdims=True)
    exp_scores = jnp.exp(scores - top_score)
    exp_total = jnp.sum(exp_scores, axis=-1, keepdims=True)
    log_total = top_score + jnp.log(exp_total)
    attend_low = (exp_scores / exp_total).astype(bf16)
    mixed = jnp.einsum("rhqk,rkhd->rqhd", attend_low, values_all, preferred_element_type=f32)
    mixed = mixed.astype(bf16).reshape(rows_dev, local_len, D)
    branch = jnp.einsum("rtd,de->rte", mixed, attn_out, preferred_element_type=f32)
    middle = inputs + branch
    scale_two = rms_scale(middle)
    normed_two = (middle * scale_two * gain_two).astype(bf16)
    gate_up = jnp.einsum("rtd,de->rte", normed_two, ffn_in, preferred_element_type=f32)
    gate_part = gate_up[..., :FF]
    up_part = gate_up[..., FF:]
    sigmoid_gate = jax.nn.sigmoid(gate_part)
    hidden_act = (gate_part * sigmoid_gate * up_part).astype(bf16)
    ffn_result = jnp.einsum("rtf,fd->rtd", hidden_act, ffn_out, preferred_element_type=f32)
    keep = (1 - local_pads).astype(f32)[..., None]
    result = (keep * (middle + ffn_result)).astype(bf16)
    upstream = cotangent.astype(f32) * keep
    upstream_low = upstream.astype(bf16)
    grad_ffn_out = jnp.einsum("rtf,rtd->fd", hidden_act, upstream_low, preferred_element_type=f32)
    grad_hidden = jnp.einsum("rtd,fd->rtf", upstream_low, ffn_out, preferred_element_type=f32)
    grad_up = grad_hidden * gate_part * sigmoid_gate
    grad_gate = grad_hidden * up_part * sigmoid_gate * (1.0 + gate_part * (1.0 - sigmoid_gate))
    gate_up_low = jnp.concatenate([grad_gate, grad_up], axis=-1).astype(bf16)
    grad_ffn_in = jnp.einsum("rtd,rte->de", normed_two, gate_up_low, preferred_element_type=f32)
    grad_normed_two = jnp.einsum("rte,de->rtd", gate_up_low, ffn_in, preferred_element_type=f32)
    grad_gain_two = jnp.sum(grad_normed_two * middle * scale_two, axis=(0, 1))
    grad_middle = upstream + norm_back(grad_normed_two * gain_two, middle, scale_two)
    middle_low = grad_middle.astype(bf16)
    grad_attn_out = jnp.einsum("rtd,rte->de", mixed, middle_low, preferred_element_type=f32)
    grad_mixed = jnp.einsum("rte,de->rtd", middle_low, attn_out, preferred_element_type=f32)
    grad_mixed = grad_mixed.astype(bf16).reshape(rows_dev, local_len, HEADS, HD)
    attend = jnp.exp(scores_of() - log_total)
    grad_attend = jnp.einsum("rqhd,rkhd->rhqk", grad_mixed, values_all, preferred_element_type=f32)
    grad_scores = (
        attend * (grad_attend - jnp.sum(attend * grad_attend, axis=-1, keepdims=True))
    ).astype(bf16)
    grad_queries = (
        jnp.einsum("rhqk,rkhd->rqhd", grad_scores, keys_all, preferred_element_type=f32)
        * score_scale
    )
    keys_part = (
        jnp.einsum("rhqk,rqhd->rkhd", grad_scores, queries, preferred_element_type=f32)
        * score_scale
    )
    values_part = jnp.einsum(
        "rhqk,rqhd->rkhd", attend.astype(bf16), grad_mixed, preferred_element_type=f32
    )
    grad_keys, grad_values = (
        lax.psum_scatter(
            keys_part.reshape(rows_dev, seq_len, D).astype(jnp.bfloat16),
            "tm",
            scatter_dimension=1,
            tiled=True,
        ).astype(jnp.float32),
        lax.psum_scatter(
            values_part.reshape(rows_dev, seq_len, D).astype(jnp.bfloat16),
            "tm",
            scatter_dimension=1,
            tiled=True,
        ).astype(jnp.float32),
    )
    grad_query_pre = rotary(grad_queries, cosine, sine, -1.0)
    grad_key_pre = rotary(grad_keys.reshape(rows_dev, local_len, HEADS, HD), cosine, sine, -1.0)
    qkv_low = jnp.concatenate(
        [
            grad_query_pre.reshape(rows_dev, local_len, D),
            grad_key_pre.reshape(rows_dev, local_len, D),
            grad_values,
        ],
        axis=-1,
    ).astype(bf16)
    grad_attn_in = jnp.einsum("rtd,rte->de", normed, qkv_low, preferred_element_type=f32)
    grad_normed = jnp.einsum("rte,de->rtd", qkv_low, attn_in, preferred_element_type=f32)
    grad_gain_one = jnp.sum(grad_normed * inputs * scale_one, axis=(0, 1))
    grad_tokens = (grad_middle + norm_back(grad_normed * gain_one, inputs, scale_one)).astype(bf16)
    grad_gains = jnp.stack([grad_gain_one, grad_gain_two], axis=0)
    summed = lax.psum(
        (grad_attn_in, grad_attn_out, grad_ffn_in, grad_ffn_out, grad_gains), ("batch", "tm")
    )
    grad_norm = jnp.sqrt(square_total(summed))
    owner = lax.axis_index("batch")
    shard_grads = (
        lax.dynamic_slice_in_dim(summed[0], owner * w_qkv.shape[0], w_qkv.shape[0], 0),
        lax.dynamic_slice_in_dim(summed[1], owner * w_out.shape[0], w_out.shape[0], 0),
        lax.dynamic_slice_in_dim(summed[2], owner * w_gate_up.shape[0], w_gate_up.shape[0], 0),
        lax.dynamic_slice_in_dim(summed[3], owner * w_down.shape[0], w_down.shape[0], 0),
        lax.dynamic_slice_in_dim(summed[4], owner * gains.shape[1], gains.shape[1], 1),
    )
    factor = clip_limit / jnp.maximum(grad_norm, clip_limit)
    masters = (w_qkv, w_out, w_gate_up, w_down, gains)
    firsts = (m_qkv, m_out, m_gate_up, m_down, m_gains)
    seconds = (v_qkv, v_out, v_gate_up, v_down, v_gains)
    rates = (D ** (-0.5), 4.0 * D ** (-0.5), D ** (-0.5), FF ** (-0.5), 0.5)
    decays = (decay_rate, decay_rate, decay_rate, decay_rate, 0.0)
    new_first = []
    new_second = []
    new_master = []
    for index in range(5):
        first_new, second_new, master_new = adam_update(
            masters[index],
            factor * shard_grads[index],
            firsts[index],
            seconds[index],
            rates[index],
            decays[index],
        )
        new_first.append(first_new)
        new_second.append(second_new)
        new_master.append(master_new)
    copies = [item.astype(bf16) for item in new_master]
    return (
        result,
        grad_tokens,
        grad_norm,
        new_first[0],
        new_first[1],
        new_first[2],
        new_first[3],
        new_first[4],
        new_second[0],
        new_second[1],
        new_second[2],
        new_second[3],
        new_second[4],
        new_master[0],
        new_master[1],
        new_master[2],
        new_master[3],
        new_master[4],
        copies[0],
        copies[1],
        copies[2],
        copies[3],
        copies[4],
    )


def solution(mesh):
    in_specs = (
        P("batch", "tm", None),
        P("batch", "tm", None),
        P("batch", None),
        P("batch", None),
        P("batch", None),
        P("batch", None),
        P("batch", None),
        P("batch", None),
        P("batch", None),
        P(None, "batch"),
        P("batch", None),
        P("batch", None),
        P("batch", None),
        P("batch", None),
        P(None, "batch"),
        P("batch", None),
        P("batch", None),
        P("batch", None),
        P("batch", None),
        P(None, "batch"),
    )
    out_specs = (
        P("batch", "tm", None),
        P("batch", "tm", None),
        P(),
        P("batch", None),
        P("batch", None),
        P("batch", None),
        P("batch", None),
        P(None, "batch"),
        P("batch", None),
        P("batch", None),
        P("batch", None),
        P("batch", None),
        P(None, "batch"),
        P("batch", None),
        P("batch", None),
        P("batch", None),
        P("batch", None),
        P(None, "batch"),
        P("batch", None),
        P("batch", None),
        P("batch", None),
        P("batch", None),
        P(None, "batch"),
    )
    return jax.shard_map(
        per_device, mesh=mesh, in_specs=in_specs, out_specs=out_specs, check_vma=False
    )
```

profile of v0, /device:TPU:0, one launch (start us, length us, event | category | flops | bytes accessed | tf_op | source)
XLA Modules:
  0.0 611.4 jit_solution(17761801884509498569)
XLA Ops:
  7.9 42.2 %all-gather = bf16[16,24,2]{1,2,0:T(2,128)(2,1)S(1)} all-gather(bf16[1,24,2]{1,2,0:T(2,128)(2,1)S(1)} %convert_bitcast_fusion), channel_id=1, replica_groups=mesh['batch'=16,'tm'=2] {'batch'}, dimensions={0}, use_global_device_ids=true | all-gather | bytes 1632 | tf_op jit(solution)/shard_map/all_gather | solution.py:100
  52.8 40.8 %all_gather.22 = bf16[384,1152]{1,0:T(8,128)(2,1)S(1)} all-gather(bf16[24,1152]{1,0:T(8,128)(2,1)S(1)} %convert_element_type.197), channel_id=1, replica_groups=mesh['batch'=16,'tm'=2] {'batch'}, dimensions={0}, use_global_device_ids=true | all-gather | bytes 940032 | tf_op jit(solution)/shard_map/all_gather | solution.py:96
  100.8 2.8 fusion.58
  108.0 39.6 %all_gather.25 = bf16[384,384]{1,0:T(8,128)(2,1)S(1)} all-gather(bf16[24,384]{1,0:T(8,128)(2,1)S(1)} %convert_element_type.205), channel_id=1, replica_groups=mesh['batch'=16,'tm'=2] {'batch'}, dimensions={0}, use_global_device_ids=true | all-gather | bytes 313344 | tf_op jit(solution)/shard_map/all_gather | solution.py:97
  147.6 45.3 %all_gather.27 = bf16[1024,384]{1,0:T(8,128)(2,1)} all-gather(bf16[64,384]{1,0:T(8,128)(2,1)S(1)} %convert_element_type.211), channel_id=1, replica_groups=mesh['batch'=16,'tm'=2] {'batch'}, dimensions={0}, use_global_device_ids=true | all-gather | bytes 835584 | tf_op jit(solution)/shard_map/all_gather | solution.py:99
  196.7 22.1 %fusion.6 = (f32[6,1024]{1,0:T(8,128)S(1)}, f32[6,1024,2048]{2,1,0:T(8,128)}) fusion(pred[1024,2048]{1,0:T(8,128)(4,1)S(1)} %compare_and_fusion, bf16[2048,6,64]{0,2,1:T(8,128)(2,1)} %bitcast.162, bf16[1024,6,32]{0,2,1:T(8,128)(2,1)} %get-tuple-element.134, bf16[1024,6,32]{0,2,1:T(8,128)(2,1)} %get-tuple-element.133), kind=kOutput, calls=%fused_computation.11 | convolution fusion | flops 1649928192 | bytes 54812672 | tf_op jit(solution)/shard_map/rqhd,rkhd->rhqk/dot_general | solution.py:136
  218.8 22.6 %fusion = f32[6,1024]{1,0:T(8,128)S(1)} fusion(f32[6,1024]{1,0:T(8,128)S(1)} %get-tuple-element.144, f32[6,1024,2048]{2,1,0:T(8,128)} %get-tuple-element.145, pred[1024,2048]{1,0:T(8,128)(4,1)S(1)} %compare_and_fusion), kind=kLoop, calls=%fused_computation.6 | loop fusion | flops 50325504 | bytes 52477952 | tf_op jit(solution)/shard_map/reduce_sum | solution.py:144
  241.4 20.4 %fusion.44 = bf16[6,64,1024]{2,1,0:T(8,128)(2,1)S(1)} fusion(bf16[2048,6,64]{0,2,1:T(8,128)(2,1)} %bitcast.160, f32[6,1024]{1,0:T(8,128)S(1)} %fusion, f32[6,1024]{1,0:T(8,128)S(1)} %get-tuple-element.144, f32[6,1024,2048]{2,1,0:T(8,128)} %get-tuple-element.145, pred[1024,2048]{1,0:T(8,128)(4,1)S(1)} %compare_and_fusion), kind=kOutput, calls=%fused_computation.75 | convolution fusion | flops 1673920512 | bytes 54837248 | tf_op jit(solution)/shard_map/rhqk,rkhd->rqhd/dot_general | solution.py:147
  263.7 4.5 convolution_bitcast_fusion
  268.3 4.1 fusion.22
  276.8 35.6 %multiply_reduce_fusion = (f32[6,1024]{1,0:T(8,128)S(1)}, f32[6,1024,2048]{2,1,0:T(8,128)}) fusion(f32[6,1024]{1,0:T(8,128)S(1)} %log_add_fusion, f32[6,1024,2048]{2,1,0:T(8,128)} %get-tuple-element.145, pred[1024,2048]{1,0:T(8,128)(4,1)S(1)} %compare_and_fusion, bf16[1024,6,64]{0,2,1:T(8,128)(2,1)S(1)} %bitcast.154, bf16[2048,6,64]{0,2,1:T(8,128)(2,1)} %bitcast.161), kind=kOutput, calls=%fused_computation.1 | convolution fusion | flops 1673521152 | bytes 105168896 | tf_op jit(solution)/shard_map/rqhd,rkhd->rhqk/dot_general | solution.py:177
  312.4 40.8 %multiply_convert_fusion = bf16[6,1024,2048]{2,1,0:T(8,128)(2,1)} fusion(f32[6,1024,2048]{2,1,0:T(8,128)} %get-tuple-element.150, f32[6,1024]{1,0:T(8,128)S(1)} %get-tuple-element.149, f32[6,1024]{1,0:T(8,128)S(1)} %log_add_fusion, f32[6,1024,2048]{2,1,0:T(8,128)} %get-tuple-element.145, pred[1024,2048]{1,0:T(8,128)(4,1)S(1)} %compare_and_fusion), kind=kLoop, calls=%fused_computation | loop fusion | flops 75497472 | bytes 127975424 | tf_op jit(solution)/shard_map/convert_element_type | solution.py:180
  353.1 13.8 %multiply_convert_fusion.2 = bf16[6,64,2048]{2,1,0:T(8,128)(2,1)} fusion(bf16[6,1024,2048]{2,1,0:T(8,128)(2,1)} %multiply_convert_fusion, bf16[1024,6,32]{0,2,1:T(8,128)(2,1)S(1)} %copy-done.14, bf16[1024,6,32]{0,2,1:T(8,128)(2,1)S(1)} %copy-done.13), kind=kOutput, calls=%fused_computation.25 | convolution fusion | flops 1613758464 | bytes 27525120 | tf_op jit(solution)/shard_map/rhqk,rqhd->rkhd/dot_general | solution.py:186
  367.0 21.7 %fusion.12 = bf16[6,64,2048]{2,1,0:T(8,128)(2,1)} fusion(bf16[1024,6,64]{0,2,1:T(8,128)(2,1)S(1)} %bitcast.155, f32[6,1024]{1,0:T(8,128)S(1)} %log_add_fusion, f32[6,1024,2048]{2,1,0:T(8,128)} %get-tuple-element.145, pred[1024,2048]{1,0:T(8,128)(4,1)S(1)} %compare_and_fusion), kind=kOutput, calls=%fused_computation.31 | convolution fusion | flops 1661730816 | bytes 54812672 | tf_op jit(solution)/shard_map/rhqk,rqhd->rkhd/dot_general | solution.py:189
  390.1 2.8 fusion.50
  392.9 3.8 fusion.17
  396.7 3.5 fusion.15
  400.2 14.1 %multiply_bitcast_fusion = f32[1,1024,6,64]{1,3,2,0:T(8,128)} fusion(bf16[2048,6,64]{0,2,1:T(8,128)(2,1)} %bitcast.163, bf16[6,1024,2048]{2,1,0:T(8,128)(2,1)} %multiply_convert_fusion), kind=kOutput, calls=%fused_computation.69 | convolution fusion | flops 1611005952 | bytes 28311552 | tf_op jit(solution)/shard_map/rhqk,rkhd->rqhd/dot_general | solution.py:182
  418.6 4.3 fusion.45
  423.0 4.0 fusion.40
  429.2 3.7 fusion.34
  434.7 38.1 %psum.39 = f32[2,384]{1,0:T(2,128)S(1)} all-reduce(f32[2,384]{1,0:T(2,128)S(1)} %pad_maximum_fusion.12), channel_id=1, replica_groups=mesh['batch'=16,'tm'=2] {'batch','tm'}, use_global_device_ids=true, to_apply=%region_19.20 | all-reduce | flops 768 | bytes 6144 | tf_op jit(solution)/shard_map/psum | solution.py:221
  473.3 112.0 %all-reduce.3.cloned.1.call-done = (f32[384,1152]{1,0:T(8,128)}, f32[384,384]{1,0:T(8,128)}, f32[384,2048]{1,0:T(8,128)}, f32[1024,384]{1,0:T(8,128)}) async-done(((f32[384,1152]{1,0:T(8,128)}, f32[384,384]{1,0:T(8,128)}, f32[384,2048]{1,0:T(8,128)}, f32[1024,384]{1,0:T(8,128)}), (f32[384,1152]{1,0:T(8,128)}, f32[384,384]{1,0:T(8,128)}, f32[384,2048]{1,0:T(8,128)}, ...) | async-done | bytes 7077904 | tf_op jit(solution)/shard_map/psum | solution.py:221
  587.8 3.5 multiply_reduce_fusion.1
  (162 shorter events, 45.9 us)
Async XLA Ops:
  7.2 189.5 %all-gather.7.cloned.1.call-start = ((), (), s32[]{:S(2)}) async-start(), calls=%async_computation.3 | async-start | bytes 2359296 | tf_op jit(solution)/shard_map/all_gather | solution.py:128
  50.2 44.2 %copy-start.40 = (f32[384]{0:T(512)}, f32[384]{0:T(512)S(1)}, u32[]{:S(2)}) copy-start(f32[384]{0:T(512)S(1)} %get-tuple-element.97) | copy-start | bytes 4612
  52.6 209.3 %copy-start.4 = (bf16[1,1024,384]{1,2,0:T(8,128)(2,1)}, bf16[1,1024,384]{1,2,0:T(8,128)(2,1)S(1)}, u32[]{:S(2)}) copy-start(bf16[1,1024,384]{1,2,0:T(8,128)(2,1)S(1)} %copy.68) | copy-start | bytes 2359300
  52.8 43.2 %copy-start.34 = (f32[1024]{0:T(1024)}, f32[1024]{0:T(1024)S(1)}, u32[]{:S(2)}) copy-start(f32[1024]{0:T(1024)S(1)} %add_rsqrt_fusion.1) | copy-start | bytes 12292
  104.5 88.4 %copy-start.19 = (bf16[1,1024,384]{2,1,0:T(8,128)(2,1)S(1)}, bf16[1,1024,384]{2,1,0:T(8,128)(2,1)}, u32[]{:S(2)}) copy-start(bf16[1,1024,384]{2,1,0:T(8,128)(2,1)} %param.21) | copy-start | bytes 2359300
  104.5 136.9 %all-gather.5.cloned.1.call-start = ((), (), s32[]{:S(2)}) async-start(), calls=%async_computation.2 | async-start | bytes 2359296 | tf_op jit(solution)/shard_map/all_gather | solution.py:129
  107.1 156.6 %all-gather.9.cloned.1.call-start = ((), (), s32[]{:S(2)}) async-start(), calls=%async_computation.4 | async-start | bytes 1671168 | tf_op jit(solution)/shard_map/all_gather | solution.py:98
  107.8 306.5 %reduce-scatter.3.cloned.1.call-start = ((), (), s32[]{:S(2)}) async-start(), calls=%async_computation.5 | async-start | bytes 2359296 | tf_op jit(solution)/shard_map/reduce_scatter | solution.py:193
  312.4 40.8 %copy-start.13 = (bf16[1024,6,32]{0,2,1:T(8,128)(2,1)S(1)}, bf16[1024,6,32]{0,2,1:T(8,128)(2,1)}, u32[]{:S(2)}) copy-start(bf16[1024,6,32]{0,2,1:T(8,128)(2,1)} %get-tuple-element.133) | copy-start | bytes 1179652
  312.4 40.8 %copy-start.14 = (bf16[1024,6,32]{0,2,1:T(8,128)(2,1)S(1)}, bf16[1024,6,32]{0,2,1:T(8,128)(2,1)}, u32[]{:S(2)}) copy-start(bf16[1024,6,32]{0,2,1:T(8,128)(2,1)} %get-tuple-element.134) | copy-start | bytes 1179652
  366.9 51.6 %reduce-scatter.5.cloned.1.call-start = ((), (), s32[]{:S(2)}) async-start(), calls=%async_computation.6 | async-start | bytes 2359296 | tf_op jit(solution)/shard_map/reduce_scatter | solution.py:199
  388.7 196.6 %all-reduce.3.cloned.1.call-start = ((), (), s32[]{:S(2)}) async-start(), calls=%async_computation.7 | async-start | bytes 14155776 | tf_op jit(solution)/shard_map/psum | solution.py:221
  585.3 5.9 copy-start.21
  587.8 8.6 %copy-start.18 = (f32[24,2048]{1,0:T(8,128)S(1)}, f32[24,2048]{1,0:T(8,128)}, u32[]{:S(2)}) copy-start(f32[24,2048]{1,0:T(8,128)} %param.27) | copy-start | bytes 589828
  587.8 8.6 %copy-start.26 = (f32[24,2048]{1,0:T(8,128)S(1)}, f32[24,2048]{1,0:T(8,128)}, u32[]{:S(2)}) copy-start(f32[24,2048]{1,0:T(8,128)} %param.37) | copy-start | bytes 589828
  587.8 8.6 %copy-start.27 = (f32[24,2048]{1,0:T(8,128)S(1)}, f32[24,2048]{1,0:T(8,128)}, u32[]{:S(2)}) copy-start(f32[24,2048]{1,0:T(8,128)} %param.32) | copy-start | bytes 589828
  591.3 7.1 %copy-start.23 = (f32[24,1152]{1,0:T(8,128)S(1)}, f32[24,1152]{1,0:T(8,128)}, u32[]{:S(2)}) copy-start(f32[24,1152]{1,0:T(8,128)} %param.25) | copy-start | bytes 331780
  591.3 7.1 %copy-start.30 = (f32[24,1152]{1,0:T(8,128)S(1)}, f32[24,1152]{1,0:T(8,128)}, u32[]{:S(2)}) copy-start(f32[24,1152]{1,0:T(8,128)} %param.35) | copy-start | bytes 331780
  591.3 7.1 %copy-start.31 = (f32[24,1152]{1,0:T(8,128)S(1)}, f32[24,1152]{1,0:T(8,128)}, u32[]{:S(2)}) copy-start(f32[24,1152]{1,0:T(8,128)} %param.30) | copy-start | bytes 331780
  592.0 7.2 %copy-start.29 = (f32[24,384]{1,0:T(8,128)S(1)}, f32[24,384]{1,0:T(8,128)}, u32[]{:S(2)}) copy-start(f32[24,384]{1,0:T(8,128)} %param.26) | copy-start | bytes 110596
  592.0 7.2 %copy-start.36 = (f32[24,384]{1,0:T(8,128)S(1)}, f32[24,384]{1,0:T(8,128)}, u32[]{:S(2)}) copy-start(f32[24,384]{1,0:T(8,128)} %param.36) | copy-start | bytes 110596
  592.0 9.2 %copy-start.25 = (f32[64,384]{1,0:T(8,128)S(1)}, f32[64,384]{1,0:T(8,128)}, u32[]{:S(2)}) copy-start(f32[64,384]{1,0:T(8,128)} %param.28) | copy-start | bytes 294916
  592.0 9.2 %copy-start.32 = (f32[64,384]{1,0:T(8,128)S(1)}, f32[64,384]{1,0:T(8,128)}, u32[]{:S(2)}) copy-start(f32[64,384]{1,0:T(8,128)} %param.38) | copy-start | bytes 294916
  596.5 4.8 copy-start.33
  (30 other events, 82.0 us)
Sparse Core Ops, SparseCore 0:
  104.6 7.7 all-gather.6
  114.6 10.9 all-gather.4
  129.0 60.4 all-gather.8
  367.1 4.9 reduce-scatter.2
  388.8 4.9 reduce-scatter.4
  423.1 162.1 all-reduce.2
where the time goes:
time: 616 us; the launch traced here: 611 us
  blocking collectives  206 us (33%)
  matrix products  164 us (27%)
  waiting for transfers between devices  112 us (18%)
  other arithmetic  93 us (15%)
  between operations  19.6 us (3%)
  local copies, waits for them, and re-layouts  16.1 us (3%)
    psum x1, waiting for transfers between devices, per_device(): lax.psum((grad_attn_in, grad_attn_out, grad_ffn_in, grad_ffn_out, grad_ga...  112 us
    all_gather x1, blocking collectives, per_device(): lax.all_gather(w_down.astype(bf16), 'batch', axis=0, tiled=True)  45.3 us
    all_gather x1, blocking collectives, per_device(): lax.all_gather(gains.astype(bf16), 'batch', axis=1, tiled=True)  42.2 us
    all_gather x1, blocking collectives, per_device(): lax.all_gather(w_qkv.astype(bf16), 'batch', axis=0, tiled=True)  40.8 us
    convert_element_type x1, other arithmetic, per_device(): grad_scores = (attend * (grad_attend - jnp.sum(attend * grad_attend, axis...  40.8 us
    all_gather x1, blocking collectives, per_device(): lax.all_gather(w_out.astype(bf16), 'batch', axis=0, tiled=True)  39.6 us
    psum x1, blocking collectives, per_device(): lax.psum((grad_attn_in, grad_attn_out, grad_ffn_in, grad_ffn_out, grad_ga...  38.1 us
    dot_general x1, matrix products, per_device(): jnp.einsum('rqhd,rkhd->rhqk', grad_mixed, values_all, preferred_element_t...  35.6 us
  transfers between devices with their start and end apart: 6, of which 1 were waited for; matrix products, arithmetic and copies ran while one was open for 22% of the time, Pallas kernels for 0%

commit v1 on v0

--- a/solution.py
+++ b/solution.py
@@ -1,4 +1,5 @@
 import math
+from functools import partial
 
 import jax
 import jax.numpy as jnp
@@ -68,7 +69,81 @@
     return total
 
 
+def bit_groups(count):
+    groups = []
+    low, bits = 0, count.bit_length() - 1
+    while low < bits:
+        width = min(2, bits - low)
+        groups.append((low, width))
+        low += width
+    return groups
+
+
+def permute_batch(value, flip, count):
+    return lax.ppermute(value, "batch", [(i, i ^ flip) for i in range(count)])
+
+
+def swap_tm(value):
+    return lax.ppermute(value, "tm", [(0, 1), (1, 0)])
+
+
+def gather_batch(chunk, owner, count):
+    held = chunk[None]
+    for low, width in reversed(bit_groups(count)):
+        pieces = [held] + [permute_batch(held, k << low, count) for k in range(1, 1 << width)]
+        for bit in range(width):
+            flag = ((owner >> (low + bit)) & 1) == 1
+            pieces = [
+                jnp.where(flag, pieces[p ^ (1 << bit)], pieces[p]) for p in range(1 << width)
+            ]
+        held = jnp.stack(pieces, axis=1).reshape((-1,) + chunk.shape)
+    return held
+
+
+def scatter_sum(parts, owner, count):
+    held = parts
+    rest = parts.shape[1:]
+    for low, width in bit_groups(count):
+        fan = 1 << width
+        view = held.reshape((-1, fan) + rest)
+        mine = (owner >> low) & (fan - 1)
+        total = lax.dynamic_index_in_dim(view, mine, 1, keepdims=False).astype(jnp.float32)
+        got = []
+        for k in range(1, fan):
+            piece = lax.dynamic_index_in_dim(view, mine ^ k, 1, keepdims=False)
+            got.append(permute_batch(piece.astype(jnp.bfloat16), k << low, count))
+        for item in got:
+            total = total + item.astype(jnp.float32)
+        held = total
+    return held.reshape(rest)
+
+
+def sum_all(value, count):
+    value = value + swap_tm(value)
+    for low, width in bit_groups(count):
+        pieces = [value] + [permute_batch(value, k << low, count) for k in range(1, 1 << width)]
+        while len(pieces) > 1:
+            pieces = [pieces[i] + pieces[i + 1] for i in range(0, len(pieces), 2)]
+        value = pieces[0]
+    return value
+
+
+def slabs(matrix):
+    rows, columns = matrix.shape
+    return matrix.reshape(rows, columns // 128, 128).transpose(1, 0, 2)
+
+
+def unslab(stack):
+    count, rows, _ = stack.shape
+    return stack.transpose(1, 0, 2).reshape(rows, count * 128)
+
+
+def pad_rows(array, rows):
+    return jnp.pad(array, ((0, rows - array.shape[0]), (0, 0)))
+
+
 def per_device(
+    count,
     tokens,
     cotangent,
     sample_ids,
@@ -92,12 +167,65 @@
 ):
     bf16 = jnp.bfloat16
     f32 = jnp.float32
-    attn_in, attn_out, ffn_in, ffn_out, gain_pair = (
-        lax.all_gather(w_qkv.astype(bf16), "batch", axis=0, tiled=True),
-        lax.all_gather(w_out.astype(bf16), "batch", axis=0, tiled=True),
-        lax.all_gather(w_gate_up.astype(bf16), "batch", axis=0, tiled=True),
-        lax.all_gather(w_down.astype(bf16), "batch", axis=0, tiled=True),
-        lax.all_gather(gains.astype(bf16), "batch", axis=1, tiled=True),
+    owner = lax.axis_index("batch")
+    core = lax.axis_index("tm")
+    shard = w_qkv.shape[0]
+    shard_down = w_down.shape[0]
+    low_qkv, low_out, low_gate_up, low_down = (
+        slabs(w_qkv.astype(bf16)),
+        slabs(w_out.astype(bf16)),
+        slabs(w_gate_up.astype(bf16)),
+        slabs(w_down.astype(bf16)),
+    )
+    low_gains = jnp.pad(gains.astype(bf16).reshape(1, -1), ((0, 0), (0, 128 - 2 * shard)))
+    first_rows = -(-(5 * shard + 1) // 16) * 16
+    first_slabs = jnp.concatenate([low_qkv, low_out[:1]], axis=0).reshape(2, 5 * shard, 128)
+    first_send = jnp.where(core == 0, first_slabs[0], first_slabs[1])
+    first_send = pad_rows(jnp.concatenate([first_send, low_gains], axis=0), first_rows)
+    second_slabs = jnp.concatenate([low_out[1:], low_gate_up], axis=0).reshape(2, 9 * shard, 128)
+    half_down = shard_down // 2
+    down_halves = low_down.reshape(3, 2, half_down, 128).transpose(1, 0, 2, 3).reshape(2, 3 * half_down, 128)
+    second_send = jnp.where(
+        core == 0,
+        jnp.concatenate([second_slabs[0], down_halves[0]], axis=0),
+        jnp.concatenate([second_slabs[1], down_halves[1]], axis=0),
+    )
+    second_rows = -(-second_send.shape[0] // 16) * 16
+    second_send = pad_rows(second_send, second_rows)
+
+    def whole(send):
+        mine = gather_batch(send, owner, count)
+        other = swap_tm(mine)
+        return jnp.where(core == 0, mine, other), jnp.where(core == 0, other, mine)
+
+    first_low, first_high = whole(first_send)
+    second_low, second_high = whole(second_send)
+
+    def take(source, start, number, rows):
+        return (
+            source[:, start : start + number * rows]
+            .reshape(count, number, rows, 128)
+            .transpose(1, 0, 2, 3)
+            .reshape(number, count * rows, 128)
+        )
+
+    first_all = jnp.concatenate(
+        [take(first_low, 0, 5, shard), take(first_high, 0, 5, shard)], axis=0
+    )
+    second_all = jnp.concatenate(
+        [take(second_low, 0, 9, shard), take(second_high, 0, 9, shard)], axis=0
+    )
+    attn_in = unslab(first_all[:9])
+    attn_out = unslab(jnp.concatenate([first_all[9:], second_all[:2]], axis=0))
+    ffn_in = unslab(second_all[2:])
+    down_at = 9 * shard
+    down_parts = [
+        item[:, down_at : down_at + 3 * half_down].reshape(count, 3, half_down, 128)
+        for item in (second_low, second_high)
+    ]
+    ffn_out = jnp.stack(down_parts, axis=1).transpose(0, 1, 3, 2, 4).reshape(count * shard_down, D)
+    gain_pair = (
+        first_low[:, 5 * shard, : 2 * shard].reshape(count, 2, shard).transpose(1, 0, 2).reshape(2, D)
     )
     gain_one = gain_pair[0].astype(f32)
     gain_two = gain_pair[1].astype(f32)
@@ -124,9 +252,12 @@
         rotary(split_heads[:, :, 1], cosine, sine, 1.0).astype(bf16).reshape(rows_dev, local_len, D)
     )
     values_here = split_heads[:, :, 2].astype(bf16).reshape(rows_dev, local_len, D)
-    keys_flat, values_flat = (
-        lax.all_gather(keys_here, "tm", axis=1, tiled=True),
-        lax.all_gather(values_here, "tm", axis=1, tiled=True),
+    both_here = jnp.stack([keys_here, values_here])
+    both_there = swap_tm(both_here)
+    keys_flat, values_flat = jnp.where(
+        core == 0,
+        jnp.concatenate([both_here, both_there], axis=2),
+        jnp.concatenate([both_there, both_here], axis=2),
     )
     keys_all = keys_flat.reshape(rows_dev, seq_len, HEADS, HD)
     values_all = values_flat.reshape(rows_dev, seq_len, HEADS, HD)
@@ -189,20 +320,10 @@
     values_part = jnp.einsum(
         "rhqk,rqhd->rkhd", attend.astype(bf16), grad_mixed, preferred_element_type=f32
     )
-    grad_keys, grad_values = (
-        lax.psum_scatter(
-            keys_part.reshape(rows_dev, seq_len, D).astype(jnp.bfloat16),
-            "tm",
-            scatter_dimension=1,
-            tiled=True,
-        ).astype(jnp.float32),
-        lax.psum_scatter(
-            values_part.reshape(rows_dev, seq_len, D).astype(jnp.bfloat16),
-            "tm",
-            scatter_dimension=1,
-            tiled=True,
-        ).astype(jnp.float32),
-    )
+    parts = jnp.stack([keys_part.reshape(rows_dev, seq_len, D), values_part.reshape(rows_dev, seq_len, D)])
+    there = lax.dynamic_slice_in_dim(parts, (1 - core) * local_len, local_len, 2).astype(bf16)
+    here = lax.dynamic_slice_in_dim(parts, start, local_len, 2)
+    grad_keys, grad_values = here + swap_tm(there).astype(f32)
     grad_query_pre = rotary(grad_queries, cosine, sine, -1.0)
     grad_key_pre = rotary(grad_keys.reshape(rows_dev, local_len, HEADS, HD), cosine, sine, -1.0)
     qkv_low = jnp.concatenate(
@@ -218,17 +339,58 @@
     grad_gain_one = jnp.sum(grad_normed * inputs * scale_one, axis=(0, 1))
     grad_tokens = (grad_middle + norm_back(grad_normed * gain_one, inputs, scale_one)).astype(bf16)
     grad_gains = jnp.stack([grad_gain_one, grad_gain_two], axis=0)
-    summed = lax.psum(
-        (grad_attn_in, grad_attn_out, grad_ffn_in, grad_ffn_out, grad_gains), ("batch", "tm")
-    )
-    grad_norm = jnp.sqrt(square_total(summed))
-    owner = lax.axis_index("batch")
+    column_one, column_two = [
+        jnp.pad(item[:, None], ((0, 0), (0, 127)))[None] for item in (grad_gain_one, grad_gain_two)
+    ]
+
+    def reduce(halves):
+        keep = jnp.where(core == 0, halves[0], halves[1])
+        give = jnp.where(core == 0, halves[1], halves[0]).astype(bf16)
+        return scatter_sum(keep + swap_tm(give).astype(f32), owner, count)
+
+    def by_device(stack, rows):
+        number = stack.shape[0]
+        return (
+            stack.reshape(number, count, rows, 128)
+            .transpose(1, 0, 2, 3)
+            .reshape(count, number * rows, 128)
+        )
+
+    second_grads = jnp.concatenate(
+        [slabs(grad_attn_out), slabs(grad_ffn_in), column_two], axis=0
+    )
+    down_grads = (
+        slabs(grad_ffn_out)
+        .reshape(3, count, 2, half_down, 128)
+        .transpose(2, 1, 0, 3, 4)
+        .reshape(2, count, 3 * half_down, 128)
+    )
+    second_sum = reduce(
+        [
+            jnp.concatenate([by_device(second_grads[:10], shard), down_grads[0]], axis=1),
+            jnp.concatenate([by_device(second_grads[10:], shard), down_grads[1]], axis=1),
+        ]
+    )
+    first_grads = jnp.concatenate([slabs(grad_attn_in), column_one], axis=0)
+    first_sum = reduce([by_device(first_grads[:5], shard), by_device(first_grads[5:], shard)])
+    squares = jnp.sum(first_sum * first_sum) + jnp.sum(second_sum * second_sum)
+    grad_norm = jnp.sqrt(sum_all(squares.reshape(1, 1), count)[0, 0])
+    sums = jnp.concatenate([first_sum, second_sum], axis=0)
+    sums_there = swap_tm(sums)
+    sums_low = jnp.where(core == 0, sums, sums_there)
+    sums_high = jnp.where(core == 0, sums_there, sums)
+    five, fifteen = 5 * shard, 15 * shard
+    first_shard = jnp.concatenate([sums_low[:five], sums_high[:five]]).reshape(10, shard, 128)
+    second_shard = jnp.concatenate([sums_low[five:fifteen], sums_high[five:fifteen]]).reshape(20, shard, 128)
+    down_shard = jnp.stack(
+        [item[fifteen:].reshape(3, half_down, 128) for item in (sums_low, sums_high)], axis=1
+    ).reshape(3, shard_down, 128)
     shard_grads = (
-        lax.dynamic_slice_in_dim(summed[0], owner * w_qkv.shape[0], w_qkv.shape[0], 0),
-        lax.dynamic_slice_in_dim(summed[1], owner * w_out.shape[0], w_out.shape[0], 0),
-        lax.dynamic_slice_in_dim(summed[2], owner * w_gate_up.shape[0], w_gate_up.shape[0], 0),
-        lax.dynamic_slice_in_dim(summed[3], owner * w_down.shape[0], w_down.shape[0], 0),
-        lax.dynamic_slice_in_dim(summed[4], owner * gains.shape[1], gains.shape[1], 1),
+        unslab(first_shard[:9]),
+        unslab(second_shard[:3]),
+        unslab(second_shard[3:19]),
+        unslab(down_shard),
+        jnp.stack([first_shard[9, :, 0], second_shard[19, :, 0]]),
     )
     factor = clip_limit / jnp.maximum(grad_norm, clip_limit)
     masters = (w_qkv, w_out, w_gate_up, w_down, gains)
@@ -328,5 +490,5 @@
         P(None, "batch"),
     )
     return jax.shard_map(
-        per_device, mesh=mesh, in_specs=in_specs, out_specs=out_specs, check_vma=False
-    )
+        partial(per_device, mesh.shape["batch"]), mesh=mesh, in_specs=in_specs, out_specs=out_specs, check_vma=False
+    )

time: 616 us -> 383 us (0.62)
  blocking collectives: 206 us -> 0 us
  waiting for transfers between devices: 112 us -> 23.9 us
  starting transfers between devices: 0.25 us -> 51 us
  local copies, waits for them, and re-layouts: 16.1 us -> 35.6 us
  other arithmetic: 93 us -> 107 us
  matrix products: 164 us -> 151 us
  between operations: 19.6 us -> 9.43 us
    all_gather x4 -> x0, blocking collectives: 168 us -> none  [the longest x1 45.3 us: per_device(): lax.all_gather(w_down.astype(bf16), 'batch', axis=0, tiled=True)]
    psum x1 -> x0, waiting for transfers between devices: 112 us -> none  [per_device(): lax.psum((grad_attn_in, grad_attn_out, grad_ffn_in, grad_ffn_out, grad_ga...]
    ppermute x0 -> x38, starting transfers between devices: none -> 51 us  [the longest x30 48.3 us: permute_batch(): return lax.ppermute(value, 'batch', [(i, i ^ flip) for i in range(count)])]
    psum x1 -> x0, blocking collectives: 38.1 us -> none  [per_device(): lax.psum((grad_attn_in, grad_attn_out, grad_ffn_in, grad_ffn_out, grad_ga...]
    ppermute x0 -> x38, waiting for transfers between devices: none -> 23.9 us  [the longest x30 22.2 us: permute_batch(): return lax.ppermute(value, 'batch', [(i, i ^ flip) for i in range(count)])]
    transpose x0 -> x8, local copies, waits for them, and re-layouts: none -> 7.55 us  [the longest x3 4.72 us: unslab(): return stack.transpose(1, 0, 2).reshape(rows, count * 128)]
    reduce_sum x5 -> x2, other arithmetic: 8.33 us -> 1.27 us  [per_device(): squares = jnp.sum(first_sum * first_sum) + jnp.sum(second_sum * second_sum)]
    convert_element_type x1 -> x7, other arithmetic: 0.65 us -> 7.47 us  [the longest x1 3.36 us: per_device(): lax.dynamic_slice_in_dim(parts, (1 - core) * local_len, local_len, 2)]
  transfers between devices with their start and end apart: 6 -> 38, of which waited for: 1 -> 11; matrix products, arithmetic and copies ran while one was open for 22% -> 32% of each run, Pallas kernels for 0% -> 0%
where the time goes in v1:
time: 383 us; the launch traced here: 378 us
  matrix products  151 us (39%)
  other arithmetic  107 us (28%)
  starting transfers between devices  51 us (13%)
  local copies, waits for them, and re-layouts  35.6 us (9%)
  waiting for transfers between devices  23.9 us (6%)
  between operations  9.43 us (2%)
    ppermute x30, starting transfers between devices, permute_batch(): return lax.ppermute(value, 'batch', [(i, i ^ flip) for i in range(count)])  48.3 us
    convert_element_type x1, other arithmetic, per_device(): grad_scores = (attend * (grad_attend - jnp.sum(attend * grad_attend, axis...  40.7 us
    dot_general x1, matrix products, per_device(): jnp.einsum('rqhd,rkhd->rhqk', grad_mixed, values_all, preferred_element_t...  35.8 us
    reduce_sum x1, other arithmetic, per_device(): exp_total = jnp.sum(exp_scores, axis=-1, keepdims=True)  23 us
    ppermute x30, waiting for transfers between devices, permute_batch(): return lax.ppermute(value, 'batch', [(i, i ^ flip) for i in range(count)])  22.2 us
    dot_general x1, matrix products, scores_of(): jnp.einsum('rqhd,rkhd->rhqk', queries, keys_all, preferred_element_type=f32)  22 us
    dot_general x1, matrix products, per_device(): jnp.einsum('rhqk,rqhd->rkhd', attend.astype(bf16), grad_mixed, preferred_...  21.2 us
    dot_general x1, matrix products, per_device(): jnp.einsum('rhqk,rkhd->rqhd', attend_low, values_all, preferred_element_t...  20.2 us
  transfers between devices with their start and end apart: 38, of which 11 were waited for; matrix products, arithmetic and copies ran while one was open for 32% of the time, Pallas kernels for 0%

profile of v1, /device:TPU:0, one launch (start us, length us, event | category | flops | bytes accessed | tf_op | source)
XLA Modules:
  0.0 377.9 jit_solution(2928121479952308107)
XLA Ops:
  3.4 3.1 collective-permute-start.2
  12.2 3.5 collective-permute-start.9
  29.4 6.2 %collective-permute-done.13 = bf16[4,320,128]{2,1,0:T(8,128)(2,1)S(1)} collective-permute-done((bf16[4,320,128]{2,1,0:T(8,128)(2,1)S(1)}, bf16[4,320,128]{2,1,0:T(8,128)(2,1)S(1)}, u32[]{:S(2)}, u32[]{:S(2)}) %collective-permute-start.13) | collective-permute-done | bytes 327712 | tf_op jit(solution)/shard_map/ppermute | solution.py:83
  35.7 6.0 %collective-permute-done.12 = bf16[4,320,128]{2,1,0:T(8,128)(2,1)S(1)} collective-permute-done((bf16[4,320,128]{2,1,0:T(8,128)(2,1)S(1)}, bf16[4,320,128]{2,1,0:T(8,128)(2,1)S(1)}, u32[]{:S(2)}, u32[]{:S(2)}) %collective-permute-start.12) | collective-permute-done | bytes 327712 | tf_op jit(solution)/shard_map/ppermute | solution.py:83
  49.6 2.6 convolution_bitcast_fusion.1
  72.7 2.6 maximum_select_fusion
  77.3 22.0 %fusion.6 = (f32[6,1024]{1,0:T(8,128)S(1)}, f32[6,1024,2048]{2,1,0:T(8,128)}) fusion(pred[1024,2048]{1,0:T(8,128)(4,1)S(1)} %compare_and_fusion, bf16[2048,6,64]{0,2,1:T(8,128)(2,1)} %bitcast.465, bf16[1024,6,32]{0,2,1:T(8,128)(2,1)} %get-tuple-element.143, bf16[1024,6,32]{0,2,1:T(8,128)(2,1)} %get-tuple-element.142), kind=kOutput, calls=%fused_computation.11 | convolution fusion | flops 1649928192 | bytes 54812672 | tf_op jit(solution)/shard_map/rqhd,rkhd->rhqk/dot_general | solution.py:267
  99.4 23.0 %fusion = f32[6,1024]{1,0:T(8,128)S(1)} fusion(f32[6,1024]{1,0:T(8,128)S(1)} %get-tuple-element.184, f32[6,1024,2048]{2,1,0:T(8,128)} %get-tuple-element.185, pred[1024,2048]{1,0:T(8,128)(4,1)S(1)} %compare_and_fusion), kind=kLoop, calls=%fused_computation.6 | loop fusion | flops 50325504 | bytes 52477952 | tf_op jit(solution)/shard_map/reduce_sum | solution.py:275
  122.4 20.2 %fusion.46 = bf16[6,64,1024]{2,1,0:T(8,128)(2,1)S(1)} fusion(bf16[2048,6,64]{0,2,1:T(8,128)(2,1)} %bitcast.463, f32[6,1024]{1,0:T(8,128)S(1)} %fusion, f32[6,1024]{1,0:T(8,128)S(1)} %get-tuple-element.184, f32[6,1024,2048]{2,1,0:T(8,128)} %get-tuple-element.185, pred[1024,2048]{1,0:T(8,128)(4,1)S(1)} %compare_and_fusion), kind=kOutput, calls=%fused_computation.93 | convolution fusion | flops 1673920512 | bytes 54837248 | tf_op jit(solution)/shard_map/rhqk,rkhd->rqhd/dot_general | solution.py:278
  147.2 4.5 %fusion.23 = (bf16[1024,1024]{1,0:T(8,128)(2,1)S(1)}, bf16[1024,1024]{1,0:T(8,128)(2,1)S(1)}, bf16[1,1024,1024]{2,1,0:T(8,128)(2,1)}) fusion(f32[1,1024,2048]{2,1,0:T(8,128)S(1)} %convolution_bitcast_fusion, bf16[128,8,3,128]{3,2,1,0:T(4,128)(2,1)S(1)} %bitcast.502, bf16[1,1024,384]{1,2,0:T(8,128)(2,1)S(1)} %copy-done.37), kind=kOutput, calls=%fused_computation.52 | convolution fusion | flops 822083584 | bytes 16252928 | tf_op jit(solution)/shard_map/rtd,fd->rtf/dot_general | solution.py:295
  158.4 21.2 %fusion.2 = f32[6,64,2048]{2,1,0:T(8,128)} fusion(bf16[1024,6,64]{0,2,1:T(8,128)(2,1)S(1)} %bitcast.480, f32[6,1024]{1,0:T(8,128)S(1)} %log_add_fusion, f32[6,1024,2048]{2,1,0:T(8,128)} %get-tuple-element.185, pred[1024,2048]{1,0:T(8,128)(4,1)S(1)} %compare_and_fusion), kind=kOutput, calls=%fused_computation.8 | convolution fusion | flops 1660944384 | bytes 56385536 | tf_op jit(solution)/shard_map/rhqk,rqhd->rkhd/dot_general | solution.py:320
  179.6 35.8 %multiply_reduce_fusion = (f32[6,1024]{1,0:T(8,128)S(1)}, f32[6,1024,2048]{2,1,0:T(8,128)}) fusion(f32[6,1024]{1,0:T(8,128)S(1)} %log_add_fusion, f32[6,1024,2048]{2,1,0:T(8,128)} %get-tuple-element.185, pred[1024,2048]{1,0:T(8,128)(4,1)S(1)} %compare_and_fusion, bf16[1024,6,64]{0,2,1:T(8,128)(2,1)} %bitcast.481, bf16[2048,6,64]{0,2,1:T(8,128)(2,1)} %bitcast.464), kind=kOutput, calls=%fused_computation.1 | convolution fusion | flops 1673521152 | bytes 105168896 | tf_op jit(solution)/shard_map/rqhd,rkhd->rhqk/dot_general | solution.py:308
  215.4 6.4 %copy.148 = bf16[2048,1024]{1,0:T(8,128)(2,1)} copy(bf16[2048,1024]{0,1:T(8,128)(2,1)} %fusion.16) | data formatting | bytes 8388608 | tf_op jit(solution)/shard_map/rtd,rte->de/dot_general | solution.py:299
  221.8 4.4 %convolution_bitcast_fusion.2 = f32[16,384,128]{2,1,0:T(8,128)S(1)} fusion(bf16[16,128,1024]{2,1,0:T(8,128)(2,1)} %bitcast.475, f32[1,1024,384]{1,2,0:T(8,128)} %copy-done, f32[384]{0:T(512)S(1)} %reshape.820, f32[1024]{0:T(1024)S(1)} %add_rsqrt_fusion), kind=kOutput, calls=%fused_computation.55 | convolution fusion | flops 1611792384 | bytes 8918528 | tf_op jit(solution)/shard_map/rtd,rte->de/dot_general | solution.py:299
  234.0 40.7 %multiply_convert_fusion = bf16[6,1024,2048]{2,1,0:T(8,128)(2,1)} fusion(f32[6,1024,2048]{2,1,0:T(8,128)} %get-tuple-element.190, f32[6,1024]{1,0:T(8,128)S(1)} %get-tuple-element.189, f32[6,1024]{1,0:T(8,128)S(1)} %log_add_fusion, f32[6,1024,2048]{2,1,0:T(8,128)} %get-tuple-element.185, pred[1024,2048]{1,0:T(8,128)(4,1)S(1)} %compare_and_fusion), kind=kLoop, calls=%fused_computation | loop fusion | flops 75497472 | bytes 127975424 | tf_op jit(solution)/shard_map/convert_element_type | solution.py:311
  274.7 14.4 %convolution_multiply_fusion = f32[6,64,2048]{2,1,0:T(8,128)} fusion(bf16[6,1024,2048]{2,1,0:T(8,128)(2,1)} %multiply_convert_fusion, bf16[1024,6,32]{0,2,1:T(8,128)(2,1)S(1)} %copy-done.29, bf16[1024,6,32]{0,2,1:T(8,128)(2,1)S(1)} %copy-done.28), kind=kOutput, calls=%fused_computation.38 | convolution fusion | flops 1612972032 | bytes 29097984 | tf_op jit(solution)/shard_map/rhqk,rqhd->rkhd/dot_general | solution.py:317
  291.4 3.4 fusion.13
  295.2 14.2 %multiply_bitcast_fusion = f32[1,1024,6,64]{1,3,2,0:T(8,128)} fusion(bf16[2048,6,64]{0,2,1:T(8,128)(2,1)} %bitcast.466, bf16[6,1024,2048]{2,1,0:T(8,128)(2,1)} %multiply_convert_fusion), kind=kOutput, calls=%fused_computation.86 | convolution fusion | flops 1611005952 | bytes 28311552 | tf_op jit(solution)/shard_map/rhqk,rkhd->rqhd/dot_general | solution.py:313
  309.4 2.9 convert_add_fusion.1
  331.7 3.0 collective-permute-start.29
  339.8 4.0 %collective-permute-done.28 = bf16[1,336,128]{2,1,0:T(8,128)(2,1)S(1)} collective-permute-done((bf16[1,336,128]{2,1,0:T(8,128)(2,1)S(1)}, bf16[1,336,128]{2,1,0:T(8,128)(2,1)S(1)}, u32[]{:S(2)}, u32[]{:S(2)}) %collective-permute-start.28) | collective-permute-done | bytes 86048 | tf_op jit(solution)/shard_map/ppermute | solution.py:83
  355.9 2.7 collective-permute-start.31
  361.3 3.9 %collective-permute-start.36 = (f32[1,1]{1,0:T(1,128)}, f32[1,1]{1,0:T(1,128)}, u32[]{:S(2)}, u32[]{:S(2)}) collective-permute-start(f32[1,1]{1,0:T(1,128)} %add.315), channel_id=1, source_target_pairs={{0,24},{2,26},{4,28},{6,30},{8,16},{10,18},{12,20},{14,22},{16,8},... | collective-permute-start | bytes 20 | tf_op jit(solution)/shard_map/ppermute | solution.py:83
  366.5 3.1 collective-permute-start.34
  (356 shorter events, 114.6 us)
Async XLA Ops:
  3.4 15.1 %collective-permute-start.2 = (bf16[1,128,128]{2,1,0:T(8,128)(2,1)S(1)}, bf16[1,128,128]{2,1,0:T(8,128)(2,1)S(1)}, u32[]{:S(2)}, u32[]{:S(2)}) collective-permute-start(bf16[1,128,128]{2,1,0:T(8,128)(2,1)S(1)} %pad_bitcast_fusion.3), channel_id=1, source_target_pairs={{0,8},{2,10},{4,12},{6,14},{8,0},{10,2},{12,4},{14,6},{16,24},{18,... | collective-permute-start | bytes 98312 | tf_op jit(solution)/shard_map/ppermute | solution.py:83
  6.5 12.1 %collective-permute-start.1 = (bf16[1,128,128]{2,1,0:T(8,128)(2,1)S(1)}, bf16[1,128,128]{2,1,0:T(8,128)(2,1)S(1)}, u32[]{:S(2)}, u32[]{:S(2)}) collective-permute-start(bf16[1,128,128]{2,1,0:T(8,128)(2,1)S(1)} %pad_bitcast_fusion.3), channel_id=1, source_target_pairs={{0,16},{2,18},{4,20},{6,22},{8,24},{10,26},{12,28},{14,30},{16,0},... | collective-permute-start | bytes 98312 | tf_op jit(solution)/shard_map/ppermute | solution.py:83
  9.1 9.5 %collective-permute-start = (bf16[1,128,128]{2,1,0:T(8,128)(2,1)S(1)}, bf16[1,128,128]{2,1,0:T(8,128)(2,1)S(1)}, u32[]{:S(2)}, u32[]{:S(2)}) collective-permute-start(bf16[1,128,128]{2,1,0:T(8,128)(2,1)S(1)} %pad_bitcast_fusion.3), channel_id=1, source_target_pairs={{0,24},{2,26},{4,28},{6,30},{8,16},{10,18},{12,20},{14,22},{16,8},... | collective-permute-start | bytes 98312 | tf_op jit(solution)/shard_map/ppermute | solution.py:83
  11.2 10.7 %collective-permute-start.10 = (bf16[1,320,128]{2,1,0:T(8,128)(2,1)S(1)}, bf16[1,320,128]{2,1,0:T(8,128)(2,1)S(1)}, u32[]{:S(2)}, u32[]{:S(2)}) collective-permute-start(bf16[1,320,128]{2,1,0:T(8,128)(2,1)S(1)} %pad_bitcast_fusion.2), channel_id=1, source_target_pairs={{0,8},{2,10},{4,12},{6,14},{8,0},{10,2},{12,4},{14,6},{16,24},{18,... | collective-permute-start | bytes 245768 | tf_op jit(solution)/shard_map/ppermute | solution.py:83
  12.2 10.0 %collective-permute-start.9 = (bf16[1,320,128]{2,1,0:T(8,128)(2,1)S(1)}, bf16[1,320,128]{2,1,0:T(8,128)(2,1)S(1)}, u32[]{:S(2)}, u32[]{:S(2)}) collective-permute-start(bf16[1,320,128]{2,1,0:T(8,128)(2,1)S(1)} %pad_bitcast_fusion.2), channel_id=1, source_target_pairs={{0,16},{2,18},{4,20},{6,22},{8,24},{10,26},{12,28},{14,30},{16,0},... | collective-permute-start | bytes 245768 | tf_op jit(solution)/shard_map/ppermute | solution.py:83
  18.7 9.4 %collective-permute-start.5 = (bf16[4,128,128]{2,1,0:T(8,128)(2,1)S(1)}, bf16[4,128,128]{2,1,0:T(8,128)(2,1)S(1)}, u32[]{:S(2)}, u32[]{:S(2)}) collective-permute-start(bf16[4,128,128]{2,1,0:T(8,128)(2,1)S(1)} %maximum_bitcast_fusion.3), channel_id=1, source_target_pairs={{0,2},{2,0},{4,6},{6,4},{8,10},{10,8},{12,14},{14,12},{16,18},{18,... | collective-permute-start | bytes 393224 | tf_op jit(solution)/shard_map/ppermute | solution.py:83
  24.9 10.7 %collective-permute-start.13 = (bf16[4,320,128]{2,1,0:T(8,128)(2,1)S(1)}, bf16[4,320,128]{2,1,0:T(8,128)(2,1)S(1)}, u32[]{:S(2)}, u32[]{:S(2)}) collective-permute-start(bf16[4,320,128]{2,1,0:T(8,128)(2,1)S(1)} %maximum_bitcast_fusion.1), channel_id=1, source_target_pairs={{0,2},{2,0},{4,6},{6,4},{8,10},{10,8},{12,14},{14,12},{16,18},{18,... | collective-permute-start | bytes 983048 | tf_op jit(solution)/shard_map/ppermute | solution.py:83
  26.5 15.1 %collective-permute-start.12 = (bf16[4,320,128]{2,1,0:T(8,128)(2,1)S(1)}, bf16[4,320,128]{2,1,0:T(8,128)(2,1)S(1)}, u32[]{:S(2)}, u32[]{:S(2)}) collective-permute-start(bf16[4,320,128]{2,1,0:T(8,128)(2,1)S(1)} %maximum_bitcast_fusion.1), channel_id=1, source_target_pairs={{0,4},{2,6},{4,0},{6,2},{8,12},{10,14},{12,8},{14,10},{16,20},{18,... | collective-permute-start | bytes 983048 | tf_op jit(solution)/shard_map/ppermute | solution.py:83
  28.0 13.6 %collective-permute-start.11 = (bf16[4,320,128]{2,1,0:T(8,128)(2,1)S(1)}, bf16[4,320,128]{2,1,0:T(8,128)(2,1)S(1)}, u32[]{:S(2)}, u32[]{:S(2)}) collective-permute-start(bf16[4,320,128]{2,1,0:T(8,128)(2,1)S(1)} %maximum_bitcast_fusion.1), channel_id=1, source_target_pairs={{0,6},{2,4},{4,2},{6,0},{8,14},{10,12},{12,10},{14,8},{16,22},{18,... | collective-permute-start | bytes 983048 | tf_op jit(solution)/shard_map/ppermute | solution.py:83
  29.4 13.9 %collective-permute-start.6 = (bf16[16,128,128]{2,1,0:T(8,128)(2,1)S(1)}, bf16[16,128,128]{2,1,0:T(8,128)(2,1)S(1)}, u32[]{:S(2)}, u32[]{:S(2)}) collective-permute-start(bf16[16,128,128]{2,1,0:T(8,128)(2,1)S(1)} %bitcast.471), channel_id=1, source_target_pairs={{0,1},{1,0},{2,3},{3,2},{4,5},{5,4},{6,7},{7,6},{8,9},{9,8},{10,11... | collective-permute-start | bytes 1572872 | tf_op jit(solution)/shard_map/ppermute | solution.py:87
  43.2 18.3 %collective-permute-start.14 = (bf16[16,320,128]{2,1,0:T(8,128)(2,1)}, bf16[16,320,128]{2,1,0:T(8,128)(2,1)}, u32[]{:S(2)}, u32[]{:S(2)}) collective-permute-start(bf16[16,320,128]{2,1,0:T(8,128)(2,1)} %bitcast.65), channel_id=1, source_target_pairs={{0,1},{1,0},{2,3},{3,2},{4,5},{5,4},{6,7},{7,6},{8,9},{9,8},{10,11... | collective-permute-start | bytes 3932168 | tf_op jit(solution)/shard_map/ppermute | solution.py:87
  56.4 16.3 %collective-permute-start.7 = (bf16[2,1,1024,384]{2,3,1,0:T(8,128)(2,1)}, bf16[2,1,1024,384]{2,3,1,0:T(8,128)(2,1)}, u32[]{:S(2)}, u32[]{:S(2)}) collective-permute-start(bf16[2,1,1024,384]{2,3,1,0:T(8,128)(2,1)} %pad_maximum_fusion.8), channel_id=1, source_target_pairs={{0,1},{1,0},{2,3},{3,2},{4,5},{5,4},{6,7},{7,6},{8,9},{9,8},{10,11... | collective-permute-start | bytes 4718600 | tf_op jit(solution)/shard_map/ppermute | solution.py:87
  234.0 75.4 %collective-permute-start.23 = (bf16[16,336,128]{2,1,0:T(8,128)(2,1)}, bf16[16,336,128]{2,1,0:T(8,128)(2,1)}, u32[]{:S(2)}, u32[]{:S(2)}) collective-permute-start(bf16[16,336,128]{2,1,0:T(8,128)(2,1)} %select_convert_fusion), channel_id=1, source_target_pairs={{0,1},{1,0},{2,3},{3,2},{4,5},{5,4},{6,7},{7,6},{8,9},{9,8},{10,11... | collective-permute-start | bytes 4128776 | tf_op jit(solution)/shard_map/ppermute | solution.py:87
  294.7 21.3 %collective-permute-start.15 = (bf16[2,1,1024,384]{2,3,1,0:T(8,128)(2,1)}, bf16[2,1,1024,384]{2,3,1,0:T(8,128)(2,1)}, u32[]{:S(2)}, u32[]{:S(2)}) collective-permute-start(bf16[2,1,1024,384]{2,3,1,0:T(8,128)(2,1)} %fusion.13), channel_id=1, source_target_pairs={{0,1},{1,0},{2,3},{3,2},{4,5},{5,4},{6,7},{7,6},{8,9},{9,8},{10,11... | collective-permute-start | bytes 4718600 | tf_op jit(solution)/shard_map/ppermute | solution.py:87
  312.5 15.4 %collective-permute-start.24 = (bf16[4,336,128]{2,1,0:T(8,128)(2,1)S(1)}, bf16[4,336,128]{2,1,0:T(8,128)(2,1)S(1)}, u32[]{:S(2)}, u32[]{:S(2)}) collective-permute-start(bf16[4,336,128]{2,1,0:T(8,128)(2,1)S(1)} %get-tuple-element.133), channel_id=1, source_target_pairs={{0,2},{2,0},{4,6},{6,4},{8,10},{10,8},{12,14},{14,12},{16,18},{18,... | collective-permute-start | bytes 1032200 | tf_op jit(solution)/shard_map/ppermute | solution.py:83
  313.3 16.9 %collective-permute-start.25 = (bf16[4,336,128]{2,1,0:T(8,128)(2,1)S(1)}, bf16[4,336,128]{2,1,0:T(8,128)(2,1)S(1)}, u32[]{:S(2)}, u32[]{:S(2)}) collective-permute-start(bf16[4,336,128]{2,1,0:T(8,128)(2,1)S(1)} %get-tuple-element.134), channel_id=1, source_target_pairs={{0,4},{2,6},{4,0},{6,2},{8,12},{10,14},{12,8},{14,10},{16,20},{18,... | collective-permute-start | bytes 1032200 | tf_op jit(solution)/shard_map/ppermute | solution.py:83
  313.8 17.2 %collective-permute-start.26 = (bf16[4,336,128]{2,1,0:T(8,128)(2,1)S(1)}, bf16[4,336,128]{2,1,0:T(8,128)(2,1)S(1)}, u32[]{:S(2)}, u32[]{:S(2)}) collective-permute-start(bf16[4,336,128]{2,1,0:T(8,128)(2,1)S(1)} %get-tuple-element.135), channel_id=1, source_target_pairs={{0,6},{2,4},{4,2},{6,0},{8,14},{10,12},{12,10},{14,8},{16,22},{18,... | collective-permute-start | bytes 1032200 | tf_op jit(solution)/shard_map/ppermute | solution.py:83
  326.6 8.1 %collective-permute-start.17 = (bf16[4,120,128]{2,1,0:T(8,128)(2,1)S(1)}, bf16[4,120,128]{2,1,0:T(8,128)(2,1)S(1)}, u32[]{:S(2)}, u32[]{:S(2)}) collective-permute-start(bf16[4,120,128]{2,1,0:T(8,128)(2,1)S(1)} %get-tuple-element.151), channel_id=1, source_target_pairs={{0,2},{2,0},{4,6},{6,4},{8,10},{10,8},{12,14},{14,12},{16,18},{18,... | collective-permute-start | bytes 368648 | tf_op jit(solution)/shard_map/ppermute | solution.py:83
  331.2 8.1 %collective-permute-start.27 = (bf16[1,336,128]{2,1,0:T(8,128)(2,1)S(1)}, bf16[1,336,128]{2,1,0:T(8,128)(2,1)S(1)}, u32[]{:S(2)}, u32[]{:S(2)}) collective-permute-start(bf16[1,336,128]{2,1,0:T(8,128)(2,1)S(1)} %get-tuple-element.154), channel_id=1, source_target_pairs={{0,8},{2,10},{4,12},{6,14},{8,0},{10,2},{12,4},{14,6},{16,24},{18,... | collective-permute-start | bytes 258056 | tf_op jit(solution)/shard_map/ppermute | solution.py:83
  334.7 9.1 %collective-permute-start.28 = (bf16[1,336,128]{2,1,0:T(8,128)(2,1)S(1)}, bf16[1,336,128]{2,1,0:T(8,128)(2,1)S(1)}, u32[]{:S(2)}, u32[]{:S(2)}) collective-permute-start(bf16[1,336,128]{2,1,0:T(8,128)(2,1)S(1)} %get-tuple-element.156), channel_id=1, source_target_pairs={{0,16},{2,18},{4,20},{6,22},{8,24},{10,26},{12,28},{14,30},{16,0},... | collective-permute-start | bytes 258056 | tf_op jit(solution)/shard_map/ppermute | solution.py:83
  335.8 8.6 %collective-permute-start.20 = (bf16[1,120,128]{2,1,0:T(8,128)(2,1)S(1)}, bf16[1,120,128]{2,1,0:T(8,128)(2,1)S(1)}, u32[]{:S(2)}, u32[]{:S(2)}) collective-permute-start(bf16[1,120,128]{2,1,0:T(8,128)(2,1)S(1)} %get-tuple-element.170), channel_id=1, source_target_pairs={{0,8},{2,10},{4,12},{6,14},{8,0},{10,2},{12,4},{14,6},{16,24},{18,... | collective-permute-start | bytes 92168 | tf_op jit(solution)/shard_map/ppermute | solution.py:83
  345.4 26.4 %collective-permute-start.37 = (f32[456,128]{1,0:T(8,128)S(1)}, f32[456,128]{1,0:T(8,128)S(1)}, u32[]{:S(2)}, u32[]{:S(2)}) collective-permute-start(f32[456,128]{1,0:T(8,128)S(1)} %pad_maximum_fusion.20), channel_id=1, source_target_pairs={{0,1},{1,0},{2,3},{3,2},{4,5},{5,4},{6,7},{7,6},{8,9},{9,8},{10,11... | collective-permute-start | bytes 700424 | tf_op jit(solution)/shard_map/ppermute | solution.py:87
  351.2 8.9 %collective-permute-start.33 = (f32[1,1]{1,0:T(1,128)}, f32[1,1]{1,0:T(1,128)}, u32[]{:S(2)}, u32[]{:S(2)}) collective-permute-start(f32[1,1]{1,0:T(1,128)} %add.312), channel_id=1, source_target_pairs={{0,6},{2,4},{4,2},{6,0},{8,14},{10,12},{12,10},{14,8},{16,22},{18,... | collective-permute-start | bytes 20 | tf_op jit(solution)/shard_map/ppermute | solution.py:83
  361.3 9.3 %collective-permute-start.36 = (f32[1,1]{1,0:T(1,128)}, f32[1,1]{1,0:T(1,128)}, u32[]{:S(2)}, u32[]{:S(2)}) collective-permute-start(f32[1,1]{1,0:T(1,128)} %add.315), channel_id=1, source_target_pairs={{0,24},{2,26},{4,28},{6,30},{8,16},{10,18},{12,20},{14,22},{16,8},... | collective-permute-start | bytes 20 | tf_op jit(solution)/shard_map/ppermute | solution.py:83
  (84 other events, 819.2 us)

commit v2 on v0

v2 whole, which is shorter than its diff:
```python
import math
from functools import partial

import jax
import jax.numpy as jnp
from jax import lax
from jax.experimental import pallas as pl
from jax.experimental.pallas import tpu as pltpu
from jax.sharding import PartitionSpec as P

D = 384
FF = 1024
HEADS = 6
HD = 64
STEP = 3


norm_eps = 1e-06
beta_one = 0.5
beta_two = 0.5
adam_eps = 1e-08
decay_rate = 0.1
clip_limit = 1.0
masked_score = -1e30


def adam_update(master, grad, first, second, rate, decay):
    first_new = beta_one * first + (1.0 - beta_one) * grad
    second_new = beta_two * second + (1.0 - beta_two) * grad * grad
    direction = (
        first_new
        / (1.0 - beta_one**STEP)
        / (jnp.sqrt(second_new / (1.0 - beta_two**STEP)) + adam_eps)
    )
    return (first_new, second_new, master - rate * (direction + decay * master))


def bit_groups(count):
    groups = []
    low, bits = 0, count.bit_length() - 1
    while low < bits:
        width = min(2, bits - low)
        groups.append((low, width))
        low += width
    return groups


def permute_batch(value, flip, count):
    return lax.ppermute(value, "batch", [(i, i ^ flip) for i in range(count)])


def swap_tm(value):
    return lax.ppermute(value, "tm", [(0, 1), (1, 0)])


def scatter_sum(parts, owner, count):
    held = parts
    rest = parts.shape[1:]
    for low, width in bit_groups(count):
        fan = 1 << width
        view = held.reshape((-1, fan) + rest)
        mine = (owner >> low) & (fan - 1)
        total = lax.dynamic_index_in_dim(view, mine, 1, keepdims=False).astype(jnp.float32)
        got = []
        for k in range(1, fan):
            piece = lax.dynamic_index_in_dim(view, mine ^ k, 1, keepdims=False)
            got.append(permute_batch(piece.astype(jnp.bfloat16), k << low, count))
        for item in got:
            total = total + item.astype(jnp.float32)
        held = total
    return held.reshape(rest)


def sum_all(value, count):
    value = value + swap_tm(value)
    for low, width in bit_groups(count):
        pieces = [value] + [permute_batch(value, k << low, count) for k in range(1, 1 << width)]
        while len(pieces) > 1:
            pieces = [pieces[i] + pieces[i + 1] for i in range(0, len(pieces), 2)]
        value = pieces[0]
    return value


def slabs(matrix):
    rows, columns = matrix.shape
    return matrix.reshape(rows, columns // 128, 128).transpose(1, 0, 2)


def unslab(stack):
    count, rows, _ = stack.shape
    return stack.transpose(1, 0, 2).reshape(rows, count * 128)


bf16 = jnp.bfloat16
f32 = jnp.float32
BLOCK = 256
LANES = 128
VMEM_LIMIT = 56 * 2**20
NN = (((1,), (0,)), ((), ()))
NT = (((1,), (1,)), ((), ()))
TN = (((0,), (0,)), ((), ()))


def dot(left, right, dims):
    return lax.dot_general(left, right, dims, preferred_element_type=f32)


def cost(flops, moved):
    return pl.CostEstimate(flops=flops, bytes_accessed=moved, transcendentals=0)


def block(start, size=BLOCK):
    return pl.ds(pl.multiple_of(start * size, size), size)


def row_scale(values):
    return lax.rsqrt(jnp.mean(values * values, axis=-1, keepdims=True) + norm_eps)


def norm_back(grad_normed, values, scale):
    return scale * grad_normed - values * scale * scale * scale * jnp.mean(
        grad_normed * values, axis=-1, keepdims=True
    )


def split_three(values):
    high = values.astype(bf16)
    rest = values - high.astype(f32)
    middle = rest.astype(bf16)
    return high, middle, (rest - middle.astype(f32)).astype(bf16)


def swap_halves(pair):
    lane = lax.broadcasted_iota(jnp.int32, pair.shape, 1)
    return jnp.where(lane % HD < HD // 2, pltpu.roll(pair, 96, 1), pltpu.roll(pair, 32, 1))


def gather_relative(chunk, count):
    held = chunk[None]
    for low, width in reversed(bit_groups(count)):
        pieces = [held] + [permute_batch(held, k << low, count) for k in range(1, 1 << width)]
        held = jnp.concatenate(pieces, axis=0)
    return held


def relative_places(owner, count):
    flips = jnp.arange(count, dtype=jnp.int32) ^ owner
    place = jnp.zeros((count,), jnp.int32)
    scale = 1
    for low, width in reversed(bit_groups(count)):
        place = place + ((flips >> low) & ((1 << width) - 1)) * scale
        scale <<= width
    return place


def assemble_kernel(count, number, shard, down, scalars, mine, other, *refs):
    outs, stage = refs[:-1], refs[-1]
    core = scalars[0]
    for source, half in ((mine, core), (other, 1 - core)):

        def one(device, carry, source=source, half=half):
            chunk = source[scalars[1 + device]].astype(f32)
            for i in range(number):
                stage[half * number + i, pl.ds(pl.multiple_of(device * shard, 8), shard), :] = chunk[
                    i * shard : (i + 1) * shard
                ]
            if down:
                at = number * shard
                for i in range(3):
                    outs[2][
                        pl.ds(pl.multiple_of(device * 2 * down + half * down, 16), down),
                        i * LANES : (i + 1) * LANES,
                    ] = chunk[at + i * down : at + (i + 1) * down].astype(bf16)
            return carry

        lax.fori_loop(0, count, one, 0)
    if down:
        for i in range(3):
            outs[0][:, i * LANES : (i + 1) * LANES] = stage[i].astype(bf16)
        for i in range(16):
            outs[1][:, i * LANES : (i + 1) * LANES] = stage[3 + i].astype(bf16)
    else:
        for i in range(9):
            outs[0][:, i * LANES : (i + 1) * LANES] = stage[i].astype(bf16)
        outs[1][...] = stage[9].T[:8]


def assemble(count, core, places, mine, number, shard, down):
    other = swap_tm(mine)
    if down:
        shapes = [((D, D), bf16), ((D, 2 * FF), bf16), ((FF, D), bf16)]
    else:
        shapes = [((D, 3 * D), bf16), ((8, D), f32)]
    if shard % 8 == 0 and down % 16 == 0:
        spec = pl.BlockSpec(memory_space=pltpu.VMEM)
        return pl.pallas_call(
            partial(assemble_kernel, count, number, shard, down),
            out_shape=[jax.ShapeDtypeStruct(*item) for item in shapes],
            in_specs=[pl.BlockSpec(memory_space=pltpu.SMEM), spec, spec],
            out_specs=[spec] * len(shapes),
            scratch_shapes=[pltpu.VMEM((2 * number, D, LANES), f32)],
            compiler_params=pltpu.CompilerParams(vmem_limit_bytes=VMEM_LIMIT),
            name="assemble_ffn" if down else "assemble_qkv",
        )(jnp.concatenate([core[None], places]), mine, other)
    low = jnp.take(jnp.where(core == 0, mine, other), places, axis=0)
    high = jnp.take(jnp.where(core == 0, other, mine), places, axis=0)

    def part(source):
        return (
            source[:, : number * shard]
            .reshape(count, number, shard, LANES)
            .transpose(1, 0, 2, 3)
            .reshape(number, D, LANES)
        )

    stack = jnp.concatenate([part(low), part(high)], axis=0)
    if not down:
        return unslab(stack[:9]), stack[9].T[:8].astype(f32)
    downs = [
        item[:, number * shard : number * shard + 3 * down].reshape(count, 3, down, LANES)
        for item in (low, high)
    ]
    w_down = jnp.stack(downs, axis=1).transpose(0, 1, 3, 2, 4).reshape(FF, D)
    return unslab(stack[:3]), unslab(stack[3:19]), w_down


def pack_kernel(count, number, shard, down, scalars, *refs):
    if down:
        grads, (keep, give, give_stage, column) = refs[:4], refs[4:]
        slab_refs = [(grads[0], i) for i in range(3)] + [(grads[1], i) for i in range(16)]
        gain = grads[3]
    else:
        grads, (keep, give, give_stage, column) = refs[:2], refs[2:]
        slab_refs = [(grads[0], i) for i in range(9)]
        gain = grads[1]
    column[...] = jnp.concatenate([gain[...], jnp.zeros((LANES - 8, D), f32)], axis=0).T
    slab_refs.append((column, 0))
    core = scalars[0]

    def copy(low_to, high_to):
        def one(device, carry):
            rows = pl.ds(pl.multiple_of(device * shard, 8), shard)
            for half, target in ((0, low_to), (1, high_to)):
                for i in range(number):
                    source, at = slab_refs[half * number + i]
                    target[device, i * shard : (i + 1) * shard, :] = source[
                        rows, at * LANES : (at + 1) * LANES
                    ]
                if down:
                    rows_down = pl.ds(pl.multiple_of(device * 2 * down + half * down, 8), down)
                    for i in range(3):
                        start = number * shard + i * down
                        target[device, start : start + down, :] = grads[2][
                            rows_down, i * LANES : (i + 1) * LANES
                        ]
            return carry

        lax.fori_loop(0, count, one, 0)

    @pl.when(core == 0)
    def _():
        copy(keep, give_stage)

    @pl.when(core == 1)
    def _():
        copy(give_stage, keep)

    give[...] = give_stage[...].astype(bf16)


def pack(count, core, grads, number, shard, down):
    rows = number * shard + 3 * down
    if shard % 8 == 0 and down % 8 == 0:
        spec = pl.BlockSpec(memory_space=pltpu.VMEM)
        return pl.pallas_call(
            partial(pack_kernel, count, number, shard, down),
            out_shape=[
                jax.ShapeDtypeStruct((count, rows, LANES), f32),
                jax.ShapeDtypeStruct((count, rows, LANES), bf16),
            ],
            in_specs=[pl.BlockSpec(memory_space=pltpu.SMEM)] + [spec] * len(grads),
            out_specs=[spec] * 2,
            scratch_shapes=[
                pltpu.VMEM((count, rows, LANES), f32),
                pltpu.VMEM((D, LANES), f32),
            ],
            compiler_params=pltpu.CompilerParams(vmem_limit_bytes=VMEM_LIMIT),
            name="pack_ffn" if down else "pack_qkv",
        )(core[None], *grads)
    column = jnp.pad(grads[-1][:1].T, ((0, 0), (0, LANES - 1)))[None]
    stack = jnp.concatenate([slabs(item) for item in (grads[:2] if down else grads[:1])] + [column])

    def by_device(part):
        return (
            part.reshape(number, count, shard, LANES)
            .transpose(1, 0, 2, 3)
            .reshape(count, number * shard, LANES)
        )

    halves = [by_device(stack[:number]), by_device(stack[number:])]
    if down:
        downs = (
            slabs(grads[2])
            .reshape(3, count, 2, down, LANES)
            .transpose(2, 1, 0, 3, 4)
            .reshape(2, count, 3 * down, LANES)
        )
        halves = [jnp.concatenate([halves[i], downs[i]], axis=1) for i in range(2)]
    return (
        jnp.where(core == 0, halves[0], halves[1]),
        jnp.where(core == 0, halves[1], halves[0]).astype(bf16),
    )


def project_kernel(
    own, there, cosine, sine, key_aux, query_aux, w, gains, qa, ka, va, kt, vt
):
    step = pl.program_id(0)
    is_own = step < pl.num_programs(0) // 2
    x = jnp.where(is_own, own[...], there[...]).astype(f32)
    normed = (x * row_scale(x) * gains[0:1, :]).astype(bf16)
    cos, sin = cosine[...], sine[...]
    low = lax.broadcasted_iota(jnp.int32, (BLOCK, LANES), 1) < HD
    key_extra = key_aux[...].astype(f32)
    query_extra = query_aux[...].astype(f32)
    lane = lax.broadcasted_iota(jnp.int32, (BLOCK, LANES), 1)
    value_extra = jnp.where((lane >= HD) & (lane < HD + 3), 1.0, 0.0)
    ones = jnp.ones((8, BLOCK), bf16)

    @pl.when(is_own)
    def _():
        for pair in range(HEADS // 2):
            z = dot(normed, w[:, pair * LANES : (pair + 1) * LANES], NN)
            z = (z * cos + swap_halves(z) * sin).astype(bf16).astype(f32) * HD**-0.5
            qa[2 * pair] = jnp.where(low, z, query_extra).astype(bf16)
            qa[2 * pair + 1] = jnp.where(low, pltpu.roll(z, HD, 1), query_extra).astype(bf16)

    for pair in range(HEADS // 2):
        z = dot(normed, w[:, D + pair * LANES : D + (pair + 1) * LANES], NN)
        z = z * cos + swap_halves(z) * sin
        ka[2 * pair] = jnp.where(low, z, key_extra).astype(bf16)
        ka[2 * pair + 1] = jnp.where(low, pltpu.roll(z, HD, 1), key_extra).astype(bf16)
        turned = z.T.astype(bf16)
        kt[2 * pair] = turned[:HD]
        kt[2 * pair + 1] = turned[HD:]
    for pair in range(HEADS // 2):
        z = dot(normed, w[:, 2 * D + pair * LANES : 2 * D + (pair + 1) * LANES], NN)
        va[2 * pair] = jnp.where(low, z, value_extra).astype(bf16)
        va[2 * pair + 1] = jnp.where(low, pltpu.roll(z, HD, 1), value_extra).astype(bf16)
        turned = z.T.astype(bf16)
        vt[2 * pair, :HD] = turned[:HD]
        vt[2 * pair + 1, :HD] = turned[HD:]
        vt[2 * pair, HD:] = ones
        vt[2 * pair + 1, HD:] = ones


def project(own, there, cosine, sine, key_aux, query_aux, w, gains):
    length = own.shape[0]
    steps = length // BLOCK
    whole = 2 * length
    first = lambda i: (jnp.minimum(i, steps - 1), 0)
    last = lambda i: (jnp.maximum(i - steps, 0), 0)
    return pl.pallas_call(
        project_kernel,
        out_shape=[
            jax.ShapeDtypeStruct((HEADS, length, LANES), bf16),
            jax.ShapeDtypeStruct((HEADS, whole, LANES), bf16),
            jax.ShapeDtypeStruct((HEADS, whole, LANES), bf16),
            jax.ShapeDtypeStruct((HEADS, HD, whole), bf16),
            jax.ShapeDtypeStruct((HEADS, HD + 8, whole), bf16),
        ],
        grid=(2 * steps,),
        in_specs=[
            pl.BlockSpec((BLOCK, D), first),
            pl.BlockSpec((BLOCK, D), last),
            pl.BlockSpec((BLOCK, LANES), lambda i: (i, 0)),
            pl.BlockSpec((BLOCK, LANES), lambda i: (i, 0)),
            pl.BlockSpec((BLOCK, LANES), lambda i: (i, 0)),
            pl.BlockSpec((BLOCK, LANES), first),
            pl.BlockSpec((D, 3 * D), lambda i: (0, 0)),
            pl.BlockSpec((8, D), lambda i: (0, 0)),
        ],
        out_specs=[
            pl.BlockSpec((HEADS, BLOCK, LANES), lambda i: (0, jnp.minimum(i, steps - 1), 0)),
            pl.BlockSpec((HEADS, BLOCK, LANES), lambda i: (0, i, 0)),
            pl.BlockSpec((HEADS, BLOCK, LANES), lambda i: (0, i, 0)),
            pl.BlockSpec((HEADS, HD, BLOCK), lambda i: (0, 0, i)),
            pl.BlockSpec((HEADS, HD + 8, BLOCK), lambda i: (0, 0, i)),
        ],
        compiler_params=pltpu.CompilerParams(vmem_limit_bytes=VMEM_LIMIT),
        cost_estimate=cost(2 * whole * D * 3 * D, 16 * 2**20),
        name="project",
    )(own, there, cosine, sine, key_aux, query_aux, w, gains)


def key_block(ranges, step, n):
    return jnp.where(n < ranges[1, step], ranges[0, step] + n, ranges[2, step] + n)


def attend_kernel(ranges, qa, ka, vt, mixed, exact, qb, total, peak):
    step = pl.program_id(0)
    peak[...] = jnp.full((HEADS, 8, BLOCK), -3e38, f32)
    total[...] = jnp.zeros_like(total)

    def body(n, carry):
        rows = block(key_block(ranges, step, n))
        scores = [dot(ka[h, rows, :], qa[h], NT) for h in range(HEADS)]
        weights = []
        for h in range(HEADS):
            old = peak[h][:1]
            new = jnp.maximum(old, jnp.max(scores[h], axis=0, keepdims=True))
            weights.append((jnp.exp(scores[h] - new).astype(bf16), jnp.exp(old - new)))
            peak[h] = jnp.broadcast_to(new, (8, BLOCK))
        for h in range(HEADS):
            weight, shrink = weights[h]
            total[h] = total[h] * shrink + dot(vt[h, :, rows], weight, NN)
        return carry

    lax.fori_loop(0, ranges[3, step], body, 0)
    terms = []
    for h in range(HEADS):
        bottom = total[h][HD : HD + 1]
        terms.append(total[h][:HD] / bottom)
        logs = -(peak[h][:1] + jnp.log(bottom))
        for piece in split_three(logs):
            terms.append(piece.astype(f32))
    for pair in range(HEADS // 2):
        both = jnp.concatenate([terms[8 * pair], terms[8 * pair + 4]], axis=0).T
        mixed[:, pair * LANES : (pair + 1) * LANES] = both.astype(bf16)
        exact[:, pair * LANES : (pair + 1) * LANES] = both
    pieces = [terms[4 * h + 1 + i] for h in range(HEADS) for i in range(3)]
    table = jnp.concatenate(
        [jnp.zeros((HD + 8, BLOCK), f32)]
        + pieces
        + [jnp.zeros((LANES - HD - 8 - 3 * HEADS, BLOCK), f32)],
        axis=0,
    ).T
    lane = lax.broadcasted_iota(jnp.int32, (BLOCK, LANES), 1)
    for h in range(HEADS):
        start = HD + 8 + 3 * h
        qb[h] = jnp.where(
            (lane >= start) & (lane < start + 3), table, qa[h].astype(f32)
        ).astype(bf16)


def attend(ranges, qa, ka, vt):
    heads, length, _ = qa.shape
    whole = ka.shape[1]
    return pl.pallas_call(
        attend_kernel,
        out_shape=[
            jax.ShapeDtypeStruct((length, D), bf16),
            jax.ShapeDtypeStruct((length, D), f32),
            jax.ShapeDtypeStruct(qa.shape, bf16),
        ],
        grid_spec=pltpu.PrefetchScalarGridSpec(
            num_scalar_prefetch=1,
            grid=(length // BLOCK,),
            in_specs=[
                pl.BlockSpec((heads, BLOCK, LANES), lambda i, *_: (0, i, 0)),
                pl.BlockSpec((heads, whole, LANES), lambda i, *_: (0, 0, 0)),
                pl.BlockSpec((heads, HD + 8, whole), lambda i, *_: (0, 0, 0)),
            ],
            out_specs=[
                pl.BlockSpec((BLOCK, D), lambda i, *_: (i, 0)),
                pl.BlockSpec((BLOCK, D), lambda i, *_: (i, 0)),
                pl.BlockSpec((heads, BLOCK, LANES), lambda i, *_: (0, i, 0)),
            ],
            scratch_shapes=[
                pltpu.VMEM((heads, HD + 8, BLOCK), f32),
                pltpu.VMEM((heads, 8, BLOCK), f32),
            ],
        ),
        compiler_params=pltpu.CompilerParams(vmem_limit_bytes=VMEM_LIMIT),
        cost_estimate=cost(12 * 10**9, 12 * 2**20),
        name="attend",
    )(ranges, qa, ka, vt)


def attend_back_kernel(ranges, qb, ka, da, va, kt, dq, own, there, sums, acc):
    step = pl.program_id(0)
    heads = qb.shape[0]

    @pl.when(step == 0)
    def _():
        sums[...] = jnp.zeros_like(sums)

    acc[...] = jnp.zeros_like(acc)
    zero = jnp.zeros((BLOCK, HD), bf16)

    def body(n, carry):
        rows = block(key_block(ranges, step, n))
        first = [
            (dot(ka[h, rows, :], qb[h], NT), dot(va[h, rows, :], da[h], NT)) for h in range(heads)
        ]
        second = []
        for scores, grads in first:
            probs = jnp.exp(scores)
            second.append((probs.astype(bf16), (probs * grads).astype(bf16)))
        for h in range(heads):
            probs_low, grads_low = second[h]
            grad_side = jnp.concatenate([da[h][:, :HD], zero], axis=1)
            query_side = jnp.concatenate([zero, qb[h][:, :HD]], axis=1)
            sums[h, rows, :] += dot(probs_low, grad_side, NN) + dot(grads_low, query_side, NN)
            acc[h] += dot(kt[h, :, rows], grads_low, NN)
        return carry

    lax.fori_loop(0, ranges[3, step], body, 0)
    dq[...] = acc[...]

    @pl.when(step == pl.num_programs(0) - 1)
    def _():
        length = own.shape[1]
        own[...] = sums[:, :length, :]
        there[...] = sums[:, length:, :].astype(bf16)


def attend_back(group, heads, ranges, qb, ka, da, va, kt):
    length, whole = qb.shape[1], ka.shape[1]
    return pl.pallas_call(
        attend_back_kernel,
        out_shape=[
            jax.ShapeDtypeStruct((heads, HD, length), f32),
            jax.ShapeDtypeStruct((heads, length, LANES), f32),
            jax.ShapeDtypeStruct((heads, whole - length, LANES), bf16),
        ],
        grid_spec=pltpu.PrefetchScalarGridSpec(
            num_scalar_prefetch=1,
            grid=(length // BLOCK,),
            in_specs=[
                pl.BlockSpec((heads, BLOCK, LANES), lambda i, *_: (group, i, 0)),
                pl.BlockSpec((heads, whole, LANES), lambda i, *_: (group, 0, 0)),
                pl.BlockSpec((heads, BLOCK, LANES), lambda i, *_: (group, i, 0)),
                pl.BlockSpec((heads, whole, LANES), lambda i, *_: (group, 0, 0)),
                pl.BlockSpec((heads, HD, whole), lambda i, *_: (group, 0, 0)),
            ],
            out_specs=[
                pl.BlockSpec((heads, HD, BLOCK), lambda i, *_: (0, 0, i)),
                pl.BlockSpec((heads, length, LANES), lambda i, *_: (0, 0, 0)),
                pl.BlockSpec((heads, whole - length, LANES), lambda i, *_: (0, 0, 0)),
            ],
            scratch_shapes=[
                pltpu.VMEM((heads, whole, LANES), f32),
                pltpu.VMEM((heads, HD, BLOCK), f32),
            ],
        ),
        compiler_params=pltpu.CompilerParams(vmem_limit_bytes=VMEM_LIMIT),
        cost_estimate=cost(12 * 10**9, 8 * 2**20),
        name="attend_back",
    )(ranges, qb, ka, da, va, kt)


def feed_kernel(
    own, mixed, exact, cotangent, keep, wo, wgu, wd, gains,
    result, grad_middle, da, g_out, g_gate_up, g_down, g_gain,
    normed_all, low_all, hidden_all, up_all, middle_all,
):
    gain = gains[1:2, :]
    g_gain[...] = jnp.zeros_like(g_gain)
    chunks = FF // BLOCK
    lane = lax.broadcasted_iota(jnp.int32, (BLOCK, LANES), 1)

    def body(i, carry):
        rows = block(i)
        x = own[rows, :].astype(f32)
        middle = x + dot(mixed[rows, :], wo[...], NN)
        scale = row_scale(middle)
        normed = (middle * scale * gain).astype(bf16)
        normed_all[rows, :] = normed
        kept = keep[rows, :]
        upstream = cotangent[rows, :].astype(f32) * kept
        up_low = upstream.astype(bf16)
        up_all[rows, :] = up_low
        gates = [dot(normed, wgu[:, c * BLOCK : (c + 1) * BLOCK], NN) for c in range(chunks)]
        ups = [
            dot(normed, wgu[:, FF + c * BLOCK : FF + (c + 1) * BLOCK], NN) for c in range(chunks)
        ]
        hiddens = [dot(up_low, wd[c * BLOCK : (c + 1) * BLOCK, :], NT) for c in range(chunks)]
        for c in range(chunks):
            gate, up, grad_hidden = gates[c], ups[c], hiddens[c]
            sig = 1.0 / (1.0 + jnp.exp(-gate))
            silu = gate * sig
            hidden_all[rows, c * BLOCK : (c + 1) * BLOCK] = (silu * up).astype(bf16)
            low_all[rows, FF + c * BLOCK : FF + (c + 1) * BLOCK] = (grad_hidden * silu).astype(bf16)
            low_all[rows, c * BLOCK : (c + 1) * BLOCK] = (
                grad_hidden * up * (sig + silu * (1.0 - sig))
            ).astype(bf16)
        ffn = dot(hidden_all[rows, :], wd[...], NN)
        result[rows, :] = (kept * (middle + ffn)).astype(bf16)
        grad_normed = dot(low_all[rows, :], wgu[...], NT)
        g_gain[0:1, :] += jnp.sum(grad_normed * middle * scale, axis=0, keepdims=True)
        grad = upstream + norm_back(grad_normed * gain, middle, scale)
        grad_middle[rows, :] = grad
        low = grad.astype(bf16)
        middle_all[rows, :] = low
        grad_mixed = dot(low, wo[...], NT).astype(bf16).astype(f32)
        products = grad_mixed * exact[rows, :]
        for h in range(HEADS):
            pair = h // 2
            head = grad_mixed[:, pair * LANES : (pair + 1) * LANES]
            product = products[:, pair * LANES : (pair + 1) * LANES]
            mine = (lane < HD) if h % 2 == 0 else (lane >= HD)
            delta = -jnp.sum(jnp.where(mine, product, 0.0), axis=1, keepdims=True)
            if h % 2:
                head = pltpu.roll(head, HD, 1)
            high, mid, last = split_three(delta)
            extra = jnp.where(
                lane == HD,
                high.astype(f32),
                jnp.where(
                    lane == HD + 1,
                    mid.astype(f32),
                    jnp.where(lane == HD + 2, last.astype(f32), 0.0),
                ),
            )
            da[h, rows, :] = jnp.where(lane < HD, head, extra).astype(bf16)
        return carry

    lax.fori_loop(0, own.shape[0] // BLOCK, body, 0)
    g_out[...] = dot(mixed[...], middle_all[...], TN)
    for c in range(2 * FF // 512):
        g_gate_up[:, c * 512 : (c + 1) * 512] = dot(
            normed_all[...], low_all[:, c * 512 : (c + 1) * 512], TN
        )
    for c in range(chunks):
        g_down[c * BLOCK : (c + 1) * BLOCK, :] = dot(
            hidden_all[:, c * BLOCK : (c + 1) * BLOCK], up_all[...], TN
        )


def feed(own, mixed, exact, cotangent, keep, wo, wgu, wd, gains):
    length = own.shape[0]
    spec = pl.BlockSpec(memory_space=pltpu.VMEM)
    return pl.pallas_call(
        feed_kernel,
        out_shape=[
            jax.ShapeDtypeStruct((length, D), bf16),
            jax.ShapeDtypeStruct((length, D), f32),
            jax.ShapeDtypeStruct((HEADS, length, LANES), bf16),
            jax.ShapeDtypeStruct((D, D), f32),
            jax.ShapeDtypeStruct((D, 2 * FF), f32),
            jax.ShapeDtypeStruct((FF, D), f32),
            jax.ShapeDtypeStruct((8, D), f32),
        ],
        in_specs=[spec] * 9,
        out_specs=[spec] * 7,
        scratch_shapes=[
            pltpu.VMEM((length, D), bf16),
            pltpu.VMEM((length, 2 * FF), bf16),
            pltpu.VMEM((length, FF), bf16),
            pltpu.VMEM((length, D), bf16),
            pltpu.VMEM((length, D), bf16),
        ],
        compiler_params=pltpu.CompilerParams(vmem_limit_bytes=VMEM_LIMIT),
        cost_estimate=cost(10 * 10**9, 16 * 2**20),
        name="feed",
    )(own, mixed, exact, cotangent, keep, wo, wgu, wd, gains)


def project_back_kernel(
    own, grad_middle, cosine, sine, w, gains, *refs
):
    groups = (len(refs) - 5) // 3
    dqs, owns, recvs = refs[:groups], refs[groups : 2 * groups], refs[2 * groups : 3 * groups]
    grad_tokens, g_qkv, g_gain, normed_all, low_all = refs[3 * groups :]
    heads = HEADS // groups
    step = pl.program_id(0)
    rows = block(step)
    cos, sin = cosine[...], -sine[...]
    low = lax.broadcasted_iota(jnp.int32, (BLOCK, LANES), 1) < HD
    for pair in range(HEADS // 2):
        spots = [((2 * pair + i) // heads, (2 * pair + i) % heads) for i in range(2)]
        z = jnp.concatenate([dqs[g][h] for g, h in spots], axis=0).T * HD**-0.5
        low_all[rows, pair * LANES : (pair + 1) * LANES] = (
            z * cos + swap_halves(z) * sin
        ).astype(bf16)
        first, second = [owns[g][h] + recvs[g][h].astype(f32) for g, h in spots]
        z = jnp.where(low, pltpu.roll(first, HD, 1), second)
        low_all[rows, D + pair * LANES : D + (pair + 1) * LANES] = (
            z * cos + swap_halves(z) * sin
        ).astype(bf16)
        low_all[rows, 2 * D + pair * LANES : 2 * D + (pair + 1) * LANES] = jnp.where(
            low, first, pltpu.roll(second, HD, 1)
        ).astype(bf16)
    x = own[...].astype(f32)
    scale = row_scale(x)
    gain = gains[0:1, :]
    normed_all[rows, :] = (x * scale * gain).astype(bf16)
    grad_normed = dot(low_all[rows, :], w[...], NT)
    sums = jnp.sum(grad_normed * x * scale, axis=0, keepdims=True)

    @pl.when(step == 0)
    def _():
        g_gain[...] = jnp.zeros_like(g_gain)

    g_gain[0:1, :] += sums
    grad_tokens[...] = (grad_middle[...] + norm_back(grad_normed * gain, x, scale)).astype(bf16)

    @pl.when(step == pl.num_programs(0) - 1)
    def _():
        for c in range(3):
            g_qkv[:, c * D : (c + 1) * D] = dot(
                normed_all[...], low_all[:, c * D : (c + 1) * D], TN
            )


def project_back(own, grad_middle, cosine, sine, w, gains, dqs, owns, recvs):
    length = own.shape[0]
    heads = dqs[0].shape[0]
    groups = len(dqs)
    return pl.pallas_call(
        project_back_kernel,
        out_shape=[
            jax.ShapeDtypeStruct((length, D), bf16),
            jax.ShapeDtypeStruct((D, 3 * D), f32),
            jax.ShapeDtypeStruct((8, D), f32),
        ],
        grid=(length // BLOCK,),
        in_specs=[
            pl.BlockSpec((BLOCK, D), lambda i: (i, 0)),
            pl.BlockSpec((BLOCK, D), lambda i: (i, 0)),
            pl.BlockSpec((BLOCK, LANES), lambda i: (i, 0)),
            pl.BlockSpec((BLOCK, LANES), lambda i: (i, 0)),
            pl.BlockSpec((D, 3 * D), lambda i: (0, 0)),
            pl.BlockSpec((8, D), lambda i: (0, 0)),
        ]
        + [pl.BlockSpec((heads, HD, BLOCK), lambda i: (0, 0, i))] * groups
        + [pl.BlockSpec((heads, BLOCK, LANES), lambda i: (0, i, 0))] * (2 * groups),
        out_specs=[
            pl.BlockSpec((BLOCK, D), lambda i: (i, 0)),
            pl.BlockSpec((D, 3 * D), lambda i: (0, 0)),
            pl.BlockSpec((8, D), lambda i: (0, 0)),
        ],
        scratch_shapes=[pltpu.VMEM((length, D), bf16), pltpu.VMEM((length, 3 * D), bf16)],
        compiler_params=pltpu.CompilerParams(vmem_limit_bytes=VMEM_LIMIT),
        cost_estimate=cost(4 * 10**9, 10 * 2**20),
        name="project_back",
    )(own, grad_middle, cosine, sine, w, gains, *dqs, *owns, *recvs)


def per_device(
    count,
    tokens,
    cotangent,
    sample_ids,
    pad_flags,
    offsets,
    w_qkv,
    w_out,
    w_gate_up,
    w_down,
    gains,
    m_qkv,
    m_out,
    m_gate_up,
    m_down,
    m_gains,
    v_qkv,
    v_out,
    v_gate_up,
    v_down,
    v_gains,
):
    owner = lax.axis_index("batch")
    core = lax.axis_index("tm")
    shard = w_qkv.shape[0]
    down = w_down.shape[0] // 2
    own = tokens[0]
    length = own.shape[0]
    places = relative_places(owner, count)

    gain_slab = jnp.pad(gains.T, ((0, 0), (0, LANES - 2)))[None]
    first = jnp.concatenate([slabs(w_qkv), gain_slab]).reshape(2, 5 * shard, LANES)
    first = jnp.where(core == 0, first[0], first[1]).astype(bf16)
    first_rows = -(-first.shape[0] // 16) * 16
    first = jnp.pad(first, ((0, first_rows - first.shape[0]), (0, 0)))
    second = jnp.concatenate(
        [slabs(w_out), slabs(w_gate_up), jnp.zeros((1, shard, LANES), f32)]
    ).reshape(2, 10 * shard, LANES)
    downs = slabs(w_down).reshape(3, 2, down, LANES).transpose(1, 0, 2, 3)
    downs = downs.reshape(2, 3 * down, LANES)
    second = jnp.where(
        core == 0,
        jnp.concatenate([second[0], downs[0]]),
        jnp.concatenate([second[1], downs[1]]),
    ).astype(bf16)
    first_held = gather_relative(first, count)
    second_held = gather_relative(second, count)
    there = swap_tm(own)

    def rotate(row):
        both = row[0].reshape(2, length)
        return jnp.where(core == 0, both, both[::-1]).reshape(-1)

    starts = jnp.stack([core, 1 - core]) * length
    place = (starts[:, None] + jnp.arange(length, dtype=jnp.int32)).reshape(-1)
    positions = (place + rotate(offsets)).astype(f32)
    frequency = jnp.exp(
        jnp.arange(HD // 2, dtype=f32) * (-2.0 * math.log(10000.0) / HD)
    )
    angles = positions[:, None] * frequency
    cosine = jnp.tile(jnp.cos(angles), (1, 4))
    sine = jnp.sin(angles)
    sine = jnp.tile(jnp.concatenate([-sine, sine], axis=1), (1, 2))
    classes = 2 * sample_ids[0] + pad_flags[0]
    turned = 2 * rotate(sample_ids) + rotate(pad_flags)
    lane = jnp.arange(LANES, dtype=jnp.int32)[None, :]
    is_class = (lane >= HD) & (lane < HD + 8)
    same = turned[:, None] == lane - HD
    is_log = (lane >= HD + 8) & (lane < HD + 8 + 3 * HEADS)
    key_aux = jnp.where((is_class & same) | is_log, 1.0, 0.0).astype(bf16)
    query_aux = jnp.where(is_class & ~same[:length], masked_score, 0.0).astype(bf16)
    own_classes = turned[:length].reshape(-1, BLOCK)
    low_key = jnp.sum(classes[None, :] < own_classes[:, :1], axis=1)
    high_key = jnp.sum(classes[None, :] <= own_classes[:, -1:], axis=1)
    bounds = []
    for part in range(2):
        low_part = jnp.clip(low_key - starts[part], 0, length)
        high_part = jnp.clip(high_key - starts[part], 0, length)
        bounds.append((low_part // BLOCK, (high_part + BLOCK - 1) // BLOCK))
    near = jnp.maximum(bounds[0][1] - bounds[0][0], 0)
    far = jnp.maximum(bounds[1][1] - bounds[1][0], 0)
    ranges = jnp.stack(
        [bounds[0][0], near, bounds[1][0] + length // BLOCK - near, near + far]
    ).astype(jnp.int32)
    keep = (turned[:length, None] % 2 == 0).astype(f32)

    attn_in, gain_pair = assemble(count, core, places, first_held, 5, shard, 0)
    qa, ka, va, kt, vt = project(
        own, there, cosine, sine, key_aux, query_aux, attn_in, gain_pair
    )
    mixed, exact, qb = attend(ranges, qa, ka, vt)
    attn_out, ffn_in, ffn_out = assemble(count, core, places, second_held, 10, shard, down)
    result, grad_middle, da, g_out, g_gate_up, g_down, g_gain_two = feed(
        own, mixed, exact, cotangent[0], keep, attn_out, ffn_in, ffn_out, gain_pair
    )

    def reduce(kept, given):
        return scatter_sum(kept + swap_tm(given).astype(f32), owner, count)

    second_sum = reduce(
        *pack(count, core, (g_out, g_gate_up, g_down, g_gain_two), 10, shard, down)
    )
    dqs, owns, recvs = [], [], []
    for group in range(2):
        dq, kept, given = attend_back(group, HEADS // 2, ranges, qb, ka, da, va, kt)
        dqs.append(dq)
        owns.append(kept)
        recvs.append(swap_tm(given))
    grad_tokens, g_qkv, g_gain_one = project_back(
        own, grad_middle, cosine, sine, attn_in, gain_pair, dqs, owns, recvs
    )
    first_sum = reduce(*pack(count, core, (g_qkv, g_gain_one), 5, shard, 0))

    squares = jnp.sum(first_sum * first_sum) + jnp.sum(second_sum * second_sum)
    grad_norm = jnp.sqrt(sum_all(squares.reshape(1, 1), count)[0, 0])
    sums = jnp.concatenate([first_sum, second_sum], axis=0)
    sums_there = swap_tm(sums)
    sums_low = jnp.where(core == 0, sums, sums_there)
    sums_high = jnp.where(core == 0, sums_there, sums)
    five, fifteen = 5 * shard, 15 * shard
    first_shard = jnp.concatenate([sums_low[:five], sums_high[:five]]).reshape(10, shard, LANES)
    second_shard = jnp.concatenate([sums_low[five:fifteen], sums_high[five:fifteen]])
    second_shard = second_shard.reshape(20, shard, LANES)
    down_shard = jnp.stack(
        [item[fifteen:].reshape(3, down, LANES) for item in (sums_low, sums_high)], axis=1
    ).reshape(3, 2 * down, LANES)
    shard_grads = (
        unslab(first_shard[:9]),
        unslab(second_shard[:3]),
        unslab(second_shard[3:19]),
        unslab(down_shard),
        jnp.stack([first_shard[9, :, 0], second_shard[19, :, 0]]),
    )
    factor = clip_limit / jnp.maximum(grad_norm, clip_limit)
    masters = (w_qkv, w_out, w_gate_up, w_down, gains)
    firsts = (m_qkv, m_out, m_gate_up, m_down, m_gains)
    seconds = (v_qkv, v_out, v_gate_up, v_down, v_gains)
    rates = (D ** (-0.5), 4.0 * D ** (-0.5), D ** (-0.5), FF ** (-0.5), 0.5)
    decays = (decay_rate, decay_rate, decay_rate, decay_rate, 0.0)
    updates = [
        adam_update(
            masters[i], factor * shard_grads[i], firsts[i], seconds[i], rates[i], decays[i]
        )
        for i in range(5)
    ]
    new_first, new_second, new_master = zip(*updates)
    copies = [item.astype(bf16) for item in new_master]
    return (
        result[None],
        grad_tokens[None],
        grad_norm,
        *new_first,
        *new_second,
        *new_master,
        *copies,
    )


def solution(mesh):
    in_specs = (
        P("batch", "tm", None),
        P("batch", "tm", None),
        P("batch", None),
        P("batch", None),
        P("batch", None),
        P("batch", None),
        P("batch", None),
        P("batch", None),
        P("batch", None),
        P(None, "batch"),
        P("batch", None),
        P("batch", None),
        P("batch", None),
        P("batch", None),
        P(None, "batch"),
        P("batch", None),
        P("batch", None),
        P("batch", None),
        P("batch", None),
        P(None, "batch"),
    )
    out_specs = (
        P("batch", "tm", None),
        P("batch", "tm", None),
        P(),
        P("batch", None),
        P("batch", None),
        P("batch", None),
        P("batch", None),
        P(None, "batch"),
        P("batch", None),
        P("batch", None),
        P("batch", None),
        P("batch", None),
        P(None, "batch"),
        P("batch", None),
        P("batch", None),
        P("batch", None),
        P("batch", None),
        P(None, "batch"),
        P("batch", None),
        P("batch", None),
        P("batch", None),
        P("batch", None),
        P(None, "batch"),
    )
    return jax.shard_map(
        partial(per_device, mesh.shape["batch"]), mesh=mesh, in_specs=in_specs, out_specs=out_specs, check_vma=False
    )
```

time: 616 us -> 249 us (0.40)
  blocking collectives: 206 us -> 0 us
  matrix products: 164 us -> 0 us
  Pallas kernels: 0 us -> 116 us
  waiting for transfers between devices: 112 us -> 33.6 us
  other arithmetic: 93 us -> 18 us
  starting transfers between devices: 0.25 us -> 54.8 us
  between operations: 19.6 us -> 8.36 us
    all_gather x4 -> x0, blocking collectives: 168 us -> none  [the longest x1 45.3 us: per_device(): lax.all_gather(w_down.astype(bf16), 'batch', axis=0, tiled=True)]
    dot_general x18 -> x0, matrix products: 164 us -> none  [the longest x1 35.6 us: per_device(): jnp.einsum('rqhd,rkhd->rhqk', grad_mixed, values_all, preferred_element_t...]
    pallas_call x0 -> x10, Pallas kernels: none -> 116 us  [the longest x2 35.6 us: attend_back(): pl.pallas_call(attend_back_kernel, out_shape=[jax.ShapeDtypeStruct((heads...]
    psum x1 -> x0, waiting for transfers between devices: 112 us -> none  [per_device(): lax.psum((grad_attn_in, grad_attn_out, grad_ffn_in, grad_ffn_out, grad_ga...]
    ppermute x0 -> x39, starting transfers between devices: none -> 54.8 us  [the longest x30 52.1 us: permute_batch(): return lax.ppermute(value, 'batch', [(i, i ^ flip) for i in range(count)])]
    convert_element_type x8 -> x4, other arithmetic: 42.9 us -> 2.02 us  [the longest x1 1.14 us: per_device(): key_aux = jnp.where(is_class & same | is_log, 1.0, 0.0).astype(bf16)]
    psum x1 -> x0, blocking collectives: 38.1 us -> none  [per_device(): lax.psum((grad_attn_in, grad_attn_out, grad_ffn_in, grad_ffn_out, grad_ga...]
    ppermute x0 -> x39, waiting for transfers between devices: none -> 33.6 us  [the longest x30 31.6 us: permute_batch(): return lax.ppermute(value, 'batch', [(i, i ^ flip) for i in range(count)])]
  transfers between devices with their start and end apart: 6 -> 39, of which waited for: 1 -> 13; matrix products, arithmetic and copies ran while one was open for 22% -> 9% of each run, Pallas kernels for 0% -> 22%
where the time goes in v2:
time: 249 us; the launch traced here: 248 us
  Pallas kernels  116 us (47%)
  starting transfers between devices  54.8 us (22%)
  waiting for transfers between devices  33.6 us (13%)
  other arithmetic  18 us (7%)
  local copies, waits for them, and re-layouts  17.2 us (7%)
  between operations  8.36 us (3%)
    ppermute x30, starting transfers between devices, permute_batch(): return lax.ppermute(value, 'batch', [(i, i ^ flip) for i in range(count)])  52.1 us
    pallas_call x2, Pallas kernels, attend_back(): pl.pallas_call(attend_back_kernel, out_shape=[jax.ShapeDtypeStruct((heads...  35.6 us
    ppermute x30, waiting for transfers between devices, permute_batch(): return lax.ppermute(value, 'batch', [(i, i ^ flip) for i in range(count)])  31.6 us
    pallas_call x1, Pallas kernels, attend(): pl.pallas_call(attend_kernel, out_shape=[jax.ShapeDtypeStruct((length, D)...  21.1 us
    pallas_call x1, Pallas kernels, feed(): pl.pallas_call(feed_kernel, out_shape=[jax.ShapeDtypeStruct((length, D),...  20.8 us
    pallas_call x1, Pallas kernels, project(): pl.pallas_call(project_kernel, out_shape=[jax.ShapeDtypeStruct((HEADS, le...  13.7 us
    pallas_call x1, Pallas kernels, project_back(): pl.pallas_call(project_back_kernel, out_shape=[jax.ShapeDtypeStruct((leng...  10.3 us
    pallas_call x2, Pallas kernels, pack(): pl.pallas_call(partial(pack_kernel, count, number, shard, down), out_shap...  7.93 us
  transfers between devices with their start and end apart: 39, of which 13 were waited for; matrix products, arithmetic and copies ran while one was open for 9% of the time, Pallas kernels for 22%

profile of v2, /device:TPU:0, one launch (start us, length us, event | category | flops | bytes accessed | tf_op | source)
XLA Modules:
  0.0 248.4 jit_solution(12892250647965221896)
XLA Ops:
  3.5 5.1 %collective-permute-start.10 = (bf16[1,336,128]{2,1,0:T(8,128)(2,1)S(1)}, bf16[1,336,128]{2,1,0:T(8,128)(2,1)S(1)}, u32[]{:S(2)}, u32[]{:S(2)}) collective-permute-start(bf16[1,336,128]{2,1,0:T(8,128)(2,1)S(1)} %get-tuple-element.118), channel_id=1, source_target_pairs={{0,24},{2,26},{4,28},{6,30},{8,16},{10,18},{12,20},{14,22},{16,8},... | collective-permute-start | bytes 258056 | tf_op jit(solution)/shard_map/ppermute | solution.py:49
  11.4 2.4 collective-permute-start.3
  43.7 4.4 %collective-permute-done.11 = bf16[4,336,128]{2,1,0:T(8,128)(2,1)S(1)} collective-permute-done((bf16[4,336,128]{2,1,0:T(8,128)(2,1)S(1)}, bf16[4,336,128]{2,1,0:T(8,128)(2,1)S(1)}, u32[]{:S(2)}, u32[]{:S(2)}) %collective-permute-start.11) | collective-permute-done | bytes 344096 | tf_op jit(solution)/shard_map/ppermute | solution.py:49
  48.1 7.9 %collective-permute-done.12 = bf16[4,336,128]{2,1,0:T(8,128)(2,1)S(1)} collective-permute-done((bf16[4,336,128]{2,1,0:T(8,128)(2,1)S(1)}, bf16[4,336,128]{2,1,0:T(8,128)(2,1)S(1)}, u32[]{:S(2)}, u32[]{:S(2)}) %collective-permute-start.12) | collective-permute-done | bytes 344096 | tf_op jit(solution)/shard_map/ppermute | solution.py:49
  57.8 2.6 %assemble_qkv.1 = (bf16[384,1152]{1,0:T(8,128)(2,1)}, f32[8,384]{1,0:T(8,128)}) custom-call(s32[17]{0:T(128)} %pad_add_fusion.1.scalars, bf16[16,128,128]{2,1,0:T(8,128)(2,1)} %copy-done.4, bf16[16,128,128]{2,1,0:T(8,128)(2,1)} %copy-done.5), custom_call_target="tpu_custom_call" | custom-call | tf_op jit(solution)/shard_map/assemble_qkv/pallas_call | solution.py:196
  61.3 13.7 %project.1 = (bf16[6,1024,128]{2,1,0:T(8,128)(2,1)}, bf16[6,2048,128]{2,1,0:T(8,128)(2,1)}, bf16[6,2048,128]{2,1,0:T(8,128)(2,1)}, bf16[6,64,2048]{2,1,0:T(8,128)(2,1)}, bf16[6,72,2048]{2,1,0:T(8,128)(2,1)}) custom-call(bf16[1024,384]{1,0:T(8,128)(2,1)} %bitcast.232, bf16[1024,384]{1,0:T(8,128)(2,1)} %copy-done.23, f32[2048,128]{1,0:T(8,128)} %copy.118.cosine, ...), custom_call_target="tpu_custom_call" | custom-call | flops 1811939328 | bytes 16777216 | tf_op jit(solution)/shard_map/project/pallas_call | solution.py:363
  75.0 21.1 %attend.1 = (bf16[1024,384]{1,0:T(8,128)(2,1)}, f32[1024,384]{1,0:T(8,128)}, bf16[6,1024,128]{2,1,0:T(8,128)(2,1)}) custom-call(s32[4,4]{1,0:T(4,128)} %pad_add_fusion.ranges, bf16[6,1024,128]{2,1,0:T(8,128)(2,1)} %get-tuple-element.58.qa, bf16[6,2048,128]{2,1,0:T(8,128)(2,1)} %get-tuple-element.59.ka, bf16[6,72,2048]{2,1,0:T(8,128)(2,1)} %get-tuple-element.60.vt), custom_call_target="tpu_custom_call" | custom-call | flops 12000000000 | bytes 12582912 | tf_op jit(solution)/shard_map/attend/pallas_call | solution.py:449
  97.3 4.3 %assemble_ffn.1 = (bf16[384,384]{1,0:T(8,128)(2,1)}, bf16[384,2048]{1,0:T(8,128)(2,1)}, bf16[1024,384]{1,0:T(8,128)(2,1)}) custom-call(s32[17]{0:T(128)} %pad_add_fusion.1.scalars, bf16[16,336,128]{2,1,0:T(8,128)(2,1)} %copy-done.1, bf16[16,336,128]{2,1,0:T(8,128)(2,1)} %copy-done.2), custom_call_target="tpu_custom_call" | custom-call | tf_op jit(solution)/shard_map/assemble_ffn/pallas_call | solution.py:196
  101.6 20.8 %feed.1 = (bf16[1024,384]{1,0:T(8,128)(2,1)}, f32[1024,384]{1,0:T(8,128)}, bf16[6,1024,128]{2,1,0:T(8,128)(2,1)}, f32[384,384]{1,0:T(8,128)}, f32[384,2048]{1,0:...) custom-call(bf16[1024,384]{1,0:T(8,128)(2,1)} %bitcast.233, bf16[1024,384]{1,0:T(8,128)(2,1)} %get-tuple-element.61.mixed, ...), custom_call_target="tpu_custom_call" | custom-call | flops 10000000000 | bytes 16777216 | tf_op jit(solution)/shard_map/feed/pallas_call | solution.py:634
  122.4 17.7 %attend_back.3 = (f32[3,64,1024]{2,1,0:T(8,128)}, f32[3,1024,128]{2,1,0:T(8,128)}, bf16[3,1024,128]{2,1,0:T(8,128)(2,1)}) custom-call(s32[4,4]{1,0:T(4,128)} %pad_add_fusion.ranges, bf16[6,1024,128]{2,1,0:T(8,128)(2,1)} %get-tuple-element.68.qb, bf16[6,2048,128]{2,1,0:T(8,128)(2,1)} %get-tuple-element.59.ka, bf16[6,1024,128]{2,1,0:T(8,128)(2,1)} %get-tuple-element.69.da, ...), custom_call_target="tpu_custom_call" | custom-call | flops 12000000000 | bytes 8388608 | tf_op jit(solution)/shard_map/attend_back/pallas_call | solution.py:520
  140.2 17.9 %attend_back.2 = (f32[3,64,1024]{2,1,0:T(8,128)}, f32[3,1024,128]{2,1,0:T(8,128)}, bf16[3,1024,128]{2,1,0:T(8,128)(2,1)}) custom-call(s32[4,4]{1,0:T(4,128)} %pad_add_fusion.ranges, bf16[6,1024,128]{2,1,0:T(8,128)(2,1)} %get-tuple-element.68.qb, bf16[6,2048,128]{2,1,0:T(8,128)(2,1)} %get-tuple-element.59.ka, bf16[6,1024,128]{2,1,0:T(8,128)(2,1)} %get-tuple-element.69.da, ...), custom_call_target="tpu_custom_call" | custom-call | flops 12000000000 | bytes 8388608 | tf_op jit(solution)/shard_map/attend_back/pallas_call | solution.py:520
  158.7 5.0 %pack_ffn.1 = (f32[16,336,128]{2,1,0:T(8,128)}, bf16[16,336,128]{2,1,0:T(8,128)(2,1)}) custom-call(s32[1]{0:T(128)} %bitcast.2.scalars, f32[384,384]{1,0:T(8,128)} %get-tuple-element.83.refs_0_, f32[384,2048]{1,0:T(8,128)} %get-tuple-element.84.refs_1_, f32[1024,384]{1,0:T(8,128)} %get-tuple-element.85.refs_2_, f32[8,384]{1,0:T(8,128)} %get-tuple-element.86.refs_3_), custom_call_target="tpu_custom_call" | custom-call | tf_op jit(solution)/shard_map/pack_ffn/pallas_call | solution.py:275
  165.2 10.3 %project_back.1 = (bf16[1024,384]{1,0:T(8,128)(2,1)}, f32[384,1152]{1,0:T(8,128)}, f32[8,384]{1,0:T(8,128)}) custom-call(bf16[1024,384]{1,0:T(8,128)(2,1)} %bitcast.234, f32[1024,384]{1,0:T(8,128)} %get-tuple-element.67.grad_middle, f32[2048,128]{1,0:T(8,128)} %copy.118.cosine, f32[2048,128]{1,0:T(8,128)} %copy.119.sine, ...), custom_call_target="tpu_custom_call" | custom-call | flops 4000000000 | bytes 10485760 | tf_op jit(solution)/shard_map/project_back/pallas_call | solution.py:711
  175.5 2.9 %pack_qkv.1 = (f32[16,120,128]{2,1,0:T(8,128)}, bf16[16,120,128]{2,1,0:T(8,128)(2,1)}) custom-call(s32[1]{0:T(128)} %bitcast.2.scalars, f32[384,1152]{1,0:T(8,128)} %get-tuple-element.79.refs_0_, f32[8,384]{1,0:T(8,128)} %get-tuple-element.80.refs_1_), custom_call_target="tpu_custom_call" | custom-call | tf_op jit(solution)/shard_map/pack_qkv/pallas_call | solution.py:275
  189.6 2.3 collective-permute-done.20
  195.5 2.8 %collective-permute-done.25 = bf16[4,336,128]{2,1,0:T(8,128)(2,1)S(1)} collective-permute-done((bf16[4,336,128]{2,1,0:T(8,128)(2,1)S(1)}, bf16[4,336,128]{2,1,0:T(8,128)(2,1)S(1)}, u32[]{:S(2)}, u32[]{:S(2)}) %collective-permute-start.25) | collective-permute-done | bytes 344096 | tf_op jit(solution)/shard_map/ppermute | solution.py:49
  198.3 2.9 %collective-permute-start.23 = (bf16[1,120,128]{2,1,0:T(8,128)(2,1)S(1)}, bf16[1,120,128]{2,1,0:T(8,128)(2,1)S(1)}, u32[]{:S(2)}, u32[]{:S(2)}) collective-permute-start(bf16[1,120,128]{2,1,0:T(8,128)(2,1)S(1)} %get-tuple-element.133), channel_id=1, source_target_pairs={{0,24},{2,26},{4,28},{6,30},{8,16},{10,18},{12,20},{14,22},{16,8},... | collective-permute-start | bytes 92168 | tf_op jit(solution)/shard_map/ppermute | solution.py:49
  201.2 2.9 %collective-permute-done.26 = bf16[4,336,128]{2,1,0:T(8,128)(2,1)S(1)} collective-permute-done((bf16[4,336,128]{2,1,0:T(8,128)(2,1)S(1)}, bf16[4,336,128]{2,1,0:T(8,128)(2,1)S(1)}, u32[]{:S(2)}, u32[]{:S(2)}) %collective-permute-start.26) | collective-permute-done | bytes 344096 | tf_op jit(solution)/shard_map/ppermute | solution.py:49
  211.3 5.2 %collective-permute-done.29 = bf16[1,336,128]{2,1,0:T(8,128)(2,1)S(1)} collective-permute-done((bf16[1,336,128]{2,1,0:T(8,128)(2,1)S(1)}, bf16[1,336,128]{2,1,0:T(8,128)(2,1)S(1)}, u32[]{:S(2)}, u32[]{:S(2)}) %collective-permute-start.29) | collective-permute-done | bytes 86048 | tf_op jit(solution)/shard_map/ppermute | solution.py:49
  222.5 2.4 collective-permute-start.34
  224.9 3.1 %collective-permute-start.32 = (f32[1,1]{1,0:T(1,128)}, f32[1,1]{1,0:T(1,128)}, u32[]{:S(2)}, u32[]{:S(2)}) collective-permute-start(f32[1,1]{1,0:T(1,128)} %add.391), channel_id=1, source_target_pairs={{0,2},{2,0},{4,6},{6,4},{8,10},{10,8},{12,14},{14,12},{16,18},{18,... | collective-permute-start | bytes 20 | tf_op jit(solution)/shard_map/ppermute | solution.py:49
  230.3 3.7 %collective-permute-start.36 = (f32[1,1]{1,0:T(1,128)}, f32[1,1]{1,0:T(1,128)}, u32[]{:S(2)}, u32[]{:S(2)}) collective-permute-start(f32[1,1]{1,0:T(1,128)} %add.394), channel_id=1, source_target_pairs={{0,16},{2,18},{4,20},{6,22},{8,24},{10,26},{12,28},{14,30},{16,0},... | collective-permute-start | bytes 20 | tf_op jit(solution)/shard_map/ppermute | solution.py:49
  234.1 2.8 %collective-permute-start.37 = (f32[1,1]{1,0:T(1,128)}, f32[1,1]{1,0:T(1,128)}, u32[]{:S(2)}, u32[]{:S(2)}) collective-permute-start(f32[1,1]{1,0:T(1,128)} %add.394), channel_id=1, source_target_pairs={{0,24},{2,26},{4,28},{6,30},{8,16},{10,18},{12,20},{14,22},{16,8},... | collective-permute-start | bytes 20 | tf_op jit(solution)/shard_map/ppermute | solution.py:49
  238.1 2.2 collective-permute-done.35
  (218 shorter events, 73.4 us)
Async XLA Ops:
  3.5 29.3 %collective-permute-start.10 = (bf16[1,336,128]{2,1,0:T(8,128)(2,1)S(1)}, bf16[1,336,128]{2,1,0:T(8,128)(2,1)S(1)}, u32[]{:S(2)}, u32[]{:S(2)}) collective-permute-start(bf16[1,336,128]{2,1,0:T(8,128)(2,1)S(1)} %get-tuple-element.118), channel_id=1, source_target_pairs={{0,24},{2,26},{4,28},{6,30},{8,16},{10,18},{12,20},{14,22},{16,8},... | collective-permute-start | bytes 258056 | tf_op jit(solution)/shard_map/ppermute | solution.py:49
  8.6 25.8 %collective-permute-start.8 = (bf16[1,336,128]{2,1,0:T(8,128)(2,1)S(1)}, bf16[1,336,128]{2,1,0:T(8,128)(2,1)}, u32[]{:S(2)}, u32[]{:S(2)}) collective-permute-start(bf16[1,336,128]{2,1,0:T(8,128)(2,1)S(1)} %get-tuple-element.118), channel_id=1, source_target_pairs={{0,8},{2,10},{4,12},{6,14},{8,0},{10,2},{12,4},{14,6},{16,24},{18,... | collective-permute-start | bytes 258056 | tf_op jit(solution)/shard_map/ppermute | solution.py:49
  9.4 18.9 %collective-permute-start.1 = (bf16[1,128,128]{2,1,0:T(8,128)(2,1)}, bf16[1,128,128]{2,1,0:T(8,128)(2,1)S(1)}, u32[]{:S(2)}, u32[]{:S(2)}) collective-permute-start(bf16[1,128,128]{2,1,0:T(8,128)(2,1)} %pad_bitcast_fusion), channel_id=1, source_target_pairs={{0,8},{2,10},{4,12},{6,14},{8,0},{10,2},{12,4},{14,6},{16,24},{18,... | collective-permute-start | bytes 98312 | tf_op jit(solution)/shard_map/ppermute | solution.py:49
  11.4 17.5 %collective-permute-start.2 = (bf16[1,128,128]{2,1,0:T(8,128)(2,1)}, bf16[1,128,128]{2,1,0:T(8,128)(2,1)}, u32[]{:S(2)}, u32[]{:S(2)}) collective-permute-start(bf16[1,128,128]{2,1,0:T(8,128)(2,1)} %pad_bitcast_fusion), channel_id=1, source_target_pairs={{0,16},{2,18},{4,20},{6,22},{8,24},{10,26},{12,28},{14,30},{16,0},... | collective-permute-start | bytes 98312 | tf_op jit(solution)/shard_map/ppermute | solution.py:49
  11.4 17.5 %collective-permute-start.3 = (bf16[1,128,128]{2,1,0:T(8,128)(2,1)}, bf16[1,128,128]{2,1,0:T(8,128)(2,1)}, u32[]{:S(2)}, u32[]{:S(2)}) collective-permute-start(bf16[1,128,128]{2,1,0:T(8,128)(2,1)} %pad_bitcast_fusion), channel_id=1, source_target_pairs={{0,24},{2,26},{4,28},{6,30},{8,16},{10,18},{12,20},{14,22},{16,8},... | collective-permute-start | bytes 98312 | tf_op jit(solution)/shard_map/ppermute | solution.py:49
  28.9 31.5 %collective-permute-start = (bf16[1024,384]{1,0:T(8,128)(2,1)}, bf16[1024,384]{1,0:T(8,128)(2,1)S(1)}, u32[]{:S(2)}, u32[]{:S(2)}) collective-permute-start(bf16[1024,384]{1,0:T(8,128)(2,1)} %bitcast.231), channel_id=1, source_target_pairs={{0,1},{1,0},{2,3},{3,2},{4,5},{5,4},{6,7},{7,6},{8,9},{9,8},{10,11... | collective-permute-start | bytes 2359304 | tf_op jit(solution)/shard_map/ppermute | solution.py:53
  29.7 8.6 %collective-permute-start.4 = (bf16[4,128,128]{2,1,0:T(8,128)(2,1)S(1)}, bf16[4,128,128]{2,1,0:T(8,128)(2,1)S(1)}, u32[]{:S(2)}, u32[]{:S(2)}) collective-permute-start(bf16[4,128,128]{2,1,0:T(8,128)(2,1)S(1)} %pad_maximum_fusion.5), channel_id=1, source_target_pairs={{0,2},{2,0},{4,6},{6,4},{8,10},{10,8},{12,14},{14,12},{16,18},{18,... | collective-permute-start | bytes 393224 | tf_op jit(solution)/shard_map/ppermute | solution.py:49
  32.8 8.6 %collective-permute-start.5 = (bf16[4,128,128]{2,1,0:T(8,128)(2,1)S(1)}, bf16[4,128,128]{2,1,0:T(8,128)(2,1)S(1)}, u32[]{:S(2)}, u32[]{:S(2)}) collective-permute-start(bf16[4,128,128]{2,1,0:T(8,128)(2,1)S(1)} %pad_maximum_fusion.5), channel_id=1, source_target_pairs={{0,4},{2,6},{4,0},{6,2},{8,12},{10,14},{12,8},{14,10},{16,20},{18,... | collective-permute-start | bytes 393224 | tf_op jit(solution)/shard_map/ppermute | solution.py:49
  34.4 9.1 %collective-permute-start.6 = (bf16[4,128,128]{2,1,0:T(8,128)(2,1)S(1)}, bf16[4,128,128]{2,1,0:T(8,128)(2,1)S(1)}, u32[]{:S(2)}, u32[]{:S(2)}) collective-permute-start(bf16[4,128,128]{2,1,0:T(8,128)(2,1)S(1)} %pad_maximum_fusion.5), channel_id=1, source_target_pairs={{0,6},{2,4},{4,2},{6,0},{8,14},{10,12},{12,10},{14,8},{16,22},{18,... | collective-permute-start | bytes 393224 | tf_op jit(solution)/shard_map/ppermute | solution.py:49
  35.8 12.3 %collective-permute-start.11 = (bf16[4,336,128]{2,1,0:T(8,128)(2,1)S(1)}, bf16[4,336,128]{2,1,0:T(8,128)(2,1)S(1)}, u32[]{:S(2)}, u32[]{:S(2)}) collective-permute-start(bf16[4,336,128]{2,1,0:T(8,128)(2,1)S(1)} %pad_maximum_fusion.1), channel_id=1, source_target_pairs={{0,2},{2,0},{4,6},{6,4},{8,10},{10,8},{12,14},{14,12},{16,18},{18,... | collective-permute-start | bytes 1032200 | tf_op jit(solution)/shard_map/ppermute | solution.py:49
  38.3 17.7 %collective-permute-start.12 = (bf16[4,336,128]{2,1,0:T(8,128)(2,1)S(1)}, bf16[4,336,128]{2,1,0:T(8,128)(2,1)S(1)}, u32[]{:S(2)}, u32[]{:S(2)}) collective-permute-start(bf16[4,336,128]{2,1,0:T(8,128)(2,1)S(1)} %pad_maximum_fusion.1), channel_id=1, source_target_pairs={{0,4},{2,6},{4,0},{6,2},{8,12},{10,14},{12,8},{14,10},{16,20},{18,... | collective-permute-start | bytes 1032200 | tf_op jit(solution)/shard_map/ppermute | solution.py:49
  41.4 14.7 %collective-permute-start.13 = (bf16[4,336,128]{2,1,0:T(8,128)(2,1)S(1)}, bf16[4,336,128]{2,1,0:T(8,128)(2,1)S(1)}, u32[]{:S(2)}, u32[]{:S(2)}) collective-permute-start(bf16[4,336,128]{2,1,0:T(8,128)(2,1)S(1)} %pad_maximum_fusion.1), channel_id=1, source_target_pairs={{0,6},{2,4},{4,2},{6,0},{8,14},{10,12},{12,10},{14,8},{16,22},{18,... | collective-permute-start | bytes 1032200 | tf_op jit(solution)/shard_map/ppermute | solution.py:49
  43.6 13.4 %collective-permute-start.7 = (bf16[16,128,128]{2,1,0:T(8,128)(2,1)S(1)}, bf16[16,128,128]{2,1,0:T(8,128)(2,1)S(1)}, u32[]{:S(2)}, u32[]{:S(2)}) collective-permute-start(bf16[16,128,128]{2,1,0:T(8,128)(2,1)S(1)} %constant_dynamic-update-slice_fusion.mine), channel_id=1, source_target_pairs={{0,1},{1,0},{2,3},{3,2},{4,5},{5,4},{6,7},{7,6},{8,9},{9,8},{10,11... | collective-permute-start | bytes 1572872 | tf_op jit(solution)/shard_map/ppermute | solution.py:53
  56.2 40.0 %collective-permute-start.14 = (bf16[16,336,128]{2,1,0:T(8,128)(2,1)S(1)}, bf16[16,336,128]{2,1,0:T(8,128)(2,1)S(1)}, u32[]{:S(2)}, u32[]{:S(2)}) collective-permute-start(bf16[16,336,128]{2,1,0:T(8,128)(2,1)S(1)} %constant_dynamic-update-slice_fusion.7.mine), channel_id=1, source_target_pairs={{0,1},{1,0},{2,3},{3,2},{4,5},{5,4},{6,7},{7,6},{8,9},{9,8},{10,11... | collective-permute-start | bytes 4128776 | tf_op jit(solution)/shard_map/ppermute | solution.py:53
  163.7 21.9 %collective-permute-start.24 = (bf16[16,336,128]{2,1,0:T(8,128)(2,1)}, bf16[16,336,128]{2,1,0:T(8,128)(2,1)S(1)}, u32[]{:S(2)}, u32[]{:S(2)}) collective-permute-start(bf16[16,336,128]{2,1,0:T(8,128)(2,1)} %get-tuple-element.88), channel_id=1, source_target_pairs={{0,1},{1,0},{2,3},{3,2},{4,5},{5,4},{6,7},{7,6},{8,9},{9,8},{10,11... | collective-permute-start | bytes 4128776 | tf_op jit(solution)/shard_map/ppermute | solution.py:53
  186.0 12.3 %collective-permute-start.25 = (bf16[4,336,128]{2,1,0:T(8,128)(2,1)S(1)}, bf16[4,336,128]{2,1,0:T(8,128)(2,1)S(1)}, u32[]{:S(2)}, u32[]{:S(2)}) collective-permute-start(bf16[4,336,128]{2,1,0:T(8,128)(2,1)S(1)} %get-tuple-element.121), channel_id=1, source_target_pairs={{0,2},{2,0},{4,6},{6,4},{8,10},{10,8},{12,14},{14,12},{16,18},{18,... | collective-permute-start | bytes 1032200 | tf_op jit(solution)/shard_map/ppermute | solution.py:49
  186.6 17.5 %collective-permute-start.26 = (bf16[4,336,128]{2,1,0:T(8,128)(2,1)S(1)}, bf16[4,336,128]{2,1,0:T(8,128)(2,1)S(1)}, u32[]{:S(2)}, u32[]{:S(2)}) collective-permute-start(bf16[4,336,128]{2,1,0:T(8,128)(2,1)S(1)} %get-tuple-element.122), channel_id=1, source_target_pairs={{0,4},{2,6},{4,0},{6,2},{8,12},{10,14},{12,8},{14,10},{16,20},{18,... | collective-permute-start | bytes 1032200 | tf_op jit(solution)/shard_map/ppermute | solution.py:49
  188.2 17.6 %collective-permute-start.27 = (bf16[4,336,128]{2,1,0:T(8,128)(2,1)S(1)}, bf16[4,336,128]{2,1,0:T(8,128)(2,1)S(1)}, u32[]{:S(2)}, u32[]{:S(2)}) collective-permute-start(bf16[4,336,128]{2,1,0:T(8,128)(2,1)S(1)} %get-tuple-element.123), channel_id=1, source_target_pairs={{0,6},{2,4},{4,2},{6,0},{8,14},{10,12},{12,10},{14,8},{16,22},{18,... | collective-permute-start | bytes 1032200 | tf_op jit(solution)/shard_map/ppermute | solution.py:49
  192.0 17.6 %collective-permute-start.21 = (bf16[1,120,128]{2,1,0:T(8,128)(2,1)S(1)}, bf16[1,120,128]{2,1,0:T(8,128)(2,1)S(1)}, u32[]{:S(2)}, u32[]{:S(2)}) collective-permute-start(bf16[1,120,128]{2,1,0:T(8,128)(2,1)S(1)} %get-tuple-element.132), channel_id=1, source_target_pairs={{0,8},{2,10},{4,12},{6,14},{8,0},{10,2},{12,4},{14,6},{16,24},{18,... | collective-permute-start | bytes 92168 | tf_op jit(solution)/shard_map/ppermute | solution.py:49
  193.5 17.0 %collective-permute-start.22 = (bf16[1,120,128]{2,1,0:T(8,128)(2,1)S(1)}, bf16[1,120,128]{2,1,0:T(8,128)(2,1)S(1)}, u32[]{:S(2)}, u32[]{:S(2)}) collective-permute-start(bf16[1,120,128]{2,1,0:T(8,128)(2,1)S(1)} %get-tuple-element.134), channel_id=1, source_target_pairs={{0,16},{2,18},{4,20},{6,22},{8,24},{10,26},{12,28},{14,30},{16,0},... | collective-permute-start | bytes 92168 | tf_op jit(solution)/shard_map/ppermute | solution.py:49
  198.3 12.2 %collective-permute-start.23 = (bf16[1,120,128]{2,1,0:T(8,128)(2,1)S(1)}, bf16[1,120,128]{2,1,0:T(8,128)(2,1)S(1)}, u32[]{:S(2)}, u32[]{:S(2)}) collective-permute-start(bf16[1,120,128]{2,1,0:T(8,128)(2,1)S(1)} %get-tuple-element.133), channel_id=1, source_target_pairs={{0,24},{2,26},{4,28},{6,30},{8,16},{10,18},{12,20},{14,22},{16,8},... | collective-permute-start | bytes 92168 | tf_op jit(solution)/shard_map/ppermute | solution.py:49
  207.5 9.0 %collective-permute-start.29 = (bf16[1,336,128]{2,1,0:T(8,128)(2,1)S(1)}, bf16[1,336,128]{2,1,0:T(8,128)(2,1)S(1)}, u32[]{:S(2)}, u32[]{:S(2)}) collective-permute-start(bf16[1,336,128]{2,1,0:T(8,128)(2,1)S(1)} %get-tuple-element.129), channel_id=1, source_target_pairs={{0,16},{2,18},{4,20},{6,22},{8,24},{10,26},{12,28},{14,30},{16,0},... | collective-permute-start | bytes 258056 | tf_op jit(solution)/shard_map/ppermute | solution.py:49
  217.2 25.1 %collective-permute-start.38 = (f32[456,128]{1,0:T(8,128)S(1)}, f32[456,128]{1,0:T(8,128)S(1)}, u32[]{:S(2)}, u32[]{:S(2)}) collective-permute-start(f32[456,128]{1,0:T(8,128)S(1)} %pad_maximum_fusion.3), channel_id=1, source_target_pairs={{0,1},{1,0},{2,3},{3,2},{4,5},{5,4},{6,7},{7,6},{8,9},{9,8},{10,11... | collective-permute-start | bytes 700424 | tf_op jit(solution)/shard_map/ppermute | solution.py:53
  230.3 10.7 %collective-permute-start.36 = (f32[1,1]{1,0:T(1,128)}, f32[1,1]{1,0:T(1,128)}, u32[]{:S(2)}, u32[]{:S(2)}) collective-permute-start(f32[1,1]{1,0:T(1,128)} %add.394), channel_id=1, source_target_pairs={{0,16},{2,18},{4,20},{6,22},{8,24},{10,26},{12,28},{14,30},{16,0},... | collective-permute-start | bytes 20 | tf_op jit(solution)/shard_map/ppermute | solution.py:49
  (42 other events, 226.7 us)

commit v3 on v2

v3 whole, which is shorter than its diff:
```python
import math
from functools import partial

import jax
import jax.numpy as jnp
from jax import lax
from jax.experimental import pallas as pl
from jax.experimental.pallas import tpu as pltpu
from jax.sharding import PartitionSpec as P

D = 384
FF = 1024
HEADS = 6
HD = 64
STEP = 3


norm_eps = 1e-06
beta_one = 0.5
beta_two = 0.5
adam_eps = 1e-08
decay_rate = 0.1
clip_limit = 1.0
masked_score = -1e30


def adam_update(master, grad, first, second, rate, decay):
    first_new = beta_one * first + (1.0 - beta_one) * grad
    second_new = beta_two * second + (1.0 - beta_two) * grad * grad
    direction = (
        first_new
        / (1.0 - beta_one**STEP)
        / (jnp.sqrt(second_new / (1.0 - beta_two**STEP)) + adam_eps)
    )
    return (first_new, second_new, master - rate * (direction + decay * master))


def bit_groups(count):
    groups = []
    low, bits = 0, count.bit_length() - 1
    while low < bits:
        width = min(2, bits - low)
        groups.append((low, width))
        low += width
    return groups


def permute_batch(value, flip, count):
    return lax.ppermute(value, "batch", [(i, i ^ flip) for i in range(count)])


def swap_tm(value):
    return lax.ppermute(value, "tm", [(0, 1), (1, 0)])


def slabs(matrix):
    rows, columns = matrix.shape
    return matrix.reshape(rows, columns // 128, 128).transpose(1, 0, 2)


def unslab(stack):
    count, rows, _ = stack.shape
    return stack.transpose(1, 0, 2).reshape(rows, count * 128)


bf16 = jnp.bfloat16
f32 = jnp.float32
BLOCK = 256
LANES = 128
KEEP_LANE = 96
STORED = (2, 3, 4, 5, 0, 1)
SPOT = tuple(STORED.index(head) for head in range(HEADS))
GROUPS = ((2, 2), (4, 0))
VMEM_LIMIT = 58 * 2**20
NN = (((1,), (0,)), ((), ()))
NT = (((1,), (1,)), ((), ()))
TN = (((0,), (0,)), ((), ()))


def dot(left, right, dims):
    return lax.dot_general(left, right, dims, preferred_element_type=f32)


def cost(flops, moved):
    return pl.CostEstimate(flops=flops, bytes_accessed=moved, transcendentals=0)


def block(start, size=BLOCK):
    return pl.ds(pl.multiple_of(start * size, size), size)


def sum_batch(value, count):
    for low, width in bit_groups(count):
        pieces = [value] + [permute_batch(value, k << low, count) for k in range(1, 1 << width)]
        while len(pieces) > 1:
            pieces = [pieces[i] + pieces[i + 1] for i in range(0, len(pieces), 2)]
        value = pieces[0]
    return value


def row_scale(values):
    return lax.rsqrt(jnp.mean(values * values, axis=-1, keepdims=True) + norm_eps)


def norm_back(grad_normed, values, scale):
    return scale * grad_normed - values * scale * scale * scale * jnp.mean(
        grad_normed * values, axis=-1, keepdims=True
    )


def split_three(values):
    high = values.astype(bf16)
    rest = values - high.astype(f32)
    middle = rest.astype(bf16)
    return high, middle, (rest - middle.astype(f32)).astype(bf16)


def swap_halves(pair):
    lane = lax.broadcasted_iota(jnp.int32, pair.shape, 1)
    return jnp.where(lane % HD < HD // 2, pltpu.roll(pair, 96, 1), pltpu.roll(pair, 32, 1))


def relative_place(device, owner, count):
    flips = device ^ owner
    place, scale = 0, 1
    for low, width in reversed(bit_groups(count)):
        place = place + ((flips >> low) & ((1 << width) - 1)) * scale
        scale <<= width
    return place


def tie(value, other):
    if other is None:
        return value
    return value + other.reshape(-1)[0] * jnp.zeros((), value.dtype)


def gather_steps(chunk, count, after=None, first_after=None, last_after=None):
    held, steps = chunk[None], []
    for n, (low, width) in enumerate(reversed(bit_groups(count))):
        held = tie(held, after[n] if after else None)
        pieces = [held] + [permute_batch(held, k << low, count) for k in range(1, 1 << width)]
        held = jnp.concatenate(pieces, axis=0)
        if n == 0:
            held = tie(held, first_after)
        steps.append(held)
    return steps


def send_kernel(shard, down, where, w_qkv, w_out, w_gate_up, w_down, gains, first, second, a, b, c):
    core = where[0]
    a[...] = jnp.zeros_like(a)
    c[...] = jnp.zeros_like(c)
    c[0:2, 0:shard] = gains[...]
    column = c[...].T
    pieces = [(w_qkv, i) for i in range(9)] + [(None, 0)]
    more = [(w_out, i) for i in range(3)] + [(w_gate_up, i) for i in range(16)] + [(None, 1)]

    def fill(half):
        for target, items in ((a, pieces), (b, more)):
            number = len(items) // 2
            for i in range(number):
                source, at = items[half * number + i]
                rows = slice(i * shard, (i + 1) * shard)
                if source is not None:
                    target[rows, :] = source[:, at * LANES : (at + 1) * LANES]
                else:
                    target[rows, :] = column[:shard] if at == 0 else jnp.zeros((shard, LANES), f32)
        for i in range(3):
            start = 10 * shard + i * down
            b[start : start + down, :] = w_down[
                half * down : (half + 1) * down, i * LANES : (i + 1) * LANES
            ]

    @pl.when(core == 0)
    def _():
        fill(0)

    @pl.when(core == 1)
    def _():
        fill(1)

    first[...] = a[...].astype(bf16)
    second[...] = b[...].astype(bf16)


def send_chunks(where, w_qkv, w_out, w_gate_up, w_down, gains):
    shard, down = w_qkv.shape[0], w_down.shape[0] // 2
    core = where[0]
    first_rows = -(-5 * shard // 16) * 16
    second_rows = 10 * shard + 3 * down
    if shard % 8 == 0 and down % 8 == 0:
        spec = pl.BlockSpec(memory_space=pltpu.VMEM)
        return pl.pallas_call(
            partial(send_kernel, shard, down),
            out_shape=[
                jax.ShapeDtypeStruct((first_rows, LANES), bf16),
                jax.ShapeDtypeStruct((second_rows, LANES), bf16),
            ],
            in_specs=[pl.BlockSpec(memory_space=pltpu.SMEM)] + [spec] * 5,
            out_specs=[spec] * 2,
            scratch_shapes=[
                pltpu.VMEM((first_rows, LANES), f32),
                pltpu.VMEM((second_rows, LANES), f32),
                pltpu.VMEM((LANES, LANES), f32),
            ],
            compiler_params=pltpu.CompilerParams(vmem_limit_bytes=VMEM_LIMIT),
            name="send_chunks",
        )(where, w_qkv, w_out, w_gate_up, w_down, gains)
    gain_slab = jnp.pad(gains.T, ((0, 0), (0, LANES - 2)))[None]
    first = jnp.concatenate([slabs(w_qkv), gain_slab]).reshape(2, 5 * shard, LANES)
    first = jnp.where(core == 0, first[0], first[1]).astype(bf16)
    first = jnp.pad(first, ((0, first_rows - first.shape[0]), (0, 0)))
    second = jnp.concatenate(
        [slabs(w_out), slabs(w_gate_up), jnp.zeros((1, shard, LANES), f32)]
    ).reshape(2, 10 * shard, LANES)
    downs = slabs(w_down).reshape(3, 2, down, LANES).transpose(1, 0, 2, 3)
    downs = downs.reshape(2, 3 * down, LANES)
    second = jnp.where(
        core == 0,
        jnp.concatenate([second[0], downs[0]]),
        jnp.concatenate([second[1], downs[1]]),
    ).astype(bf16)
    return first, second


def unpack(count, number, shard, down, where, mine, other, stage, w_down):
    core, owner = where[0], where[1]
    for source, half in ((mine, core), (other, 1 - core)):

        def one(device, carry, source=source, half=half):
            chunk = source[relative_place(device, owner, count)].astype(f32)
            for i in range(number):
                rows = pl.ds(pl.multiple_of(device * shard, 8), shard)
                stage[half * number + i, rows, :] = chunk[i * shard : (i + 1) * shard]
            for i in range(3 if down else 0):
                start = number * shard + i * down
                rows = pl.ds(pl.multiple_of((device * 2 + half) * down, 16), down)
                w_down[rows, i * LANES : (i + 1) * LANES] = chunk[start : start + down].astype(bf16)
            return carry

        lax.fori_loop(0, count, one, 0)


def can_unpack(shard, down):
    return shard % 8 == 0 and down % 16 == 0


def unpack_plain(count, number, shard, down, where, mine, other):
    core, owner = where[0], where[1]
    places = relative_place(jnp.arange(count, dtype=jnp.int32), owner, count)
    low = jnp.take(jnp.where(core == 0, mine, other), places, axis=0)
    high = jnp.take(jnp.where(core == 0, other, mine), places, axis=0)

    def part(source):
        return (
            source[:, : number * shard]
            .reshape(count, number, shard, LANES)
            .transpose(1, 0, 2, 3)
            .reshape(number, D, LANES)
        )

    stack = jnp.concatenate([part(low), part(high)], axis=0)
    if number == 5:
        return unslab(stack[:9]), stack[9].T[:8].astype(f32)
    downs = [
        item[:, number * shard : number * shard + 3 * down].reshape(count, 3, down, LANES)
        for item in (low, high)
    ]
    w_down = jnp.stack(downs, axis=1).transpose(0, 1, 3, 2, 4).reshape(FF, D)
    return unslab(stack[:3]), unslab(stack[3:19]), w_down


def put_slab(stage, core, number, shard, at, slab):
    half, row = at // number, (at % number) * shard
    slot = core if half == 0 else 1 - core
    stage[slot, :, row : row + shard, :] = slab.reshape(-1, shard, LANES)


def put_down(stage, core, number, shard, down, column, slab, first):
    parts = slab.reshape(-1, 2, down, LANES)
    row = number * shard + column * down
    devices = slice(first, first + parts.shape[0])
    stage[core, devices, row : row + down, :] = parts[:, 0]
    stage[1 - core, devices, row : row + down, :] = parts[:, 1]


def gain_column(row):
    return jnp.concatenate([row, jnp.zeros((LANES - 8, D), f32)], axis=0).T


def pack_plain(count, core, grads, number, shard, down):
    column = jnp.pad(grads[-1][:1].T, ((0, 0), (0, LANES - 1)))[None]
    stack = jnp.concatenate([slabs(item) for item in (grads[:2] if down else grads[:1])] + [column])

    def by_device(part):
        return (
            part.reshape(number, count, shard, LANES)
            .transpose(1, 0, 2, 3)
            .reshape(count, number * shard, LANES)
        )

    halves = [by_device(stack[:number]), by_device(stack[number:])]
    if down:
        downs = (
            slabs(grads[2])
            .reshape(3, count, 2, down, LANES)
            .transpose(2, 1, 0, 3, 4)
            .reshape(2, count, 3 * down, LANES)
        )
        halves = [jnp.concatenate([halves[i], downs[i]], axis=1) for i in range(2)]
    return (
        jnp.where(core == 0, jnp.stack(halves), jnp.stack(halves[::-1])),
        jnp.where(core == 0, halves[1], halves[0]).astype(bf16),
    )


def scatter_steps(parts, count, owner):
    held, steps = parts, []
    rest = parts.shape[1:]
    for low, width in bit_groups(count):
        fan = 1 << width
        view = held.reshape((-1, fan) + rest)
        mine = (owner >> low) & (fan - 1)
        total = lax.dynamic_index_in_dim(view, mine, 1, keepdims=False).astype(f32)
        got = []
        for k in range(1, fan):
            piece = lax.dynamic_index_in_dim(view, mine ^ k, 1, keepdims=False)
            got.append(permute_batch(piece.astype(bf16), k << low, count))
        for item in got:
            total = total + item.astype(f32)
        held = total
        steps.append(held)
    return steps


def tables_kernel(length, where, ids, pads, offsets, cosine, sine, key_aux, query_aux, ranges):
    core = where[0]
    whole = 2 * length

    def turn(row):
        low, high = row[:, :length], row[:, length:]
        return jnp.concatenate(
            [jnp.where(core == 0, low, high), jnp.where(core == 0, high, low)], axis=1
        )

    classes = (2 * ids[...] + pads[...]).astype(f32)
    spot = lax.broadcasted_iota(jnp.int32, (1, whole), 1)
    position = (turn(spot) + turn(offsets[...])).astype(f32)
    turned = turn(classes)
    index = lax.broadcasted_iota(jnp.int32, (HD // 2, whole), 0).astype(f32)
    angle = position * jnp.exp(index * (-2.0 * math.log(10000.0) / HD))
    cos, sin = jnp.cos(angle), jnp.sin(angle)
    cosine[...] = jnp.concatenate([cos, cos, cos, cos], axis=0).T
    sine[...] = jnp.concatenate([-sin, sin, -sin, sin], axis=0).T
    at = lax.broadcasted_iota(jnp.int32, (LANES, whole), 0)
    is_class = (at >= HD) & (at < HD + 8)
    same = (at - HD).astype(f32) == turned
    is_log = (at >= HD + 8) & (at < HD + 8 + 3 * HEADS)
    key_aux[...] = jnp.where((is_class & same) | is_log, 1.0, 0.0).T.astype(bf16)
    own = turned[:, :length]
    kept = jnp.where(turn(pads[...])[:, :length] == 0, 1.0, 0.0)
    extra = jnp.where(is_class & ~same, masked_score, 0.0)[:, :length]
    query_aux[...] = jnp.where(at[:, :length] == KEEP_LANE, kept, extra).T.astype(bf16)
    starts = (core * length, (1 - core) * length)
    for n in range(length // BLOCK):
        mine = own[:, n * BLOCK : (n + 1) * BLOCK]
        first = jnp.min(mine)
        last = jnp.max(mine)
        low_key = jnp.sum(jnp.where(classes < first, 1.0, 0.0)).astype(jnp.int32)
        high_key = jnp.sum(jnp.where(classes <= last, 1.0, 0.0)).astype(jnp.int32)
        bounds = []
        for start in starts:
            low_part = jnp.clip(low_key - start, 0, length)
            high_part = jnp.clip(high_key - start, 0, length)
            low_block = low_part // BLOCK
            bounds.append((low_block, jnp.maximum((high_part + BLOCK - 1) // BLOCK - low_block, 0)))
        ranges[0, n] = bounds[0][0]
        ranges[1, n] = bounds[0][1]
        ranges[2, n] = bounds[1][0] + length // BLOCK - bounds[0][1]
        ranges[3, n] = bounds[0][1] + bounds[1][1]


def tables(where, ids, pads, offsets):
    whole = ids.shape[1]
    length = whole // 2
    spec = pl.BlockSpec(memory_space=pltpu.VMEM)
    smem = pl.BlockSpec(memory_space=pltpu.SMEM)
    return pl.pallas_call(
        partial(tables_kernel, length),
        out_shape=[
            jax.ShapeDtypeStruct((whole, LANES), f32),
            jax.ShapeDtypeStruct((whole, LANES), f32),
            jax.ShapeDtypeStruct((whole, LANES), bf16),
            jax.ShapeDtypeStruct((length, LANES), bf16),
            jax.ShapeDtypeStruct((4, length // BLOCK), jnp.int32),
        ],
        in_specs=[smem, spec, spec, spec],
        out_specs=[spec] * 4 + [smem],
        compiler_params=pltpu.CompilerParams(vmem_limit_bytes=VMEM_LIMIT),
        cost_estimate=cost(3 * 10**9, 4 * 2**20),
        name="tables",
    )(where, ids, pads, offsets)


def project_kernel(
    fused, own, there, cosine, sine, key_aux, query_aux, *refs
):
    if fused:
        where, mine, other, qa, ka, va, kt, vt, w, gains, stage = refs[:3] + refs[-8:]
    else:
        w_in, gains_in, qa, ka, va, kt, vt, w, gains = refs[:2] + refs[-7:]

    @pl.when(pl.program_id(0) == 0)
    def _():
        if fused:
            unpack(*fused, where, mine, other, stage, None)
            for i in range(9):
                w[:, i * LANES : (i + 1) * LANES] = stage[i].astype(bf16)
            gains[...] = stage[9].T[:8]
        else:
            w[...] = w_in[...]
            gains[...] = gains_in[...]

    step = pl.program_id(0)
    is_own = step < pl.num_programs(0) // 2
    x = jnp.where(is_own, own[...], there[...]).astype(f32)
    normed = (x * row_scale(x) * gains[0:1, :]).astype(bf16)
    cos, sin = cosine[...], sine[...]
    low = lax.broadcasted_iota(jnp.int32, (BLOCK, LANES), 1) < HD
    products = [dot(normed, w[:, i * LANES : (i + 1) * LANES], NN) for i in range(3, 9)]
    key_extra = key_aux[...].astype(f32)
    query_extra = query_aux[...].astype(f32)
    lane = lax.broadcasted_iota(jnp.int32, (BLOCK, LANES), 1)
    value_extra = jnp.where((lane >= HD) & (lane < HD + 3), 1.0, 0.0)
    ones = jnp.ones((8, BLOCK), bf16)

    @pl.when(is_own)
    def _():
        for pair in range(HEADS // 2):
            z = dot(normed, w[:, pair * LANES : (pair + 1) * LANES], NN)
            z = (z * cos + swap_halves(z) * sin).astype(bf16).astype(f32) * HD**-0.5
            qa[SPOT[2 * pair]] = jnp.where(low, z, query_extra).astype(bf16)
            qa[SPOT[2 * pair + 1]] = jnp.where(low, pltpu.roll(z, HD, 1), query_extra).astype(bf16)

    for pair in range(HEADS // 2):
        z = products[pair]
        z = z * cos + swap_halves(z) * sin
        ka[SPOT[2 * pair]] = jnp.where(low, z, key_extra).astype(bf16)
        ka[SPOT[2 * pair + 1]] = jnp.where(low, pltpu.roll(z, HD, 1), key_extra).astype(bf16)
        turned = z.T.astype(bf16)
        kt[SPOT[2 * pair]] = turned[:HD]
        kt[SPOT[2 * pair + 1]] = turned[HD:]
    for pair in range(HEADS // 2):
        z = products[3 + pair]
        va[SPOT[2 * pair]] = jnp.where(low, z, value_extra).astype(bf16)
        va[SPOT[2 * pair + 1]] = jnp.where(low, pltpu.roll(z, HD, 1), value_extra).astype(bf16)
        turned = z.T.astype(bf16)
        vt[SPOT[2 * pair], :HD] = turned[:HD]
        vt[SPOT[2 * pair + 1], :HD] = turned[HD:]
        vt[SPOT[2 * pair], HD:] = ones
        vt[SPOT[2 * pair + 1], HD:] = ones


def project(own, there, cosine, sine, key_aux, query_aux, weights, fused, waits):
    length = own.shape[0]
    steps = length // BLOCK
    whole = 2 * length
    first = lambda i: (jnp.minimum(i, steps - 1), 0)
    last = lambda i: (jnp.maximum(i - steps, 0), 0)
    spec = pl.BlockSpec(memory_space=pltpu.VMEM)
    if fused:
        weight_specs = [pl.BlockSpec(memory_space=pltpu.SMEM), spec, spec]
    else:
        weight_specs = [spec, spec]
    return pl.pallas_call(
        partial(project_kernel, fused),
        out_shape=[
            jax.ShapeDtypeStruct((HEADS, length, LANES), bf16),
            jax.ShapeDtypeStruct((HEADS, whole, LANES), bf16),
            jax.ShapeDtypeStruct((HEADS, whole, LANES), bf16),
            jax.ShapeDtypeStruct((HEADS, HD, whole), bf16),
            jax.ShapeDtypeStruct((HEADS, HD + 8, whole), bf16),
            jax.ShapeDtypeStruct((D, 3 * D), bf16),
            jax.ShapeDtypeStruct((8, D), f32),
        ],
        grid=(2 * steps,),
        in_specs=[
            pl.BlockSpec((BLOCK, D), first),
            pl.BlockSpec((BLOCK, D), last),
            pl.BlockSpec((BLOCK, LANES), lambda i: (i, 0)),
            pl.BlockSpec((BLOCK, LANES), lambda i: (i, 0)),
            pl.BlockSpec((BLOCK, LANES), lambda i: (i, 0)),
            pl.BlockSpec((BLOCK, LANES), first),
        ]
        + weight_specs
        + [pl.BlockSpec(memory_space=pl.ANY)] * len(waits),
        out_specs=[
            pl.BlockSpec((HEADS, BLOCK, LANES), lambda i: (0, jnp.minimum(i, steps - 1), 0)),
            pl.BlockSpec((HEADS, BLOCK, LANES), lambda i: (0, i, 0)),
            pl.BlockSpec((HEADS, BLOCK, LANES), lambda i: (0, i, 0)),
            pl.BlockSpec((HEADS, HD, BLOCK), lambda i: (0, 0, i)),
            pl.BlockSpec((HEADS, HD + 8, BLOCK), lambda i: (0, 0, i)),
            pl.BlockSpec((D, 3 * D), lambda i: (0, 0)),
            pl.BlockSpec((8, D), lambda i: (0, 0)),
        ],
        scratch_shapes=[pltpu.VMEM((10, D, LANES), f32)] if fused else [],
        compiler_params=pltpu.CompilerParams(vmem_limit_bytes=VMEM_LIMIT),
        cost_estimate=cost(9 * 10**9, 16 * 2**20),
        name="project",
    )(own, there, cosine, sine, key_aux, query_aux, *weights, *waits)


def key_block(ranges, step, n):
    return jnp.where(n < ranges[1, step], ranges[0, step] + n, ranges[2, step] + n)


def attend_kernel(ranges, qa, ka, vt, mixed, exact, qb, total, peak):
    step = pl.program_id(0)
    peak[...] = jnp.full((HEADS, 8, BLOCK), -3e38, f32)
    total[...] = jnp.zeros_like(total)

    def body(n, carry):
        rows = block(key_block(ranges, step, n))
        scores = [dot(ka[h, rows, :], qa[h], NT) for h in range(HEADS)]
        weights = []
        for h in range(HEADS):
            old = peak[h][:1]
            new = jnp.maximum(old, jnp.max(scores[h], axis=0, keepdims=True))
            weights.append((jnp.exp(scores[h] - new).astype(bf16), jnp.exp(old - new)))
            peak[h] = jnp.broadcast_to(new, (8, BLOCK))
        for h in range(HEADS):
            weight, shrink = weights[h]
            total[h] = total[h] * shrink + dot(vt[h, :, rows], weight, NN)
        return carry

    lax.fori_loop(0, ranges[3, step], body, 0)
    terms = []
    for h in range(HEADS):
        bottom = total[h][HD : HD + 1]
        terms.append(total[h][:HD] / bottom)
        logs = -(peak[h][:1] + jnp.log(bottom))
        for piece in split_three(logs):
            terms.append(piece.astype(f32))
    for pair in range(HEADS // 2):
        spots = (SPOT[2 * pair], SPOT[2 * pair + 1])
        both = jnp.concatenate([terms[4 * spot] for spot in spots], axis=0).T
        mixed[:, pair * LANES : (pair + 1) * LANES] = both.astype(bf16)
        exact[:, pair * LANES : (pair + 1) * LANES] = both
    pieces = [terms[4 * h + 1 + i] for h in range(HEADS) for i in range(3)]
    table = jnp.concatenate(
        [jnp.zeros((HD + 8, BLOCK), f32)]
        + pieces
        + [jnp.zeros((LANES - HD - 8 - 3 * HEADS, BLOCK), f32)],
        axis=0,
    ).T
    lane = lax.broadcasted_iota(jnp.int32, (BLOCK, LANES), 1)
    for h in range(HEADS):
        start = HD + 8 + 3 * h
        qb[h] = jnp.where(
            (lane >= start) & (lane < start + 3), table, qa[h].astype(f32)
        ).astype(bf16)


def attend(ranges, qa, ka, vt):
    heads, length, _ = qa.shape
    whole = ka.shape[1]
    return pl.pallas_call(
        attend_kernel,
        out_shape=[
            jax.ShapeDtypeStruct((length, D), bf16),
            jax.ShapeDtypeStruct((length, D), f32),
            jax.ShapeDtypeStruct(qa.shape, bf16),
        ],
        grid_spec=pltpu.PrefetchScalarGridSpec(
            num_scalar_prefetch=1,
            grid=(length // BLOCK,),
            in_specs=[
                pl.BlockSpec((heads, BLOCK, LANES), lambda i, *_: (0, i, 0)),
                pl.BlockSpec((heads, whole, LANES), lambda i, *_: (0, 0, 0)),
                pl.BlockSpec((heads, HD + 8, whole), lambda i, *_: (0, 0, 0)),
            ],
            out_specs=[
                pl.BlockSpec((BLOCK, D), lambda i, *_: (i, 0)),
                pl.BlockSpec((BLOCK, D), lambda i, *_: (i, 0)),
                pl.BlockSpec((heads, BLOCK, LANES), lambda i, *_: (0, i, 0)),
            ],
            scratch_shapes=[
                pltpu.VMEM((heads, HD + 8, BLOCK), f32),
                pltpu.VMEM((heads, 8, BLOCK), f32),
            ],
        ),
        compiler_params=pltpu.CompilerParams(vmem_limit_bytes=VMEM_LIMIT),
        cost_estimate=cost(12 * 10**9, 12 * 2**20),
        name="attend",
    )(ranges, qa, ka, vt)


def attend_back_kernel(ranges, qb, ka, da, va, kt, *refs):
    dq, own, there, sums, acc = refs[-5:]
    step = pl.program_id(0)
    heads = qb.shape[0]

    @pl.when(step == 0)
    def _():
        sums[...] = jnp.zeros_like(sums)

    acc[...] = jnp.zeros_like(acc)
    zero = jnp.zeros((BLOCK, HD), bf16)

    def body(n, carry):
        rows = block(key_block(ranges, step, n))
        first = [
            (dot(ka[h, rows, :], qb[h], NT), dot(va[h, rows, :], da[h], NT)) for h in range(heads)
        ]
        second = []
        for scores, grads in first:
            probs = jnp.exp(scores)
            second.append((probs.astype(bf16), (probs * grads).astype(bf16)))
        for h in range(heads):
            probs_low, grads_low = second[h]
            grad_side = jnp.concatenate([da[h][:, :HD], zero], axis=1)
            query_side = jnp.concatenate([zero, qb[h][:, :HD]], axis=1)
            sums[h, rows, :] += dot(probs_low, grad_side, NN) + dot(grads_low, query_side, NN)
            acc[h] += dot(kt[h, :, rows], grads_low, NN)
        return carry

    lax.fori_loop(0, ranges[3, step], body, 0)
    dq[...] = acc[...]

    @pl.when(step == pl.num_programs(0) - 1)
    def _():
        length = own.shape[1]
        own[...] = sums[:, :length, :]
        there[...] = sums[:, length:, :].astype(bf16)


def attend_back(heads, group, ranges, qb, ka, da, va, kt, waits):
    length, whole = qb.shape[1], ka.shape[1]
    return pl.pallas_call(
        attend_back_kernel,
        out_shape=[
            jax.ShapeDtypeStruct((heads, HD, length), f32),
            jax.ShapeDtypeStruct((heads, length, LANES), f32),
            jax.ShapeDtypeStruct((heads, whole - length, LANES), bf16),
        ],
        grid_spec=pltpu.PrefetchScalarGridSpec(
            num_scalar_prefetch=1,
            grid=(length // BLOCK,),
            in_specs=[
                pl.BlockSpec((heads, BLOCK, LANES), lambda i, *_: (group, i, 0)),
                pl.BlockSpec((heads, whole, LANES), lambda i, *_: (group, 0, 0)),
                pl.BlockSpec((heads, BLOCK, LANES), lambda i, *_: (group, i, 0)),
                pl.BlockSpec((heads, whole, LANES), lambda i, *_: (group, 0, 0)),
                pl.BlockSpec((heads, HD, whole), lambda i, *_: (group, 0, 0)),
            ]
            + [pl.BlockSpec(memory_space=pl.ANY)] * len(waits),
            out_specs=[
                pl.BlockSpec((heads, HD, BLOCK), lambda i, *_: (0, 0, i)),
                pl.BlockSpec((heads, length, LANES), lambda i, *_: (0, 0, 0)),
                pl.BlockSpec((heads, whole - length, LANES), lambda i, *_: (0, 0, 0)),
            ],
            scratch_shapes=[
                pltpu.VMEM((heads, whole, LANES), f32),
                pltpu.VMEM((heads, HD, BLOCK), f32),
            ],
        ),
        compiler_params=pltpu.CompilerParams(vmem_limit_bytes=VMEM_LIMIT),
        cost_estimate=cost(12 * 10**9, 8 * 2**20),
        name="attend_back",
    )(ranges, qb, ka, da, va, kt, *waits)


def feed_kernel(fused, own, mixed, exact, cotangent, query_aux, gains, *refs):
    if fused:
        where, mine, other = refs[:3]
        result, grad_middle, da, sums, give = refs[3:8]
        normed_all, low_all, hidden_all, up_all, middle_all, wo, wgu, wd, stage, g_gain = refs[8:-1]
    else:
        wo, wgu, wd = refs[:3]
        result, grad_middle, da, g_out, g_gate_up, g_down, g_gain = refs[3:10]
        normed_all, low_all, hidden_all, up_all, middle_all = refs[10:-1]
    step = pl.program_id(0)
    steps = pl.num_programs(0)
    gain = gains[1:2, :]

    @pl.when(step == 0)
    def _():
        g_gain[...] = jnp.zeros_like(g_gain)
        if fused:
            unpack(*fused, where, mine, other, stage, wd)
            for i in range(3):
                wo[:, i * LANES : (i + 1) * LANES] = stage[i].astype(bf16)
            for i in range(16):
                wgu[:, i * LANES : (i + 1) * LANES] = stage[3 + i].astype(bf16)

    chunks = FF // BLOCK
    lane = lax.broadcasted_iota(jnp.int32, (BLOCK, LANES), 1)

    rows = block(step)
    x = own[...].astype(f32)
    middle = x + dot(mixed[...], wo[...], NN)
    scale = row_scale(middle)
    normed = (middle * scale * gain).astype(bf16)
    normed_all[rows, :] = normed
    kept = query_aux[...].astype(f32)[:, KEEP_LANE : KEEP_LANE + 1]
    upstream = cotangent[...].astype(f32) * kept
    up_low = upstream.astype(bf16)
    up_all[rows, :] = up_low
    gates = [dot(normed, wgu[:, c * BLOCK : (c + 1) * BLOCK], NN) for c in range(chunks)]
    ups = [dot(normed, wgu[:, FF + c * BLOCK : FF + (c + 1) * BLOCK], NN) for c in range(chunks)]
    hiddens = [dot(up_low, wd[c * BLOCK : (c + 1) * BLOCK, :], NT) for c in range(chunks)]
    for c in range(chunks):
        gate, up, grad_hidden = gates[c], ups[c], hiddens[c]
        sig = 1.0 / (1.0 + jnp.exp(-gate))
        silu = gate * sig
        hidden_all[rows, c * BLOCK : (c + 1) * BLOCK] = (silu * up).astype(bf16)
        low_all[rows, FF + c * BLOCK : FF + (c + 1) * BLOCK] = (grad_hidden * silu).astype(bf16)
        low_all[rows, c * BLOCK : (c + 1) * BLOCK] = (
            grad_hidden * up * (sig + silu * (1.0 - sig))
        ).astype(bf16)
    ffn = dot(hidden_all[rows, :], wd[...], NN)
    grad_normed = dot(low_all[rows, :], wgu[...], NT)
    result[...] = (kept * (middle + ffn)).astype(bf16)
    g_gain[0:1, :] += jnp.sum(grad_normed * middle * scale, axis=0, keepdims=True)
    grad = upstream + norm_back(grad_normed * gain, middle, scale)
    grad_middle[...] = grad
    low = grad.astype(bf16)
    middle_all[rows, :] = low
    grad_mixed = dot(low, wo[...], NT).astype(bf16).astype(f32)
    products = grad_mixed * exact[...]
    for h in range(HEADS):
        pair = h // 2
        head = grad_mixed[:, pair * LANES : (pair + 1) * LANES]
        product = products[:, pair * LANES : (pair + 1) * LANES]
        mine_lanes = (lane < HD) if h % 2 == 0 else (lane >= HD)
        delta = -jnp.sum(jnp.where(mine_lanes, product, 0.0), axis=1, keepdims=True)
        if h % 2:
            head = pltpu.roll(head, HD, 1)
        high, mid, last = split_three(delta)
        extra = jnp.where(
            lane == HD,
            high.astype(f32),
            jnp.where(
                lane == HD + 1,
                mid.astype(f32),
                jnp.where(lane == HD + 2, last.astype(f32), 0.0),
            ),
        )
        da[SPOT[h]] = jnp.where(lane < HD, head, extra).astype(bf16)

    mixed_all = refs[-1]
    mixed_all[rows, :] = mixed[...]

    @pl.when(step == steps - 1)
    def _():
        if not fused:
            g_out[...] = dot(mixed_all[...], middle_all[...], TN)
            for c in range(2 * FF // 512):
                g_gate_up[:, c * 512 : (c + 1) * 512] = dot(
                    normed_all[...], low_all[:, c * 512 : (c + 1) * 512], TN
                )
            for c in range(chunks):
                g_down[c * BLOCK : (c + 1) * BLOCK, :] = dot(
                    hidden_all[:, c * BLOCK : (c + 1) * BLOCK], up_all[...], TN
                )
            return
        count, number, shard, down = fused
        core = where[0]

        def put(at, value):
            for i in range(value.shape[1] // LANES):
                put_slab(sums, core, number, shard, at + i, value[:, i * LANES : (i + 1) * LANES])

        put(0, dot(mixed_all[...], middle_all[...], TN))
        for c in range(2 * FF // 512):
            put(3 + 4 * c, dot(normed_all[...], low_all[:, c * 512 : (c + 1) * 512], TN))
        put(19, gain_column(g_gain[...]))
        for c in range(chunks):
            value = dot(hidden_all[:, c * BLOCK : (c + 1) * BLOCK], up_all[...], TN)
            for i in range(3):
                put_down(
                    sums, core, number, shard, down, i,
                    value[:, i * LANES : (i + 1) * LANES], c * BLOCK // (2 * down),
                )
        give[...] = sums[1].astype(bf16)


def feed(own, mixed, exact, cotangent, query_aux, gains, weights, fused):
    length = own.shape[0]
    spec = pl.BlockSpec(memory_space=pltpu.VMEM)
    scratch = [
        pltpu.VMEM((length, D), bf16),
        pltpu.VMEM((length, 2 * FF), bf16),
        pltpu.VMEM((length, FF), bf16),
        pltpu.VMEM((length, D), bf16),
        pltpu.VMEM((length, D), bf16),
    ]
    rows_of = lambda i: (i, 0)
    out_shape = [
        jax.ShapeDtypeStruct((length, D), bf16),
        jax.ShapeDtypeStruct((length, D), f32),
        jax.ShapeDtypeStruct((HEADS, length, LANES), bf16),
    ]
    out_specs = [
        pl.BlockSpec((BLOCK, D), rows_of),
        pl.BlockSpec((BLOCK, D), rows_of),
        pl.BlockSpec((HEADS, BLOCK, LANES), lambda i: (0, i, 0)),
    ]
    if fused:
        count, number, shard, down = fused
        rows = number * shard + 3 * down
        weight_specs = [pl.BlockSpec(memory_space=pltpu.SMEM), spec, spec]
        out_shape += [
            jax.ShapeDtypeStruct((2, count, rows, LANES), f32),
            jax.ShapeDtypeStruct((count, rows, LANES), bf16),
        ]
        out_specs += [spec, spec]
        scratch += [
            pltpu.VMEM((D, D), bf16),
            pltpu.VMEM((D, 2 * FF), bf16),
            pltpu.VMEM((FF, D), bf16),
            pltpu.VMEM((2 * number, D, LANES), f32),
            pltpu.VMEM((8, D), f32),
        ]
    else:
        weight_specs = [spec] * 3
        out_shape += [
            jax.ShapeDtypeStruct((D, D), f32),
            jax.ShapeDtypeStruct((D, 2 * FF), f32),
            jax.ShapeDtypeStruct((FF, D), f32),
            jax.ShapeDtypeStruct((8, D), f32),
        ]
        out_specs += [spec] * 4
    scratch.append(pltpu.VMEM((length, D), bf16))
    return pl.pallas_call(
        partial(feed_kernel, fused),
        out_shape=out_shape,
        grid=(length // BLOCK,),
        in_specs=[
            pl.BlockSpec((BLOCK, D), rows_of),
            pl.BlockSpec((BLOCK, D), rows_of),
            pl.BlockSpec((BLOCK, D), rows_of),
            pl.BlockSpec((BLOCK, D), rows_of),
            pl.BlockSpec((BLOCK, LANES), rows_of),
            pl.BlockSpec((8, D), lambda i: (0, 0)),
        ]
        + weight_specs,
        out_specs=out_specs,
        scratch_shapes=scratch,
        compiler_params=pltpu.CompilerParams(vmem_limit_bytes=VMEM_LIMIT),
        cost_estimate=cost(14 * 10**9, 16 * 2**20),
        name="feed",
    )(own, mixed, exact, cotangent, query_aux, gains, *weights)


PARTS = ((0, 1, 2, 3, 6), (4, 5, 7, 8))


def runs(part):
    found = []
    for at, slab in enumerate(part):
        if found and slab == found[-1][0] + found[-1][1]:
            found[-1][1] += 1
        else:
            found.append([slab, 1, at])
    return found


def project_back_kernel(number, fused, own, cosine, sine, w, gains, *refs):
    part = PARTS[number]
    step = pl.program_id(0)
    rows = block(step)
    cos, sin = cosine[...], -sine[...]
    low = lax.broadcasted_iota(jnp.int32, (BLOCK, LANES), 1) < HD
    if number == 0:
        dqs, (kept, got) = refs[:2], refs[2:4]
        partial_sum, grads, normed_all, low_all = refs[-4:]
    else:
        kept, got, grad_middle, before, grads_before = refs[:5]
        if fused:
            where = refs[5]
            grad_tokens, sums, give, g_gain, normed_all, low_all = refs[-6:]
        else:
            grad_tokens, grads, g_gain, normed_all, low_all = refs[-5:]
    x = own[...].astype(f32)
    scale = row_scale(x)
    gain = gains[0:1, :]
    normed_all[rows, :] = (x * scale * gain).astype(bf16)
    for at, slab in enumerate(part):
        kind, pair = divmod(slab, 3)
        if kind == 0:
            source, first = (dqs[0], 0) if pair == 0 else (dqs[1], 2 * pair - 2)
            z = jnp.concatenate([source[first], source[first + 1]], axis=0).T * HD**-0.5
        else:
            first = 0 if pair == 0 else 2 * pair - 2
            one, two = [kept[i] + got[i].astype(f32) for i in (first, first + 1)]
            if kind == 1:
                z = jnp.where(low, pltpu.roll(one, HD, 1), two)
            else:
                z = jnp.where(low, one, pltpu.roll(two, HD, 1))
        if kind < 2:
            z = z * cos + swap_halves(z) * sin
        low_all[rows, at * LANES : (at + 1) * LANES] = z.astype(bf16)
    grad_normed = sum(
        dot(
            low_all[rows, at * LANES : (at + many) * LANES],
            w[:, slab * LANES : (slab + many) * LANES],
            NT,
        )
        for slab, many, at in runs(part)
    )
    if number == 0:
        partial_sum[...] = grad_normed
    else:
        grad_normed = grad_normed + before[...]
        gain_sum = jnp.sum(grad_normed * x * scale, axis=0, keepdims=True)

        @pl.when(step == 0)
        def _():
            g_gain[...] = jnp.zeros_like(g_gain)

        g_gain[0:1, :] += gain_sum
        grad_tokens[...] = (
            grad_middle[...] + norm_back(grad_normed * gain, x, scale)
        ).astype(bf16)

    @pl.when(step == pl.num_programs(0) - 1)
    def _():
        value = dot(normed_all[...], low_all[...], TN)
        if number == 0 or not fused:
            grads[...] = value
            return
        core = where[0]
        for done, source in ((PARTS[0], grads_before), (PARTS[1], value)):
            for at, slab in enumerate(done):
                put_slab(sums, core, *fused, slab, source[:, at * LANES : (at + 1) * LANES])
        put_slab(sums, core, *fused, 9, gain_column(g_gain[...]))
        give[...] = sums[1].astype(bf16)


def project_back(number, fused, where, tables, arrays, waits):
    own, cosine, sine, w, gains = tables
    length = own.shape[0]
    columns = len(PARTS[number]) * LANES
    whole = pl.BlockSpec(memory_space=pltpu.VMEM)
    rows_of = lambda i: (i, 0)
    wide = pl.BlockSpec((BLOCK, D), rows_of)
    narrow = pl.BlockSpec((BLOCK, LANES), rows_of)
    scratch = [pltpu.VMEM((length, D), bf16), pltpu.VMEM((length, columns), bf16)]

    def heads(array, turned):
        if turned:
            return pl.BlockSpec((array.shape[0], HD, BLOCK), lambda i: (0, 0, i))
        return pl.BlockSpec((array.shape[0], BLOCK, LANES), lambda i: (0, i, 0))

    if number == 0:
        specs = [heads(arrays[0], True), heads(arrays[1], True)]
        specs += [heads(arrays[2], False), heads(arrays[3], False)]
        shapes = [((length, D), f32), ((D, columns), f32)]
        out_specs = [wide, whole]
    else:
        specs = [heads(arrays[0], False), heads(arrays[1], False), wide, wide, whole]
        if fused:
            size, shard = fused
            chunk = (D // shard, size * shard, LANES)
            specs.append(pl.BlockSpec(memory_space=pltpu.SMEM))
            arrays = [*arrays, where]
            shapes = [((length, D), bf16), ((2,) + chunk, f32), (chunk, bf16)]
            out_specs = [wide, whole, whole]
            scratch = [pltpu.VMEM((8, D), f32)] + scratch
        else:
            shapes = [((length, D), bf16), ((D, columns), f32), ((8, D), f32)]
            out_specs = [wide, whole, whole]
    return pl.pallas_call(
        partial(project_back_kernel, number, fused),
        out_shape=[jax.ShapeDtypeStruct(*item) for item in shapes],
        grid=(length // BLOCK,),
        in_specs=[
            wide,
            narrow,
            narrow,
            pl.BlockSpec((D, 3 * D), lambda i: (0, 0)),
            pl.BlockSpec((8, D), lambda i: (0, 0)),
        ]
        + specs
        + [pl.BlockSpec(memory_space=pl.ANY)] * len(waits),
        out_specs=out_specs,
        scratch_shapes=scratch,
        compiler_params=pltpu.CompilerParams(vmem_limit_bytes=VMEM_LIMIT),
        cost_estimate=cost(4 * 10**9, 8 * 2**20),
        name="project_back",
    )(own, cosine, sine, w, gains, *arrays, *waits)


def update_kernel(shard, down, where, total, sums, there, *refs):
    core = where[0]
    masters, firsts, seconds = refs[:5], refs[5:10], refs[10:15]
    norm = refs[15]
    outs = [refs[16 + 5 * i : 21 + 5 * i] for i in range(4)]
    low, high, square = refs[36:]

    @pl.when(core == 0)
    def _():
        low[...] = sums[...]
        high[...] = there[...]

    @pl.when(core == 1)
    def _():
        low[...] = there[...]
        high[...] = sums[...]

    length = jnp.sqrt(total[...])
    norm[...] = length
    factor = clip_limit / jnp.maximum(length, clip_limit)
    halves = (low, high)

    def step(which, grad, rows, columns, rate, decay):
        at = (rows, columns)
        new = adam_update(
            masters[which][at], factor * grad, firsts[which][at], seconds[which][at], rate, decay
        )
        outs[0][which][at] = new[0]
        outs[1][which][at] = new[1]
        outs[2][which][at] = new[2]
        outs[3][which][at] = new[2].astype(bf16)

    every = slice(None)
    places = [(0, i, i // 5, (i % 5) * shard) for i in range(9)]
    for i in range(19):
        which, column = (1, i) if i < 3 else (2, i - 3)
        places.append((which, column, i // 10, (5 + i % 10) * shard))
    for which, column, half, row in places:
        rate = 4.0 * D**-0.5 if which == 1 else D**-0.5
        grad = halves[half][row : row + shard, :]
        step(which, grad, every, slice(column * LANES, (column + 1) * LANES), rate, decay_rate)
    for half in range(2):
        for i in range(3):
            row = 15 * shard + i * down
            step(
                3, halves[half][row : row + down, :], slice(half * down, (half + 1) * down),
                slice(i * LANES, (i + 1) * LANES), FF**-0.5, decay_rate,
            )
    gain_rows = []
    for row in (4 * shard, 14 * shard):
        square[...] = jnp.zeros_like(square)
        square[0:shard, :] = high[row : row + shard, :]
        gain_rows.append(square[...].T[0:1, :shard])
    for i in range(2):
        step(4, gain_rows[i], slice(i, i + 1), every, 0.5, 0.0)


def update(where, total, sums, there, masters, firsts, seconds):
    shard, down = masters[0].shape[0], masters[3].shape[0] // 2
    spec = pl.BlockSpec(memory_space=pltpu.VMEM)
    shapes = [item.shape for item in masters]
    outs = pl.pallas_call(
        partial(update_kernel, shard, down),
        out_shape=[jax.ShapeDtypeStruct((1, 1), f32)]
        + [jax.ShapeDtypeStruct(shape, f32) for _ in range(3) for shape in shapes]
        + [jax.ShapeDtypeStruct(shape, bf16) for shape in shapes],
        in_specs=[pl.BlockSpec(memory_space=pltpu.SMEM)] + [spec] * 18,
        out_specs=[spec] * 21,
        scratch_shapes=[
            pltpu.VMEM(sums.shape, f32),
            pltpu.VMEM(sums.shape, f32),
            pltpu.VMEM((LANES, LANES), f32),
        ],
        compiler_params=pltpu.CompilerParams(vmem_limit_bytes=VMEM_LIMIT),
        name="update",
    )(where, total, sums, there, *masters, *firsts, *seconds)
    return outs[0][0, 0], outs[1:6], outs[6:11], outs[11:16], outs[16:21]


def update_plain(core, total, sums, there, masters, firsts, seconds):
    shard, down = masters[0].shape[0], masters[3].shape[0] // 2
    low = jnp.where(core == 0, sums, there)
    high = jnp.where(core == 0, there, sums)
    five, fifteen = 5 * shard, 15 * shard
    first_shard = jnp.concatenate([low[:five], high[:five]]).reshape(10, shard, LANES)
    second_shard = jnp.concatenate([low[five:fifteen], high[five:fifteen]])
    second_shard = second_shard.reshape(20, shard, LANES)
    down_shard = jnp.stack(
        [item[fifteen:].reshape(3, down, LANES) for item in (low, high)], axis=1
    ).reshape(3, 2 * down, LANES)
    shard_grads = (
        unslab(first_shard[:9]),
        unslab(second_shard[:3]),
        unslab(second_shard[3:19]),
        unslab(down_shard),
        jnp.stack([first_shard[9, :, 0], second_shard[19, :, 0]]),
    )
    grad_norm = jnp.sqrt(total[0, 0])
    factor = clip_limit / jnp.maximum(grad_norm, clip_limit)
    rates = (D ** (-0.5), 4.0 * D ** (-0.5), D ** (-0.5), FF ** (-0.5), 0.5)
    decays = (decay_rate, decay_rate, decay_rate, decay_rate, 0.0)
    updates = [
        adam_update(
            masters[i], factor * shard_grads[i], firsts[i], seconds[i], rates[i], decays[i]
        )
        for i in range(5)
    ]
    new_first, new_second, new_master = zip(*updates)
    return grad_norm, new_first, new_second, new_master, [item.astype(bf16) for item in new_master]


def per_device(
    count,
    tokens,
    cotangent,
    sample_ids,
    pad_flags,
    offsets,
    w_qkv,
    w_out,
    w_gate_up,
    w_down,
    gains,
    m_qkv,
    m_out,
    m_gate_up,
    m_down,
    m_gains,
    v_qkv,
    v_out,
    v_gate_up,
    v_down,
    v_gains,
):
    owner = lax.axis_index("batch")
    core = lax.axis_index("tm")
    where = jnp.stack([core, owner]).astype(jnp.int32)
    shard = w_qkv.shape[0]
    down = w_down.shape[0] // 2
    own = tokens[0]
    fuse_in = can_unpack(shard, down)
    masters = (w_qkv, w_out, w_gate_up, w_down, gains)

    first, second = send_chunks(where, *masters)
    cosine, sine, key_aux, query_aux, ranges = tables(where, sample_ids, pad_flags, offsets)
    first_steps = gather_steps(first, count, first_after=query_aux)
    first_held = first_steps[-1]
    second_steps = gather_steps(second, count, first_steps)
    there = swap_tm(own)

    def gathered(held, number, down):
        other = swap_tm(held)
        if fuse_in:
            return (where, held, other), (count, number, shard, down)
        return unpack_plain(count, number, shard, down, where, held, other), None

    weights, fused = gathered(first_held, 5, 0)
    waits = second_steps[-2:-1] if len(second_steps) > 1 else []
    qa, ka, va, kt, vt, attn_in, gain_pair = project(
        own, there, cosine, sine, key_aux, query_aux, weights, fused, waits
    )
    second_held = tie(second_steps[-1], gain_pair)
    mixed, exact, qb = attend(ranges, qa, ka, vt)
    weights, fused = gathered(second_held, 10, down)
    result, grad_middle, da, *grads = feed(
        own, mixed, exact, cotangent[0], query_aux, gain_pair, weights, fused
    )
    if not fused:
        grads = pack_plain(count, core, grads, 10, shard, down)
    kept, given = grads
    second_total = kept[0] + swap_tm(given).astype(f32)
    second_sums = scatter_steps(second_total, count, owner)

    dqs, owns, recvs = [], [], []
    for group, waits in zip(GROUPS, ([given], [second_total])):
        dq, kept, part = attend_back(*group, ranges, qb, ka, da, va, kt, waits)
        dqs.append(dq)
        owns.append(kept)
        recvs.append(swap_tm(part))
    fused = (5, shard) if fuse_in else None
    shared = (own, cosine, sine, attn_in, gain_pair)
    several = len(second_sums) > 1
    before, grads_before = project_back(
        0, fused, where, shared, [*dqs, owns[0], recvs[0]], second_sums[:1] if several else []
    )
    grad_tokens, *grads = project_back(
        1, fused, where, shared, [owns[1], recvs[1], grad_middle, before, grads_before],
        second_sums[1:2] if several else [],
    )
    if not fused:
        order = [(PARTS[0] + PARTS[1]).index(i) for i in range(9)]
        both = jnp.concatenate([slabs(grads_before), slabs(grads[0])])
        grads = pack_plain(count, core, [unslab(both[jnp.array(order)]), grads[1]], 5, shard, 0)
    kept, given = grads
    first_total = kept[0] + swap_tm(given).astype(f32)
    first_sum = scatter_steps(first_total, count, owner)[-1].reshape(-1, LANES)
    second_sum = second_sums[-1].reshape(-1, LANES)

    sums = jnp.concatenate([first_sum, second_sum], axis=0)
    sums_there = swap_tm(sums)
    squares = jnp.sum(sums * sums) + jnp.sum(sums_there * sums_there)
    total = sum_batch(squares.reshape(1, 1), count)
    firsts = (m_qkv, m_out, m_gate_up, m_down, m_gains)
    seconds = (v_qkv, v_out, v_gate_up, v_down, v_gains)
    if fuse_in:
        updates = update(where, total, sums, sums_there, masters, firsts, seconds)
    else:
        updates = update_plain(core, total, sums, sums_there, masters, firsts, seconds)
    grad_norm, new_first, new_second, new_master, copies = updates
    return (
        result[None],
        grad_tokens[None],
        grad_norm,
        *new_first,
        *new_second,
        *new_master,
        *copies,
    )


def solution(mesh):
    in_specs = (
        P("batch", "tm", None),
        P("batch", "tm", None),
        P("batch", None),
        P("batch", None),
        P("batch", None),
        P("batch", None),
        P("batch", None),
        P("batch", None),
        P("batch", None),
        P(None, "batch"),
        P("batch", None),
        P("batch", None),
        P("batch", None),
        P("batch", None),
        P(None, "batch"),
        P("batch", None),
        P("batch", None),
        P("batch", None),
        P("batch", None),
        P(None, "batch"),
    )
    out_specs = (
        P("batch", "tm", None),
        P("batch", "tm", None),
        P(),
        P("batch", None),
        P("batch", None),
        P("batch", None),
        P("batch", None),
        P(None, "batch"),
        P("batch", None),
        P("batch", None),
        P("batch", None),
        P("batch", None),
        P(None, "batch"),
        P("batch", None),
        P("batch", None),
        P("batch", None),
        P("batch", None),
        P(None, "batch"),
        P("batch", None),
        P("batch", None),
        P("batch", None),
        P("batch", None),
        P(None, "batch"),
    )
    return jax.shard_map(
        partial(per_device, mesh.shape["batch"]), mesh=mesh, in_specs=in_specs, out_specs=out_specs, check_vma=False
    )
```

time: 249 us -> 225 us (0.904)
  local copies, waits for them, and re-layouts: 17.2 us -> 7.31 us
  other arithmetic: 18 us -> 9.52 us
  Pallas kernels: 116 us -> 123 us
  waiting for transfers between devices: 33.6 us -> 26.8 us
  starting transfers between devices: 54.8 us -> 48.8 us
    ppermute x30, waiting for transfers between devices: 31.6 us -> 23.2 us  [permute_batch(): return lax.ppermute(value, 'batch', [(i, i ^ flip) for i in range(count)])]
    pallas_call x7, Pallas kernels: 59.7 us -> 66.3 us  [the longest x1 24.3 us: feed(): pl.pallas_call(partial(feed_kernel, fused), out_shape=out_shape, grid=(le...]
    convert_element_type x9 -> x0, other arithmetic: 5.79 us -> none  [the longest x5 3.77 us: per_device(): copies = [item.astype(bf16) for item in new_master]]
    add x6 -> x9, other arithmetic: 1.94 us -> 7.46 us  [the longest x3 2.94 us: scatter_steps(): total = total + item.astype(f32)]
    ppermute x30, starting transfers between devices: 52.1 us -> 48 us  [permute_batch(): return lax.ppermute(value, 'batch', [(i, i ^ flip) for i in range(count)])]
    unnamed x69 -> x26, local copies, waits for them, and re-layouts: 7.62 us -> 3.56 us
    another operation x7 -> x0, local copies, waits for them, and re-layouts: 2.94 us -> none  [the longest x2 1.47 us: per_device(): cosine = jnp.tile(jnp.cos(angles), (1, 4))]
  transfers between devices with their start and end apart: 39 -> 38, of which waited for: 13 -> 14; matrix products, arithmetic and copies ran while one was open for 9% -> 4% of each run, Pallas kernels for 22% -> 38%
where the time goes in v3:
time: 225 us
  Pallas kernels  123 us (55%)
  starting transfers between devices  48.8 us (22%)
  waiting for transfers between devices  26.8 us (12%)
  other arithmetic  9.52 us (4%)
  between operations  8.82 us (4%)
  local copies, waits for them, and re-layouts  7.31 us (3%)
    ppermute x30, starting transfers between devices, permute_batch(): return lax.ppermute(value, 'batch', [(i, i ^ flip) for i in range(count)])  48 us
    pallas_call x2, Pallas kernels, attend_back(): pl.pallas_call(attend_back_kernel, out_shape=[jax.ShapeDtypeStruct((heads...  35.8 us
    pallas_call x1, Pallas kernels, feed(): pl.pallas_call(partial(feed_kernel, fused), out_shape=out_shape, grid=(le...  24.3 us
    ppermute x30, waiting for transfers between devices, permute_batch(): return lax.ppermute(value, 'batch', [(i, i ^ flip) for i in range(count)])  23.2 us
    pallas_call x1, Pallas kernels, attend(): pl.pallas_call(attend_kernel, out_shape=[jax.ShapeDtypeStruct((length, D)...  21.2 us
    pallas_call x1, Pallas kernels, project(): pl.pallas_call(partial(project_kernel, fused), out_shape=[jax.ShapeDtypeS...  17.2 us
    pallas_call x2, Pallas kernels, project_back(): pl.pallas_call(partial(project_back_kernel, number, fused), out_shape=[ja...  16 us
  transfers between devices with their start and end apart: 38, of which 14 were waited for; matrix products, arithmetic and copies ran while one was open for 4% of the time, Pallas kernels for 38%

profile of v3, /device:TPU:0, one launch (start us, length us, event | category | flops | bytes accessed | tf_op | source)
XLA Modules:
  0.0 224.5 jit_solution(13214967352099696285)
XLA Ops:
  3.1 3.0 %collective-permute-start.1 = (bf16[1,128,128]{2,1,0:T(8,128)(2,1)}, bf16[1,128,128]{2,1,0:T(8,128)(2,1)S(1)}, u32[]{:S(2)}, u32[]{:S(2)}) collective-permute-start(bf16[1,128,128]{2,1,0:T(8,128)(2,1)} %bitcast.82), channel_id=1, source_target_pairs={{0,8},{2,10},{4,12},{6,14},{8,0},{10,2},{12,4},{14,6},{16,24},{18,... | collective-permute-start | bytes 98312 | tf_op jit(solution)/shard_map/ppermute | solution.py:49
  6.1 2.6 %collective-permute-start.2 = (bf16[1,128,128]{2,1,0:T(8,128)(2,1)}, bf16[1,128,128]{2,1,0:T(8,128)(2,1)S(1)}, u32[]{:S(2)}, u32[]{:S(2)}) collective-permute-start(bf16[1,128,128]{2,1,0:T(8,128)(2,1)} %bitcast.83), channel_id=1, source_target_pairs={{0,16},{2,18},{4,20},{6,22},{8,24},{10,26},{12,28},{14,30},{16,0},... | collective-permute-start | bytes 98312 | tf_op jit(solution)/shard_map/ppermute | solution.py:49
  8.8 4.1 %tables.1 = (f32[2048,128]{1,0:T(8,128)}, f32[2048,128]{1,0:T(8,128)}, bf16[2048,128]{1,0:T(8,128)(2,1)}, bf16[1024,128]{1,0:T(8,128)(2,1)}, s32[4,4]{1,0:T(4,128)}) custom-call(s32[2]{0:T(128)} %pad_add_fusion.where.refs_0_.refs_5_, s32[1,2048]{1,0:T(1,128)} %ids.1, s32[1,2048]{1,0:T(1,128)} %pads.1, s32[1,2048]{1,0:T(1,128)} %offsets.1), custom_call_target="tpu_custom_call" | custom-call | flops 3000000000 | bytes 4194304 | tf_op jit(solution)/shard_map/tables/pallas_call | solution.py:389
  18.2 2.5 %collective-permute-done.4 = bf16[4,128,128]{2,1,0:T(8,128)(2,1)S(1)} collective-permute-done((bf16[4,128,128]{2,1,0:T(8,128)(2,1)S(1)}, bf16[4,128,128]{2,1,0:T(8,128)(2,1)S(1)}, u32[]{:S(2)}, u32[]{:S(2)}) %collective-permute-start.4) | collective-permute-done | bytes 131104 | tf_op jit(solution)/shard_map/ppermute | solution.py:49
  20.8 4.1 %collective-permute-done.5 = bf16[4,128,128]{2,1,0:T(8,128)(2,1)S(1)} collective-permute-done((bf16[4,128,128]{2,1,0:T(8,128)(2,1)S(1)}, bf16[4,128,128]{2,1,0:T(8,128)(2,1)S(1)}, u32[]{:S(2)}, u32[]{:S(2)}) %collective-permute-start.5) | collective-permute-done | bytes 131104 | tf_op jit(solution)/shard_map/ppermute | solution.py:49
  26.3 3.7 %collective-permute-start.10 = (bf16[1,336,128]{2,1,0:T(8,128)(2,1)S(1)}, bf16[1,336,128]{2,1,0:T(8,128)(2,1)S(1)}, u32[]{:S(2)}, u32[]{:S(2)}) collective-permute-start(bf16[1,336,128]{2,1,0:T(8,128)(2,1)S(1)} %add_bitcast_fusion), channel_id=1, source_target_pairs={{0,24},{2,26},{4,28},{6,30},{8,16},{10,18},{12,20},{14,22},{16,8},... | collective-permute-start | bytes 258056 | tf_op jit(solution)/shard_map/ppermute | solution.py:49
  33.6 2.9 %collective-permute-done.8 = bf16[1,336,128]{2,1,0:T(8,128)(2,1)S(1)} collective-permute-done((bf16[1,336,128]{2,1,0:T(8,128)(2,1)S(1)}, bf16[1,336,128]{2,1,0:T(8,128)(2,1)S(1)}, u32[]{:S(2)}, u32[]{:S(2)}) %collective-permute-start.8) | collective-permute-done | bytes 86048 | tf_op jit(solution)/shard_map/ppermute | solution.py:49
  42.7 17.2 %project.1 = (bf16[6,1024,128]{2,1,0:T(8,128)(2,1)}, bf16[6,2048,128]{2,1,0:T(8,128)(2,1)}, bf16[6,2048,128]{2,1,0:T(8,128)(2,1)}, bf16[6,64,2048]{2,1,0:T(8,128...) custom-call(bf16[1024,384]{1,0:T(8,128)(2,1)} %bitcast.88, ...), custom_call_target="tpu_custom_call" | custom-call | flops 8999999488 | bytes 16777216 | tf_op jit(solution)/shard_map/project/pallas_call | solution.py:476
  62.2 21.2 %attend.1 = (bf16[1024,384]{1,0:T(8,128)(2,1)}, f32[1024,384]{1,0:T(8,128)}, bf16[6,1024,128]{2,1,0:T(8,128)(2,1)}) custom-call(s32[4,4]{1,0:T(4,128)} %get-tuple-element.77.ranges, bf16[6,1024,128]{2,1,0:T(8,128)(2,1)} %get-tuple-element.84.qa, bf16[6,2048,128]{2,1,0:T(8,128)(2,1)} %get-tuple-element.85.ka, bf16[6,72,2048]{2,1,0:T(8,128)(2,1)} %get-tuple-element.86.vt), custom_call_target="tpu_custom_call" | custom-call | flops 12000000000 | bytes 12582912 | tf_op jit(solution)/shard_map/attend/pallas_call | solution.py:568
  84.9 24.3 %feed.1 = (bf16[1024,384]{1,0:T(8,128)(2,1)}, f32[1024,384]{1,0:T(8,128)}, bf16[6,1024,128]{2,1,0:T(8,128)(2,1)}, f32[2,16,336,128]{3,2,1,0:T(8,128)}, bf16[16,336,128]{2,1,0:T(8,128)(2,1)}) custom-call(bf16[1024,384]{1,0:T(8,128)(2,1)} %bitcast.89, bf16[1024,384]{1,0:T(8,128)(2,1)} %get-tuple-element.87.mixed, f32[1024,384]{1,0:T(8,128)} %get-tuple-element.88.exact, ...), custom_call_target="tpu_custom_call" | custom-call | flops 14000000000 | bytes 16777216 | tf_op jit(solution)/shard_map/feed/pallas_call | solution.py:836
  109.7 13.9 %attend_back.3 = (f32[2,64,1024]{2,1,0:T(8,128)}, f32[2,1024,128]{2,1,0:T(8,128)}, bf16[2,1024,128]{2,1,0:T(8,128)(2,1)}) custom-call(s32[4,4]{1,0:T(4,128)} %get-tuple-element.77.ranges, bf16[6,1024,128]{2,1,0:T(8,128)(2,1)} %get-tuple-element.92.qb, bf16[6,2048,128]{2,1,0:T(8,128)(2,1)} %get-tuple-element.85.ka, ...), custom_call_target="tpu_custom_call" | custom-call | flops 12000000000 | bytes 8388608 | tf_op jit(solution)/shard_map/attend_back/pallas_call | solution.py:640
  129.4 21.9 %attend_back.2 = (f32[4,64,1024]{2,1,0:T(8,128)}, f32[4,1024,128]{2,1,0:T(8,128)}, bf16[4,1024,128]{2,1,0:T(8,128)(2,1)}) custom-call(s32[4,4]{1,0:T(4,128)} %get-tuple-element.77.ranges, bf16[6,1024,128]{2,1,0:T(8,128)(2,1)} %get-tuple-element.92.qb, bf16[6,2048,128]{2,1,0:T(8,128)(2,1)} %get-tuple-element.85.ka, ...), custom_call_target="tpu_custom_call" | custom-call | flops 12000000000 | bytes 8388608 | tf_op jit(solution)/shard_map/attend_back/pallas_call | solution.py:640
  155.0 2.1 collective-permute-start.23
  157.1 7.6 %project_back.2 = (f32[1024,384]{1,0:T(8,128)}, f32[384,640]{1,0:T(8,128)}) custom-call(bf16[1024,384]{1,0:T(8,128)(2,1)} %bitcast.90, f32[2048,128]{1,0:T(8,128)} %get-tuple-element.78.cosine, f32[2048,128]{1,0:T(8,128)} %get-tuple-element.79.sine, bf16[384,1152]{1,0:T(8,128)(2,1)} %get-tuple-element.91.w, f32[8,384]{1,0:T(8,128)} %get-tuple-element.89.gains, ...), custom_call_target="tpu_custom_call" | custom-call | flops 4000000000 | bytes 8388608 | tf_op jit(solution)/shard_map/project_back/pallas_call | solution.py:975
  167.4 8.4 %project_back.3 = (bf16[1024,384]{1,0:T(8,128)(2,1)}, f32[2,16,120,128]{3,2,1,0:T(8,128)}, bf16[16,120,128]{2,1,0:T(8,128)(2,1)}) custom-call(bf16[1024,384]{1,0:T(8,128)(2,1)} %bitcast.91, f32[2048,128]{1,0:T(8,128)} %get-tuple-element.78.cosine, f32[2048,128]{1,0:T(8,128)} %get-tuple-element.79.sine, bf16[384,1152]{1,0:T(8,128)(2,1)} %get-tuple-element.91.w, ...), custom_call_target="tpu_custom_call" | custom-call | flops 4000000000 | bytes 8388608 | tf_op jit(solution)/shard_map/project_back/pallas_call | solution.py:975
  182.9 2.3 %collective-permute-done.25 = bf16[4,120,128]{2,1,0:T(8,128)(2,1)S(1)} collective-permute-done((bf16[4,120,128]{2,1,0:T(8,128)(2,1)S(1)}, bf16[4,120,128]{2,1,0:T(8,128)(2,1)S(1)}, u32[]{:S(2)}, u32[]{:S(2)}) %collective-permute-start.25) | collective-permute-done | bytes 122912 | tf_op jit(solution)/shard_map/ppermute | solution.py:49
  188.7 2.2 collective-permute-start.29
  193.5 3.0 %collective-permute-done.30 = bf16[1,120,128]{2,1,0:T(8,128)(2,1)S(1)} collective-permute-done((bf16[1,120,128]{2,1,0:T(8,128)(2,1)S(1)}, bf16[1,120,128]{2,1,0:T(8,128)(2,1)S(1)}, u32[]{:S(2)}, u32[]{:S(2)}) %collective-permute-start.30) | collective-permute-done | bytes 30752 | tf_op jit(solution)/shard_map/ppermute | solution.py:49
  200.7 2.2 collective-permute-start.33
  202.8 2.7 %collective-permute-start.34 = (f32[1,1]{1,0:T(1,128)}, f32[1,1]{1,0:T(1,128)}, u32[]{:S(2)}, u32[]{:S(2)}) collective-permute-start(f32[1,1]{1,0:T(1,128)} %bitcast.29), channel_id=1, source_target_pairs={{0,6},{2,4},{4,2},{6,0},{8,14},{10,12},{12,10},{14,8},{16,22},{18,... | collective-permute-start | bytes 20 | tf_op jit(solution)/shard_map/ppermute | solution.py:49
  205.6 2.6 %collective-permute-start.32 = (f32[1,1]{1,0:T(1,128)}, f32[1,1]{1,0:T(1,128)}, u32[]{:S(2)}, u32[]{:S(2)}) collective-permute-start(f32[1,1]{1,0:T(1,128)} %bitcast.29), channel_id=1, source_target_pairs={{0,2},{2,0},{4,6},{6,4},{8,10},{10,8},{12,14},{14,12},{16,18},{18,... | collective-permute-start | bytes 20 | tf_op jit(solution)/shard_map/ppermute | solution.py:49
  212.4 3.4 %collective-permute-start.37 = (f32[1,1]{1,0:T(1,128)}, f32[1,1]{1,0:T(1,128)}, u32[]{:S(2)}, u32[]{:S(2)}) collective-permute-start(f32[1,1]{1,0:T(1,128)} %add.165), channel_id=1, source_target_pairs={{0,24},{2,26},{4,28},{6,30},{8,16},{10,18},{12,20},{14,22},{16,8},... | collective-permute-start | bytes 20 | tf_op jit(solution)/shard_map/ppermute | solution.py:49
  215.8 2.6 %collective-permute-start.35 = (f32[1,1]{1,0:T(1,128)}, f32[1,1]{1,0:T(1,128)}, u32[]{:S(2)}, u32[]{:S(2)}) collective-permute-start(f32[1,1]{1,0:T(1,128)} %add.165), channel_id=1, source_target_pairs={{0,8},{2,10},{4,12},{6,14},{8,0},{10,2},{12,4},{14,6},{16,24},{18,... | collective-permute-start | bytes 20 | tf_op jit(solution)/shard_map/ppermute | solution.py:49
  221.3 3.0 %update.1 = (f32[1,1]{1,0:T(1,128)}, f32[24,1152]{1,0:T(8,128)}, f32[24,384]{1,0:T(8,128)}, f32[24,2048]{1,0:T(8,128)}, f32[64,384]{1,0:T(8,128)}, /*index=5*/f3...) custom-call(s32[2]{0:T(128)} %pad_add_fusion.where.refs_0_.refs_5_, ...), custom_call_target="tpu_custom_call" | custom-call | tf_op jit(solution)/shard_map/update/pallas_call | solution.py:1057
  (111 shorter events, 52.2 us)
Async XLA Ops:
  3.1 11.5 %collective-permute-start.1 = (bf16[1,128,128]{2,1,0:T(8,128)(2,1)}, bf16[1,128,128]{2,1,0:T(8,128)(2,1)S(1)}, u32[]{:S(2)}, u32[]{:S(2)}) collective-permute-start(bf16[1,128,128]{2,1,0:T(8,128)(2,1)} %bitcast.82), channel_id=1, source_target_pairs={{0,8},{2,10},{4,12},{6,14},{8,0},{10,2},{12,4},{14,6},{16,24},{18,... | collective-permute-start | bytes 98312 | tf_op jit(solution)/shard_map/ppermute | solution.py:49
  6.1 8.5 %collective-permute-start.2 = (bf16[1,128,128]{2,1,0:T(8,128)(2,1)}, bf16[1,128,128]{2,1,0:T(8,128)(2,1)S(1)}, u32[]{:S(2)}, u32[]{:S(2)}) collective-permute-start(bf16[1,128,128]{2,1,0:T(8,128)(2,1)} %bitcast.83), channel_id=1, source_target_pairs={{0,16},{2,18},{4,20},{6,22},{8,24},{10,26},{12,28},{14,30},{16,0},... | collective-permute-start | bytes 98312 | tf_op jit(solution)/shard_map/ppermute | solution.py:49
  8.7 32.9 %collective-permute-start = (bf16[1024,384]{1,0:T(8,128)(2,1)}, bf16[1024,384]{1,0:T(8,128)(2,1)S(1)}, u32[]{:S(2)}, u32[]{:S(2)}) collective-permute-start(bf16[1024,384]{1,0:T(8,128)(2,1)} %bitcast.87), channel_id=1, source_target_pairs={{0,1},{1,0},{2,3},{3,2},{4,5},{5,4},{6,7},{7,6},{8,9},{9,8},{10,11... | collective-permute-start | bytes 2359304 | tf_op jit(solution)/shard_map/ppermute | solution.py:53
  16.5 8.4 %collective-permute-start.5 = (bf16[4,128,128]{2,1,0:T(8,128)(2,1)S(1)}, bf16[4,128,128]{2,1,0:T(8,128)(2,1)S(1)}, u32[]{:S(2)}, u32[]{:S(2)}) collective-permute-start(bf16[4,128,128]{2,1,0:T(8,128)(2,1)S(1)} %maximum_add_fusion), channel_id=1, source_target_pairs={{0,4},{2,6},{4,0},{6,2},{8,12},{10,14},{12,8},{14,10},{16,20},{18,... | collective-permute-start | bytes 393224 | tf_op jit(solution)/shard_map/ppermute | solution.py:49
  25.0 16.7 %collective-permute-start.7 = (bf16[16,128,128]{2,1,0:T(8,128)(2,1)S(1)}, bf16[16,128,128]{2,1,0:T(8,128)(2,1)S(1)}, u32[]{:S(2)}, u32[]{:S(2)}) collective-permute-start(bf16[16,128,128]{2,1,0:T(8,128)(2,1)S(1)} %pad_maximum_fusion.refs_1_), channel_id=1, source_target_pairs={{0,1},{1,0},{2,3},{3,2},{4,5},{5,4},{6,7},{7,6},{8,9},{9,8},{10,11... | collective-permute-start | bytes 1572872 | tf_op jit(solution)/shard_map/ppermute | solution.py:53
  26.3 7.2 %collective-permute-start.10 = (bf16[1,336,128]{2,1,0:T(8,128)(2,1)S(1)}, bf16[1,336,128]{2,1,0:T(8,128)(2,1)S(1)}, u32[]{:S(2)}, u32[]{:S(2)}) collective-permute-start(bf16[1,336,128]{2,1,0:T(8,128)(2,1)S(1)} %add_bitcast_fusion), channel_id=1, source_target_pairs={{0,24},{2,26},{4,28},{6,30},{8,16},{10,18},{12,20},{14,22},{16,8},... | collective-permute-start | bytes 258056 | tf_op jit(solution)/shard_map/ppermute | solution.py:49
  30.0 7.3 %collective-permute-start.9 = (bf16[1,336,128]{2,1,0:T(8,128)(2,1)S(1)}, bf16[1,336,128]{2,1,0:T(8,128)(2,1)S(1)}, u32[]{:S(2)}, u32[]{:S(2)}) collective-permute-start(bf16[1,336,128]{2,1,0:T(8,128)(2,1)S(1)} %add_bitcast_fusion), channel_id=1, source_target_pairs={{0,16},{2,18},{4,20},{6,22},{8,24},{10,26},{12,28},{14,30},{16,0},... | collective-permute-start | bytes 258056 | tf_op jit(solution)/shard_map/ppermute | solution.py:49
  38.1 23.6 %collective-permute-start.11 = (bf16[4,336,128]{2,1,0:T(8,128)(2,1)S(1)}, bf16[4,336,128]{2,1,0:T(8,128)(2,1)S(1)}, u32[]{:S(2)}, u32[]{:S(2)}) collective-permute-start(bf16[4,336,128]{2,1,0:T(8,128)(2,1)S(1)} %get-tuple-element.140), channel_id=1, source_target_pairs={{0,2},{2,0},{4,6},{6,4},{8,10},{10,8},{12,14},{14,12},{16,18},{18,... | collective-permute-start | bytes 1032200 | tf_op jit(solution)/shard_map/ppermute | solution.py:49
  39.4 22.4 %collective-permute-start.12 = (bf16[4,336,128]{2,1,0:T(8,128)(2,1)S(1)}, bf16[4,336,128]{2,1,0:T(8,128)(2,1)S(1)}, u32[]{:S(2)}, u32[]{:S(2)}) collective-permute-start(bf16[4,336,128]{2,1,0:T(8,128)(2,1)S(1)} %get-tuple-element.140), channel_id=1, source_target_pairs={{0,4},{2,6},{4,0},{6,2},{8,12},{10,14},{12,8},{14,10},{16,20},{18,... | collective-permute-start | bytes 1032200 | tf_op jit(solution)/shard_map/ppermute | solution.py:49
  40.2 21.6 %collective-permute-start.13 = (bf16[4,336,128]{2,1,0:T(8,128)(2,1)S(1)}, bf16[4,336,128]{2,1,0:T(8,128)(2,1)S(1)}, u32[]{:S(2)}, u32[]{:S(2)}) collective-permute-start(bf16[4,336,128]{2,1,0:T(8,128)(2,1)S(1)} %get-tuple-element.140), channel_id=1, source_target_pairs={{0,6},{2,4},{4,2},{6,0},{8,14},{10,12},{12,10},{14,8},{16,22},{18,... | collective-permute-start | bytes 1032200 | tf_op jit(solution)/shard_map/ppermute | solution.py:49
  62.1 21.3 %collective-permute-start.14 = (f32[16,336,128]{2,1,0:T(8,128)S(1)}, f32[16,336,128]{2,1,0:T(8,128)S(1)}, u32[]{:S(2)}, u32[]{:S(2)}) collective-permute-start(f32[16,336,128]{2,1,0:T(8,128)S(1)} %convert_add_fusion.refs_1_), channel_id=1, source_target_pairs={{0,1},{1,0},{2,3},{3,2},{4,5},{5,4},{6,7},{7,6},{8,9},{9,8},{10,11... | collective-permute-start | bytes 8257544 | tf_op jit(solution)/shard_map/ppermute | solution.py:53
  109.2 14.4 %collective-permute-start.15 = (bf16[16,336,128]{2,1,0:T(8,128)(2,1)}, bf16[16,336,128]{2,1,0:T(8,128)(2,1)S(1)}, u32[]{:S(2)}, u32[]{:S(2)}) collective-permute-start(bf16[16,336,128]{2,1,0:T(8,128)(2,1)} %get-tuple-element.97.refs_0_), channel_id=1, source_target_pairs={{0,1},{1,0},{2,3},{3,2},{4,5},{5,4},{6,7},{7,6},{8,9},{9,8},{10,11... | collective-permute-start | bytes 4128776 | tf_op jit(solution)/shard_map/ppermute | solution.py:53
  123.5 33.6 %collective-permute-start.17 = (bf16[2,1024,128]{2,1,0:T(8,128)(2,1)}, bf16[2,1024,128]{2,1,0:T(8,128)(2,1)}, u32[]{:S(2)}, u32[]{:S(2)}) collective-permute-start(bf16[2,1024,128]{2,1,0:T(8,128)(2,1)} %get-tuple-element.104), channel_id=1, source_target_pairs={{0,1},{1,0},{2,3},{3,2},{4,5},{5,4},{6,7},{7,6},{8,9},{9,8},{10,11... | collective-permute-start | bytes 1572872 | tf_op jit(solution)/shard_map/ppermute | solution.py:53
  125.8 25.5 %collective-permute-start.18 = (bf16[4,336,128]{2,1,0:T(8,128)(2,1)S(1)}, bf16[4,336,128]{2,1,0:T(8,128)(2,1)S(1)}, u32[]{:S(2)}, u32[]{:S(2)}) collective-permute-start(bf16[4,336,128]{2,1,0:T(8,128)(2,1)S(1)} %get-tuple-element.131), channel_id=1, source_target_pairs={{0,2},{2,0},{4,6},{6,4},{8,10},{10,8},{12,14},{14,12},{16,18},{18,... | collective-permute-start | bytes 1032200 | tf_op jit(solution)/shard_map/ppermute | solution.py:49
  127.1 24.2 %collective-permute-start.19 = (bf16[4,336,128]{2,1,0:T(8,128)(2,1)S(1)}, bf16[4,336,128]{2,1,0:T(8,128)(2,1)S(1)}, u32[]{:S(2)}, u32[]{:S(2)}) collective-permute-start(bf16[4,336,128]{2,1,0:T(8,128)(2,1)S(1)} %get-tuple-element.132), channel_id=1, source_target_pairs={{0,4},{2,6},{4,0},{6,2},{8,12},{10,14},{12,8},{14,10},{16,20},{18,... | collective-permute-start | bytes 1032200 | tf_op jit(solution)/shard_map/ppermute | solution.py:49
  127.9 23.4 %collective-permute-start.20 = (bf16[4,336,128]{2,1,0:T(8,128)(2,1)S(1)}, bf16[4,336,128]{2,1,0:T(8,128)(2,1)S(1)}, u32[]{:S(2)}, u32[]{:S(2)}) collective-permute-start(bf16[4,336,128]{2,1,0:T(8,128)(2,1)S(1)} %get-tuple-element.133), channel_id=1, source_target_pairs={{0,6},{2,4},{4,2},{6,0},{8,14},{10,12},{12,10},{14,8},{16,22},{18,... | collective-permute-start | bytes 1032200 | tf_op jit(solution)/shard_map/ppermute | solution.py:49
  151.3 15.1 %collective-permute-start.16 = (bf16[4,1024,128]{2,1,0:T(8,128)(2,1)}, bf16[4,1024,128]{2,1,0:T(8,128)(2,1)S(1)}, u32[]{:S(2)}, u32[]{:S(2)}) collective-permute-start(bf16[4,1024,128]{2,1,0:T(8,128)(2,1)} %get-tuple-element.99), channel_id=1, source_target_pairs={{0,1},{1,0},{2,3},{3,2},{4,5},{5,4},{6,7},{7,6},{8,9},{9,8},{10,11... | collective-permute-start | bytes 3145736 | tf_op jit(solution)/shard_map/ppermute | solution.py:53
  152.7 12.1 %collective-permute-start.21 = (bf16[1,336,128]{2,1,0:T(8,128)(2,1)S(1)}, bf16[1,336,128]{2,1,0:T(8,128)(2,1)S(1)}, u32[]{:S(2)}, u32[]{:S(2)}) collective-permute-start(bf16[1,336,128]{2,1,0:T(8,128)(2,1)S(1)} %get-tuple-element.137), channel_id=1, source_target_pairs={{0,8},{2,10},{4,12},{6,14},{8,0},{10,2},{12,4},{14,6},{16,24},{18,... | collective-permute-start | bytes 258056 | tf_op jit(solution)/shard_map/ppermute | solution.py:49
  152.9 11.9 %collective-permute-start.22 = (bf16[1,336,128]{2,1,0:T(8,128)(2,1)S(1)}, bf16[1,336,128]{2,1,0:T(8,128)(2,1)S(1)}, u32[]{:S(2)}, u32[]{:S(2)}) collective-permute-start(bf16[1,336,128]{2,1,0:T(8,128)(2,1)S(1)} %get-tuple-element.139), channel_id=1, source_target_pairs={{0,16},{2,18},{4,20},{6,22},{8,24},{10,26},{12,28},{14,30},{16,0},... | collective-permute-start | bytes 258056 | tf_op jit(solution)/shard_map/ppermute | solution.py:49
  155.0 9.8 %collective-permute-start.23 = (bf16[1,336,128]{2,1,0:T(8,128)(2,1)S(1)}, bf16[1,336,128]{2,1,0:T(8,128)(2,1)S(1)}, u32[]{:S(2)}, u32[]{:S(2)}) collective-permute-start(bf16[1,336,128]{2,1,0:T(8,128)(2,1)S(1)} %get-tuple-element.138), channel_id=1, source_target_pairs={{0,24},{2,26},{4,28},{6,30},{8,16},{10,18},{12,20},{14,22},{16,8},... | collective-permute-start | bytes 258056 | tf_op jit(solution)/shard_map/ppermute | solution.py:49
  200.7 9.1 %collective-permute-start.33 = (f32[1,1]{1,0:T(1,128)}, f32[1,1]{1,0:T(1,128)}, u32[]{:S(2)}, u32[]{:S(2)}) collective-permute-start(f32[1,1]{1,0:T(1,128)} %bitcast.29), channel_id=1, source_target_pairs={{0,4},{2,6},{4,0},{6,2},{8,12},{10,14},{12,8},{14,10},{16,20},{18,... | collective-permute-start | bytes 20 | tf_op jit(solution)/shard_map/ppermute | solution.py:49
  202.8 6.9 %collective-permute-start.34 = (f32[1,1]{1,0:T(1,128)}, f32[1,1]{1,0:T(1,128)}, u32[]{:S(2)}, u32[]{:S(2)}) collective-permute-start(f32[1,1]{1,0:T(1,128)} %bitcast.29), channel_id=1, source_target_pairs={{0,6},{2,4},{4,2},{6,0},{8,14},{10,12},{12,10},{14,8},{16,22},{18,... | collective-permute-start | bytes 20 | tf_op jit(solution)/shard_map/ppermute | solution.py:49
  211.0 9.0 %collective-permute-start.36 = (f32[1,1]{1,0:T(1,128)}, f32[1,1]{1,0:T(1,128)}, u32[]{:S(2)}, u32[]{:S(2)}) collective-permute-start(f32[1,1]{1,0:T(1,128)} %add.165), channel_id=1, source_target_pairs={{0,16},{2,18},{4,20},{6,22},{8,24},{10,26},{12,28},{14,30},{16,0},... | collective-permute-start | bytes 20 | tf_op jit(solution)/shard_map/ppermute | solution.py:49
  212.4 7.6 %collective-permute-start.37 = (f32[1,1]{1,0:T(1,128)}, f32[1,1]{1,0:T(1,128)}, u32[]{:S(2)}, u32[]{:S(2)}) collective-permute-start(f32[1,1]{1,0:T(1,128)} %add.165), channel_id=1, source_target_pairs={{0,24},{2,26},{4,28},{6,30},{8,16},{10,18},{12,20},{14,22},{16,8},... | collective-permute-start | bytes 20 | tf_op jit(solution)/shard_map/ppermute | solution.py:49
  (27 other events, 209.6 us)

commit v4 on v3

--- a/solution.py
+++ b/solution.py
@@ -90,12 +90,9 @@
 
 
 def sum_batch(value, count):
-    for low, width in bit_groups(count):
-        pieces = [value] + [permute_batch(value, k << low, count) for k in range(1, 1 << width)]
-        while len(pieces) > 1:
-            pieces = [pieces[i] + pieces[i + 1] for i in range(0, len(pieces), 2)]
-        value = pieces[0]
-    return value
+    value = jnp.broadcast_to(value[:, None], (count, 1, LANES))
+    value = lax.all_to_all(value, "batch", 0, 0, tiled=True)
+    return jnp.sum(value, axis=0)
 
 
 def row_scale(values):
@@ -129,46 +126,46 @@
     return place
 
 
-def tie(value, other):
-    if other is None:
-        return value
-    return value + other.reshape(-1)[0] * jnp.zeros((), value.dtype)
-
-
-def gather_steps(chunk, count, after=None, first_after=None, last_after=None):
-    held, steps = chunk[None], []
-    for n, (low, width) in enumerate(reversed(bit_groups(count))):
-        held = tie(held, after[n] if after else None)
-        pieces = [held] + [permute_batch(held, k << low, count) for k in range(1, 1 << width)]
-        held = jnp.concatenate(pieces, axis=0)
-        if n == 0:
-            held = tie(held, first_after)
-        steps.append(held)
-    return steps
-
-
-def send_kernel(shard, down, where, w_qkv, w_out, w_gate_up, w_down, gains, first, second, a, b, c):
+def exchange_all(held, low, width, count):
+    return [held] + [permute_batch(held, k << low, count) for k in range(1, 1 << width)]
+
+
+def hold(values, waits):
+    spec = pl.BlockSpec(memory_space=pl.ANY)
+    number = len(values)
+    return pl.pallas_call(
+        lambda *refs: None,
+        out_shape=[jax.ShapeDtypeStruct(item.shape, item.dtype) for item in values],
+        in_specs=[spec] * (number + len(waits)),
+        out_specs=[spec] * number,
+        input_output_aliases={i: i for i in range(number)},
+        name="hold",
+    )(*values, *waits)
+
+
+def send_kernel(shard, plan, down, where, *refs):
+    sources, (target, stage, square) = refs[: len(refs) - 3], refs[len(refs) - 3 :]
+    number = len(plan) // 2
     core = where[0]
-    a[...] = jnp.zeros_like(a)
-    c[...] = jnp.zeros_like(c)
-    c[0:2, 0:shard] = gains[...]
-    column = c[...].T
-    pieces = [(w_qkv, i) for i in range(9)] + [(None, 0)]
-    more = [(w_out, i) for i in range(3)] + [(w_gate_up, i) for i in range(16)] + [(None, 1)]
+    stage[...] = jnp.zeros_like(stage)
+    gain_at = [i for i, item in enumerate(plan) if item == "gain"]
+    if gain_at:
+        square[...] = jnp.zeros_like(square)
+        square[0:2, 0:shard] = sources[-1][...]
+        column = square[...].T
 
     def fill(half):
-        for target, items in ((a, pieces), (b, more)):
-            number = len(items) // 2
-            for i in range(number):
-                source, at = items[half * number + i]
-                rows = slice(i * shard, (i + 1) * shard)
-                if source is not None:
-                    target[rows, :] = source[:, at * LANES : (at + 1) * LANES]
-                else:
-                    target[rows, :] = column[:shard] if at == 0 else jnp.zeros((shard, LANES), f32)
-        for i in range(3):
-            start = 10 * shard + i * down
-            b[start : start + down, :] = w_down[
+        for i in range(number):
+            item = plan[half * number + i]
+            rows = slice(i * shard, (i + 1) * shard)
+            if item == "gain":
+                stage[rows, :] = column[:shard]
+            elif item is not None:
+                which, at = item
+                stage[rows, :] = sources[which][:, at * LANES : (at + 1) * LANES]
+        for i in range(3 if down else 0):
+            start = number * shard + i * down
+            stage[start : start + down, :] = sources[2][
                 half * down : (half + 1) * down, i * LANES : (i + 1) * LANES
             ]
 
@@ -180,66 +177,98 @@
     def _():
         fill(1)
 
-    first[...] = a[...].astype(bf16)
-    second[...] = b[...].astype(bf16)
-
-
-def send_chunks(where, w_qkv, w_out, w_gate_up, w_down, gains):
-    shard, down = w_qkv.shape[0], w_down.shape[0] // 2
+    target[...] = stage[...].astype(bf16)
+
+
+def send_chunk(where, plan, down, sources, waits):
+    shard = sources[0].shape[0]
+    rows = len(plan) // 2 * shard + 3 * down
+    rows = -(-rows // 16) * 16
     core = where[0]
-    first_rows = -(-5 * shard // 16) * 16
-    second_rows = 10 * shard + 3 * down
     if shard % 8 == 0 and down % 8 == 0:
         spec = pl.BlockSpec(memory_space=pltpu.VMEM)
+
+        def kernel(where, *refs):
+            kept = refs[: len(sources)] + refs[len(sources) + len(waits) :]
+            send_kernel(shard, plan, down, where, *kept)
+
         return pl.pallas_call(
-            partial(send_kernel, shard, down),
-            out_shape=[
-                jax.ShapeDtypeStruct((first_rows, LANES), bf16),
-                jax.ShapeDtypeStruct((second_rows, LANES), bf16),
-            ],
-            in_specs=[pl.BlockSpec(memory_space=pltpu.SMEM)] + [spec] * 5,
-            out_specs=[spec] * 2,
-            scratch_shapes=[
-                pltpu.VMEM((first_rows, LANES), f32),
-                pltpu.VMEM((second_rows, LANES), f32),
-                pltpu.VMEM((LANES, LANES), f32),
-            ],
+            kernel,
+            out_shape=jax.ShapeDtypeStruct((rows, LANES), bf16),
+            in_specs=[pl.BlockSpec(memory_space=pltpu.SMEM)]
+            + [spec] * len(sources)
+            + [pl.BlockSpec(memory_space=pl.ANY)] * len(waits),
+            out_specs=spec,
+            scratch_shapes=[pltpu.VMEM((rows, LANES), f32), pltpu.VMEM((LANES, LANES), f32)],
             compiler_params=pltpu.CompilerParams(vmem_limit_bytes=VMEM_LIMIT),
-            name="send_chunks",
-        )(where, w_qkv, w_out, w_gate_up, w_down, gains)
-    gain_slab = jnp.pad(gains.T, ((0, 0), (0, LANES - 2)))[None]
-    first = jnp.concatenate([slabs(w_qkv), gain_slab]).reshape(2, 5 * shard, LANES)
-    first = jnp.where(core == 0, first[0], first[1]).astype(bf16)
-    first = jnp.pad(first, ((0, first_rows - first.shape[0]), (0, 0)))
-    second = jnp.concatenate(
-        [slabs(w_out), slabs(w_gate_up), jnp.zeros((1, shard, LANES), f32)]
-    ).reshape(2, 10 * shard, LANES)
-    downs = slabs(w_down).reshape(3, 2, down, LANES).transpose(1, 0, 2, 3)
-    downs = downs.reshape(2, 3 * down, LANES)
-    second = jnp.where(
-        core == 0,
-        jnp.concatenate([second[0], downs[0]]),
-        jnp.concatenate([second[1], downs[1]]),
-    ).astype(bf16)
-    return first, second
-
-
-def unpack(count, number, shard, down, where, mine, other, stage, w_down):
+            name="send_chunk",
+        )(where, *sources, *waits)
+    stacks = {i: slabs(item) for i, item in enumerate(sources) if item.shape[1] % LANES == 0}
+    pieces = []
+    for item in plan:
+        if item == "gain":
+            pieces.append(jnp.pad(sources[-1].T, ((0, 0), (0, LANES - 2))))
+        elif item is None:
+            pieces.append(jnp.zeros((shard, LANES), f32))
+        else:
+            pieces.append(stacks[item[0]][item[1]])
+    half = len(plan) // 2
+    halves = [jnp.concatenate(pieces[:half]), jnp.concatenate(pieces[half:])]
+    if down:
+        for i in range(2):
+            part = stacks[2][:, i * down : (i + 1) * down].reshape(3 * down, LANES)
+            halves[i] = jnp.concatenate([halves[i], part])
+    chunk = jnp.where(core == 0, halves[0], halves[1]).astype(bf16)
+    return jnp.pad(chunk, ((0, rows - chunk.shape[0]), (0, 0)))
+
+
+FIRST_PLAN = tuple((0, i) for i in range(9)) + ("gain",)
+SECOND_PLAN = tuple((0, i) for i in range(3)) + tuple((1, i) for i in range(16)) + (None,)
+
+
+def gather(chunk, count, waits):
+    held = chunk[None]
+    groups = bit_groups(count)[::-1]
+    for n, (low, width) in enumerate(groups):
+        pieces = exchange_all(held, low, width, count)
+        if n == 0:
+            pieces[1:] = hold(pieces[1:], waits)
+        if n + 1 < len(groups):
+            held = jnp.concatenate(pieces, axis=0)
+    return held, pieces
+
+
+def unpack(count, number, shard, down, where, pieces, others, stage, w_down):
     core, owner = where[0], where[1]
-    for source, half in ((mine, core), (other, 1 - core)):
-
-        def one(device, carry, source=source, half=half):
-            chunk = source[relative_place(device, owner, count)].astype(f32)
-            for i in range(number):
-                rows = pl.ds(pl.multiple_of(device * shard, 8), shard)
-                stage[half * number + i, rows, :] = chunk[i * shard : (i + 1) * shard]
-            for i in range(3 if down else 0):
-                start = number * shard + i * down
-                rows = pl.ds(pl.multiple_of((device * 2 + half) * down, 16), down)
-                w_down[rows, i * LANES : (i + 1) * LANES] = chunk[start : start + down].astype(bf16)
-            return carry
-
-        lax.fori_loop(0, count, one, 0)
+    last = bit_groups(count)[0][1]
+    for sources, half in ((pieces, core), (others, 1 - core)):
+        for flip, source in enumerate(sources):
+
+            def one(n, carry, source=source, half=half, flip=flip):
+                inner = n // (count >> last)
+                device = owner ^ (flip + inner) ^ (relative_flips(n % (count >> last), count) << last)
+                chunk = source[n].astype(f32)
+                for i in range(number):
+                    rows = pl.ds(pl.multiple_of(device * shard, 8), shard)
+                    stage[half * number + i, rows, :] = chunk[i * shard : (i + 1) * shard]
+                for i in range(3 if down else 0):
+                    start = number * shard + i * down
+                    rows = pl.ds(pl.multiple_of((device * 2 + half) * down, 16), down)
+                    w_down[rows, i * LANES : (i + 1) * LANES] = chunk[start : start + down].astype(
+                        bf16
+                    )
+                return carry
+
+            lax.fori_loop(0, source.shape[0], one, 0, unroll=True)
+
+
+def relative_flips(place, count):
+    last = bit_groups(count)[0][1]
+    flips, scale = 0, 1
+    for low, width in reversed(bit_groups(count)[1:]):
+        flips = flips + (((place // scale) & ((1 << width) - 1)) << (low - last))
+        scale <<= width
+    return flips
 
 
 def can_unpack(shard, down):
@@ -249,6 +278,7 @@
 def unpack_plain(count, number, shard, down, where, mine, other):
     core, owner = where[0], where[1]
     places = relative_place(jnp.arange(count, dtype=jnp.int32), owner, count)
+    mine, other = jnp.concatenate(mine), jnp.concatenate(other)
     low = jnp.take(jnp.where(core == 0, mine, other), places, axis=0)
     high = jnp.take(jnp.where(core == 0, other, mine), places, axis=0)
 
@@ -334,7 +364,8 @@
     return steps
 
 
-def tables_kernel(length, where, ids, pads, offsets, cosine, sine, key_aux, query_aux, ranges):
+def tables_kernel(length, where, ids, pads, offsets, *refs):
+    cosine, sine, key_aux, query_aux, ranges = refs[-5:]
     core = where[0]
     whole = 2 * length
 
@@ -381,7 +412,7 @@
         ranges[3, n] = bounds[0][1] + bounds[1][1]
 
 
-def tables(where, ids, pads, offsets):
+def tables(where, ids, pads, offsets, waits):
     whole = ids.shape[1]
     length = whole // 2
     spec = pl.BlockSpec(memory_space=pltpu.VMEM)
@@ -395,19 +426,20 @@
             jax.ShapeDtypeStruct((length, LANES), bf16),
             jax.ShapeDtypeStruct((4, length // BLOCK), jnp.int32),
         ],
-        in_specs=[smem, spec, spec, spec],
+        in_specs=[smem, spec, spec, spec] + [pl.BlockSpec(memory_space=pl.ANY)] * len(waits),
         out_specs=[spec] * 4 + [smem],
         compiler_params=pltpu.CompilerParams(vmem_limit_bytes=VMEM_LIMIT),
         cost_estimate=cost(3 * 10**9, 4 * 2**20),
         name="tables",
-    )(where, ids, pads, offsets)
+    )(where, ids, pads, offsets, *waits)
 
 
 def project_kernel(
     fused, own, there, cosine, sine, key_aux, query_aux, *refs
 ):
     if fused:
-        where, mine, other, qa, ka, va, kt, vt, w, gains, stage = refs[:3] + refs[-8:]
+        where, (qa, ka, va, kt, vt, w, gains, stage) = refs[0], refs[-8:]
+        mine, other = refs[1:2], refs[2:3]
     else:
         w_in, gains_in, qa, ka, va, kt, vt, w, gains = refs[:2] + refs[-7:]
 
@@ -470,7 +502,7 @@
     last = lambda i: (jnp.maximum(i - steps, 0), 0)
     spec = pl.BlockSpec(memory_space=pltpu.VMEM)
     if fused:
-        weight_specs = [pl.BlockSpec(memory_space=pltpu.SMEM), spec, spec]
+        weight_specs = [pl.BlockSpec(memory_space=pltpu.SMEM)] + [spec] * (len(weights) - 1)
     else:
         weight_specs = [spec, spec]
     return pl.pallas_call(
@@ -515,7 +547,8 @@
     return jnp.where(n < ranges[1, step], ranges[0, step] + n, ranges[2, step] + n)
 
 
-def attend_kernel(ranges, qa, ka, vt, mixed, exact, qb, total, peak):
+def attend_kernel(ranges, qa, ka, vt, *refs):
+    mixed, exact, qb, total, peak = refs[-5:]
     step = pl.program_id(0)
     peak[...] = jnp.full((HEADS, 8, BLOCK), -3e38, f32)
     total[...] = jnp.zeros_like(total)
@@ -562,7 +595,7 @@
         ).astype(bf16)
 
 
-def attend(ranges, qa, ka, vt):
+def attend(ranges, qa, ka, vt, waits):
     heads, length, _ = qa.shape
     whole = ka.shape[1]
     return pl.pallas_call(
@@ -579,7 +612,8 @@
                 pl.BlockSpec((heads, BLOCK, LANES), lambda i, *_: (0, i, 0)),
                 pl.BlockSpec((heads, whole, LANES), lambda i, *_: (0, 0, 0)),
                 pl.BlockSpec((heads, HD + 8, whole), lambda i, *_: (0, 0, 0)),
-            ],
+            ]
+            + [pl.BlockSpec(memory_space=pl.ANY)] * len(waits),
             out_specs=[
                 pl.BlockSpec((BLOCK, D), lambda i, *_: (i, 0)),
                 pl.BlockSpec((BLOCK, D), lambda i, *_: (i, 0)),
@@ -593,7 +627,7 @@
         compiler_params=pltpu.CompilerParams(vmem_limit_bytes=VMEM_LIMIT),
         cost_estimate=cost(12 * 10**9, 12 * 2**20),
         name="attend",
-    )(ranges, qa, ka, vt)
+    )(ranges, qa, ka, vt, *waits)
 
 
 def attend_back_kernel(ranges, qb, ka, da, va, kt, *refs):
@@ -673,9 +707,12 @@
 
 def feed_kernel(fused, own, mixed, exact, cotangent, query_aux, gains, *refs):
     if fused:
-        where, mine, other = refs[:3]
-        result, grad_middle, da, sums, give = refs[3:8]
-        normed_all, low_all, hidden_all, up_all, middle_all, wo, wgu, wd, stage, g_gain = refs[8:-1]
+        pieces = 1 << bit_groups(fused[0])[0][1]
+        where, mine, other = refs[0], refs[1 : 1 + pieces], refs[1 + pieces : 1 + 2 * pieces]
+        result, grad_middle, da, sums, give = refs[1 + 2 * pieces : 6 + 2 * pieces]
+        normed_all, low_all, hidden_all, up_all, middle_all, wo, wgu, wd, stage, g_gain = refs[
+            6 + 2 * pieces : -1
+        ]
     else:
         wo, wgu, wd = refs[:3]
         result, grad_middle, da, g_out, g_gate_up, g_down, g_gain = refs[3:10]
@@ -810,7 +847,7 @@
     if fused:
         count, number, shard, down = fused
         rows = number * shard + 3 * down
-        weight_specs = [pl.BlockSpec(memory_space=pltpu.SMEM), spec, spec]
+        weight_specs = [pl.BlockSpec(memory_space=pltpu.SMEM)] + [spec] * (len(weights) - 1)
         out_shape += [
             jax.ShapeDtypeStruct((2, count, rows, LANES), f32),
             jax.ShapeDtypeStruct((count, rows, LANES), bf16),
@@ -993,24 +1030,45 @@
     )(own, cosine, sine, w, gains, *arrays, *waits)
 
 
-def update_kernel(shard, down, where, total, sums, there, *refs):
+def squares_kernel(*refs):
+    total = sum(jnp.sum(ref[...] * ref[...]) for ref in refs[0:4:2]) + 0.0
+    other = sum(jnp.sum(ref[...] * ref[...]) for ref in refs[1:4:2]) + 0.0
+    refs[4][...] = jnp.full((1, LANES), total + other, f32)
+
+
+def squares(sums):
+    spec = pl.BlockSpec(memory_space=pltpu.VMEM)
+    return pl.pallas_call(
+        squares_kernel,
+        out_shape=jax.ShapeDtypeStruct((1, LANES), f32),
+        in_specs=[spec] * 4,
+        out_specs=spec,
+        compiler_params=pltpu.CompilerParams(vmem_limit_bytes=VMEM_LIMIT),
+        name="squares",
+    )(*sums)
+
+
+def update_kernel(shard, down, where, total, *refs):
     core = where[0]
-    masters, firsts, seconds = refs[:5], refs[5:10], refs[10:15]
-    norm = refs[15]
-    outs = [refs[16 + 5 * i : 21 + 5 * i] for i in range(4)]
-    low, high, square = refs[36:]
+    chunks, masters, firsts, seconds = refs[:4], refs[4:9], refs[9:14], refs[14:19]
+    norm = refs[19]
+    outs = [refs[20 + 5 * i : 25 + 5 * i] for i in range(4)]
+    low, high, square = refs[40:]
+    split = 5 * shard
 
     @pl.when(core == 0)
     def _():
-        low[...] = sums[...]
-        high[...] = there[...]
+        for i, target in ((0, low), (1, high)):
+            target[:split] = chunks[i][...]
+            target[split:] = chunks[2 + i][...]
 
     @pl.when(core == 1)
     def _():
-        low[...] = there[...]
-        high[...] = sums[...]
-
-    length = jnp.sqrt(total[...])
+        for i, target in ((0, high), (1, low)):
+            target[:split] = chunks[i][...]
+            target[split:] = chunks[2 + i][...]
+
+    length = jnp.sqrt(total[0:1, 0:1])
     norm[...] = length
     factor = clip_limit / jnp.maximum(length, clip_limit)
     halves = (low, high)
@@ -1050,7 +1108,7 @@
         step(4, gain_rows[i], slice(i, i + 1), every, 0.5, 0.0)
 
 
-def update(where, total, sums, there, masters, firsts, seconds):
+def update(where, total, sums, masters, firsts, seconds):
     shard, down = masters[0].shape[0], masters[3].shape[0] // 2
     spec = pl.BlockSpec(memory_space=pltpu.VMEM)
     shapes = [item.shape for item in masters]
@@ -1059,23 +1117,25 @@
         out_shape=[jax.ShapeDtypeStruct((1, 1), f32)]
         + [jax.ShapeDtypeStruct(shape, f32) for _ in range(3) for shape in shapes]
         + [jax.ShapeDtypeStruct(shape, bf16) for shape in shapes],
-        in_specs=[pl.BlockSpec(memory_space=pltpu.SMEM)] + [spec] * 18,
+        in_specs=[pl.BlockSpec(memory_space=pltpu.SMEM)] + [spec] * 20,
         out_specs=[spec] * 21,
         scratch_shapes=[
-            pltpu.VMEM(sums.shape, f32),
-            pltpu.VMEM(sums.shape, f32),
+            pltpu.VMEM((15 * shard + 3 * down, LANES), f32),
+            pltpu.VMEM((15 * shard + 3 * down, LANES), f32),
             pltpu.VMEM((LANES, LANES), f32),
         ],
         compiler_params=pltpu.CompilerParams(vmem_limit_bytes=VMEM_LIMIT),
         name="update",
-    )(where, total, sums, there, *masters, *firsts, *seconds)
+    )(where, total, *sums, *masters, *firsts, *seconds)
     return outs[0][0, 0], outs[1:6], outs[6:11], outs[11:16], outs[16:21]
 
 
-def update_plain(core, total, sums, there, masters, firsts, seconds):
+def update_plain(core, total, sums, masters, firsts, seconds):
     shard, down = masters[0].shape[0], masters[3].shape[0] // 2
-    low = jnp.where(core == 0, sums, there)
-    high = jnp.where(core == 0, there, sums)
+    mine = jnp.concatenate([sums[0], sums[2]])
+    there = jnp.concatenate([sums[1], sums[3]])
+    low = jnp.where(core == 0, mine, there)
+    high = jnp.where(core == 0, there, mine)
     five, fifteen = 5 * shard, 15 * shard
     first_shard = jnp.concatenate([low[:five], high[:five]]).reshape(10, shard, LANES)
     second_shard = jnp.concatenate([low[five:fifteen], high[five:fifteen]])
@@ -1136,27 +1196,28 @@
     fuse_in = can_unpack(shard, down)
     masters = (w_qkv, w_out, w_gate_up, w_down, gains)
 
-    first, second = send_chunks(where, *masters)
-    cosine, sine, key_aux, query_aux, ranges = tables(where, sample_ids, pad_flags, offsets)
-    first_steps = gather_steps(first, count, first_after=query_aux)
-    first_held = first_steps[-1]
-    second_steps = gather_steps(second, count, first_steps)
+    first = send_chunk(where, FIRST_PLAN, 0, [w_qkv, gains], [])
     there = swap_tm(own)
-
-    def gathered(held, number, down):
-        other = swap_tm(held)
+    cosine, sine, key_aux, query_aux, ranges = tables(
+        where, sample_ids, pad_flags, offsets, [there]
+    )
+    first_held, first_pieces = gather(first, count, [query_aux])
+    second = send_chunk(where, SECOND_PLAN, down, [w_out, w_gate_up, w_down], [first_held])
+
+    def gathered(pieces, number, down):
+        others = [swap_tm(piece) for piece in pieces]
         if fuse_in:
-            return (where, held, other), (count, number, shard, down)
-        return unpack_plain(count, number, shard, down, where, held, other), None
-
-    weights, fused = gathered(first_held, 5, 0)
-    waits = second_steps[-2:-1] if len(second_steps) > 1 else []
+            return (where, *pieces, *others), (count, number, shard, down)
+        return unpack_plain(count, number, shard, down, where, pieces, others), None
+
+    weights, fused = gathered([jnp.concatenate(first_pieces)], 5, 0)
     qa, ka, va, kt, vt, attn_in, gain_pair = project(
-        own, there, cosine, sine, key_aux, query_aux, weights, fused, waits
+        own, there, cosine, sine, key_aux, query_aux, weights, fused, []
     )
-    second_held = tie(second_steps[-1], gain_pair)
-    mixed, exact, qb = attend(ranges, qa, ka, vt)
-    weights, fused = gathered(second_held, 10, down)
+    second_held, second_pieces = gather(second, count, [gain_pair])
+    mixed, exact, qb = attend(ranges, qa, ka, vt, [second_held])
+    second_pieces[1:] = hold(second_pieces[1:], [mixed])
+    weights, fused = gathered(second_pieces, 10, down)
     result, grad_middle, da, *grads = feed(
         own, mixed, exact, cotangent[0], query_aux, gain_pair, weights, fused
     )
@@ -1191,16 +1252,14 @@
     first_sum = scatter_steps(first_total, count, owner)[-1].reshape(-1, LANES)
     second_sum = second_sums[-1].reshape(-1, LANES)
 
-    sums = jnp.concatenate([first_sum, second_sum], axis=0)
-    sums_there = swap_tm(sums)
-    squares = jnp.sum(sums * sums) + jnp.sum(sums_there * sums_there)
-    total = sum_batch(squares.reshape(1, 1), count)
+    sums = (first_sum, swap_tm(first_sum), second_sum, swap_tm(second_sum))
+    total = sum_batch(squares(sums), count)
     firsts = (m_qkv, m_out, m_gate_up, m_down, m_gains)
     seconds = (v_qkv, v_out, v_gate_up, v_down, v_gains)
     if fuse_in:
-        updates = update(where, total, sums, sums_there, masters, firsts, seconds)
+        updates = update(where, total, sums, masters, firsts, seconds)
     else:
-        updates = update_plain(core, total, sums, sums_there, masters, firsts, seconds)
+        updates = update_plain(core, total, sums, masters, firsts, seconds)
     grad_norm, new_first, new_second, new_master, copies = updates
     return (
         result[None],

time: 225 us -> 213 us (0.947)
  starting transfers between devices: 48.8 us -> 35.1 us
  blocking collectives: 0 us -> 10.2 us
  between operations: 8.82 us -> 1.28 us
  waiting for transfers between devices: 26.8 us -> 19.7 us
  local copies, waits for them, and re-layouts: 7.31 us -> 10.5 us
    ppermute x30 -> x24, starting transfers between devices: 48 us -> 32.7 us  [permute_batch(): return lax.ppermute(value, 'batch', [(i, i ^ flip) for i in range(count)])]
    all_to_all x0 -> x1, blocking collectives: none -> 10.2 us  [sum_batch(): value = lax.all_to_all(value, 'batch', 0, 0, tiled=True)]
    ppermute x30 -> x24, waiting for transfers between devices: 23.2 us -> 14.4 us  [permute_batch(): return lax.ppermute(value, 'batch', [(i, i ^ flip) for i in range(count)])]
    unnamed x26 -> x60, local copies, waits for them, and re-layouts: 3.56 us -> 9.49 us
    pallas_call x1 -> x6, Pallas kernels: 1.8 us -> 5.16 us  [the longest x2 3.4 us: send_chunk(): pl.pallas_call(kernel, out_shape=jax.ShapeDtypeStruct((rows, LANES), bf16...]
    slice x4 -> x0, local copies, waits for them, and re-layouts: 2.76 us -> none  [tie(): return value + other.reshape(-1)[0] * jnp.zeros((), value.dtype)]
    ppermute x8 -> x12, waiting for transfers between devices: 3.57 us -> 5.25 us  [swap_tm(): return lax.ppermute(value, 'tm', [(0, 1), (1, 0)])]
  transfers between devices with their start and end apart: 38 -> 36, of which waited for: 14 -> 12; matrix products, arithmetic and copies ran while one was open for 4% -> 4% of each run, Pallas kernels for 38% -> 42%
where the time goes in v4:
time: 213 us; the launch traced here: 211 us
  Pallas kernels  125 us (59%)
  starting transfers between devices  35.1 us (16%)
  waiting for transfers between devices  19.7 us (9%)
  local copies, waits for them, and re-layouts  10.5 us (5%)
  blocking collectives  10.2 us (5%)
  other arithmetic  9.34 us (4%)
    pallas_call x2, Pallas kernels, attend_back(): pl.pallas_call(attend_back_kernel, out_shape=[jax.ShapeDtypeStruct((heads...  35.8 us
    ppermute x24, starting transfers between devices, permute_batch(): return lax.ppermute(value, 'batch', [(i, i ^ flip) for i in range(count)])  32.7 us
    pallas_call x1, Pallas kernels, feed(): pl.pallas_call(partial(feed_kernel, fused), out_shape=out_shape, grid=(le...  23.3 us
    pallas_call x1, Pallas kernels, attend(): pl.pallas_call(attend_kernel, out_shape=[jax.ShapeDtypeStruct((length, D)...  21.1 us
    pallas_call x1, Pallas kernels, project(): pl.pallas_call(partial(project_kernel, fused), out_shape=[jax.ShapeDtypeS...  17 us
    pallas_call x2, Pallas kernels, project_back(): pl.pallas_call(partial(project_back_kernel, number, fused), out_shape=[ja...  16.1 us
    ppermute x24, waiting for transfers between devices, permute_batch(): return lax.ppermute(value, 'batch', [(i, i ^ flip) for i in range(count)])  14.4 us
    all_to_all x1, blocking collectives, sum_batch(): value = lax.all_to_all(value, 'batch', 0, 0, tiled=True)  10.2 us
  transfers between devices with their start and end apart: 36, of which 12 were waited for; matrix products, arithmetic and copies ran while one was open for 4% of the time, Pallas kernels for 42%

profile of v4, /device:TPU:0, one launch (start us, length us, event | category | flops | bytes accessed | tf_op | source)
XLA Modules:
  0.0 211.3 jit_solution(16750478173235582506)
XLA Ops:
  3.4 2.6 %collective-permute-start.1 = (bf16[1,128,128]{2,1,0:T(8,128)(2,1)}, bf16[1,128,128]{2,1,0:T(8,128)(2,1)S(1)}, u32[]{:S(2)}, u32[]{:S(2)}) collective-permute-start(bf16[1,128,128]{2,1,0:T(8,128)(2,1)} %bitcast.81), channel_id=1, source_target_pairs={{0,8},{2,10},{4,12},{6,14},{8,0},{10,2},{12,4},{14,6},{16,24},{18,... | collective-permute-start | bytes 98312 | tf_op jit(solution)/shard_map/ppermute | solution.py:49
  6.0 2.6 %collective-permute-start.2 = (bf16[1,128,128]{2,1,0:T(8,128)(2,1)}, bf16[1,128,128]{2,1,0:T(8,128)(2,1)S(1)}, u32[]{:S(2)}, u32[]{:S(2)}) collective-permute-start(bf16[1,128,128]{2,1,0:T(8,128)(2,1)} %bitcast.82), channel_id=1, source_target_pairs={{0,16},{2,18},{4,20},{6,22},{8,24},{10,26},{12,28},{14,30},{16,0},... | collective-permute-start | bytes 98312 | tf_op jit(solution)/shard_map/ppermute | solution.py:49
  10.3 4.0 %tables.1 = (f32[2048,128]{1,0:T(8,128)}, f32[2048,128]{1,0:T(8,128)}, bf16[2048,128]{1,0:T(8,128)(2,1)}, bf16[1024,128]{1,0:T(8,128)(2,1)}, s32[4,4]{1,0:T(4,128)}) custom-call(s32[2]{0:T(128)} %pad_add_fusion.where.refs_0_.refs_5_, s32[1,2048]{1,0:T(1,128)} %ids.1, s32[1,2048]{1,0:T(1,128)} %pads.1, s32[1,2048]{1,0:T(1,128)} %offsets.1, ...), custom_call_target="tpu_custom_call" | custom-call | flops 3000000000 | bytes 4194304 | tf_op jit(solution)/shard_map/tables/pallas_call | solution.py:420
  16.0 1.6 collective-permute-start.4
  21.9 3.5 %collective-permute-done.5 = bf16[4,128,128]{2,1,0:T(8,128)(2,1)S(1)} collective-permute-done((bf16[4,128,128]{2,1,0:T(8,128)(2,1)S(1)}, bf16[4,128,128]{2,1,0:T(8,128)(2,1)S(1)}, u32[]{:S(2)}, u32[]{:S(2)}) %collective-permute-start.5) | collective-permute-done | bytes 131104 | tf_op jit(solution)/shard_map/ppermute | solution.py:49
  25.6 1.8 send_chunk.3
  27.4 3.6 %collective-permute-start.10 = (bf16[1,336,128]{2,1,0:T(8,128)(2,1)}, bf16[1,336,128]{2,1,0:T(8,128)(2,1)S(1)}, u32[]{:S(2)}, u32[]{:S(2)}) collective-permute-start(bf16[1,336,128]{2,1,0:T(8,128)(2,1)} %bitcast.77), channel_id=1, source_target_pairs={{0,24},{2,26},{4,28},{6,30},{8,16},{10,18},{12,20},{14,22},{16,8},... | collective-permute-start | bytes 258056 | tf_op jit(solution)/shard_map/ppermute | solution.py:49
  32.6 17.0 %project.1 = (bf16[6,1024,128]{2,1,0:T(8,128)(2,1)}, bf16[6,2048,128]{2,1,0:T(8,128)(2,1)}, bf16[6,2048,128]{2,1,0:T(8,128)(2,1)}, bf16[6,64,2048]{2,1,0:T(8,128...) custom-call(bf16[1024,384]{1,0:T(8,128)(2,1)} %bitcast.90, ...), custom_call_target="tpu_custom_call" | custom-call | flops 8999999488 | bytes 16777216 | tf_op jit(solution)/shard_map/project/pallas_call | solution.py:508
  55.0 21.1 %attend.1 = (bf16[1024,384]{1,0:T(8,128)(2,1)}, f32[1024,384]{1,0:T(8,128)}, bf16[6,1024,128]{2,1,0:T(8,128)(2,1)}) custom-call(s32[4,4]{1,0:T(4,128)} %get-tuple-element.84.ranges, bf16[6,1024,128]{2,1,0:T(8,128)(2,1)} %get-tuple-element.92.qa, bf16[6,2048,128]{2,1,0:T(8,128)(2,1)} %get-tuple-element.93.ka, bf16[6,72,2048]{2,1,0:T(8,128)(2,1)} %get-tuple-element.94.vt, ...), custom_call_target="tpu_custom_call" | custom-call | flops 12000000000 | bytes 12582912 | tf_op jit(solution)/shard_map/attend/pallas_call | solution.py:601
  80.7 23.3 %feed.1 = (bf16[1024,384]{1,0:T(8,128)(2,1)}, f32[1024,384]{1,0:T(8,128)}, bf16[6,1024,128]{2,1,0:T(8,128)(2,1)}, f32[2,16,336,128]{3,2,1,0:T(8,128)}, bf16[16,336,128]{2,1,0:T(8,128)(2,1)}) custom-call(bf16[1024,384]{1,0:T(8,128)(2,1)} %bitcast.91, bf16[1024,384]{1,0:T(8,128)(2,1)} %get-tuple-element.99.refs_3_.mixed, ...), custom_call_target="tpu_custom_call" | custom-call | flops 14000000000 | bytes 16777216 | tf_op jit(solution)/shard_map/feed/pallas_call | solution.py:873
  104.4 13.8 %attend_back.3 = (f32[2,64,1024]{2,1,0:T(8,128)}, f32[2,1024,128]{2,1,0:T(8,128)}, bf16[2,1024,128]{2,1,0:T(8,128)(2,1)}) custom-call(s32[4,4]{1,0:T(4,128)} %get-tuple-element.84.ranges, bf16[6,1024,128]{2,1,0:T(8,128)(2,1)} %get-tuple-element.106.qb, bf16[6,2048,128]{2,1,0:T(8,128)(2,1)} %get-tuple-element.93.ka, ...), custom_call_target="tpu_custom_call" | custom-call | flops 12000000000 | bytes 8388608 | tf_op jit(solution)/shard_map/attend_back/pallas_call | solution.py:674
  118.4 2.0 bitcast_add_fusion.refs_0_
  124.1 22.0 %attend_back.2 = (f32[4,64,1024]{2,1,0:T(8,128)}, f32[4,1024,128]{2,1,0:T(8,128)}, bf16[4,1024,128]{2,1,0:T(8,128)(2,1)}) custom-call(s32[4,4]{1,0:T(4,128)} %get-tuple-element.84.ranges, bf16[6,1024,128]{2,1,0:T(8,128)(2,1)} %get-tuple-element.106.qb, bf16[6,2048,128]{2,1,0:T(8,128)(2,1)} %get-tuple-element.93.ka, ...), custom_call_target="tpu_custom_call" | custom-call | flops 12000000000 | bytes 8388608 | tf_op jit(solution)/shard_map/attend_back/pallas_call | solution.py:674
  148.8 2.9 %collective-permute-start.25 = (bf16[1,336,128]{2,1,0:T(8,128)(2,1)S(1)}, bf16[1,336,128]{2,1,0:T(8,128)(2,1)S(1)}, u32[]{:S(2)}, u32[]{:S(2)}) collective-permute-start(bf16[1,336,128]{2,1,0:T(8,128)(2,1)S(1)} %get-tuple-element.153), channel_id=1, source_target_pairs={{0,16},{2,18},{4,20},{6,22},{8,24},{10,26},{12,28},{14,30},{16,0},... | collective-permute-start | bytes 258056 | tf_op jit(solution)/shard_map/ppermute | solution.py:49
  151.9 7.7 %project_back.2 = (f32[1024,384]{1,0:T(8,128)}, f32[384,640]{1,0:T(8,128)}) custom-call(bf16[1024,384]{1,0:T(8,128)(2,1)} %bitcast.92, f32[2048,128]{1,0:T(8,128)} %get-tuple-element.85.cosine, f32[2048,128]{1,0:T(8,128)} %get-tuple-element.86.sine, bf16[384,1152]{1,0:T(8,128)(2,1)} %get-tuple-element.105.w, f32[8,384]{1,0:T(8,128)} %get-tuple-element.95.refs_3_.gains, ...), custom_call_target="tpu_custom_call" | custom-call | flops 4000000000 | bytes 8388608 | tf_op jit(solution)/shard_map/project_back/pallas_call | solution.py:1012
  162.3 8.4 %project_back.3 = (bf16[1024,384]{1,0:T(8,128)(2,1)}, f32[2,16,120,128]{3,2,1,0:T(8,128)}, bf16[16,120,128]{2,1,0:T(8,128)(2,1)}) custom-call(bf16[1024,384]{1,0:T(8,128)(2,1)} %bitcast.93, f32[2048,128]{1,0:T(8,128)} %get-tuple-element.85.cosine, f32[2048,128]{1,0:T(8,128)} %get-tuple-element.86.sine, bf16[384,1152]{1,0:T(8,128)(2,1)} %get-tuple-element.105.w, ...), custom_call_target="tpu_custom_call" | custom-call | flops 4000000000 | bytes 8388608 | tf_op jit(solution)/shard_map/project_back/pallas_call | solution.py:1012
  170.8 2.1 collective-permute-done.27
  177.8 2.5 %collective-permute-done.28 = bf16[4,120,128]{2,1,0:T(8,128)(2,1)S(1)} collective-permute-done((bf16[4,120,128]{2,1,0:T(8,128)(2,1)S(1)}, bf16[4,120,128]{2,1,0:T(8,128)(2,1)S(1)}, u32[]{:S(2)}, u32[]{:S(2)}) %collective-permute-start.28) | collective-permute-done | bytes 122912 | tf_op jit(solution)/shard_map/ppermute | solution.py:49
  181.3 1.9 collective-permute-done.30
  184.3 3.1 %collective-permute-start.32 = (bf16[1,120,128]{2,1,0:T(8,128)(2,1)S(1)}, bf16[1,120,128]{2,1,0:T(8,128)(2,1)S(1)}, u32[]{:S(2)}, u32[]{:S(2)}) collective-permute-start(bf16[1,120,128]{2,1,0:T(8,128)(2,1)S(1)} %get-tuple-element.156), channel_id=1, source_target_pairs={{0,16},{2,18},{4,20},{6,22},{8,24},{10,26},{12,28},{14,30},{16,0},... | collective-permute-start | bytes 92168 | tf_op jit(solution)/shard_map/ppermute | solution.py:49
  189.3 3.8 %collective-permute-done.33 = bf16[1,120,128]{2,1,0:T(8,128)(2,1)S(1)} collective-permute-done((bf16[1,120,128]{2,1,0:T(8,128)(2,1)S(1)}, bf16[1,120,128]{2,1,0:T(8,128)(2,1)S(1)}, u32[]{:S(2)}, u32[]{:S(2)}) %collective-permute-start.33) | collective-permute-done | bytes 30752 | tf_op jit(solution)/shard_map/ppermute | solution.py:49
  195.1 1.8 squares.1
  197.5 10.2 %all_to_all.5 = f32[16,1,128]{2,1,0:T(1,128)S(1)} all-to-all(f32[16,1,128]{2,1,0:T(1,128)S(1)} %broadcast_in_dim.25), channel_id=1, replica_groups=mesh['batch'=16,'tm'=2] {'batch'}, dimensions={0} | all-to-all | bytes 16384 | tf_op jit(solution)/shard_map/all_to_all | solution.py:94
  208.3 2.9 %update.1 = (f32[1,1]{1,0:T(1,128)}, f32[24,1152]{1,0:T(8,128)}, f32[24,384]{1,0:T(8,128)}, f32[24,2048]{1,0:T(8,128)}, f32[64,384]{1,0:T(8,128)}, /*index=5*/f3...) custom-call(s32[2]{0:T(128)} %pad_add_fusion.where.refs_0_.refs_5_, ...), custom_call_target="tpu_custom_call" | custom-call | tf_op jit(solution)/shard_map/update/pallas_call | solution.py:1115
  (140 shorter events, 43.9 us)
Async XLA Ops:
  0.7 8.8 %collective-permute-start = (bf16[1024,384]{1,0:T(8,128)(2,1)}, bf16[1024,384]{1,0:T(8,128)(2,1)S(1)}, u32[]{:S(2)}, u32[]{:S(2)}) collective-permute-start(bf16[1024,384]{1,0:T(8,128)(2,1)} %bitcast.89), channel_id=1, source_target_pairs={{0,1},{1,0},{2,3},{3,2},{4,5},{5,4},{6,7},{7,6},{8,9},{9,8},{10,11... | collective-permute-start | bytes 2359304 | tf_op jit(solution)/shard_map/ppermute | solution.py:53
  3.4 11.0 %collective-permute-start.1 = (bf16[1,128,128]{2,1,0:T(8,128)(2,1)}, bf16[1,128,128]{2,1,0:T(8,128)(2,1)S(1)}, u32[]{:S(2)}, u32[]{:S(2)}) collective-permute-start(bf16[1,128,128]{2,1,0:T(8,128)(2,1)} %bitcast.81), channel_id=1, source_target_pairs={{0,8},{2,10},{4,12},{6,14},{8,0},{10,2},{12,4},{14,6},{16,24},{18,... | collective-permute-start | bytes 98312 | tf_op jit(solution)/shard_map/ppermute | solution.py:49
  6.0 8.4 %collective-permute-start.2 = (bf16[1,128,128]{2,1,0:T(8,128)(2,1)}, bf16[1,128,128]{2,1,0:T(8,128)(2,1)S(1)}, u32[]{:S(2)}, u32[]{:S(2)}) collective-permute-start(bf16[1,128,128]{2,1,0:T(8,128)(2,1)} %bitcast.82), channel_id=1, source_target_pairs={{0,16},{2,18},{4,20},{6,22},{8,24},{10,26},{12,28},{14,30},{16,0},... | collective-permute-start | bytes 98312 | tf_op jit(solution)/shard_map/ppermute | solution.py:49
  17.6 7.8 %collective-permute-start.5 = (bf16[4,128,128]{2,1,0:T(8,128)(2,1)S(1)}, bf16[4,128,128]{2,1,0:T(8,128)(2,1)S(1)}, u32[]{:S(2)}, u32[]{:S(2)}) collective-permute-start(bf16[4,128,128]{2,1,0:T(8,128)(2,1)S(1)} %pad_maximum_fusion.1.refs_3_), channel_id=1, source_target_pairs={{0,4},{2,6},{4,0},{6,2},{8,12},{10,14},{12,8},{14,10},{16,20},{18,... | collective-permute-start | bytes 393224 | tf_op jit(solution)/shard_map/ppermute | solution.py:49
  19.2 6.3 %collective-permute-start.6 = (bf16[4,128,128]{2,1,0:T(8,128)(2,1)S(1)}, bf16[4,128,128]{2,1,0:T(8,128)(2,1)S(1)}, u32[]{:S(2)}, u32[]{:S(2)}) collective-permute-start(bf16[4,128,128]{2,1,0:T(8,128)(2,1)S(1)} %pad_maximum_fusion.1.refs_3_), channel_id=1, source_target_pairs={{0,6},{2,4},{4,2},{6,0},{8,14},{10,12},{12,10},{14,8},{16,22},{18,... | collective-permute-start | bytes 393224 | tf_op jit(solution)/shard_map/ppermute | solution.py:49
  25.5 6.3 %collective-permute-start.7 = (bf16[16,128,128]{2,1,0:T(8,128)(2,1)S(1)}, bf16[16,128,128]{2,1,0:T(8,128)(2,1)S(1)}, u32[]{:S(2)}, u32[]{:S(2)}) collective-permute-start(bf16[16,128,128]{2,1,0:T(8,128)(2,1)S(1)} %constant_dynamic-update-slice_fusion.refs_1_), channel_id=1, source_target_pairs={{0,1},{1,0},{2,3},{3,2},{4,5},{5,4},{6,7},{7,6},{8,9},{9,8},{10,11... | collective-permute-start | bytes 1572872 | tf_op jit(solution)/shard_map/ppermute | solution.py:53
  27.4 22.3 %collective-permute-start.10 = (bf16[1,336,128]{2,1,0:T(8,128)(2,1)}, bf16[1,336,128]{2,1,0:T(8,128)(2,1)S(1)}, u32[]{:S(2)}, u32[]{:S(2)}) collective-permute-start(bf16[1,336,128]{2,1,0:T(8,128)(2,1)} %bitcast.77), channel_id=1, source_target_pairs={{0,24},{2,26},{4,28},{6,30},{8,16},{10,18},{12,20},{14,22},{16,8},... | collective-permute-start | bytes 258056 | tf_op jit(solution)/shard_map/ppermute | solution.py:49
  31.0 18.7 %collective-permute-start.8 = (bf16[1,336,128]{2,1,0:T(8,128)(2,1)}, bf16[1,336,128]{2,1,0:T(8,128)(2,1)S(1)}, u32[]{:S(2)}, u32[]{:S(2)}) collective-permute-start(bf16[1,336,128]{2,1,0:T(8,128)(2,1)} %bitcast.78), channel_id=1, source_target_pairs={{0,8},{2,10},{4,12},{6,14},{8,0},{10,2},{12,4},{14,6},{16,24},{18,... | collective-permute-start | bytes 258056 | tf_op jit(solution)/shard_map/ppermute | solution.py:49
  31.0 18.7 %collective-permute-start.9 = (bf16[1,336,128]{2,1,0:T(8,128)(2,1)}, bf16[1,336,128]{2,1,0:T(8,128)(2,1)S(1)}, u32[]{:S(2)}, u32[]{:S(2)}) collective-permute-start(bf16[1,336,128]{2,1,0:T(8,128)(2,1)} %bitcast.79), channel_id=1, source_target_pairs={{0,16},{2,18},{4,20},{6,22},{8,24},{10,26},{12,28},{14,30},{16,0},... | collective-permute-start | bytes 258056 | tf_op jit(solution)/shard_map/ppermute | solution.py:49
  51.4 24.6 %collective-permute-start.11 = (bf16[4,336,128]{2,1,0:T(8,128)(2,1)S(1)}, bf16[4,336,128]{2,1,0:T(8,128)(2,1)S(1)}, u32[]{:S(2)}, u32[]{:S(2)}) collective-permute-start(bf16[4,336,128]{2,1,0:T(8,128)(2,1)S(1)} %pad_maximum_fusion.refs_0_.refs_1_), channel_id=1, source_target_pairs={{0,2},{2,0},{4,6},{6,4},{8,10},{10,8},{12,14},{14,12},{16,18},{18,... | collective-permute-start | bytes 1032200 | tf_op jit(solution)/shard_map/ppermute | solution.py:49
  52.6 23.5 %collective-permute-start.12 = (bf16[4,336,128]{2,1,0:T(8,128)(2,1)S(1)}, bf16[4,336,128]{2,1,0:T(8,128)(2,1)S(1)}, u32[]{:S(2)}, u32[]{:S(2)}) collective-permute-start(bf16[4,336,128]{2,1,0:T(8,128)(2,1)S(1)} %pad_maximum_fusion.refs_0_.refs_1_), channel_id=1, source_target_pairs={{0,4},{2,6},{4,0},{6,2},{8,12},{10,14},{12,8},{14,10},{16,20},{18,... | collective-permute-start | bytes 1032200 | tf_op jit(solution)/shard_map/ppermute | solution.py:49
  53.4 22.6 %collective-permute-start.13 = (bf16[4,336,128]{2,1,0:T(8,128)(2,1)S(1)}, bf16[4,336,128]{2,1,0:T(8,128)(2,1)S(1)}, u32[]{:S(2)}, u32[]{:S(2)}) collective-permute-start(bf16[4,336,128]{2,1,0:T(8,128)(2,1)S(1)} %pad_maximum_fusion.refs_0_.refs_1_), channel_id=1, source_target_pairs={{0,6},{2,4},{4,2},{6,0},{8,14},{10,12},{12,10},{14,8},{16,22},{18,... | collective-permute-start | bytes 1032200 | tf_op jit(solution)/shard_map/ppermute | solution.py:49
  55.0 23.1 %collective-permute-start.14 = (bf16[4,336,128]{2,1,0:T(8,128)(2,1)S(1)}, bf16[4,336,128]{2,1,0:T(8,128)(2,1)S(1)}, u32[]{:S(2)}, u32[]{:S(2)}) collective-permute-start(bf16[4,336,128]{2,1,0:T(8,128)(2,1)S(1)} %pad_maximum_fusion.refs_0_.refs_1_), channel_id=1, source_target_pairs={{0,1},{1,0},{2,3},{3,2},{4,5},{5,4},{6,7},{7,6},{8,9},{9,8},{10,11... | collective-permute-start | bytes 1032200 | tf_op jit(solution)/shard_map/ppermute | solution.py:53
  104.0 14.4 %collective-permute-start.18 = (bf16[16,336,128]{2,1,0:T(8,128)(2,1)}, bf16[16,336,128]{2,1,0:T(8,128)(2,1)S(1)}, u32[]{:S(2)}, u32[]{:S(2)}) collective-permute-start(bf16[16,336,128]{2,1,0:T(8,128)(2,1)} %get-tuple-element.111.refs_0_), channel_id=1, source_target_pairs={{0,1},{1,0},{2,3},{3,2},{4,5},{5,4},{6,7},{7,6},{8,9},{9,8},{10,11... | collective-permute-start | bytes 4128776 | tf_op jit(solution)/shard_map/ppermute | solution.py:53
  118.3 33.7 %collective-permute-start.20 = (bf16[2,1024,128]{2,1,0:T(8,128)(2,1)}, bf16[2,1024,128]{2,1,0:T(8,128)(2,1)}, u32[]{:S(2)}, u32[]{:S(2)}) collective-permute-start(bf16[2,1024,128]{2,1,0:T(8,128)(2,1)} %get-tuple-element.118), channel_id=1, source_target_pairs={{0,1},{1,0},{2,3},{3,2},{4,5},{5,4},{6,7},{7,6},{8,9},{9,8},{10,11... | collective-permute-start | bytes 1572872 | tf_op jit(solution)/shard_map/ppermute | solution.py:53
  120.5 25.6 %collective-permute-start.21 = (bf16[4,336,128]{2,1,0:T(8,128)(2,1)S(1)}, bf16[4,336,128]{2,1,0:T(8,128)(2,1)S(1)}, u32[]{:S(2)}, u32[]{:S(2)}) collective-permute-start(bf16[4,336,128]{2,1,0:T(8,128)(2,1)S(1)} %get-tuple-element.145), channel_id=1, source_target_pairs={{0,2},{2,0},{4,6},{6,4},{8,10},{10,8},{12,14},{14,12},{16,18},{18,... | collective-permute-start | bytes 1032200 | tf_op jit(solution)/shard_map/ppermute | solution.py:49
  121.7 24.4 %collective-permute-start.22 = (bf16[4,336,128]{2,1,0:T(8,128)(2,1)S(1)}, bf16[4,336,128]{2,1,0:T(8,128)(2,1)S(1)}, u32[]{:S(2)}, u32[]{:S(2)}) collective-permute-start(bf16[4,336,128]{2,1,0:T(8,128)(2,1)S(1)} %get-tuple-element.146), channel_id=1, source_target_pairs={{0,4},{2,6},{4,0},{6,2},{8,12},{10,14},{12,8},{14,10},{16,20},{18,... | collective-permute-start | bytes 1032200 | tf_op jit(solution)/shard_map/ppermute | solution.py:49
  122.6 23.6 %collective-permute-start.23 = (bf16[4,336,128]{2,1,0:T(8,128)(2,1)S(1)}, bf16[4,336,128]{2,1,0:T(8,128)(2,1)S(1)}, u32[]{:S(2)}, u32[]{:S(2)}) collective-permute-start(bf16[4,336,128]{2,1,0:T(8,128)(2,1)S(1)} %get-tuple-element.147), channel_id=1, source_target_pairs={{0,6},{2,4},{4,2},{6,0},{8,14},{10,12},{12,10},{14,8},{16,22},{18,... | collective-permute-start | bytes 1032200 | tf_op jit(solution)/shard_map/ppermute | solution.py:49
  146.1 15.2 %collective-permute-start.19 = (bf16[4,1024,128]{2,1,0:T(8,128)(2,1)}, bf16[4,1024,128]{2,1,0:T(8,128)(2,1)S(1)}, u32[]{:S(2)}, u32[]{:S(2)}) collective-permute-start(bf16[4,1024,128]{2,1,0:T(8,128)(2,1)} %get-tuple-element.113), channel_id=1, source_target_pairs={{0,1},{1,0},{2,3},{3,2},{4,5},{5,4},{6,7},{7,6},{8,9},{9,8},{10,11... | collective-permute-start | bytes 3145736 | tf_op jit(solution)/shard_map/ppermute | solution.py:53
  147.5 12.2 %collective-permute-start.24 = (bf16[1,336,128]{2,1,0:T(8,128)(2,1)S(1)}, bf16[1,336,128]{2,1,0:T(8,128)(2,1)S(1)}, u32[]{:S(2)}, u32[]{:S(2)}) collective-permute-start(bf16[1,336,128]{2,1,0:T(8,128)(2,1)S(1)} %get-tuple-element.151), channel_id=1, source_target_pairs={{0,8},{2,10},{4,12},{6,14},{8,0},{10,2},{12,4},{14,6},{16,24},{18,... | collective-permute-start | bytes 258056 | tf_op jit(solution)/shard_map/ppermute | solution.py:49
  148.8 10.8 %collective-permute-start.25 = (bf16[1,336,128]{2,1,0:T(8,128)(2,1)S(1)}, bf16[1,336,128]{2,1,0:T(8,128)(2,1)S(1)}, u32[]{:S(2)}, u32[]{:S(2)}) collective-permute-start(bf16[1,336,128]{2,1,0:T(8,128)(2,1)S(1)} %get-tuple-element.153), channel_id=1, source_target_pairs={{0,16},{2,18},{4,20},{6,22},{8,24},{10,26},{12,28},{14,30},{16,0},... | collective-permute-start | bytes 258056 | tf_op jit(solution)/shard_map/ppermute | solution.py:49
  151.7 7.9 %collective-permute-start.26 = (bf16[1,336,128]{2,1,0:T(8,128)(2,1)S(1)}, bf16[1,336,128]{2,1,0:T(8,128)(2,1)S(1)}, u32[]{:S(2)}, u32[]{:S(2)}) collective-permute-start(bf16[1,336,128]{2,1,0:T(8,128)(2,1)S(1)} %get-tuple-element.152), channel_id=1, source_target_pairs={{0,24},{2,26},{4,28},{6,30},{8,16},{10,18},{12,20},{14,22},{16,8},... | collective-permute-start | bytes 258056 | tf_op jit(solution)/shard_map/ppermute | solution.py:49
  174.3 6.0 %collective-permute-start.28 = (bf16[4,120,128]{2,1,0:T(8,128)(2,1)S(1)}, bf16[4,120,128]{2,1,0:T(8,128)(2,1)S(1)}, u32[]{:S(2)}, u32[]{:S(2)}) collective-permute-start(bf16[4,120,128]{2,1,0:T(8,128)(2,1)S(1)} %get-tuple-element.148), channel_id=1, source_target_pairs={{0,2},{2,0},{4,6},{6,4},{8,10},{10,8},{12,14},{14,12},{16,18},{18,... | collective-permute-start | bytes 368648 | tf_op jit(solution)/shard_map/ppermute | solution.py:49
  176.3 6.9 %collective-permute-start.30 = (bf16[4,120,128]{2,1,0:T(8,128)(2,1)S(1)}, bf16[4,120,128]{2,1,0:T(8,128)(2,1)S(1)}, u32[]{:S(2)}, u32[]{:S(2)}) collective-permute-start(bf16[4,120,128]{2,1,0:T(8,128)(2,1)S(1)} %get-tuple-element.150), channel_id=1, source_target_pairs={{0,6},{2,4},{4,2},{6,0},{8,14},{10,12},{12,10},{14,8},{16,22},{18,... | collective-permute-start | bytes 368648 | tf_op jit(solution)/shard_map/ppermute | solution.py:49
  (39 other events, 130.9 us)

commit v5 on v4

v5 whole, which is shorter than its diff:
```python
import math
from functools import partial

import jax
import jax.numpy as jnp
from jax import lax
from jax.experimental import pallas as pl
from jax.experimental.pallas import tpu as pltpu
from jax.sharding import PartitionSpec as P

D = 384
FF = 1024
HEADS = 6
HD = 64
STEP = 3


norm_eps = 1e-06
beta_one = 0.5
beta_two = 0.5
adam_eps = 1e-08
decay_rate = 0.1
clip_limit = 1.0
masked_score = -1e30


def adam_update(master, grad, first, second, rate, decay):
    first_new = beta_one * first + (1.0 - beta_one) * grad
    second_new = beta_two * second + (1.0 - beta_two) * grad * grad
    direction = (
        first_new
        / (1.0 - beta_one**STEP)
        / (jnp.sqrt(second_new / (1.0 - beta_two**STEP)) + adam_eps)
    )
    return (first_new, second_new, master - rate * (direction + decay * master))


def bit_groups(count):
    groups = []
    low, bits = 0, count.bit_length() - 1
    while low < bits:
        width = min(2, bits - low)
        groups.append((low, width))
        low += width
    return groups


def permute_batch(value, flip, count):
    return lax.ppermute(value, "batch", [(i, i ^ flip) for i in range(count)])


def swap_tm(value):
    return lax.ppermute(value, "tm", [(0, 1), (1, 0)])


def slabs(matrix):
    rows, columns = matrix.shape
    return matrix.reshape(rows, columns // 128, 128).transpose(1, 0, 2)


def unslab(stack):
    count, rows, _ = stack.shape
    return stack.transpose(1, 0, 2).reshape(rows, count * 128)


bf16 = jnp.bfloat16
f32 = jnp.float32
BLOCK = 256
LANES = 128
KEEP_LANE = 96
LIMITS = (12, 12, 12, 34, 12, 12, 12)
NN = (((1,), (0,)), ((), ()))
NT = (((1,), (1,)), ((), ()))
TN = (((0,), (0,)), ((), ()))


def dot(left, right, dims):
    return lax.dot_general(left, right, dims, preferred_element_type=f32)


def cost(flops, moved):
    return pl.CostEstimate(flops=flops, bytes_accessed=moved, transcendentals=0)


def in_vmem(shape, dtype):
    return pltpu.VMEM(tuple(shape), dtype)


VMEM = pl.BlockSpec(memory_space=pltpu.VMEM)
SMEM = pl.BlockSpec(memory_space=pltpu.SMEM)
ANY = pl.BlockSpec(memory_space=pl.ANY)
HBM = pl.BlockSpec(memory_space=pltpu.HBM)


def fetch(sources, targets, semaphores):
    copies = [
        pltpu.make_async_copy(source, target, semaphores.at[i])
        for i, (source, target) in enumerate(zip(sources, targets))
    ]
    for copy in copies:
        copy.start()
    return copies


def landing(arrays):
    return [pltpu.VMEM(item.shape, item.dtype) for item in arrays] + [
        pltpu.SemaphoreType.DMA((len(arrays),))
    ]


def arrive(copies):
    for copy in copies:
        copy.wait()


def limit(mebibytes):
    return pltpu.CompilerParams(vmem_limit_bytes=mebibytes * 2**20)


def block(start, size=BLOCK):
    return pl.ds(pl.multiple_of(start * size, size), size)


def sum_batch(value, count):
    value = jnp.broadcast_to(value[:, None], (count, 1, LANES))
    value = lax.all_to_all(value, "batch", 0, 0, tiled=True)
    return jnp.sum(value, axis=0)


def row_scale(values):
    return lax.rsqrt(jnp.mean(values * values, axis=-1, keepdims=True) + norm_eps)


def norm_back(grad_normed, values, scale):
    return scale * grad_normed - values * scale * scale * scale * jnp.mean(
        grad_normed * values, axis=-1, keepdims=True
    )


def split_three(values):
    high = values.astype(bf16)
    rest = values - high.astype(f32)
    middle = rest.astype(bf16)
    return high, middle, (rest - middle.astype(f32)).astype(bf16)


def swap_halves(pair):
    lane = lax.broadcasted_iota(jnp.int32, pair.shape, 1)
    return jnp.where(lane % HD < HD // 2, pltpu.roll(pair, 96, 1), pltpu.roll(pair, 32, 1))


def relative_place(device, owner, count):
    flips = device ^ owner
    place, scale = 0, 1
    for low, width in reversed(bit_groups(count)):
        place = place + ((flips >> low) & ((1 << width) - 1)) * scale
        scale <<= width
    return place


def exchange_all(held, low, width, count):
    return [held] + [permute_batch(held, k << low, count) for k in range(1, 1 << width)]


def in_hbm(arrays):
    return [pltpu.with_memory_space_constraint(item, pltpu.HBM) for item in arrays]


def join_kernel(number, *refs):
    out = refs[-1]
    size = refs[0].shape[0]
    for i in range(number):
        out[i * size : (i + 1) * size] = refs[i][...]


def join(pieces, waits=()):
    first = pieces[0]
    shape = (len(pieces) * first.shape[0],) + first.shape[1:]
    return pl.pallas_call(
        partial(join_kernel, len(pieces)),
        out_shape=jax.ShapeDtypeStruct(shape, first.dtype),
        in_specs=[VMEM] * len(pieces) + [ANY] * len(waits),
        out_specs=VMEM,
        compiler_params=limit(4),
        name="join",
    )(*pieces, *waits)


def combine_kernel(number, split, where, *refs):
    items, outs = refs[:number], refs[-len(refs) + number :]
    outs = outs[-(split[1] if split else 1) :]

    def total(index):
        return sum(item[index].astype(f32) for item in items[1:]) + items[0][index].astype(f32)

    if not split:
        outs[0][...] = total(slice(None))
        return
    upper, fan, lower, which, low = split
    mine = (where[which] >> low) & (fan - 1)
    for a in range(upper):
        for b in range(lower):
            for flip in range(fan):
                index = (a * fan + (mine ^ flip)) * lower + b
                outs[flip][a * lower + b] = total(index).astype(outs[flip].dtype)


def combine(where, items, split, waits=()):
    count, rows, _ = items[0].shape
    if split:
        fan = split[1]
        shapes = [
            jax.ShapeDtypeStruct((count // fan, rows, LANES), bf16 if flip else f32)
            for flip in range(fan)
        ]
    else:
        shapes = [jax.ShapeDtypeStruct((count, rows, LANES), f32)]
    return pl.pallas_call(
        partial(combine_kernel, len(items), split),
        out_shape=shapes,
        in_specs=[SMEM] + [VMEM] * len(items) + [ANY] * len(waits),
        out_specs=[VMEM] * len(shapes),
        compiler_params=limit(12),
        name="combine",
    )(where, *items, *waits)


def scatter_parts(where, parts, count, groups, waits=None):
    for n, (low, width) in enumerate(groups):
        got = [permute_batch(item, k << low, count) for k, item in enumerate(parts) if k]
        if waits and n == 0:
            got = hold(got, waits)
        split = None
        if n + 1 < len(groups):
            fan = 1 << groups[n + 1][1]
            split = (parts[0].shape[0] // fan, fan, 1, 1, groups[n + 1][0])
        parts = combine(where, [parts[0], *got], split)
    return parts[0]


def hold(values, waits):
    spec = pl.BlockSpec(memory_space=pl.ANY)
    number = len(values)
    return pl.pallas_call(
        lambda *refs: None,
        out_shape=[jax.ShapeDtypeStruct(item.shape, item.dtype) for item in values],
        in_specs=[spec] * (number + len(waits)),
        out_specs=[spec] * number,
        input_output_aliases={i: i for i in range(number)},
        compiler_params=limit(1),
        name="hold",
    )(*values, *waits)


def send_kernel(shard, plan, down, where, *refs):
    number = (len(refs) - 4) // 2
    target, stage, square = refs[number : number + 3]
    sources = refs[number + 3 : -1]
    arrive(fetch(refs[:number], sources, refs[-1]))
    number = len(plan) // 2
    core = where[0]
    stage[...] = jnp.zeros_like(stage)
    gain_at = [i for i, item in enumerate(plan) if item == "gain"]
    if gain_at:
        square[...] = jnp.zeros_like(square)
        square[0:2, 0:shard] = sources[-1][...]
        column = square[...].T

    def fill(half):
        for i in range(number):
            item = plan[half * number + i]
            rows = slice(i * shard, (i + 1) * shard)
            if item == "gain":
                stage[rows, :] = column[:shard]
            elif item is not None:
                which, at = item
                stage[rows, :] = sources[which][:, at * LANES : (at + 1) * LANES]
        for i in range(3 if down else 0):
            start = number * shard + i * down
            stage[start : start + down, :] = sources[2][
                half * down : (half + 1) * down, i * LANES : (i + 1) * LANES
            ]

    @pl.when(core == 0)
    def _():
        fill(0)

    @pl.when(core == 1)
    def _():
        fill(1)

    target[...] = stage[...].astype(bf16)


def send_chunk(where, plan, down, sources, waits):
    shard = sources[0].shape[0]
    rows = len(plan) // 2 * shard + 3 * down
    rows = -(-rows // 16) * 16
    core = where[0]
    if shard % 8 == 0 and down % 8 == 0:
        spec = VMEM

        def kernel(where, *refs):
            kept = refs[: len(sources)] + refs[len(sources) + len(waits) :]
            send_kernel(shard, plan, down, where, *kept)

        return pl.pallas_call(
            kernel,
            out_shape=jax.ShapeDtypeStruct((rows, LANES), bf16),
            in_specs=[SMEM] + [HBM] * len(sources) + [ANY] * len(waits),
            out_specs=spec,
            scratch_shapes=[pltpu.VMEM((rows, LANES), f32), pltpu.VMEM((LANES, LANES), f32)]
            + landing(sources),
            compiler_params=limit(6),
            name="send_chunk",
        )(where, *in_hbm(sources), *waits)
    stacks = {i: slabs(item) for i, item in enumerate(sources) if item.shape[1] % LANES == 0}
    pieces = []
    for item in plan:
        if item == "gain":
            pieces.append(jnp.pad(sources[-1].T, ((0, 0), (0, LANES - 2))))
        elif item is None:
            pieces.append(jnp.zeros((shard, LANES), f32))
        else:
            pieces.append(stacks[item[0]][item[1]])
    half = len(plan) // 2
    halves = [jnp.concatenate(pieces[:half]), jnp.concatenate(pieces[half:])]
    if down:
        for i in range(2):
            part = stacks[2][:, i * down : (i + 1) * down].reshape(3 * down, LANES)
            halves[i] = jnp.concatenate([halves[i], part])
    chunk = jnp.where(core == 0, halves[0], halves[1]).astype(bf16)
    return jnp.pad(chunk, ((0, rows - chunk.shape[0]), (0, 0)))


FIRST_PLAN = tuple((0, i) for i in range(9)) + ("gain",)
SECOND_PLAN = tuple((0, i) for i in range(3)) + tuple((1, i) for i in range(16)) + (None,)


def gather(chunk, count, waits):
    held = chunk[None]
    groups = bit_groups(count)[::-1]
    for n, (low, width) in enumerate(groups):
        pieces = exchange_all(held, low, width, count)
        if n + 1 < len(groups):
            held = join(pieces, () if n else waits)
    return held, pieces


def unpack(count, number, shard, down, where, pieces, others, stage, w_down):
    core, owner = where[0], where[1]
    last = bit_groups(count)[0][1]
    for sources, half in ((pieces, core), (others, 1 - core)):
        for flip, source in enumerate(sources):

            def one(n, carry, source=source, half=half, flip=flip):
                device = owner ^ flip ^ (relative_flips(n, count) << last)
                chunk = source[n].astype(f32)
                for i in range(number):
                    rows = pl.ds(pl.multiple_of(device * shard, 8), shard)
                    stage[half * number + i, rows, :] = chunk[i * shard : (i + 1) * shard]
                for i in range(3 if down else 0):
                    start = number * shard + i * down
                    rows = pl.ds(pl.multiple_of((device * 2 + half) * down, 16), down)
                    w_down[rows, i * LANES : (i + 1) * LANES] = chunk[start : start + down].astype(
                        bf16
                    )
                return carry

            lax.fori_loop(0, source.shape[0], one, 0, unroll=True)


def relative_flips(place, count):
    last = bit_groups(count)[0][1]
    flips, scale = 0, 1
    for low, width in reversed(bit_groups(count)[1:]):
        flips = flips + (((place // scale) & ((1 << width) - 1)) << (low - last))
        scale <<= width
    return flips


def can_unpack(shard, down):
    return shard % 8 == 0 and down % 16 == 0


def unpack_plain(count, number, shard, down, where, mine, other):
    core, owner = where[0], where[1]
    places = relative_place(jnp.arange(count, dtype=jnp.int32), owner, count)
    mine, other = jnp.concatenate(mine), jnp.concatenate(other)
    low = jnp.take(jnp.where(core == 0, mine, other), places, axis=0)
    high = jnp.take(jnp.where(core == 0, other, mine), places, axis=0)

    def part(source):
        return (
            source[:, : number * shard]
            .reshape(count, number, shard, LANES)
            .transpose(1, 0, 2, 3)
            .reshape(number, D, LANES)
        )

    stack = jnp.concatenate([part(low), part(high)], axis=0)
    if number == 5:
        return unslab(stack[:9]), stack[9].T[:8].astype(f32)
    downs = [
        item[:, number * shard : number * shard + 3 * down].reshape(count, 3, down, LANES)
        for item in (low, high)
    ]
    w_down = jnp.stack(downs, axis=1).transpose(0, 1, 3, 2, 4).reshape(FF, D)
    return unslab(stack[:3]), unslab(stack[3:19]), w_down


def put_slab(stage, core, number, shard, at, slab):
    half, row = at // number, (at % number) * shard
    slot = core if half == 0 else 1 - core
    stage[slot, :, row : row + shard, :] = slab.reshape(-1, shard, LANES)


def put_down(stage, core, number, shard, down, column, slab, first):
    parts = slab.reshape(-1, 2, down, LANES)
    row = number * shard + column * down
    devices = slice(first, first + parts.shape[0])
    stage[core, devices, row : row + down, :] = parts[:, 0]
    stage[1 - core, devices, row : row + down, :] = parts[:, 1]


def gain_column(row):
    return jnp.concatenate([row, jnp.zeros((LANES - 8, D), f32)], axis=0).T


def pack_plain(count, core, grads, number, shard, down):
    column = jnp.pad(grads[-1][:1].T, ((0, 0), (0, LANES - 1)))[None]
    stack = jnp.concatenate([slabs(item) for item in (grads[:2] if down else grads[:1])] + [column])

    def by_device(part):
        return (
            part.reshape(number, count, shard, LANES)
            .transpose(1, 0, 2, 3)
            .reshape(count, number * shard, LANES)
        )

    halves = [by_device(stack[:number]), by_device(stack[number:])]
    if down:
        downs = (
            slabs(grads[2])
            .reshape(3, count, 2, down, LANES)
            .transpose(2, 1, 0, 3, 4)
            .reshape(2, count, 3 * down, LANES)
        )
        halves = [jnp.concatenate([halves[i], downs[i]], axis=1) for i in range(2)]
    return jnp.stack(halves)


def tables_kernel(length, where, ids, pads, offsets, *refs):
    cosine, sine, key_aux, query_aux, ranges = refs[-5:]
    core = where[0]
    whole = 2 * length

    def turn(row):
        low, high = row[:, :length], row[:, length:]
        return jnp.concatenate(
            [jnp.where(core == 0, low, high), jnp.where(core == 0, high, low)], axis=1
        )

    classes = (2 * ids[...] + pads[...]).astype(f32)
    spot = lax.broadcasted_iota(jnp.int32, (1, whole), 1)
    position = (turn(spot) + turn(offsets[...])).astype(f32)
    turned = turn(classes)
    index = lax.broadcasted_iota(jnp.int32, (HD // 2, whole), 0).astype(f32)
    angle = position * jnp.exp(index * (-2.0 * math.log(10000.0) / HD))
    cos, sin = jnp.cos(angle), jnp.sin(angle)
    cosine[...] = jnp.concatenate([cos, cos, cos, cos], axis=0).T
    sine[...] = jnp.concatenate([-sin, sin, -sin, sin], axis=0).T
    at = lax.broadcasted_iota(jnp.int32, (LANES, whole), 0)
    is_class = (at >= HD) & (at < HD + 8)
    same = (at - HD).astype(f32) == turned
    is_log = (at >= HD + 8) & (at < HD + 8 + 3 * HEADS)
    key_aux[...] = jnp.where((is_class & same) | is_log, 1.0, 0.0).T.astype(bf16)
    own = turned[:, :length]
    kept = jnp.where(turn(pads[...])[:, :length] == 0, 1.0, 0.0)
    extra = jnp.where(is_class & ~same, masked_score, 0.0)[:, :length]
    query_aux[...] = jnp.where(at[:, :length] == KEEP_LANE, kept, extra).T.astype(bf16)
    starts = (core * length, (1 - core) * length)
    for n in range(length // BLOCK):
        mine = own[:, n * BLOCK : (n + 1) * BLOCK]
        first = jnp.min(mine)
        last = jnp.max(mine)
        low_key = jnp.sum(jnp.where(classes < first, 1.0, 0.0)).astype(jnp.int32)
        high_key = jnp.sum(jnp.where(classes <= last, 1.0, 0.0)).astype(jnp.int32)
        bounds = []
        for start in starts:
            low_part = jnp.clip(low_key - start, 0, length)
            high_part = jnp.clip(high_key - start, 0, length)
            low_block = low_part // BLOCK
            bounds.append((low_block, jnp.maximum((high_part + BLOCK - 1) // BLOCK - low_block, 0)))
        ranges[0, n] = bounds[0][0]
        ranges[1, n] = bounds[0][1]
        ranges[2, n] = bounds[1][0] + length // BLOCK - bounds[0][1]
        ranges[3, n] = bounds[0][1] + bounds[1][1]


def tables(where, ids, pads, offsets, waits):
    whole = ids.shape[1]
    length = whole // 2
    spec = pl.BlockSpec(memory_space=pltpu.VMEM)
    smem = pl.BlockSpec(memory_space=pltpu.SMEM)
    return pl.pallas_call(
        partial(tables_kernel, length),
        out_shape=[
            in_vmem((whole, LANES), f32),
            in_vmem((whole, LANES), f32),
            in_vmem((whole, LANES), bf16),
            in_vmem((length, LANES), bf16),
            jax.ShapeDtypeStruct((4, length // BLOCK), jnp.int32),
        ],
        in_specs=[smem, spec, spec, spec] + [pl.BlockSpec(memory_space=pl.ANY)] * len(waits),
        out_specs=[spec] * 4 + [smem],
        compiler_params=limit(LIMITS[0]),
        cost_estimate=cost(3 * 10**9, 4 * 2**20),
        name="tables",
    )(where, ids, pads, offsets, *waits)


def project_kernel(fused, own, there, cosine, sine, key_aux, query_aux, *refs):
    if fused:
        pieces = 1 << bit_groups(fused[0])[0][1]
        where, scratch = refs[0], refs[-2 * pieces - 3 : -1]
        qa, ka, va, kt, vt, w, gains, stage = refs[-2 * pieces - 11 : -2 * pieces - 3]
        copies = fetch((*refs[1 : 1 + 2 * pieces], own, there), scratch, refs[-1])
        mine, other, (own, there) = (
            scratch[:pieces], scratch[pieces : 2 * pieces], scratch[2 * pieces :]
        )
        arrive(copies)
        unpack(*fused, where, mine, other, stage, None)
        for i in range(9):
            w[:, i * LANES : (i + 1) * LANES] = stage[i].astype(bf16)
        gains[...] = stage[9].T[:8]
    else:
        w_in, gains_in, (qa, ka, va, kt, vt, w, gains) = *refs[:2], refs[-7:]
        w[...] = w_in[...]
        gains[...] = gains_in[...]
    low = lax.broadcasted_iota(jnp.int32, (BLOCK, LANES), 1) < HD
    lane = lax.broadcasted_iota(jnp.int32, (BLOCK, LANES), 1)
    value_extra = jnp.where((lane >= HD) & (lane < HD + 3), 1.0, 0.0)
    ones = jnp.ones((8, BLOCK), bf16)
    blocks = own.shape[0] // BLOCK

    def body(step, carry, source, base):
        rows, keys = block(step), block(base + step)
        x = source[rows, :].astype(f32)
        normed = (x * row_scale(x) * gains[0:1, :]).astype(bf16)
        cos, sin = cosine[keys, :], sine[keys, :]
        first = 0 if base == 0 else D
        products = dot(normed, w[:, first:], NN)
        products = [
            products[:, i * LANES - first : (i + 1) * LANES - first]
            for i in range(first // LANES, 9)
        ]
        if base == 0:
            query_extra = query_aux[rows, :].astype(f32)
            for pair in range(HEADS // 2):
                z = products[pair]
                z = (z * cos + swap_halves(z) * sin).astype(bf16).astype(f32) * HD**-0.5
                qa[2 * pair, rows, :] = jnp.where(low, z, query_extra).astype(bf16)
                qa[2 * pair + 1, rows, :] = jnp.where(
                    low, pltpu.roll(z, HD, 1), query_extra
                ).astype(bf16)
        key_extra = key_aux[keys, :].astype(f32)
        for pair in range(HEADS // 2):
            z = products[pair - 6]
            z = z * cos + swap_halves(z) * sin
            ka[2 * pair, keys, :] = jnp.where(low, z, key_extra).astype(bf16)
            ka[2 * pair + 1, keys, :] = jnp.where(
                low, pltpu.roll(z, HD, 1), key_extra
            ).astype(bf16)
            turned = z.T.astype(bf16)
            kt[2 * pair, :, keys] = turned[:HD]
            kt[2 * pair + 1, :, keys] = turned[HD:]
        for pair in range(HEADS // 2):
            z = products[pair - 3]
            va[2 * pair, keys, :] = jnp.where(low, z, value_extra).astype(bf16)
            va[2 * pair + 1, keys, :] = jnp.where(
                low, pltpu.roll(z, HD, 1), value_extra
            ).astype(bf16)
            turned = z.T.astype(bf16)
            for i in range(2):
                vt[2 * pair + i, :HD, keys] = turned[i * HD : (i + 1) * HD]
                vt[2 * pair + i, HD:, keys] = ones
        return carry

    lax.fori_loop(0, blocks, partial(body, source=own, base=0), 0)
    lax.fori_loop(0, blocks, partial(body, source=there, base=blocks), 0)


def project(own, there, cosine, sine, key_aux, query_aux, weights, fused, waits):
    length = own.shape[0]
    whole = 2 * length
    scratch, specs = [], [VMEM] * 6
    weight_specs = [VMEM] * 2
    if fused:
        specs = [HBM, ANY] + [VMEM] * 4
        weight_specs = [SMEM] + [ANY] * (len(weights) - 1)
        scratch = [pltpu.VMEM((10, D, LANES), f32)] + landing([*weights[1:], own, there])
    if fused:
        (own,) = in_hbm([own])
    return pl.pallas_call(
        partial(project_kernel, fused),
        out_shape=[
            in_vmem((HEADS, length, LANES), bf16),
            in_vmem((HEADS, whole, LANES), bf16),
            in_vmem((HEADS, whole, LANES), bf16),
            in_vmem((HEADS, HD, whole), bf16),
            in_vmem((HEADS, HD + 8, whole), bf16),
            in_vmem((D, 3 * D), bf16),
            in_vmem((8, D), f32),
        ],
        in_specs=specs + weight_specs + [ANY] * len(waits),
        out_specs=[VMEM] * 7,
        scratch_shapes=scratch,
        compiler_params=limit(LIMITS[1]),
        cost_estimate=cost(9 * 10**9, 16 * 2**20),
        name="project",
    )(own, there, cosine, sine, key_aux, query_aux, *weights, *waits)


def key_block(ranges, step, n):
    return jnp.where(n < ranges[1, step], ranges[0, step] + n, ranges[2, step] + n)


def attend_kernel(ranges, qa, ka, vt, *refs):
    mixed, exact, qb, total, peak = refs[-5:]
    lane = lax.broadcasted_iota(jnp.int32, (BLOCK, LANES), 1)

    def one(step, carry):
        queries = block(step)
        peak[...] = jnp.full((HEADS, 8, BLOCK), -3e38, f32)
        total[...] = jnp.zeros_like(total)

        def body(n, carry):
            rows = block(key_block(ranges, step, n))
            scores = [dot(ka[h, rows, :], qa[h, queries, :], NT) for h in range(HEADS)]
            weights = []
            for h in range(HEADS):
                old = peak[h][:1]
                new = jnp.maximum(old, jnp.max(scores[h], axis=0, keepdims=True))
                weights.append((jnp.exp(scores[h] - new).astype(bf16), jnp.exp(old - new)))
                peak[h] = jnp.broadcast_to(new, (8, BLOCK))
            for h in range(HEADS):
                weight, shrink = weights[h]
                total[h] = total[h] * shrink + dot(vt[h, :, rows], weight, NN)
            return carry

        lax.fori_loop(0, ranges[3, step], body, 0)
        means, pieces = [], []
        for h in range(HEADS):
            bottom = total[h][HD : HD + 1]
            means.append(total[h][:HD] / bottom)
            logs = -(peak[h][:1] + jnp.log(bottom))
            pieces.extend(piece.astype(f32) for piece in split_three(logs))
        for pair in range(HEADS // 2):
            both = jnp.concatenate(means[2 * pair : 2 * pair + 2], axis=0).T
            mixed[queries, pair * LANES : (pair + 1) * LANES] = both.astype(bf16)
            exact[queries, pair * LANES : (pair + 1) * LANES] = both
        table = jnp.concatenate(
            [jnp.zeros((HD + 8, BLOCK), f32)]
            + pieces
            + [jnp.zeros((LANES - HD - 8 - 3 * HEADS, BLOCK), f32)],
            axis=0,
        ).T
        for h in range(HEADS):
            start = HD + 8 + 3 * h
            qb[h, queries, :] = jnp.where(
                (lane >= start) & (lane < start + 3), table, qa[h, queries, :].astype(f32)
            ).astype(bf16)
        return carry

    lax.fori_loop(0, qa.shape[1] // BLOCK, one, 0)


def attend(ranges, qa, ka, vt, waits):
    heads, length, _ = qa.shape
    return pl.pallas_call(
        attend_kernel,
        out_shape=[
            in_vmem((length, D), bf16),
            in_vmem((length, D), f32),
            in_vmem(qa.shape, bf16),
        ],
        in_specs=[SMEM] + [VMEM] * 3 + [ANY] * len(waits),
        out_specs=[VMEM] * 3,
        scratch_shapes=[
            pltpu.VMEM((heads, HD + 8, BLOCK), f32),
            pltpu.VMEM((heads, 8, BLOCK), f32),
        ],
        compiler_params=limit(LIMITS[2]),
        cost_estimate=cost(18 * 10**9, 12 * 2**20),
        name="attend",
    )(ranges, qa, ka, vt, *waits)


def attend_back_kernel(ranges, qb, ka, da, va, kt, *refs):
    dq, sums, there, acc = refs[-4:]
    sums[...] = jnp.zeros_like(sums)
    zero = jnp.zeros((BLOCK, HD), bf16)

    def one(step, carry):
        queries = block(step)
        acc[...] = jnp.zeros_like(acc)

        def body(n, carry):
            rows = block(key_block(ranges, step, n))
            first = [
                (
                    dot(ka[h, rows, :], qb[h, queries, :], NT),
                    dot(va[h, rows, :], da[h, queries, :], NT),
                )
                for h in range(HEADS)
            ]
            second = []
            for scores, grads in first:
                probs = jnp.exp(scores)
                second.append((probs.astype(bf16), (probs * grads).astype(bf16)))
            for h in range(HEADS):
                probs_low, grads_low = second[h]
                grad_side = jnp.concatenate([da[h, queries, :HD], zero], axis=1)
                query_side = jnp.concatenate([zero, qb[h, queries, :HD]], axis=1)
                sums[h, rows, :] += dot(probs_low, grad_side, NN) + dot(grads_low, query_side, NN)
                acc[h] += dot(kt[h, :, rows], grads_low, NN)
            return carry

        lax.fori_loop(0, ranges[3, step], body, 0)
        for h in range(HEADS):
            dq[h, :, queries] = acc[h]
        return carry

    length = qb.shape[1]
    lax.fori_loop(0, length // BLOCK, one, 0)
    there[...] = sums[:, length:, :].astype(bf16)


def attend_back(ranges, qb, ka, da, va, kt, waits):
    heads, length, _ = qb.shape
    whole = ka.shape[1]
    return pl.pallas_call(
        attend_back_kernel,
        out_shape=[
            in_vmem((heads, HD, length), f32),
            in_vmem((heads, whole, LANES), f32),
            jax.ShapeDtypeStruct((heads, whole - length, LANES), bf16),
        ],
        in_specs=[SMEM] + [VMEM] * 5 + [ANY] * len(waits),
        out_specs=[VMEM] * 3,
        scratch_shapes=[pltpu.VMEM((heads, HD, BLOCK), f32)],
        compiler_params=limit(LIMITS[4]),
        cost_estimate=cost(34 * 10**9, 8 * 2**20),
        name="attend_back",
    )(ranges, qb, ka, da, va, kt, *waits)


FEED = 512


def feed_kernel(fused, own, mixed, exact, cotangent, query_aux, gains, *refs):
    if fused:
        pieces = fan = 1 << bit_groups(fused[0])[0][1]
        where, mine, other = refs[0], refs[1 : 1 + pieces], refs[1 + pieces : 1 + 2 * pieces]
        refs = refs[1 + 2 * pieces :]
        result, grad_middle, da, gives = *refs[:3], refs[3 : 3 + fan]
        normed_all, low_all, hidden_all, up_all, middle_all, wo, wgu, wd, stage, g_gain, sums = (
            refs[3 + fan : 14 + fan]
        )
        scratch = refs[14 + fan : -1]
        copies = fetch((*mine, *other, own, cotangent), scratch, refs[-1])
        mine, other, (own, cotangent) = (
            scratch[:pieces], scratch[pieces : 2 * pieces], scratch[2 * pieces :]
        )
        arrive(copies)
    else:
        wo, wgu, wd = refs[:3]
        result, grad_middle, da, g_out, g_gate_up, g_down, g_gain = refs[3:10]
        normed_all, low_all, hidden_all, up_all, middle_all = refs[10:]
    gain = gains[1:2, :]
    g_gain[...] = jnp.zeros_like(g_gain)
    if fused:
        unpack(*fused, where, mine, other, stage, wd)
        for i in range(3):
            wo[:, i * LANES : (i + 1) * LANES] = stage[i].astype(bf16)
        for i in range(16):
            wgu[:, i * LANES : (i + 1) * LANES] = stage[3 + i].astype(bf16)

    chunks = FF // BLOCK
    lane = lax.broadcasted_iota(jnp.int32, (FEED, LANES), 1)

    def body(step, carry):
        rows = block(step, FEED)
        x = own[rows, :].astype(f32)
        middle = x + dot(mixed[rows, :], wo[...], NN)
        scale = row_scale(middle)
        normed = (middle * scale * gain).astype(bf16)
        normed_all[rows, :] = normed
        kept = query_aux[rows, :].astype(f32)[:, KEEP_LANE : KEEP_LANE + 1]
        upstream = cotangent[rows, :].astype(f32) * kept
        up_low = upstream.astype(bf16)
        up_all[rows, :] = up_low
        gates = [dot(normed, wgu[:, c * BLOCK : (c + 1) * BLOCK], NN) for c in range(chunks)]
        ups = [dot(normed, wgu[:, FF + c * BLOCK : FF + (c + 1) * BLOCK], NN) for c in range(chunks)]
        hiddens = [dot(up_low, wd[c * BLOCK : (c + 1) * BLOCK, :], NT) for c in range(chunks)]
        for c in range(chunks):
            gate, up, grad_hidden = gates[c], ups[c], hiddens[c]
            sig = 1.0 / (1.0 + jnp.exp(-gate))
            silu = gate * sig
            hidden_all[rows, c * BLOCK : (c + 1) * BLOCK] = (silu * up).astype(bf16)
            low_all[rows, FF + c * BLOCK : FF + (c + 1) * BLOCK] = (grad_hidden * silu).astype(bf16)
            low_all[rows, c * BLOCK : (c + 1) * BLOCK] = (
                grad_hidden * up * (sig + silu * (1.0 - sig))
            ).astype(bf16)
        ffn = dot(hidden_all[rows, :], wd[...], NN)
        grad_normed = dot(low_all[rows, :], wgu[...], NT)
        result[rows, :] = (kept * (middle + ffn)).astype(bf16)
        g_gain[0:1, :] += jnp.sum(grad_normed * middle * scale, axis=0, keepdims=True)
        grad = upstream + norm_back(grad_normed * gain, middle, scale)
        grad_middle[rows, :] = grad
        low = grad.astype(bf16)
        middle_all[rows, :] = low
        grad_mixed = dot(low, wo[...], NT).astype(bf16).astype(f32)
        products = grad_mixed * exact[rows, :]
        for h in range(HEADS):
            pair = h // 2
            head = grad_mixed[:, pair * LANES : (pair + 1) * LANES]
            product = products[:, pair * LANES : (pair + 1) * LANES]
            mine_lanes = (lane < HD) if h % 2 == 0 else (lane >= HD)
            delta = -jnp.sum(jnp.where(mine_lanes, product, 0.0), axis=1, keepdims=True)
            if h % 2:
                head = pltpu.roll(head, HD, 1)
            high, mid, last = split_three(delta)
            extra = jnp.where(
                lane == HD,
                high.astype(f32),
                jnp.where(
                    lane == HD + 1,
                    mid.astype(f32),
                    jnp.where(lane == HD + 2, last.astype(f32), 0.0),
                ),
            )
            da[h, rows, :] = jnp.where(lane < HD, head, extra).astype(bf16)
        return carry

    lax.fori_loop(0, own.shape[0] // FEED, body, 0)
    if not fused:
        g_out[...] = dot(mixed[...], middle_all[...], TN)
        for c in range(2 * FF // 512):
            g_gate_up[:, c * 512 : (c + 1) * 512] = dot(
                normed_all[...], low_all[:, c * 512 : (c + 1) * 512], TN
            )
        for c in range(chunks):
            g_down[c * BLOCK : (c + 1) * BLOCK, :] = dot(
                hidden_all[:, c * BLOCK : (c + 1) * BLOCK], up_all[...], TN
            )
        return
    count, number, shard, down = fused

    def put(at, value):
        for i in range(value.shape[1] // LANES):
            put_slab(sums, 0, number, shard, at + i, value[:, i * LANES : (i + 1) * LANES])

    put(0, dot(mixed[...], middle_all[...], TN))
    for c in range(2 * FF // 512):
        put(3 + 4 * c, dot(normed_all[...], low_all[:, c * 512 : (c + 1) * 512], TN))
    put(19, gain_column(g_gain[...]))
    for c in range(chunks):
        value = dot(hidden_all[:, c * BLOCK : (c + 1) * BLOCK], up_all[...], TN)
        for i in range(3):
            put_down(
                sums, 0, number, shard, down, i,
                value[:, i * LANES : (i + 1) * LANES], c * BLOCK // (2 * down),
            )
    me = where[1] & (fan - 1)
    for high in range(count // fan):
        for flip in range(fan):
            for half in range(2):
                gives[flip][half * (count // fan) + high] = sums[
                    half, high * fan + (me ^ flip)
                ].astype(gives[flip].dtype)


def feed(own, mixed, exact, cotangent, query_aux, gains, weights, fused):
    length = own.shape[0]
    scratch = [
        pltpu.VMEM((length, D), bf16),
        pltpu.VMEM((length, 2 * FF), bf16),
        pltpu.VMEM((length, FF), bf16),
        pltpu.VMEM((length, D), bf16),
        pltpu.VMEM((length, D), bf16),
    ]
    out_shape = [
        jax.ShapeDtypeStruct((length, D), bf16),
        in_vmem((length, D), f32),
        in_vmem((HEADS, length, LANES), bf16),
    ]
    if fused:
        count, number, shard, down = fused
        rows = number * shard + 3 * down
        fan = 1 << bit_groups(count)[0][1]
        weight_specs = [SMEM] + [ANY] * (len(weights) - 1)
        specs = [HBM, VMEM, VMEM, HBM, VMEM, VMEM]
        out_shape += [
            jax.ShapeDtypeStruct((2 * count // fan, rows, LANES), bf16 if flip else f32)
            for flip in range(fan)
        ]
        scratch += [
            pltpu.VMEM((D, D), bf16),
            pltpu.VMEM((D, 2 * FF), bf16),
            pltpu.VMEM((FF, D), bf16),
            pltpu.VMEM((2 * number, D, LANES), f32),
            pltpu.VMEM((8, D), f32),
            pltpu.VMEM((2, count, rows, LANES), f32),
        ]
        scratch += landing([*weights[1:], own, cotangent])
    else:
        weight_specs = [VMEM] * 3
        specs = [VMEM] * 6
        out_shape += [
            jax.ShapeDtypeStruct((D, D), f32),
            jax.ShapeDtypeStruct((D, 2 * FF), f32),
            jax.ShapeDtypeStruct((FF, D), f32),
            jax.ShapeDtypeStruct((8, D), f32),
        ]
    if fused:
        own, cotangent = in_hbm([own, cotangent])
    return pl.pallas_call(
        partial(feed_kernel, fused),
        out_shape=out_shape,
        in_specs=specs + weight_specs,
        out_specs=[VMEM] * len(out_shape),
        scratch_shapes=scratch,
        compiler_params=limit(LIMITS[3]),
        cost_estimate=cost(14 * 10**9, 16 * 2**20),
        name="feed",
    )(own, mixed, exact, cotangent, query_aux, gains, *weights)


PARTS = ((0, 1, 2), (3, 4, 5, 6, 7, 8))


def project_back_kernel(number, fused, own, cosine, sine, w, gains, *refs):
    part = PARTS[number]
    low = lax.broadcasted_iota(jnp.int32, (BLOCK, LANES), 1) < HD
    gain = gains[0:1, :]
    if number == 0:
        dq = refs[0]
        partial_sum, grads, normed_all, low_all = refs[-6:-2]
        copies = fetch((own,), refs[-2:-1], refs[-1])
        own = refs[-2]
    else:
        kept, got, grad_middle, before, grads_before = refs[:5]
        if fused:
            where = refs[5]
            grad_tokens, keep, give, sums, g_gain, normed_all, low_all = refs[-10:-3]
        else:
            grad_tokens, grads, g_gain, normed_all, low_all = refs[-8:-3]
        g_gain[...] = jnp.zeros_like(g_gain)
        copies = fetch((own, got), refs[-3:-1], refs[-1])
        own, got = refs[-3:-1]
    arrive(copies)

    def body(step, carry):
        rows = block(step)
        cos, sin = cosine[rows, :], -sine[rows, :]
        x = own[rows, :].astype(f32)
        scale = row_scale(x)
        normed_all[rows, :] = (x * scale * gain).astype(bf16)
        for at, slab in enumerate(part):
            kind, pair = divmod(slab, 3)
            heads = (2 * pair, 2 * pair + 1)
            if kind == 0:
                z = jnp.concatenate([dq[h, :, rows] for h in heads], axis=0).T * HD**-0.5
            else:
                one, two = [kept[h, rows, :] + got[h, rows, :].astype(f32) for h in heads]
                if kind == 1:
                    z = jnp.where(low, pltpu.roll(one, HD, 1), two)
                else:
                    z = jnp.where(low, one, pltpu.roll(two, HD, 1))
            if kind < 2:
                z = z * cos + swap_halves(z) * sin
            low_all[rows, at * LANES : (at + 1) * LANES] = z.astype(bf16)
        first = part[0] * LANES
        grad_normed = dot(
            low_all[rows, :], w[:, first : first + len(part) * LANES], NT
        )
        if number == 0:
            partial_sum[rows, :] = grad_normed
        else:
            grad_normed = grad_normed + before[rows, :]
            g_gain[0:1, :] += jnp.sum(grad_normed * x * scale, axis=0, keepdims=True)
            grad_tokens[rows, :] = (
                grad_middle[rows, :] + norm_back(grad_normed * gain, x, scale)
            ).astype(bf16)
        return carry

    lax.fori_loop(0, own.shape[0] // BLOCK, body, 0)
    value = dot(normed_all[...], low_all[...], TN)
    if number == 0 or not fused:
        grads[...] = value
        return
    core = where[0]
    for done, source in ((PARTS[0], grads_before), (PARTS[1], value)):
        for at, slab in enumerate(done):
            put_slab(sums, core, *fused, slab, source[:, at * LANES : (at + 1) * LANES])
    put_slab(sums, core, *fused, 9, gain_column(g_gain[...]))
    keep[...] = sums[0]
    give[...] = sums[1].astype(bf16)


def project_back(number, fused, where, shared, arrays, waits):
    own, cosine, sine, w, gains = shared
    length = own.shape[0]
    columns = len(PARTS[number]) * LANES
    scratch = [pltpu.VMEM((length, D), bf16), pltpu.VMEM((length, columns), bf16)]
    specs = [VMEM] * len(arrays)
    if number:
        specs[1] = ANY
    scratch += landing([own] + list(arrays[1:2]))
    if number == 0:
        out_shape = [in_vmem((length, D), f32), in_vmem((D, columns), f32)]
    elif fused:
        size, shard = fused
        chunk = (D // shard, size * shard, LANES)
        specs.append(SMEM)
        arrays = [*arrays, where]
        out_shape = [
            jax.ShapeDtypeStruct((length, D), bf16),
            jax.ShapeDtypeStruct(chunk, f32),
            jax.ShapeDtypeStruct(chunk, bf16),
        ]
        scratch = [pltpu.VMEM((2,) + chunk, f32), pltpu.VMEM((8, D), f32)] + scratch
    else:
        out_shape = [
            jax.ShapeDtypeStruct((length, D), bf16),
            jax.ShapeDtypeStruct((D, columns), f32),
            jax.ShapeDtypeStruct((8, D), f32),
        ]
    (own,) = in_hbm([own])
    return pl.pallas_call(
        partial(project_back_kernel, number, fused),
        out_shape=out_shape,
        in_specs=[HBM] + [VMEM] * 4 + specs + [ANY] * len(waits),
        out_specs=[VMEM] * len(out_shape),
        scratch_shapes=scratch,
        compiler_params=limit(LIMITS[5]),
        cost_estimate=cost((40 if number == 0 else 4) * 10**9, 8 * 2**20),
        name="project_back",
    )(own, cosine, sine, w, gains, *arrays, *waits)


def squares_kernel(*refs):
    total = sum(jnp.sum(ref[...] * ref[...]) for ref in refs[0:4:2]) + 0.0
    other = sum(jnp.sum(ref[...] * ref[...]) for ref in refs[1:4:2]) + 0.0
    refs[4][...] = jnp.full((1, LANES), total + other, f32)


def squares(sums):
    spec = pl.BlockSpec(memory_space=pltpu.VMEM)
    return pl.pallas_call(
        squares_kernel,
        out_shape=jax.ShapeDtypeStruct((1, LANES), f32),
        in_specs=[spec] * 4,
        out_specs=spec,
        compiler_params=limit(16),
        name="squares",
    )(*sums)


def update_kernel(shard, down, where, total, *refs):
    core = where[0]
    chunks = refs[:4]
    norm = refs[19]
    outs = [refs[20 + 5 * i : 25 + 5 * i] for i in range(4)]
    low, high, square = refs[40:43]
    copies = fetch(refs[4:19], refs[43:58], refs[58])
    masters, firsts, seconds = refs[43:48], refs[48:53], refs[53:58]
    split = 5 * shard

    @pl.when(core == 0)
    def _():
        for i, target in ((0, low), (1, high)):
            target[:split] = chunks[i][...]
            target[split:] = chunks[2 + i][...]

    @pl.when(core == 1)
    def _():
        for i, target in ((0, high), (1, low)):
            target[:split] = chunks[i][...]
            target[split:] = chunks[2 + i][...]

    arrive(copies)
    length = jnp.sqrt(total[0:1, 0:1])
    norm[...] = length
    factor = clip_limit / jnp.maximum(length, clip_limit)
    halves = (low, high)

    def step(which, grad, rows, columns, rate, decay):
        at = (rows, columns)
        new = adam_update(
            masters[which][at], factor * grad, firsts[which][at], seconds[which][at], rate, decay
        )
        outs[0][which][at] = new[0]
        outs[1][which][at] = new[1]
        outs[2][which][at] = new[2]
        outs[3][which][at] = new[2].astype(bf16)

    every = slice(None)
    places = [(0, i, i // 5, (i % 5) * shard) for i in range(9)]
    for i in range(19):
        which, column = (1, i) if i < 3 else (2, i - 3)
        places.append((which, column, i // 10, (5 + i % 10) * shard))
    for which, column, half, row in places:
        rate = 4.0 * D**-0.5 if which == 1 else D**-0.5
        grad = halves[half][row : row + shard, :]
        step(which, grad, every, slice(column * LANES, (column + 1) * LANES), rate, decay_rate)
    for half in range(2):
        for i in range(3):
            row = 15 * shard + i * down
            step(
                3, halves[half][row : row + down, :], slice(half * down, (half + 1) * down),
                slice(i * LANES, (i + 1) * LANES), FF**-0.5, decay_rate,
            )
    gain_rows = []
    for row in (4 * shard, 14 * shard):
        square[...] = jnp.zeros_like(square)
        square[0:shard, :] = high[row : row + shard, :]
        gain_rows.append(square[...].T[0:1, :shard])
    for i in range(2):
        step(4, gain_rows[i], slice(i, i + 1), every, 0.5, 0.0)


def update(where, total, sums, masters, firsts, seconds):
    shard, down = masters[0].shape[0], masters[3].shape[0] // 2
    spec = pl.BlockSpec(memory_space=pltpu.VMEM)
    shapes = [item.shape for item in masters]
    outs = pl.pallas_call(
        partial(update_kernel, shard, down),
        out_shape=[jax.ShapeDtypeStruct((1, 1), f32)]
        + [jax.ShapeDtypeStruct(shape, f32) for _ in range(3) for shape in shapes]
        + [jax.ShapeDtypeStruct(shape, bf16) for shape in shapes],
        in_specs=[pl.BlockSpec(memory_space=pltpu.SMEM)] + [VMEM] * 5 + [HBM] * 15,
        out_specs=[spec] * 21,
        scratch_shapes=[
            pltpu.VMEM((15 * shard + 3 * down, LANES), f32),
            pltpu.VMEM((15 * shard + 3 * down, LANES), f32),
            pltpu.VMEM((LANES, LANES), f32),
        ]
        + landing([*masters, *firsts, *seconds]),
        compiler_params=limit(LIMITS[6]),
        name="update",
    )(where, total, *sums, *in_hbm([*masters, *firsts, *seconds]))
    return outs[0][0, 0], outs[1:6], outs[6:11], outs[11:16], outs[16:21]


def update_plain(core, total, sums, masters, firsts, seconds):
    shard, down = masters[0].shape[0], masters[3].shape[0] // 2
    mine = jnp.concatenate([sums[0], sums[2]])
    there = jnp.concatenate([sums[1], sums[3]])
    low = jnp.where(core == 0, mine, there)
    high = jnp.where(core == 0, there, mine)
    five, fifteen = 5 * shard, 15 * shard
    first_shard = jnp.concatenate([low[:five], high[:five]]).reshape(10, shard, LANES)
    second_shard = jnp.concatenate([low[five:fifteen], high[five:fifteen]])
    second_shard = second_shard.reshape(20, shard, LANES)
    down_shard = jnp.stack(
        [item[fifteen:].reshape(3, down, LANES) for item in (low, high)], axis=1
    ).reshape(3, 2 * down, LANES)
    shard_grads = (
        unslab(first_shard[:9]),
        unslab(second_shard[:3]),
        unslab(second_shard[3:19]),
        unslab(down_shard),
        jnp.stack([first_shard[9, :, 0], second_shard[19, :, 0]]),
    )
    grad_norm = jnp.sqrt(total[0, 0])
    factor = clip_limit / jnp.maximum(grad_norm, clip_limit)
    rates = (D ** (-0.5), 4.0 * D ** (-0.5), D ** (-0.5), FF ** (-0.5), 0.5)
    decays = (decay_rate, decay_rate, decay_rate, decay_rate, 0.0)
    updates = [
        adam_update(
            masters[i], factor * shard_grads[i], firsts[i], seconds[i], rates[i], decays[i]
        )
        for i in range(5)
    ]
    new_first, new_second, new_master = zip(*updates)
    return grad_norm, new_first, new_second, new_master, [item.astype(bf16) for item in new_master]


def per_device(
    count,
    tokens,
    cotangent,
    sample_ids,
    pad_flags,
    offsets,
    w_qkv,
    w_out,
    w_gate_up,
    w_down,
    gains,
    m_qkv,
    m_out,
    m_gate_up,
    m_down,
    m_gains,
    v_qkv,
    v_out,
    v_gate_up,
    v_down,
    v_gains,
):
    owner = lax.axis_index("batch")
    core = lax.axis_index("tm")
    where = jnp.stack([core, owner]).astype(jnp.int32)
    shard = w_qkv.shape[0]
    down = w_down.shape[0] // 2
    own = tokens[0]
    fuse_in = can_unpack(shard, down)
    masters = (w_qkv, w_out, w_gate_up, w_down, gains)

    first = send_chunk(where, FIRST_PLAN, 0, [w_qkv, gains], [])
    there = swap_tm(own)
    cosine, sine, key_aux, query_aux, ranges = tables(
        where, sample_ids, pad_flags, offsets, [there]
    )
    first_held, first_pieces = gather(first, count, [query_aux])
    second = send_chunk(where, SECOND_PLAN, down, [w_out, w_gate_up, w_down], [first_held])

    def gathered(pieces, number, down):
        others = [swap_tm(piece) for piece in pieces]
        if fuse_in:
            return (where, *pieces, *others), (count, number, shard, down)
        return unpack_plain(count, number, shard, down, where, pieces, others), None

    weights, fused = gathered(first_pieces, 5, 0)
    qa, ka, va, kt, vt, attn_in, gain_pair = project(
        own, there, cosine, sine, key_aux, query_aux, weights, fused, []
    )
    second_held, second_pieces = gather(second, count, [gain_pair])
    mixed, exact, qb = attend(ranges, qa, ka, vt, [second_held])
    second_pieces[1:] = hold(second_pieces[1:], [mixed])
    weights, fused = gathered(second_pieces, 10, down)
    result, grad_middle, da, *grads = feed(
        own, mixed, exact, cotangent[0], query_aux, gain_pair, weights, fused
    )
    groups = bit_groups(count)
    fan = 1 << groups[0][1]

    def flips(halves):
        halves = halves.reshape((-1, fan) + halves.shape[-2:])
        mine = owner & (fan - 1)
        parts = [lax.dynamic_index_in_dim(halves, mine ^ k, 1, keepdims=False) for k in range(fan)]
        return [parts[0]] + [item.astype(bf16) for item in parts[1:]]

    if not fused:
        grads = flips(pack_plain(count, core, grads, 10, shard, down))
    got = [permute_batch(grads[k], k, count) for k in range(1, fan)]
    dq, kept, part = attend_back(ranges, qb, ka, da, va, kt, [])
    got = hold(got, [part])
    part_there = swap_tm(part)
    left = count // fan
    keep, give = combine(where, [grads[0], *got], (1, 2, left, 0, 0))
    split = None
    if len(groups) > 1:
        split = (left >> groups[1][1], 1 << groups[1][1], 1, 1, groups[1][0])
    parts = combine(where, [keep, swap_tm(give)], split)
    fused = (5, shard) if fuse_in else None
    shared = (own, cosine, sine, attn_in, gain_pair)
    before, grads_before = project_back(0, fused, where, shared, [dq], [parts[0]])
    if split:
        parts = [scatter_parts(where, parts, count, groups[1:], [grads_before])]
    second_sum = parts[0].reshape(-1, LANES)
    grad_tokens, *grads = project_back(
        1, fused, where, shared, [kept, part_there, grad_middle, before, grads_before], [parts[0]]
    )
    if fused:
        kept, given = grads
    else:
        grads = [jnp.concatenate([grads_before, grads[0]], axis=1), grads[1]]
        halves = pack_plain(count, core, grads, 5, shard, 0)
        kept = jnp.where(core == 0, halves[0], halves[1])
        given = jnp.where(core == 0, halves[1], halves[0]).astype(bf16)
    parts = combine(where, [kept, swap_tm(given)], (left, fan, 1, 1, 0))
    first_sum = scatter_parts(where, parts, count, groups).reshape(-1, LANES)
    sums = (first_sum, swap_tm(first_sum), second_sum, swap_tm(second_sum))
    total = sum_batch(squares(sums), count)
    firsts = (m_qkv, m_out, m_gate_up, m_down, m_gains)
    seconds = (v_qkv, v_out, v_gate_up, v_down, v_gains)
    if fuse_in:
        updates = update(where, total, sums, masters, firsts, seconds)
    else:
        updates = update_plain(core, total, sums, masters, firsts, seconds)
    grad_norm, new_first, new_second, new_master, copies = updates
    return (
        result[None],
        grad_tokens[None],
        grad_norm,
        *new_first,
        *new_second,
        *new_master,
        *copies,
    )


def solution(mesh):
    in_specs = (
        P("batch", "tm", None),
        P("batch", "tm", None),
        P("batch", None),
        P("batch", None),
        P("batch", None),
        P("batch", None),
        P("batch", None),
        P("batch", None),
        P("batch", None),
        P(None, "batch"),
        P("batch", None),
        P("batch", None),
        P("batch", None),
        P("batch", None),
        P(None, "batch"),
        P("batch", None),
        P("batch", None),
        P("batch", None),
        P("batch", None),
        P(None, "batch"),
    )
    out_specs = (
        P("batch", "tm", None),
        P("batch", "tm", None),
        P(),
        P("batch", None),
        P("batch", None),
        P("batch", None),
        P("batch", None),
        P(None, "batch"),
        P("batch", None),
        P("batch", None),
        P("batch", None),
        P("batch", None),
        P(None, "batch"),
        P("batch", None),
        P("batch", None),
        P("batch", None),
        P("batch", None),
        P(None, "batch"),
        P("batch", None),
        P("batch", None),
        P("batch", None),
        P("batch", None),
        P(None, "batch"),
    )
    return jax.shard_map(
        partial(per_device, mesh.shape["batch"]), mesh=mesh, in_specs=in_specs, out_specs=out_specs, check_vma=False
    )
```

time: 213 us -> 178 us (0.84)
  Pallas kernels: 125 us -> 97.7 us
  waiting for transfers between devices: 19.7 us -> 29.9 us
  other arithmetic: 9.34 us -> 0.09 us
  local copies, waits for them, and re-layouts: 10.5 us -> 2.1 us
    pallas_call x8 -> x15, Pallas kernels: 117 us -> 90.7 us  [the longest x1 23.4 us: attend_back(): pl.pallas_call(attend_back_kernel, out_shape=[in_vmem((heads, HD, length)...]
    ppermute x24, waiting for transfers between devices: 14.4 us -> 23.6 us  [permute_batch(): return lax.ppermute(value, 'batch', [(i, i ^ flip) for i in range(count)])]
    unnamed x60 -> x6, local copies, waits for them, and re-layouts: 9.49 us -> 2.09 us
    add x5 -> x0, other arithmetic: 6.29 us -> none  [the longest x3 2.94 us: scatter_steps(): total = total + item.astype(f32)]
    ppermute x12 -> x14, waiting for transfers between devices: 5.25 us -> 6.28 us  [swap_tm(): return lax.ppermute(value, 'tm', [(0, 1), (1, 0)])]
  transfers between devices with their start and end apart: 36 -> 38, of which waited for: 12 -> 16; matrix products, arithmetic and copies ran while one was open for 4% -> 0% of each run, Pallas kernels for 42% -> 37%
where the time goes in v5:
time: 178 us; the launch traced here: 177 us
  Pallas kernels  97.7 us (55%)
  starting transfers between devices  35.3 us (20%)
  waiting for transfers between devices  29.9 us (17%)
  blocking collectives  10.9 us (6%)
  local copies, waits for them, and re-layouts  2.1 us (1%)
    ppermute x24, starting transfers between devices, permute_batch(): return lax.ppermute(value, 'batch', [(i, i ^ flip) for i in range(count)])  32.9 us
    ppermute x24, waiting for transfers between devices, permute_batch(): return lax.ppermute(value, 'batch', [(i, i ^ flip) for i in range(count)])  23.6 us
    pallas_call x1, Pallas kernels, attend_back(): pl.pallas_call(attend_back_kernel, out_shape=[in_vmem((heads, HD, length)...  23.4 us
    pallas_call x1, Pallas kernels, feed(): pl.pallas_call(partial(feed_kernel, fused), out_shape=out_shape, in_specs...  20.4 us
    pallas_call x1, Pallas kernels, attend(): pl.pallas_call(attend_kernel, out_shape=[in_vmem((length, D), bf16), in_v...  17.3 us
    pallas_call x1, Pallas kernels, project(): pl.pallas_call(partial(project_kernel, fused), out_shape=[in_vmem((HEADS,...  12.1 us
    all_to_all x1, blocking collectives, sum_batch(): value = lax.all_to_all(value, 'batch', 0, 0, tiled=True)  10.9 us
    pallas_call x2, Pallas kernels, project_back(): pl.pallas_call(partial(project_back_kernel, number, fused), out_shape=out...  10.7 us
  transfers between devices with their start and end apart: 38, of which 16 were waited for; matrix products, arithmetic and copies ran while one was open for 0% of the time, Pallas kernels for 37%

profile of v5, /device:TPU:0, one launch (start us, length us, event | category | flops | bytes accessed | tf_op | source)
XLA Modules:
  0.0 177.1 jit_solution(13067820470940352991)
XLA Ops:
  2.8 4.7 %collective-permute-start.3 = (bf16[1,128,128]{2,1,0:T(8,128)(2,1)S(1)}, bf16[1,128,128]{2,1,0:T(8,128)(2,1)S(1)}, u32[]{:S(2)}, u32[]{:S(2)}) collective-permute-start(bf16[1,128,128]{2,1,0:T(8,128)(2,1)S(1)} %bitcast.24), channel_id=1, source_target_pairs={{0,24},{2,26},{4,28},{6,30},{8,16},{10,18},{12,20},{14,22},{16,8},... | collective-permute-start | bytes 98312 | tf_op jit(solution)/shard_map/ppermute | solution.py:49
  10.2 2.8 %tables.1 = (f32[2048,128]{1,0:T(8,128)S(1)}, f32[2048,128]{1,0:T(8,128)S(1)}, bf16[2048,128]{1,0:T(8,128)(2,1)S(1)}, bf16[1024,128]{1,0:T(8,128)(2,1)S(1)}, s32[4,4]{1,0:T(4,128)S(1)}) custom-call(s32[2]{0:T(128)S(1)} %pad_add_fusion.where.refs_0_.refs_5_, s32[1,2048]{1,0:T(1,128)S(1)} %copy-done, s32[1,2048]{1,0:T(1,128)S(1)} %copy-done.1, ...), custom_call_target="tpu_custom_call" | custom-call | flops 3000000000 | bytes 4194304 | tf_op jit(solution)/shard_map/tables/pallas_call | solution.py:506
  13.1 2.7 %collective-permute-start.6 = (bf16[4,128,128]{2,1,0:T(8,128)(2,1)S(1)}, bf16[4,128,128]{2,1,0:T(8,128)(2,1)S(1)}, u32[]{:S(2)}, u32[]{:S(2)}) collective-permute-start(bf16[4,128,128]{2,1,0:T(8,128)(2,1)S(1)} %join.2.refs_1_.refs_3_), channel_id=1, source_target_pairs={{0,6},{2,4},{4,2},{6,0},{8,14},{10,12},{12,10},{14,8},{16,22},{18,... | collective-permute-start | bytes 393224 | tf_op jit(solution)/shard_map/ppermute | solution.py:49
  16.7 3.0 %collective-permute-done.6.refs_4_ = bf16[4,128,128]{2,1,0:T(8,128)(2,1)S(1)} collective-permute-done((bf16[4,128,128]{2,1,0:T(8,128)(2,1)S(1)}, bf16[4,128,128]{2,1,0:T(8,128)(2,1)S(1)}, u32[]{:S(2)}, u32[]{:S(2)}) %collective-permute-start.6) | collective-permute-done | bytes 131104 | tf_op jit(solution)/shard_map/ppermute | solution.py:49
  19.7 2.5 %collective-permute-done.5.refs_3_ = bf16[4,128,128]{2,1,0:T(8,128)(2,1)S(1)} collective-permute-done((bf16[4,128,128]{2,1,0:T(8,128)(2,1)S(1)}, bf16[4,128,128]{2,1,0:T(8,128)(2,1)S(1)}, u32[]{:S(2)}, u32[]{:S(2)}) %collective-permute-start.5) | collective-permute-done | bytes 131104 | tf_op jit(solution)/shard_map/ppermute | solution.py:49
  22.7 1.8 %send_chunk.3 = bf16[336,128]{1,0:T(8,128)(2,1)S(1)} custom-call(s32[2]{0:T(128)S(1)} %pad_add_fusion.where.refs_0_.refs_5_, f32[24,384]{1,0:T(8,128)} %refs_5_.1, f32[24,2048]{1,0:T(8,128)} %refs_6_.1, f32[64,384]{1,0:T(8,128)} %refs_7_.1, bf16[4,128,128]{2,1,0:T(8,128)(2,1)S(1)} %join.2.refs_1_.refs_3_), custom_call_target="tpu_custom_call" | custom-call | tf_op jit(solution)/shard_map/send_chunk/pallas_call | solution.py:307
  24.5 3.5 %collective-permute-start.13 = (bf16[1,336,128]{2,1,0:T(8,128)(2,1)S(1)}, bf16[1,336,128]{2,1,0:T(8,128)(2,1)S(1)}, u32[]{:S(2)}, u32[]{:S(2)}) collective-permute-start(bf16[1,336,128]{2,1,0:T(8,128)(2,1)S(1)} %bitcast.20), channel_id=1, source_target_pairs={{0,24},{2,26},{4,28},{6,30},{8,16},{10,18},{12,20},{14,22},{16,8},... | collective-permute-start | bytes 258056 | tf_op jit(solution)/shard_map/ppermute | solution.py:49
  29.0 12.1 %project.1 = (bf16[6,1024,128]{2,1,0:T(8,128)(2,1)S(1)}, bf16[6,2048,128]{2,1,0:T(8,128)(2,1)S(1)}, bf16[6,2048,128]{2,1,0:T(8,128)(2,1)S(1)}, bf16[6,64,2048]{2...) custom-call(bf16[1024,384]{1,0:T(8,128)(2,1)} %bitcast.31, ...), custom_call_target="tpu_custom_call" | custom-call | flops 8999999488 | bytes 16777216 | tf_op jit(solution)/shard_map/project/pallas_call | solution.py:605
  41.3 1.8 %collective-permute-start.16 = (bf16[4,336,128]{2,1,0:T(8,128)(2,1)S(1)}, bf16[4,336,128]{2,1,0:T(8,128)(2,1)S(1)}, u32[]{:S(2)}, u32[]{:S(2)}) collective-permute-start(bf16[4,336,128]{2,1,0:T(8,128)(2,1)S(1)} %join.3.refs_0_.refs_1_), channel_id=1, source_target_pairs={{0,6},{2,4},{4,2},{6,0},{8,14},{10,12},{12,10},{14,8},{16,22},{18,... | collective-permute-start | bytes 1032200 | tf_op jit(solution)/shard_map/ppermute | solution.py:49
  44.8 17.3 %attend.1 = (bf16[1024,384]{1,0:T(8,128)(2,1)S(1)}, f32[1024,384]{1,0:T(8,128)S(1)}, bf16[6,1024,128]{2,1,0:T(8,128)(2,1)S(1)}) custom-call(s32[4,4]{1,0:T(4,128)S(1)} %get-tuple-element.97.ranges, bf16[6,1024,128]{2,1,0:T(8,128)(2,1)S(1)} %get-tuple-element.102.qa, bf16[6,2048,128]{2,1,0:T(8,128)(2,1)S(1)} %get-tuple-element.103.ka, ...), custom_call_target="tpu_custom_call" | custom-call | flops 17999998976 | bytes 12582912 | tf_op jit(solution)/shard_map/attend/pallas_call | solution.py:681
  64.9 20.4 %feed.1 = (bf16[1024,384]{1,0:T(8,128)(2,1)}, f32[1024,384]{1,0:T(8,128)S(1)}, bf16[6,1024,128]{2,1,0:T(8,128)(2,1)S(1)}, f32[8,336,128]{2,1,0:T(8,128)S(1)}, bf...) custom-call(bf16[1024,384]{1,0:T(8,128)(2,1)} %bitcast.32, ...), custom_call_target="tpu_custom_call" | custom-call | flops 14000000000 | bytes 16777216 | tf_op jit(solution)/shard_map/feed/pallas_call | solution.py:929
  88.9 23.4 %attend_back.1 = (f32[6,64,1024]{2,1,0:T(8,128)S(1)}, f32[6,2048,128]{2,1,0:T(8,128)S(1)}, bf16[6,1024,128]{2,1,0:T(8,128)(2,1)S(1)}) custom-call(s32[4,4]{1,0:T(4,128)S(1)} %get-tuple-element.97.ranges, bf16[6,1024,128]{2,1,0:T(8,128)(2,1)S(1)} %get-tuple-element.113.qb, bf16[6,2048,128]{2,1,0:T(8,128)(2,1)S(1)} %get-tuple-element.103.ka, ...), custom_call_target="tpu_custom_call" | custom-call | flops 33999998976 | bytes 8388608 | tf_op jit(solution)/shard_map/attend_back/pallas_call | solution.py:743
  112.3 6.5 %collective-permute-done.23.refs_1_ = bf16[8,336,128]{2,1,0:T(8,128)(2,1)S(1)} collective-permute-done((bf16[8,336,128]{2,1,0:T(8,128)(2,1)S(1)}, bf16[8,336,128]{2,1,0:T(8,128)(2,1)S(1)}, u32[]{:S(2)}, u32[]{:S(2)}) %collective-permute-start.23) | collective-permute-done | bytes 688160 | tf_op jit(solution)/shard_map/ppermute | solution.py:49
  123.3 2.9 %collective-permute-start.27 = (bf16[1,336,128]{2,1,0:T(8,128)(2,1)S(1)}, bf16[1,336,128]{2,1,0:T(8,128)(2,1)S(1)}, u32[]{:S(2)}, u32[]{:S(2)}) collective-permute-start(bf16[1,336,128]{2,1,0:T(8,128)(2,1)S(1)} %get-tuple-element.134), channel_id=1, source_target_pairs={{0,16},{2,18},{4,20},{6,22},{8,24},{10,26},{12,28},{14,30},{16,0},... | collective-permute-start | bytes 258056 | tf_op jit(solution)/shard_map/ppermute | solution.py:49
  126.5 4.3 %project_back.2 = (f32[1024,384]{1,0:T(8,128)S(1)}, f32[384,384]{1,0:T(8,128)S(1)}) custom-call(bf16[1024,384]{1,0:T(8,128)(2,1)} %bitcast.33, f32[2048,128]{1,0:T(8,128)S(1)} %get-tuple-element.98.cosine, f32[2048,128]{1,0:T(8,128)S(1)} %get-tuple-element.99.sine, bf16[384,1152]{1,0:T(8,128)(2,1)S(1)} %get-tuple-element.112.w, ...), custom_call_target="tpu_custom_call" | custom-call | flops 40000000000 | bytes 8388608 | tf_op jit(solution)/shard_map/project_back/pallas_call | solution.py:1042
  130.9 2.2 %collective-permute-done.27.refs_1_ = bf16[1,336,128]{2,1,0:T(8,128)(2,1)S(1)} collective-permute-done((bf16[1,336,128]{2,1,0:T(8,128)(2,1)S(1)}, bf16[1,336,128]{2,1,0:T(8,128)(2,1)S(1)}, u32[]{:S(2)}, u32[]{:S(2)}) %collective-permute-start.27) | collective-permute-done | bytes 86048 | tf_op jit(solution)/shard_map/ppermute | solution.py:49
  133.7 6.3 %project_back.3 = (bf16[1024,384]{1,0:T(8,128)(2,1)}, f32[16,120,128]{2,1,0:T(8,128)S(1)}, bf16[16,120,128]{2,1,0:T(8,128)(2,1)S(1)}) custom-call(bf16[1024,384]{1,0:T(8,128)(2,1)} %bitcast.34, f32[2048,128]{1,0:T(8,128)S(1)} %get-tuple-element.98.cosine, f32[2048,128]{1,0:T(8,128)S(1)} %get-tuple-element.99.sine, ...), custom_call_target="tpu_custom_call" | custom-call | flops 4000000000 | bytes 8388608 | tf_op jit(solution)/shard_map/project_back/pallas_call | solution.py:1042
  140.1 1.9 %collective-permute-done.29.refs_1_ = bf16[16,120,128]{2,1,0:T(8,128)(2,1)S(1)} collective-permute-done((bf16[16,120,128]{2,1,0:T(8,128)(2,1)S(1)}, bf16[16,120,128]{2,1,0:T(8,128)(2,1)S(1)}, u32[]{:S(2)}, u32[]{:S(2)}) %collective-permute-start.29) | collective-permute-done | bytes 491552 | tf_op jit(solution)/shard_map/ppermute | solution.py:53
  146.2 2.7 %collective-permute-done.30.refs_1_ = bf16[4,120,128]{2,1,0:T(8,128)(2,1)S(1)} collective-permute-done((bf16[4,120,128]{2,1,0:T(8,128)(2,1)S(1)}, bf16[4,120,128]{2,1,0:T(8,128)(2,1)S(1)}, u32[]{:S(2)}, u32[]{:S(2)}) %collective-permute-start.30) | collective-permute-done | bytes 122912 | tf_op jit(solution)/shard_map/ppermute | solution.py:49
  151.6 1.8 %collective-permute-start.33 = (bf16[1,120,128]{2,1,0:T(8,128)(2,1)S(1)}, bf16[1,120,128]{2,1,0:T(8,128)(2,1)S(1)}, u32[]{:S(2)}, u32[]{:S(2)}) collective-permute-start(bf16[1,120,128]{2,1,0:T(8,128)(2,1)S(1)} %get-tuple-element.147), channel_id=1, source_target_pairs={{0,8},{2,10},{4,12},{6,14},{8,0},{10,2},{12,4},{14,6},{16,24},{18,... | collective-permute-start | bytes 92168 | tf_op jit(solution)/shard_map/ppermute | solution.py:49
  156.0 2.7 %collective-permute-done.34.refs_2_ = bf16[1,120,128]{2,1,0:T(8,128)(2,1)S(1)} collective-permute-done((bf16[1,120,128]{2,1,0:T(8,128)(2,1)S(1)}, bf16[1,120,128]{2,1,0:T(8,128)(2,1)S(1)}, u32[]{:S(2)}, u32[]{:S(2)}) %collective-permute-start.34) | collective-permute-done | bytes 30752 | tf_op jit(solution)/shard_map/ppermute | solution.py:49
  158.7 1.8 %collective-permute-done.35.refs_3_ = bf16[1,120,128]{2,1,0:T(8,128)(2,1)S(1)} collective-permute-done((bf16[1,120,128]{2,1,0:T(8,128)(2,1)S(1)}, bf16[1,120,128]{2,1,0:T(8,128)(2,1)S(1)}, u32[]{:S(2)}, u32[]{:S(2)}) %collective-permute-start.35) | collective-permute-done | bytes 30752 | tf_op jit(solution)/shard_map/ppermute | solution.py:49
  162.6 10.9 %all_to_all.5 = f32[16,1,128]{2,1,0:T(1,128)S(1)} all-to-all(f32[16,1,128]{2,1,0:T(1,128)S(1)} %broadcast_in_dim.25), channel_id=1, replica_groups=mesh['batch'=16,'tm'=2] {'batch'}, dimensions={0} | all-to-all | bytes 16384 | tf_op jit(solution)/shard_map/all_to_all | solution.py:126
  173.5 3.5 %update.1 = (f32[1,1]{1,0:T(1,128)}, f32[24,1152]{1,0:T(8,128)}, f32[24,384]{1,0:T(8,128)}, f32[24,2048]{1,0:T(8,128)}, f32[64,384]{1,0:T(8,128)}, /*index=5*/f3...) custom-call(s32[2]{0:T(128)S(1)} %pad_add_fusion.where.refs_0_.refs_, ...), custom_call_target="tpu_custom_call" | custom-call | tf_op jit(solution)/shard_map/update/pallas_call | solution.py:1139
  (84 shorter events, 32.5 us)
Async XLA Ops:
  0.7 7.5 %collective-permute-start = (bf16[1024,384]{1,0:T(8,128)(2,1)}, bf16[1024,384]{1,0:T(8,128)(2,1)S(1)}, u32[]{:S(2)}, u32[]{:S(2)}) collective-permute-start(bf16[1024,384]{1,0:T(8,128)(2,1)} %bitcast.30), channel_id=1, source_target_pairs={{0,1},{1,0},{2,3},{3,2},{4,5},{5,4},{6,7},{7,6},{8,9},{9,8},{10,11... | collective-permute-start | bytes 2359304 | tf_op jit(solution)/shard_map/ppermute | solution.py:53
  2.8 10.3 %collective-permute-start.3 = (bf16[1,128,128]{2,1,0:T(8,128)(2,1)S(1)}, bf16[1,128,128]{2,1,0:T(8,128)(2,1)S(1)}, u32[]{:S(2)}, u32[]{:S(2)}) collective-permute-start(bf16[1,128,128]{2,1,0:T(8,128)(2,1)S(1)} %bitcast.24), channel_id=1, source_target_pairs={{0,24},{2,26},{4,28},{6,30},{8,16},{10,18},{12,20},{14,22},{16,8},... | collective-permute-start | bytes 98312 | tf_op jit(solution)/shard_map/ppermute | solution.py:49
  13.1 6.6 %collective-permute-start.6 = (bf16[4,128,128]{2,1,0:T(8,128)(2,1)S(1)}, bf16[4,128,128]{2,1,0:T(8,128)(2,1)S(1)}, u32[]{:S(2)}, u32[]{:S(2)}) collective-permute-start(bf16[4,128,128]{2,1,0:T(8,128)(2,1)S(1)} %join.2.refs_1_.refs_3_), channel_id=1, source_target_pairs={{0,6},{2,4},{4,2},{6,0},{8,14},{10,12},{12,10},{14,8},{16,22},{18,... | collective-permute-start | bytes 393224 | tf_op jit(solution)/shard_map/ppermute | solution.py:49
  15.8 6.5 %collective-permute-start.5 = (bf16[4,128,128]{2,1,0:T(8,128)(2,1)S(1)}, bf16[4,128,128]{2,1,0:T(8,128)(2,1)S(1)}, u32[]{:S(2)}, u32[]{:S(2)}) collective-permute-start(bf16[4,128,128]{2,1,0:T(8,128)(2,1)S(1)} %join.2.refs_1_.refs_3_), channel_id=1, source_target_pairs={{0,4},{2,6},{4,0},{6,2},{8,12},{10,14},{12,8},{14,10},{16,20},{18,... | collective-permute-start | bytes 393224 | tf_op jit(solution)/shard_map/ppermute | solution.py:49
  16.7 11.4 %collective-permute-start.7 = (bf16[4,128,128]{2,1,0:T(8,128)(2,1)S(1)}, bf16[4,128,128]{2,1,0:T(8,128)(2,1)S(1)}, u32[]{:S(2)}, u32[]{:S(2)}) collective-permute-start(bf16[4,128,128]{2,1,0:T(8,128)(2,1)S(1)} %join.2.refs_1_.refs_3_), channel_id=1, source_target_pairs={{0,1},{1,0},{2,3},{3,2},{4,5},{5,4},{6,7},{7,6},{8,9},{9,8},{10,11... | collective-permute-start | bytes 393224 | tf_op jit(solution)/shard_map/ppermute | solution.py:53
  19.7 8.4 %collective-permute-start.10 = (bf16[4,128,128]{2,1,0:T(8,128)(2,1)S(1)}, bf16[4,128,128]{2,1,0:T(8,128)(2,1)S(1)}, u32[]{:S(2)}, u32[]{:S(2)}) collective-permute-start(bf16[4,128,128]{2,1,0:T(8,128)(2,1)S(1)} %collective-permute-done.6.refs_4_), channel_id=1, source_target_pairs={{0,1},{1,0},{2,3},{3,2},{4,5},{5,4},{6,7},{7,6},{8,9},{9,8},{10,11... | collective-permute-start | bytes 393224 | tf_op jit(solution)/shard_map/ppermute | solution.py:53
  22.2 6.8 %collective-permute-start.9 = (bf16[4,128,128]{2,1,0:T(8,128)(2,1)S(1)}, bf16[4,128,128]{2,1,0:T(8,128)(2,1)S(1)}, u32[]{:S(2)}, u32[]{:S(2)}) collective-permute-start(bf16[4,128,128]{2,1,0:T(8,128)(2,1)S(1)} %collective-permute-done.5.refs_3_), channel_id=1, source_target_pairs={{0,1},{1,0},{2,3},{3,2},{4,5},{5,4},{6,7},{7,6},{8,9},{9,8},{10,11... | collective-permute-start | bytes 393224 | tf_op jit(solution)/shard_map/ppermute | solution.py:53
  22.3 6.7 %collective-permute-start.8 = (bf16[4,128,128]{2,1,0:T(8,128)(2,1)S(1)}, bf16[4,128,128]{2,1,0:T(8,128)(2,1)S(1)}, u32[]{:S(2)}, u32[]{:S(2)}) collective-permute-start(bf16[4,128,128]{2,1,0:T(8,128)(2,1)S(1)} %collective-permute-done.4.refs_2_), channel_id=1, source_target_pairs={{0,1},{1,0},{2,3},{3,2},{4,5},{5,4},{6,7},{7,6},{8,9},{9,8},{10,11... | collective-permute-start | bytes 393224 | tf_op jit(solution)/shard_map/ppermute | solution.py:53
  24.5 16.6 %collective-permute-start.13 = (bf16[1,336,128]{2,1,0:T(8,128)(2,1)S(1)}, bf16[1,336,128]{2,1,0:T(8,128)(2,1)S(1)}, u32[]{:S(2)}, u32[]{:S(2)}) collective-permute-start(bf16[1,336,128]{2,1,0:T(8,128)(2,1)S(1)} %bitcast.20), channel_id=1, source_target_pairs={{0,24},{2,26},{4,28},{6,30},{8,16},{10,18},{12,20},{14,22},{16,8},... | collective-permute-start | bytes 258056 | tf_op jit(solution)/shard_map/ppermute | solution.py:49
  28.1 13.1 %collective-permute-start.12 = (bf16[1,336,128]{2,1,0:T(8,128)(2,1)S(1)}, bf16[1,336,128]{2,1,0:T(8,128)(2,1)S(1)}, u32[]{:S(2)}, u32[]{:S(2)}) collective-permute-start(bf16[1,336,128]{2,1,0:T(8,128)(2,1)S(1)} %bitcast.21), channel_id=1, source_target_pairs={{0,16},{2,18},{4,20},{6,22},{8,24},{10,26},{12,28},{14,30},{16,0},... | collective-permute-start | bytes 258056 | tf_op jit(solution)/shard_map/ppermute | solution.py:49
  28.1 13.1 %collective-permute-start.11 = (bf16[1,336,128]{2,1,0:T(8,128)(2,1)S(1)}, bf16[1,336,128]{2,1,0:T(8,128)(2,1)S(1)}, u32[]{:S(2)}, u32[]{:S(2)}) collective-permute-start(bf16[1,336,128]{2,1,0:T(8,128)(2,1)S(1)} %bitcast.22), channel_id=1, source_target_pairs={{0,8},{2,10},{4,12},{6,14},{8,0},{10,2},{12,4},{14,6},{16,24},{18,... | collective-permute-start | bytes 258056 | tf_op jit(solution)/shard_map/ppermute | solution.py:49
  41.2 21.6 %collective-permute-start.17 = (bf16[4,336,128]{2,1,0:T(8,128)(2,1)S(1)}, bf16[4,336,128]{2,1,0:T(8,128)(2,1)S(1)}, u32[]{:S(2)}, u32[]{:S(2)}) collective-permute-start(bf16[4,336,128]{2,1,0:T(8,128)(2,1)S(1)} %join.3.refs_0_.refs_1_), channel_id=1, source_target_pairs={{0,1},{1,0},{2,3},{3,2},{4,5},{5,4},{6,7},{7,6},{8,9},{9,8},{10,11... | collective-permute-start | bytes 1032200 | tf_op jit(solution)/shard_map/ppermute | solution.py:53
  41.3 20.9 %collective-permute-start.16 = (bf16[4,336,128]{2,1,0:T(8,128)(2,1)S(1)}, bf16[4,336,128]{2,1,0:T(8,128)(2,1)S(1)}, u32[]{:S(2)}, u32[]{:S(2)}) collective-permute-start(bf16[4,336,128]{2,1,0:T(8,128)(2,1)S(1)} %join.3.refs_0_.refs_1_), channel_id=1, source_target_pairs={{0,6},{2,4},{4,2},{6,0},{8,14},{10,12},{12,10},{14,8},{16,22},{18,... | collective-permute-start | bytes 1032200 | tf_op jit(solution)/shard_map/ppermute | solution.py:49
  43.1 19.1 %collective-permute-start.15 = (bf16[4,336,128]{2,1,0:T(8,128)(2,1)S(1)}, bf16[4,336,128]{2,1,0:T(8,128)(2,1)S(1)}, u32[]{:S(2)}, u32[]{:S(2)}) collective-permute-start(bf16[4,336,128]{2,1,0:T(8,128)(2,1)S(1)} %join.3.refs_0_.refs_1_), channel_id=1, source_target_pairs={{0,4},{2,6},{4,0},{6,2},{8,12},{10,14},{12,8},{14,10},{16,20},{18,... | collective-permute-start | bytes 1032200 | tf_op jit(solution)/shard_map/ppermute | solution.py:49
  44.3 17.9 %collective-permute-start.14 = (bf16[4,336,128]{2,1,0:T(8,128)(2,1)S(1)}, bf16[4,336,128]{2,1,0:T(8,128)(2,1)S(1)}, u32[]{:S(2)}, u32[]{:S(2)}) collective-permute-start(bf16[4,336,128]{2,1,0:T(8,128)(2,1)S(1)} %join.3.refs_0_.refs_1_), channel_id=1, source_target_pairs={{0,2},{2,0},{4,6},{6,4},{8,10},{10,8},{12,14},{14,12},{16,18},{18,... | collective-permute-start | bytes 1032200 | tf_op jit(solution)/shard_map/ppermute | solution.py:49
  85.3 27.0 %collective-permute-start.22 = (bf16[8,336,128]{2,1,0:T(8,128)(2,1)S(1)}, bf16[8,336,128]{2,1,0:T(8,128)(2,1)S(1)}, u32[]{:S(2)}, u32[]{:S(2)}) collective-permute-start(bf16[8,336,128]{2,1,0:T(8,128)(2,1)S(1)} %get-tuple-element.122), channel_id=1, source_target_pairs={{0,2},{2,0},{4,6},{6,4},{8,10},{10,8},{12,14},{14,12},{16,18},{18,... | collective-permute-start | bytes 2064392 | tf_op jit(solution)/shard_map/ppermute | solution.py:49
  86.9 31.9 %collective-permute-start.23 = (bf16[8,336,128]{2,1,0:T(8,128)(2,1)S(1)}, bf16[8,336,128]{2,1,0:T(8,128)(2,1)S(1)}, u32[]{:S(2)}, u32[]{:S(2)}) collective-permute-start(bf16[8,336,128]{2,1,0:T(8,128)(2,1)S(1)} %get-tuple-element.123), channel_id=1, source_target_pairs={{0,4},{2,6},{4,0},{6,2},{8,12},{10,14},{12,8},{14,10},{16,20},{18,... | collective-permute-start | bytes 2064392 | tf_op jit(solution)/shard_map/ppermute | solution.py:49
  87.7 31.1 %collective-permute-start.24 = (bf16[8,336,128]{2,1,0:T(8,128)(2,1)S(1)}, bf16[8,336,128]{2,1,0:T(8,128)(2,1)S(1)}, u32[]{:S(2)}, u32[]{:S(2)}) collective-permute-start(bf16[8,336,128]{2,1,0:T(8,128)(2,1)S(1)} %get-tuple-element.124), channel_id=1, source_target_pairs={{0,6},{2,4},{4,2},{6,0},{8,14},{10,12},{12,10},{14,8},{16,22},{18,... | collective-permute-start | bytes 2064392 | tf_op jit(solution)/shard_map/ppermute | solution.py:49
  119.8 13.9 %collective-permute-start.21 = (bf16[6,1024,128]{2,1,0:T(8,128)(2,1)S(1)}, bf16[6,1024,128]{2,1,0:T(8,128)(2,1)S(1)}, u32[]{:S(2)}, u32[]{:S(2)}) collective-permute-start(bf16[6,1024,128]{2,1,0:T(8,128)(2,1)S(1)} %get-tuple-element.118.refs_3_), channel_id=1, source_target_pairs={{0,1},{1,0},{2,3},{3,2},{4,5},{5,4},{6,7},{7,6},{8,9},{9,8},{10,11... | collective-permute-start | bytes 4718600 | tf_op jit(solution)/shard_map/ppermute | solution.py:53
  122.1 8.8 %collective-permute-start.26 = (bf16[1,336,128]{2,1,0:T(8,128)(2,1)S(1)}, bf16[1,336,128]{2,1,0:T(8,128)(2,1)S(1)}, u32[]{:S(2)}, u32[]{:S(2)}) collective-permute-start(bf16[1,336,128]{2,1,0:T(8,128)(2,1)S(1)} %get-tuple-element.133), channel_id=1, source_target_pairs={{0,8},{2,10},{4,12},{6,14},{8,0},{10,2},{12,4},{14,6},{16,24},{18,... | collective-permute-start | bytes 258056 | tf_op jit(solution)/shard_map/ppermute | solution.py:49
  123.3 9.8 %collective-permute-start.27 = (bf16[1,336,128]{2,1,0:T(8,128)(2,1)S(1)}, bf16[1,336,128]{2,1,0:T(8,128)(2,1)S(1)}, u32[]{:S(2)}, u32[]{:S(2)}) collective-permute-start(bf16[1,336,128]{2,1,0:T(8,128)(2,1)S(1)} %get-tuple-element.134), channel_id=1, source_target_pairs={{0,16},{2,18},{4,20},{6,22},{8,24},{10,26},{12,28},{14,30},{16,0},... | collective-permute-start | bytes 258056 | tf_op jit(solution)/shard_map/ppermute | solution.py:49
  126.2 6.9 %collective-permute-start.28 = (bf16[1,336,128]{2,1,0:T(8,128)(2,1)S(1)}, bf16[1,336,128]{2,1,0:T(8,128)(2,1)S(1)}, u32[]{:S(2)}, u32[]{:S(2)}) collective-permute-start(bf16[1,336,128]{2,1,0:T(8,128)(2,1)S(1)} %get-tuple-element.135), channel_id=1, source_target_pairs={{0,24},{2,26},{4,28},{6,30},{8,16},{10,18},{12,20},{14,22},{16,8},... | collective-permute-start | bytes 258056 | tf_op jit(solution)/shard_map/ppermute | solution.py:49
  143.2 6.8 %collective-permute-start.31 = (bf16[4,120,128]{2,1,0:T(8,128)(2,1)S(1)}, bf16[4,120,128]{2,1,0:T(8,128)(2,1)S(1)}, u32[]{:S(2)}, u32[]{:S(2)}) collective-permute-start(bf16[4,120,128]{2,1,0:T(8,128)(2,1)S(1)} %get-tuple-element.144), channel_id=1, source_target_pairs={{0,4},{2,6},{4,0},{6,2},{8,12},{10,14},{12,8},{14,10},{16,20},{18,... | collective-permute-start | bytes 368648 | tf_op jit(solution)/shard_map/ppermute | solution.py:49
  146.2 15.0 %collective-permute-start.37 = (f32[336,128]{1,0:T(8,128)S(1)}, f32[336,128]{1,0:T(8,128)S(1)}, u32[]{:S(2)}, u32[]{:S(2)}) collective-permute-start(f32[336,128]{1,0:T(8,128)S(1)} %bitcast.14), channel_id=1, source_target_pairs={{0,1},{1,0},{2,3},{3,2},{4,5},{5,4},{6,7},{7,6},{8,9},{9,8},{10,11... | collective-permute-start | bytes 516104 | tf_op jit(solution)/shard_map/ppermute | solution.py:53
  (17 other events, 58.2 us)

commit v6 on v5

--- a/solution.py
+++ b/solution.py
@@ -1046,7 +1046,7 @@
         out_specs=[VMEM] * len(out_shape),
         scratch_shapes=scratch,
         compiler_params=limit(LIMITS[5]),
-        cost_estimate=cost((40 if number == 0 else 4) * 10**9, 8 * 2**20),
+        cost_estimate=cost(4 * 10**9, 8 * 2**20),
         name="project_back",
     )(own, cosine, sine, w, gains, *arrays, *waits)
 
@@ -1069,14 +1069,30 @@
     )(*sums)
 
 
+def bring_kernel(*refs):
+    number = (len(refs) - 1) // 2
+    arrive(fetch(refs[:number], refs[-number - 1 : -1], refs[-1]))
+
+
+def bring(arrays):
+    return pl.pallas_call(
+        bring_kernel,
+        out_shape=[in_vmem(item.shape, item.dtype) for item in arrays],
+        in_specs=[HBM] * len(arrays),
+        out_specs=[VMEM] * len(arrays),
+        scratch_shapes=[pltpu.SemaphoreType.DMA((len(arrays),))],
+        compiler_params=limit(1),
+        name="bring",
+    )(*in_hbm(arrays))
+
+
 def update_kernel(shard, down, where, total, *refs):
     core = where[0]
     chunks = refs[:4]
     norm = refs[19]
     outs = [refs[20 + 5 * i : 25 + 5 * i] for i in range(4)]
-    low, high, square = refs[40:43]
-    copies = fetch(refs[4:19], refs[43:58], refs[58])
-    masters, firsts, seconds = refs[43:48], refs[48:53], refs[53:58]
+    low, high, square = refs[40:]
+    masters, firsts, seconds = refs[4:9], refs[9:14], refs[14:19]
     split = 5 * shard
 
     @pl.when(core == 0)
@@ -1091,7 +1107,6 @@
             target[:split] = chunks[i][...]
             target[split:] = chunks[2 + i][...]
 
-    arrive(copies)
     length = jnp.sqrt(total[0:1, 0:1])
     norm[...] = length
     factor = clip_limit / jnp.maximum(length, clip_limit)
@@ -1141,17 +1156,16 @@
         out_shape=[jax.ShapeDtypeStruct((1, 1), f32)]
         + [jax.ShapeDtypeStruct(shape, f32) for _ in range(3) for shape in shapes]
         + [jax.ShapeDtypeStruct(shape, bf16) for shape in shapes],
-        in_specs=[pl.BlockSpec(memory_space=pltpu.SMEM)] + [VMEM] * 5 + [HBM] * 15,
+        in_specs=[pl.BlockSpec(memory_space=pltpu.SMEM)] + [VMEM] * 20,
         out_specs=[spec] * 21,
         scratch_shapes=[
             pltpu.VMEM((15 * shard + 3 * down, LANES), f32),
             pltpu.VMEM((15 * shard + 3 * down, LANES), f32),
             pltpu.VMEM((LANES, LANES), f32),
-        ]
-        + landing([*masters, *firsts, *seconds]),
+        ],
         compiler_params=limit(LIMITS[6]),
         name="update",
-    )(where, total, *sums, *in_hbm([*masters, *firsts, *seconds]))
+    )(where, total, *sums, *masters, *firsts, *seconds)
     return outs[0][0, 0], outs[1:6], outs[6:11], outs[11:16], outs[16:21]
 
 
@@ -1259,23 +1273,23 @@
         grads = flips(pack_plain(count, core, grads, 10, shard, down))
     got = [permute_batch(grads[k], k, count) for k in range(1, fan)]
     dq, kept, part = attend_back(ranges, qb, ka, da, va, kt, [])
-    got = hold(got, [part])
-    part_there = swap_tm(part)
+    fused = (5, shard) if fuse_in else None
+    shared = (own, cosine, sine, attn_in, gain_pair)
+    before, grads_before = project_back(0, fused, where, shared, [dq], [])
+    got = hold(got, [grads_before])
+    part_there = swap_tm(hold([part], got)[0])
     left = count // fan
     keep, give = combine(where, [grads[0], *got], (1, 2, left, 0, 0))
     split = None
     if len(groups) > 1:
         split = (left >> groups[1][1], 1 << groups[1][1], 1, 1, groups[1][0])
     parts = combine(where, [keep, swap_tm(give)], split)
-    fused = (5, shard) if fuse_in else None
-    shared = (own, cosine, sine, attn_in, gain_pair)
-    before, grads_before = project_back(0, fused, where, shared, [dq], [parts[0]])
-    if split:
-        parts = [scatter_parts(where, parts, count, groups[1:], [grads_before])]
-    second_sum = parts[0].reshape(-1, LANES)
     grad_tokens, *grads = project_back(
         1, fused, where, shared, [kept, part_there, grad_middle, before, grads_before], [parts[0]]
     )
+    if split:
+        parts = [scatter_parts(where, parts, count, groups[1:], [grad_tokens])]
+    second_sum = parts[0].reshape(-1, LANES)
     if fused:
         kept, given = grads
     else:
@@ -1283,12 +1297,18 @@
         halves = pack_plain(count, core, grads, 5, shard, 0)
         kept = jnp.where(core == 0, halves[0], halves[1])
         given = jnp.where(core == 0, halves[1], halves[0]).astype(bf16)
-    parts = combine(where, [kept, swap_tm(given)], (left, fan, 1, 1, 0))
+    (given,) = hold([given], [second_sum])
+    firsts = (m_qkv, m_out, m_gate_up, m_down, m_gains)
+    seconds = (v_qkv, v_out, v_gate_up, v_down, v_gains)
+    waits = []
+    if fuse_in:
+        brought = bring([*masters, *firsts, *seconds])
+        masters, firsts, seconds = brought[:5], brought[5:10], brought[10:]
+        waits = brought[:1]
+    parts = combine(where, [kept, swap_tm(given)], (left, fan, 1, 1, 0), waits)
     first_sum = scatter_parts(where, parts, count, groups).reshape(-1, LANES)
     sums = (first_sum, swap_tm(first_sum), second_sum, swap_tm(second_sum))
     total = sum_batch(squares(sums), count)
-    firsts = (m_qkv, m_out, m_gate_up, m_down, m_gains)
-    seconds = (v_qkv, v_out, v_gate_up, v_down, v_gains)
     if fuse_in:
         updates = update(where, total, sums, masters, firsts, seconds)
     else:

time: 178 us -> 173 us (0.972)
  waiting for transfers between devices: 29.9 us -> 24.2 us
    ppermute x24, waiting for transfers between devices: 23.6 us -> 18.5 us  [permute_batch(): return lax.ppermute(value, 'batch', [(i, i ^ flip) for i in range(count)])]
  transfers between devices with their start and end apart: 38 -> 38, of which waited for: 16 -> 15; matrix products, arithmetic and copies ran while one was open for 0% -> 0% of each run, Pallas kernels for 37% -> 43%
where the time goes in v6:
time: 173 us; the launch traced here: 172 us
  Pallas kernels  98.2 us (57%)
  starting transfers between devices  35.6 us (21%)
  waiting for transfers between devices  24.2 us (14%)
  blocking collectives  9.85 us (6%)
  local copies, waits for them, and re-layouts  3.23 us (2%)
    ppermute x24, starting transfers between devices, permute_batch(): return lax.ppermute(value, 'batch', [(i, i ^ flip) for i in range(count)])  32.8 us
    pallas_call x1, Pallas kernels, attend_back(): pl.pallas_call(attend_back_kernel, out_shape=[in_vmem((heads, HD, length)...  23.7 us
    pallas_call x1, Pallas kernels, feed(): pl.pallas_call(partial(feed_kernel, fused), out_shape=out_shape, in_specs...  20.4 us
    ppermute x24, waiting for transfers between devices, permute_batch(): return lax.ppermute(value, 'batch', [(i, i ^ flip) for i in range(count)])  18.5 us
    pallas_call x1, Pallas kernels, attend(): pl.pallas_call(attend_kernel, out_shape=[in_vmem((length, D), bf16), in_v...  17.4 us
    pallas_call x1, Pallas kernels, project(): pl.pallas_call(partial(project_kernel, fused), out_shape=[in_vmem((HEADS,...  12.1 us
    pallas_call x2, Pallas kernels, project_back(): pl.pallas_call(partial(project_back_kernel, number, fused), out_shape=out...  10.7 us
    all_to_all x1, blocking collectives, sum_batch(): value = lax.all_to_all(value, 'batch', 0, 0, tiled=True)  9.85 us
  transfers between devices with their start and end apart: 38, of which 15 were waited for; matrix products, arithmetic and copies ran while one was open for 0% of the time, Pallas kernels for 43%

profile of v6, /device:TPU:0, one launch (start us, length us, event | category | flops | bytes accessed | tf_op | source)
XLA Modules:
  0.0 172.3 jit_solution(5989857413088932991)
XLA Ops:
  2.8 2.7 %collective-permute-start.1 = (bf16[1,128,128]{2,1,0:T(8,128)(2,1)S(1)}, bf16[1,128,128]{2,1,0:T(8,128)(2,1)S(1)}, u32[]{:S(2)}, u32[]{:S(2)}) collective-permute-start(bf16[1,128,128]{2,1,0:T(8,128)(2,1)S(1)} %bitcast.26), channel_id=1, source_target_pairs={{0,8},{2,10},{4,12},{6,14},{8,0},{10,2},{12,4},{14,6},{16,24},{18,... | collective-permute-start | bytes 98312 | tf_op jit(solution)/shard_map/ppermute | solution.py:49
  5.5 2.6 %collective-permute-start.2 = (bf16[1,128,128]{2,1,0:T(8,128)(2,1)S(1)}, bf16[1,128,128]{2,1,0:T(8,128)(2,1)S(1)}, u32[]{:S(2)}, u32[]{:S(2)}) collective-permute-start(bf16[1,128,128]{2,1,0:T(8,128)(2,1)S(1)} %bitcast.27), channel_id=1, source_target_pairs={{0,16},{2,18},{4,20},{6,22},{8,24},{10,26},{12,28},{14,30},{16,0},... | collective-permute-start | bytes 98312 | tf_op jit(solution)/shard_map/ppermute | solution.py:49
  10.1 2.8 %tables.1 = (f32[2048,128]{1,0:T(8,128)S(1)}, f32[2048,128]{1,0:T(8,128)S(1)}, bf16[2048,128]{1,0:T(8,128)(2,1)S(1)}, bf16[1024,128]{1,0:T(8,128)(2,1)S(1)}, s32[4,4]{1,0:T(4,128)S(1)}) custom-call(s32[2]{0:T(128)S(1)} %pad_add_fusion.where.refs_0_.refs_5_, s32[1,2048]{1,0:T(1,128)S(1)} %copy-done.1, s32[1,2048]{1,0:T(1,128)S(1)} %copy-done.2, ...), custom_call_target="tpu_custom_call" | custom-call | flops 3000000000 | bytes 4194304 | tf_op jit(solution)/shard_map/tables/pallas_call | solution.py:506
  17.3 2.3 %collective-permute-done.4.refs_2_ = bf16[4,128,128]{2,1,0:T(8,128)(2,1)S(1)} collective-permute-done((bf16[4,128,128]{2,1,0:T(8,128)(2,1)S(1)}, bf16[4,128,128]{2,1,0:T(8,128)(2,1)S(1)}, u32[]{:S(2)}, u32[]{:S(2)}) %collective-permute-start.4) | collective-permute-done | bytes 131104 | tf_op jit(solution)/shard_map/ppermute | solution.py:49
  19.6 3.5 %collective-permute-done.5.refs_3_ = bf16[4,128,128]{2,1,0:T(8,128)(2,1)S(1)} collective-permute-done((bf16[4,128,128]{2,1,0:T(8,128)(2,1)S(1)}, bf16[4,128,128]{2,1,0:T(8,128)(2,1)S(1)}, u32[]{:S(2)}, u32[]{:S(2)}) %collective-permute-start.5) | collective-permute-done | bytes 131104 | tf_op jit(solution)/shard_map/ppermute | solution.py:49
  23.6 1.8 %send_chunk.3 = bf16[336,128]{1,0:T(8,128)(2,1)S(1)} custom-call(s32[2]{0:T(128)S(1)} %pad_add_fusion.where.refs_0_.refs_5_, f32[24,384]{1,0:T(8,128)} %refs_1_.5, f32[24,2048]{1,0:T(8,128)} %refs_2_.3, f32[64,384]{1,0:T(8,128)} %refs_3_.1, bf16[4,128,128]{2,1,0:T(8,128)(2,1)S(1)} %join.2.refs_1_.refs_3_), custom_call_target="tpu_custom_call" | custom-call | tf_op jit(solution)/shard_map/send_chunk/pallas_call | solution.py:307
  25.7 3.5 %collective-permute-start.12 = (bf16[1,336,128]{2,1,0:T(8,128)(2,1)S(1)}, bf16[1,336,128]{2,1,0:T(8,128)(2,1)S(1)}, u32[]{:S(2)}, u32[]{:S(2)}) collective-permute-start(bf16[1,336,128]{2,1,0:T(8,128)(2,1)S(1)} %bitcast.23), channel_id=1, source_target_pairs={{0,16},{2,18},{4,20},{6,22},{8,24},{10,26},{12,28},{14,30},{16,0},... | collective-permute-start | bytes 258056 | tf_op jit(solution)/shard_map/ppermute | solution.py:49
  29.9 12.1 %project.1 = (bf16[6,1024,128]{2,1,0:T(8,128)(2,1)S(1)}, bf16[6,2048,128]{2,1,0:T(8,128)(2,1)S(1)}, bf16[6,2048,128]{2,1,0:T(8,128)(2,1)S(1)}, bf16[6,64,2048]{2...) custom-call(bf16[1024,384]{1,0:T(8,128)(2,1)} %bitcast.33, ...), custom_call_target="tpu_custom_call" | custom-call | flops 8999999488 | bytes 16777216 | tf_op jit(solution)/shard_map/project/pallas_call | solution.py:605
  43.6 2.1 %collective-permute-start.16 = (bf16[4,336,128]{2,1,0:T(8,128)(2,1)S(1)}, bf16[4,336,128]{2,1,0:T(8,128)(2,1)S(1)}, u32[]{:S(2)}, u32[]{:S(2)}) collective-permute-start(bf16[4,336,128]{2,1,0:T(8,128)(2,1)S(1)} %join.3.refs_0_.refs_1_), channel_id=1, source_target_pairs={{0,6},{2,4},{4,2},{6,0},{8,14},{10,12},{12,10},{14,8},{16,22},{18,... | collective-permute-start | bytes 1032200 | tf_op jit(solution)/shard_map/ppermute | solution.py:49
  45.6 17.4 %attend.1 = (bf16[1024,384]{1,0:T(8,128)(2,1)S(1)}, f32[1024,384]{1,0:T(8,128)S(1)}, bf16[6,1024,128]{2,1,0:T(8,128)(2,1)S(1)}) custom-call(s32[4,4]{1,0:T(4,128)S(1)} %get-tuple-element.112.ranges, bf16[6,1024,128]{2,1,0:T(8,128)(2,1)S(1)} %get-tuple-element.117.qa, bf16[6,2048,128]{2,1,0:T(8,128)(2,1)S(1)} %get-tuple-element.118.ka, ...), custom_call_target="tpu_custom_call" | custom-call | flops 17999998976 | bytes 12582912 | tf_op jit(solution)/shard_map/attend/pallas_call | solution.py:681
  65.9 20.4 %feed.1 = (bf16[1024,384]{1,0:T(8,128)(2,1)}, f32[1024,384]{1,0:T(8,128)S(1)}, bf16[6,1024,128]{2,1,0:T(8,128)(2,1)S(1)}, f32[8,336,128]{2,1,0:T(8,128)S(1)}, bf...) custom-call(bf16[1024,384]{1,0:T(8,128)(2,1)} %bitcast.34, ...), custom_call_target="tpu_custom_call" | custom-call | flops 14000000000 | bytes 16777216 | tf_op jit(solution)/shard_map/feed/pallas_call | solution.py:929
  87.9 2.0 %collective-permute-start.23 = (bf16[8,336,128]{2,1,0:T(8,128)(2,1)S(1)}, bf16[8,336,128]{2,1,0:T(8,128)(2,1)S(1)}, u32[]{:S(2)}, u32[]{:S(2)}) collective-permute-start(bf16[8,336,128]{2,1,0:T(8,128)(2,1)S(1)} %get-tuple-element.136), channel_id=1, source_target_pairs={{0,6},{2,4},{4,2},{6,0},{8,14},{10,12},{12,10},{14,8},{16,22},{18,... | collective-permute-start | bytes 2064392 | tf_op jit(solution)/shard_map/ppermute | solution.py:49
  89.9 23.7 %attend_back.1 = (f32[6,64,1024]{2,1,0:T(8,128)S(1)}, f32[6,2048,128]{2,1,0:T(8,128)S(1)}, bf16[6,1024,128]{2,1,0:T(8,128)(2,1)S(1)}) custom-call(s32[4,4]{1,0:T(4,128)S(1)} %get-tuple-element.112.ranges, bf16[6,1024,128]{2,1,0:T(8,128)(2,1)S(1)} %get-tuple-element.128.qb, bf16[6,2048,128]{2,1,0:T(8,128)(2,1)S(1)} %get-tuple-element.118.ka, ...), custom_call_target="tpu_custom_call" | custom-call | flops 33999998976 | bytes 8388608 | tf_op jit(solution)/shard_map/attend_back/pallas_call | solution.py:743
  113.6 4.3 %project_back.2 = (f32[1024,384]{1,0:T(8,128)S(1)}, f32[384,384]{1,0:T(8,128)S(1)}) custom-call(bf16[1024,384]{1,0:T(8,128)(2,1)} %bitcast.35, f32[2048,128]{1,0:T(8,128)S(1)} %get-tuple-element.113.cosine, f32[2048,128]{1,0:T(8,128)S(1)} %get-tuple-element.114.sine, bf16[384,1152]{1,0:T(8,128)(2,1)S(1)} %get-tuple-element.127.w, ...), custom_call_target="tpu_custom_call" | custom-call | flops 4000000000 | bytes 8388608 | tf_op jit(solution)/shard_map/project_back/pallas_call | solution.py:1042
  120.8 2.5 %collective-permute-done.25.refs_1_ = bf16[4,336,128]{2,1,0:T(8,128)(2,1)S(1)} collective-permute-done((bf16[4,336,128]{2,1,0:T(8,128)(2,1)S(1)}, bf16[4,336,128]{2,1,0:T(8,128)(2,1)S(1)}, u32[]{:S(2)}, u32[]{:S(2)}) %collective-permute-start.25) | collective-permute-done | bytes 344096 | tf_op jit(solution)/shard_map/ppermute | solution.py:53
  124.2 3.8 %collective-permute-start.27 = (bf16[1,336,128]{2,1,0:T(8,128)(2,1)S(1)}, bf16[1,336,128]{2,1,0:T(8,128)(2,1)S(1)}, u32[]{:S(2)}, u32[]{:S(2)}) collective-permute-start(bf16[1,336,128]{2,1,0:T(8,128)(2,1)S(1)} %get-tuple-element.152), channel_id=1, source_target_pairs={{0,16},{2,18},{4,20},{6,22},{8,24},{10,26},{12,28},{14,30},{16,0},... | collective-permute-start | bytes 258056 | tf_op jit(solution)/shard_map/ppermute | solution.py:49
  128.4 6.3 %project_back.3 = (bf16[1024,384]{1,0:T(8,128)(2,1)}, f32[16,120,128]{2,1,0:T(8,128)S(1)}, bf16[16,120,128]{2,1,0:T(8,128)(2,1)S(1)}) custom-call(bf16[1024,384]{1,0:T(8,128)(2,1)} %bitcast.36, f32[2048,128]{1,0:T(8,128)S(1)} %get-tuple-element.113.cosine, f32[2048,128]{1,0:T(8,128)S(1)} %get-tuple-element.114.sine, ...), custom_call_target="tpu_custom_call" | custom-call | flops 4000000000 | bytes 8388608 | tf_op jit(solution)/shard_map/project_back/pallas_call | solution.py:1042
  142.7 2.4 %collective-permute-done.30.refs_1_ = bf16[4,120,128]{2,1,0:T(8,128)(2,1)S(1)} collective-permute-done((bf16[4,120,128]{2,1,0:T(8,128)(2,1)S(1)}, bf16[4,120,128]{2,1,0:T(8,128)(2,1)S(1)}, u32[]{:S(2)}, u32[]{:S(2)}) %collective-permute-start.30) | collective-permute-done | bytes 122912 | tf_op jit(solution)/shard_map/ppermute | solution.py:49
  145.1 3.1 %collective-permute-done.31.refs_2_ = bf16[4,120,128]{2,1,0:T(8,128)(2,1)S(1)} collective-permute-done((bf16[4,120,128]{2,1,0:T(8,128)(2,1)S(1)}, bf16[4,120,128]{2,1,0:T(8,128)(2,1)S(1)}, u32[]{:S(2)}, u32[]{:S(2)}) %collective-permute-start.31) | collective-permute-done | bytes 122912 | tf_op jit(solution)/shard_map/ppermute | solution.py:49
  150.4 2.1 %collective-permute-start.34 = (bf16[1,120,128]{2,1,0:T(8,128)(2,1)S(1)}, bf16[1,120,128]{2,1,0:T(8,128)(2,1)S(1)}, u32[]{:S(2)}, u32[]{:S(2)}) collective-permute-start(bf16[1,120,128]{2,1,0:T(8,128)(2,1)S(1)} %get-tuple-element.164), channel_id=1, source_target_pairs={{0,16},{2,18},{4,20},{6,22},{8,24},{10,26},{12,28},{14,30},{16,0},... | collective-permute-start | bytes 92168 | tf_op jit(solution)/shard_map/ppermute | solution.py:49
  153.3 2.5 %collective-permute-done.34.refs_2_ = bf16[1,120,128]{2,1,0:T(8,128)(2,1)S(1)} collective-permute-done((bf16[1,120,128]{2,1,0:T(8,128)(2,1)S(1)}, bf16[1,120,128]{2,1,0:T(8,128)(2,1)S(1)}, u32[]{:S(2)}, u32[]{:S(2)}) %collective-permute-start.34) | collective-permute-done | bytes 30752 | tf_op jit(solution)/shard_map/ppermute | solution.py:49
  155.8 2.4 %collective-permute-done.35.refs_3_ = bf16[1,120,128]{2,1,0:T(8,128)(2,1)S(1)} collective-permute-done((bf16[1,120,128]{2,1,0:T(8,128)(2,1)S(1)}, bf16[1,120,128]{2,1,0:T(8,128)(2,1)S(1)}, u32[]{:S(2)}, u32[]{:S(2)}) %collective-permute-start.35) | collective-permute-done | bytes 30752 | tf_op jit(solution)/shard_map/ppermute | solution.py:49
  160.3 9.9 %all_to_all.5 = f32[16,1,128]{2,1,0:T(1,128)S(1)} all-to-all(f32[16,1,128]{2,1,0:T(1,128)S(1)} %broadcast_in_dim.25), channel_id=1, replica_groups=mesh['batch'=16,'tm'=2] {'batch'}, dimensions={0} | all-to-all | bytes 16384 | tf_op jit(solution)/shard_map/all_to_all | solution.py:126
  170.2 1.9 %update.1 = (f32[1,1]{1,0:T(1,128)}, f32[24,1152]{1,0:T(8,128)}, f32[24,384]{1,0:T(8,128)}, f32[24,2048]{1,0:T(8,128)}, f32[64,384]{1,0:T(8,128)}, /*index=5*/f3...) custom-call(s32[2]{0:T(128)S(1)} %pad_add_fusion.where.refs_0_.refs_, ...), custom_call_target="tpu_custom_call" | custom-call | tf_op jit(solution)/shard_map/update/pallas_call | solution.py:1154
  (89 shorter events, 33.1 us)
Async XLA Ops:
  0.7 7.4 %collective-permute-start = (bf16[1024,384]{1,0:T(8,128)(2,1)}, bf16[1024,384]{1,0:T(8,128)(2,1)S(1)}, u32[]{:S(2)}, u32[]{:S(2)}) collective-permute-start(bf16[1024,384]{1,0:T(8,128)(2,1)} %bitcast.32), channel_id=1, source_target_pairs={{0,1},{1,0},{2,3},{3,2},{4,5},{5,4},{6,7},{7,6},{8,9},{9,8},{10,11... | collective-permute-start | bytes 2359304 | tf_op jit(solution)/shard_map/ppermute | solution.py:53
  2.8 10.2 %collective-permute-start.1 = (bf16[1,128,128]{2,1,0:T(8,128)(2,1)S(1)}, bf16[1,128,128]{2,1,0:T(8,128)(2,1)S(1)}, u32[]{:S(2)}, u32[]{:S(2)}) collective-permute-start(bf16[1,128,128]{2,1,0:T(8,128)(2,1)S(1)} %bitcast.26), channel_id=1, source_target_pairs={{0,8},{2,10},{4,12},{6,14},{8,0},{10,2},{12,4},{14,6},{16,24},{18,... | collective-permute-start | bytes 98312 | tf_op jit(solution)/shard_map/ppermute | solution.py:49
  5.5 7.6 %collective-permute-start.2 = (bf16[1,128,128]{2,1,0:T(8,128)(2,1)S(1)}, bf16[1,128,128]{2,1,0:T(8,128)(2,1)S(1)}, u32[]{:S(2)}, u32[]{:S(2)}) collective-permute-start(bf16[1,128,128]{2,1,0:T(8,128)(2,1)S(1)} %bitcast.27), channel_id=1, source_target_pairs={{0,16},{2,18},{4,20},{6,22},{8,24},{10,26},{12,28},{14,30},{16,0},... | collective-permute-start | bytes 98312 | tf_op jit(solution)/shard_map/ppermute | solution.py:49
  15.3 7.8 %collective-permute-start.5 = (bf16[4,128,128]{2,1,0:T(8,128)(2,1)S(1)}, bf16[4,128,128]{2,1,0:T(8,128)(2,1)S(1)}, u32[]{:S(2)}, u32[]{:S(2)}) collective-permute-start(bf16[4,128,128]{2,1,0:T(8,128)(2,1)S(1)} %join.2.refs_1_.refs_3_), channel_id=1, source_target_pairs={{0,4},{2,6},{4,0},{6,2},{8,12},{10,14},{12,8},{14,10},{16,20},{18,... | collective-permute-start | bytes 393224 | tf_op jit(solution)/shard_map/ppermute | solution.py:49
  17.3 8.3 %collective-permute-start.7 = (bf16[4,128,128]{2,1,0:T(8,128)(2,1)S(1)}, bf16[4,128,128]{2,1,0:T(8,128)(2,1)S(1)}, u32[]{:S(2)}, u32[]{:S(2)}) collective-permute-start(bf16[4,128,128]{2,1,0:T(8,128)(2,1)S(1)} %join.2.refs_1_.refs_3_), channel_id=1, source_target_pairs={{0,1},{1,0},{2,3},{3,2},{4,5},{5,4},{6,7},{7,6},{8,9},{9,8},{10,11... | collective-permute-start | bytes 393224 | tf_op jit(solution)/shard_map/ppermute | solution.py:53
  19.6 9.5 %collective-permute-start.8 = (bf16[4,128,128]{2,1,0:T(8,128)(2,1)S(1)}, bf16[4,128,128]{2,1,0:T(8,128)(2,1)S(1)}, u32[]{:S(2)}, u32[]{:S(2)}) collective-permute-start(bf16[4,128,128]{2,1,0:T(8,128)(2,1)S(1)} %collective-permute-done.4.refs_2_), channel_id=1, source_target_pairs={{0,1},{1,0},{2,3},{3,2},{4,5},{5,4},{6,7},{7,6},{8,9},{9,8},{10,11... | collective-permute-start | bytes 393224 | tf_op jit(solution)/shard_map/ppermute | solution.py:53
  23.1 6.8 %collective-permute-start.9 = (bf16[4,128,128]{2,1,0:T(8,128)(2,1)S(1)}, bf16[4,128,128]{2,1,0:T(8,128)(2,1)S(1)}, u32[]{:S(2)}, u32[]{:S(2)}) collective-permute-start(bf16[4,128,128]{2,1,0:T(8,128)(2,1)S(1)} %collective-permute-done.5.refs_3_), channel_id=1, source_target_pairs={{0,1},{1,0},{2,3},{3,2},{4,5},{5,4},{6,7},{7,6},{8,9},{9,8},{10,11... | collective-permute-start | bytes 393224 | tf_op jit(solution)/shard_map/ppermute | solution.py:53
  23.1 6.8 %collective-permute-start.10 = (bf16[4,128,128]{2,1,0:T(8,128)(2,1)S(1)}, bf16[4,128,128]{2,1,0:T(8,128)(2,1)S(1)}, u32[]{:S(2)}, u32[]{:S(2)}) collective-permute-start(bf16[4,128,128]{2,1,0:T(8,128)(2,1)S(1)} %collective-permute-done.6.refs_4_), channel_id=1, source_target_pairs={{0,1},{1,0},{2,3},{3,2},{4,5},{5,4},{6,7},{7,6},{8,9},{9,8},{10,11... | collective-permute-start | bytes 393224 | tf_op jit(solution)/shard_map/ppermute | solution.py:53
  25.4 16.6 %collective-permute-start.11 = (bf16[1,336,128]{2,1,0:T(8,128)(2,1)S(1)}, bf16[1,336,128]{2,1,0:T(8,128)(2,1)S(1)}, u32[]{:S(2)}, u32[]{:S(2)}) collective-permute-start(bf16[1,336,128]{2,1,0:T(8,128)(2,1)S(1)} %bitcast.22), channel_id=1, source_target_pairs={{0,8},{2,10},{4,12},{6,14},{8,0},{10,2},{12,4},{14,6},{16,24},{18,... | collective-permute-start | bytes 258056 | tf_op jit(solution)/shard_map/ppermute | solution.py:49
  25.7 16.4 %collective-permute-start.12 = (bf16[1,336,128]{2,1,0:T(8,128)(2,1)S(1)}, bf16[1,336,128]{2,1,0:T(8,128)(2,1)S(1)}, u32[]{:S(2)}, u32[]{:S(2)}) collective-permute-start(bf16[1,336,128]{2,1,0:T(8,128)(2,1)S(1)} %bitcast.23), channel_id=1, source_target_pairs={{0,16},{2,18},{4,20},{6,22},{8,24},{10,26},{12,28},{14,30},{16,0},... | collective-permute-start | bytes 258056 | tf_op jit(solution)/shard_map/ppermute | solution.py:49
  29.1 12.9 %collective-permute-start.13 = (bf16[1,336,128]{2,1,0:T(8,128)(2,1)S(1)}, bf16[1,336,128]{2,1,0:T(8,128)(2,1)S(1)}, u32[]{:S(2)}, u32[]{:S(2)}) collective-permute-start(bf16[1,336,128]{2,1,0:T(8,128)(2,1)S(1)} %bitcast.24), channel_id=1, source_target_pairs={{0,24},{2,26},{4,28},{6,30},{8,16},{10,18},{12,20},{14,22},{16,8},... | collective-permute-start | bytes 258056 | tf_op jit(solution)/shard_map/ppermute | solution.py:49
  42.1 21.0 %collective-permute-start.14 = (bf16[4,336,128]{2,1,0:T(8,128)(2,1)S(1)}, bf16[4,336,128]{2,1,0:T(8,128)(2,1)S(1)}, u32[]{:S(2)}, u32[]{:S(2)}) collective-permute-start(bf16[4,336,128]{2,1,0:T(8,128)(2,1)S(1)} %join.3.refs_0_.refs_1_), channel_id=1, source_target_pairs={{0,2},{2,0},{4,6},{6,4},{8,10},{10,8},{12,14},{14,12},{16,18},{18,... | collective-permute-start | bytes 1032200 | tf_op jit(solution)/shard_map/ppermute | solution.py:49
  42.3 20.8 %collective-permute-start.15 = (bf16[4,336,128]{2,1,0:T(8,128)(2,1)S(1)}, bf16[4,336,128]{2,1,0:T(8,128)(2,1)S(1)}, u32[]{:S(2)}, u32[]{:S(2)}) collective-permute-start(bf16[4,336,128]{2,1,0:T(8,128)(2,1)S(1)} %join.3.refs_0_.refs_1_), channel_id=1, source_target_pairs={{0,4},{2,6},{4,0},{6,2},{8,12},{10,14},{12,8},{14,10},{16,20},{18,... | collective-permute-start | bytes 1032200 | tf_op jit(solution)/shard_map/ppermute | solution.py:49
  43.6 19.5 %collective-permute-start.16 = (bf16[4,336,128]{2,1,0:T(8,128)(2,1)S(1)}, bf16[4,336,128]{2,1,0:T(8,128)(2,1)S(1)}, u32[]{:S(2)}, u32[]{:S(2)}) collective-permute-start(bf16[4,336,128]{2,1,0:T(8,128)(2,1)S(1)} %join.3.refs_0_.refs_1_), channel_id=1, source_target_pairs={{0,6},{2,4},{4,2},{6,0},{8,14},{10,12},{12,10},{14,8},{16,22},{18,... | collective-permute-start | bytes 1032200 | tf_op jit(solution)/shard_map/ppermute | solution.py:49
  45.6 18.5 %collective-permute-start.17 = (bf16[4,336,128]{2,1,0:T(8,128)(2,1)S(1)}, bf16[4,336,128]{2,1,0:T(8,128)(2,1)S(1)}, u32[]{:S(2)}, u32[]{:S(2)}) collective-permute-start(bf16[4,336,128]{2,1,0:T(8,128)(2,1)S(1)} %join.3.refs_0_.refs_1_), channel_id=1, source_target_pairs={{0,1},{1,0},{2,3},{3,2},{4,5},{5,4},{6,7},{7,6},{8,9},{9,8},{10,11... | collective-permute-start | bytes 1032200 | tf_op jit(solution)/shard_map/ppermute | solution.py:53
  86.4 31.6 %collective-permute-start.21 = (bf16[8,336,128]{2,1,0:T(8,128)(2,1)S(1)}, bf16[8,336,128]{2,1,0:T(8,128)(2,1)S(1)}, u32[]{:S(2)}, u32[]{:S(2)}) collective-permute-start(bf16[8,336,128]{2,1,0:T(8,128)(2,1)S(1)} %get-tuple-element.134), channel_id=1, source_target_pairs={{0,2},{2,0},{4,6},{6,4},{8,10},{10,8},{12,14},{14,12},{16,18},{18,... | collective-permute-start | bytes 2064392 | tf_op jit(solution)/shard_map/ppermute | solution.py:49
  86.6 31.4 %collective-permute-start.22 = (bf16[8,336,128]{2,1,0:T(8,128)(2,1)S(1)}, bf16[8,336,128]{2,1,0:T(8,128)(2,1)S(1)}, u32[]{:S(2)}, u32[]{:S(2)}) collective-permute-start(bf16[8,336,128]{2,1,0:T(8,128)(2,1)S(1)} %get-tuple-element.135), channel_id=1, source_target_pairs={{0,4},{2,6},{4,0},{6,2},{8,12},{10,14},{12,8},{14,10},{16,20},{18,... | collective-permute-start | bytes 2064392 | tf_op jit(solution)/shard_map/ppermute | solution.py:49
  87.9 31.5 %collective-permute-start.23 = (bf16[8,336,128]{2,1,0:T(8,128)(2,1)S(1)}, bf16[8,336,128]{2,1,0:T(8,128)(2,1)S(1)}, u32[]{:S(2)}, u32[]{:S(2)}) collective-permute-start(bf16[8,336,128]{2,1,0:T(8,128)(2,1)S(1)} %get-tuple-element.136), channel_id=1, source_target_pairs={{0,6},{2,4},{4,2},{6,0},{8,14},{10,12},{12,10},{14,8},{16,22},{18,... | collective-permute-start | bytes 2064392 | tf_op jit(solution)/shard_map/ppermute | solution.py:49
  119.4 9.0 %collective-permute-start.24 = (bf16[6,1024,128]{2,1,0:T(8,128)(2,1)S(1)}, bf16[6,1024,128]{2,1,0:T(8,128)(2,1)S(1)}, u32[]{:S(2)}, u32[]{:S(2)}) collective-permute-start(bf16[6,1024,128]{2,1,0:T(8,128)(2,1)S(1)} %hold.7), channel_id=1, source_target_pairs={{0,1},{1,0},{2,3},{3,2},{4,5},{5,4},{6,7},{7,6},{8,9},{9,8},{10,11... | collective-permute-start | bytes 4718600 | tf_op jit(solution)/shard_map/ppermute | solution.py:53
  123.9 10.8 %collective-permute-start.26 = (bf16[1,336,128]{2,1,0:T(8,128)(2,1)S(1)}, bf16[1,336,128]{2,1,0:T(8,128)(2,1)S(1)}, u32[]{:S(2)}, u32[]{:S(2)}) collective-permute-start(bf16[1,336,128]{2,1,0:T(8,128)(2,1)S(1)} %get-tuple-element.151), channel_id=1, source_target_pairs={{0,8},{2,10},{4,12},{6,14},{8,0},{10,2},{12,4},{14,6},{16,24},{18,... | collective-permute-start | bytes 258056 | tf_op jit(solution)/shard_map/ppermute | solution.py:49
  124.2 10.7 %collective-permute-start.27 = (bf16[1,336,128]{2,1,0:T(8,128)(2,1)S(1)}, bf16[1,336,128]{2,1,0:T(8,128)(2,1)S(1)}, u32[]{:S(2)}, u32[]{:S(2)}) collective-permute-start(bf16[1,336,128]{2,1,0:T(8,128)(2,1)S(1)} %get-tuple-element.152), channel_id=1, source_target_pairs={{0,16},{2,18},{4,20},{6,22},{8,24},{10,26},{12,28},{14,30},{16,0},... | collective-permute-start | bytes 258056 | tf_op jit(solution)/shard_map/ppermute | solution.py:49
  127.9 6.9 %collective-permute-start.28 = (bf16[1,336,128]{2,1,0:T(8,128)(2,1)S(1)}, bf16[1,336,128]{2,1,0:T(8,128)(2,1)S(1)}, u32[]{:S(2)}, u32[]{:S(2)}) collective-permute-start(bf16[1,336,128]{2,1,0:T(8,128)(2,1)S(1)} %get-tuple-element.153), channel_id=1, source_target_pairs={{0,24},{2,26},{4,28},{6,30},{8,16},{10,18},{12,20},{14,22},{16,8},... | collective-permute-start | bytes 258056 | tf_op jit(solution)/shard_map/ppermute | solution.py:49
  140.4 7.8 %collective-permute-start.31 = (bf16[4,120,128]{2,1,0:T(8,128)(2,1)S(1)}, bf16[4,120,128]{2,1,0:T(8,128)(2,1)S(1)}, u32[]{:S(2)}, u32[]{:S(2)}) collective-permute-start(bf16[4,120,128]{2,1,0:T(8,128)(2,1)S(1)} %get-tuple-element.160), channel_id=1, source_target_pairs={{0,4},{2,6},{4,0},{6,2},{8,12},{10,14},{12,8},{14,10},{16,20},{18,... | collective-permute-start | bytes 368648 | tf_op jit(solution)/shard_map/ppermute | solution.py:49
  142.7 16.2 %collective-permute-start.37 = (f32[336,128]{1,0:T(8,128)S(1)}, f32[336,128]{1,0:T(8,128)S(1)}, u32[]{:S(2)}, u32[]{:S(2)}) collective-permute-start(f32[336,128]{1,0:T(8,128)S(1)} %bitcast.15), channel_id=1, source_target_pairs={{0,1},{1,0},{2,3},{3,2},{4,5},{5,4},{6,7},{7,6},{8,9},{9,8},{10,11... | collective-permute-start | bytes 516104 | tf_op jit(solution)/shard_map/ppermute | solution.py:53
  (18 other events, 61.2 us)

commit v7 on v6

--- a/solution.py
+++ b/solution.py
@@ -68,7 +68,8 @@
 BLOCK = 256
 LANES = 128
 KEEP_LANE = 96
-LIMITS = (12, 12, 12, 34, 12, 12, 12)
+LIMITS = (12, 20, 12, 38, 12, 20, 12)
+WIDE = 512
 NN = (((1,), (0,)), ((), ()))
 NT = (((1,), (1,)), ((), ()))
 TN = (((0,), (0,)), ((), ()))
@@ -357,8 +358,10 @@
                 device = owner ^ flip ^ (relative_flips(n, count) << last)
                 chunk = source[n].astype(f32)
                 for i in range(number):
-                    rows = pl.ds(pl.multiple_of(device * shard, 8), shard)
-                    stage[half * number + i, rows, :] = chunk[i * shard : (i + 1) * shard]
+                    start = (half * number + i) * D + device * shard
+                    stage[pl.ds(pl.multiple_of(start, 8), shard), :] = chunk[
+                        i * shard : (i + 1) * shard
+                    ]
                 for i in range(3 if down else 0):
                     start = number * shard + i * down
                     rows = pl.ds(pl.multiple_of((device * 2 + half) * down, 16), down)
@@ -413,14 +416,6 @@
     half, row = at // number, (at % number) * shard
     slot = core if half == 0 else 1 - core
     stage[slot, :, row : row + shard, :] = slab.reshape(-1, shard, LANES)
-
-
-def put_down(stage, core, number, shard, down, column, slab, first):
-    parts = slab.reshape(-1, 2, down, LANES)
-    row = number * shard + column * down
-    devices = slice(first, first + parts.shape[0])
-    stage[core, devices, row : row + down, :] = parts[:, 0]
-    stage[1 - core, devices, row : row + down, :] = parts[:, 1]
 
 
 def gain_column(row):
@@ -523,29 +518,27 @@
 def project_kernel(fused, own, there, cosine, sine, key_aux, query_aux, *refs):
     if fused:
         pieces = 1 << bit_groups(fused[0])[0][1]
-        where, scratch = refs[0], refs[-2 * pieces - 3 : -1]
-        qa, ka, va, kt, vt, w, gains, stage = refs[-2 * pieces - 11 : -2 * pieces - 3]
-        copies = fetch((*refs[1 : 1 + 2 * pieces], own, there), scratch, refs[-1])
-        mine, other, (own, there) = (
-            scratch[:pieces], scratch[pieces : 2 * pieces], scratch[2 * pieces :]
-        )
-        arrive(copies)
+        where, mine, other = refs[0], refs[1 : 1 + pieces], refs[1 + pieces : 1 + 2 * pieces]
+        qa, ka, va, kt, vt, w, gains, stage = refs[-11:-3]
+        copies = fetch((own, there), refs[-3:-1], refs[-1])
+        own, there = refs[-3:-1]
         unpack(*fused, where, mine, other, stage, None)
         for i in range(9):
-            w[:, i * LANES : (i + 1) * LANES] = stage[i].astype(bf16)
-        gains[...] = stage[9].T[:8]
+            w[:, i * LANES : (i + 1) * LANES] = stage[i * D : (i + 1) * D].astype(bf16)
+        gains[...] = stage[9 * D : 10 * D].T[:8]
+        arrive(copies)
     else:
         w_in, gains_in, (qa, ka, va, kt, vt, w, gains) = *refs[:2], refs[-7:]
         w[...] = w_in[...]
         gains[...] = gains_in[...]
-    low = lax.broadcasted_iota(jnp.int32, (BLOCK, LANES), 1) < HD
-    lane = lax.broadcasted_iota(jnp.int32, (BLOCK, LANES), 1)
+    low = lax.broadcasted_iota(jnp.int32, (WIDE, LANES), 1) < HD
+    lane = lax.broadcasted_iota(jnp.int32, (WIDE, LANES), 1)
     value_extra = jnp.where((lane >= HD) & (lane < HD + 3), 1.0, 0.0)
-    ones = jnp.ones((8, BLOCK), bf16)
-    blocks = own.shape[0] // BLOCK
+    ones = jnp.ones((8, WIDE), bf16)
+    blocks = own.shape[0] // WIDE
 
     def body(step, carry, source, base):
-        rows, keys = block(step), block(base + step)
+        rows, keys = block(step, WIDE), block(base + step, WIDE)
         x = source[rows, :].astype(f32)
         normed = (x * row_scale(x) * gains[0:1, :]).astype(bf16)
         cos, sin = cosine[keys, :], sine[keys, :]
@@ -598,8 +591,8 @@
     weight_specs = [VMEM] * 2
     if fused:
         specs = [HBM, ANY] + [VMEM] * 4
-        weight_specs = [SMEM] + [ANY] * (len(weights) - 1)
-        scratch = [pltpu.VMEM((10, D, LANES), f32)] + landing([*weights[1:], own, there])
+        weight_specs = [SMEM] + [VMEM] * (len(weights) - 1)
+        scratch = [pltpu.VMEM((10 * D, LANES), f32)] + landing([own, there])
     if fused:
         (own,) = in_hbm([own])
     return pl.pallas_call(
@@ -756,7 +749,7 @@
     )(ranges, qb, ka, da, va, kt, *waits)
 
 
-FEED = 512
+FEED = 1024
 
 
 def feed_kernel(fused, own, mixed, exact, cotangent, query_aux, gains, *refs):
@@ -765,15 +758,11 @@
         where, mine, other = refs[0], refs[1 : 1 + pieces], refs[1 + pieces : 1 + 2 * pieces]
         refs = refs[1 + 2 * pieces :]
         result, grad_middle, da, gives = *refs[:3], refs[3 : 3 + fan]
-        normed_all, low_all, hidden_all, up_all, middle_all, wo, wgu, wd, stage, g_gain, sums = (
-            refs[3 + fan : 14 + fan]
-        )
-        scratch = refs[14 + fan : -1]
-        copies = fetch((*mine, *other, own, cotangent), scratch, refs[-1])
-        mine, other, (own, cotangent) = (
-            scratch[:pieces], scratch[pieces : 2 * pieces], scratch[2 * pieces :]
-        )
-        arrive(copies)
+        normed_all, low_all, hidden_all, up_all, middle_all, wo, wgu, wd, g_gain, sums = refs[
+            3 + fan : 13 + fan
+        ]
+        copies = fetch((own, cotangent), refs[13 + fan : 15 + fan], refs[-1])
+        own, cotangent = refs[13 + fan : 15 + fan]
     else:
         wo, wgu, wd = refs[:3]
         result, grad_middle, da, g_out, g_gate_up, g_down, g_gain = refs[3:10]
@@ -781,11 +770,12 @@
     gain = gains[1:2, :]
     g_gain[...] = jnp.zeros_like(g_gain)
     if fused:
-        unpack(*fused, where, mine, other, stage, wd)
+        unpack(*fused, where, mine, other, sums, wd)
         for i in range(3):
-            wo[:, i * LANES : (i + 1) * LANES] = stage[i].astype(bf16)
+            wo[:, i * LANES : (i + 1) * LANES] = sums[i * D : (i + 1) * D].astype(bf16)
         for i in range(16):
-            wgu[:, i * LANES : (i + 1) * LANES] = stage[3 + i].astype(bf16)
+            wgu[:, i * LANES : (i + 1) * LANES] = sums[(3 + i) * D : (4 + i) * D].astype(bf16)
+        arrive(copies)
 
     chunks = FF // BLOCK
     lane = lax.broadcasted_iota(jnp.int32, (FEED, LANES), 1)
@@ -858,9 +848,16 @@
         return
     count, number, shard, down = fused
 
+    size = number * shard + 3 * down
+
     def put(at, value):
         for i in range(value.shape[1] // LANES):
-            put_slab(sums, 0, number, shard, at + i, value[:, i * LANES : (i + 1) * LANES])
+            half, row = divmod(at + i, number)
+            for device in range(count):
+                start = (half * count + device) * size + row * shard
+                sums[start : start + shard, :] = value[
+                    device * shard : (device + 1) * shard, i * LANES : (i + 1) * LANES
+                ]
 
     put(0, dot(mixed[...], middle_all[...], TN))
     for c in range(2 * FF // 512):
@@ -868,17 +865,20 @@
     put(19, gain_column(g_gain[...]))
     for c in range(chunks):
         value = dot(hidden_all[:, c * BLOCK : (c + 1) * BLOCK], up_all[...], TN)
-        for i in range(3):
-            put_down(
-                sums, 0, number, shard, down, i,
-                value[:, i * LANES : (i + 1) * LANES], c * BLOCK // (2 * down),
-            )
+        for n in range(BLOCK // down):
+            device, half = divmod(c * BLOCK // down + n, 2)
+            for i in range(3):
+                start = (half * count + device) * size + number * shard + i * down
+                sums[start : start + down, :] = value[
+                    n * down : (n + 1) * down, i * LANES : (i + 1) * LANES
+                ]
     me = where[1] & (fan - 1)
     for high in range(count // fan):
         for flip in range(fan):
             for half in range(2):
+                start = (half * count + high * fan + (me ^ flip)) * size
                 gives[flip][half * (count // fan) + high] = sums[
-                    half, high * fan + (me ^ flip)
+                    pl.ds(pl.multiple_of(start, 8), size), :
                 ].astype(gives[flip].dtype)
 
 
@@ -900,7 +900,7 @@
         count, number, shard, down = fused
         rows = number * shard + 3 * down
         fan = 1 << bit_groups(count)[0][1]
-        weight_specs = [SMEM] + [ANY] * (len(weights) - 1)
+        weight_specs = [SMEM] + [VMEM] * (len(weights) - 1)
         specs = [HBM, VMEM, VMEM, HBM, VMEM, VMEM]
         out_shape += [
             jax.ShapeDtypeStruct((2 * count // fan, rows, LANES), bf16 if flip else f32)
@@ -910,11 +910,10 @@
             pltpu.VMEM((D, D), bf16),
             pltpu.VMEM((D, 2 * FF), bf16),
             pltpu.VMEM((FF, D), bf16),
-            pltpu.VMEM((2 * number, D, LANES), f32),
             pltpu.VMEM((8, D), f32),
-            pltpu.VMEM((2, count, rows, LANES), f32),
+            pltpu.VMEM((2 * count * rows, LANES), f32),
         ]
-        scratch += landing([*weights[1:], own, cotangent])
+        scratch += landing([own, cotangent])
     else:
         weight_specs = [VMEM] * 3
         specs = [VMEM] * 6
@@ -943,7 +942,7 @@
 
 def project_back_kernel(number, fused, own, cosine, sine, w, gains, *refs):
     part = PARTS[number]
-    low = lax.broadcasted_iota(jnp.int32, (BLOCK, LANES), 1) < HD
+    low = lax.broadcasted_iota(jnp.int32, (WIDE, LANES), 1) < HD
     gain = gains[0:1, :]
     if number == 0:
         dq = refs[0]
@@ -963,7 +962,7 @@
     arrive(copies)
 
     def body(step, carry):
-        rows = block(step)
+        rows = block(step, WIDE)
         cos, sin = cosine[rows, :], -sine[rows, :]
         x = own[rows, :].astype(f32)
         scale = row_scale(x)
@@ -996,7 +995,7 @@
             ).astype(bf16)
         return carry
 
-    lax.fori_loop(0, own.shape[0] // BLOCK, body, 0)
+    lax.fori_loop(0, own.shape[0] // WIDE, body, 0)
     value = dot(normed_all[...], low_all[...], TN)
     if number == 0 or not fused:
         grads[...] = value
@@ -1288,7 +1287,7 @@
         1, fused, where, shared, [kept, part_there, grad_middle, before, grads_before], [parts[0]]
     )
     if split:
-        parts = [scatter_parts(where, parts, count, groups[1:], [grad_tokens])]
+        parts = [scatter_parts(where, parts, count, groups[1:], [grads[1]])]
     second_sum = parts[0].reshape(-1, LANES)
     if fused:
         kept, given = grads

time: 173 us -> 163 us (0.942)
  Pallas kernels: 98.2 us -> 88.3 us
    pallas_call x1, Pallas kernels: 20.4 us -> 15.7 us  [feed(): pl.pallas_call(partial(feed_kernel, fused), out_shape=out_shape, in_specs...]
    pallas_call x1, Pallas kernels: 12.1 us -> 7.88 us  [project(): pl.pallas_call(partial(project_kernel, fused), out_shape=[in_vmem((HEADS,...]
    unnamed x8 -> x10, local copies, waits for them, and re-layouts: 3.22 us -> 3.5 us
where the time goes in v7:
time: 163 us; the launch traced here: 162 us
  Pallas kernels  88.3 us (54%)
  starting transfers between devices  35.7 us (22%)
  waiting for transfers between devices  23.1 us (14%)
  blocking collectives  10.3 us (6%)
  local copies, waits for them, and re-layouts  3.51 us (2%)
    ppermute x24, starting transfers between devices, permute_batch(): return lax.ppermute(value, 'batch', [(i, i ^ flip) for i in range(count)])  32.8 us
    pallas_call x1, Pallas kernels, attend_back(): pl.pallas_call(attend_back_kernel, out_shape=[in_vmem((heads, HD, length)...  23.9 us
    pallas_call x1, Pallas kernels, attend(): pl.pallas_call(attend_kernel, out_shape=[in_vmem((length, D), bf16), in_v...  17.6 us
    ppermute x24, waiting for transfers between devices, permute_batch(): return lax.ppermute(value, 'batch', [(i, i ^ flip) for i in range(count)])  17.4 us
    pallas_call x1, Pallas kernels, feed(): pl.pallas_call(partial(feed_kernel, fused), out_shape=out_shape, in_specs...  15.7 us
    all_to_all x1, blocking collectives, sum_batch(): value = lax.all_to_all(value, 'batch', 0, 0, tiled=True)  10.3 us
    pallas_call x2, Pallas kernels, project_back(): pl.pallas_call(partial(project_back_kernel, number, fused), out_shape=out...  9.61 us
    pallas_call x1, Pallas kernels, project(): pl.pallas_call(partial(project_kernel, fused), out_shape=[in_vmem((HEADS,...  7.88 us
  transfers between devices with their start and end apart: 38, of which 15 were waited for; matrix products, arithmetic and copies ran while one was open for 0% of the time, Pallas kernels for 43%

profile of v7, /device:TPU:0, one launch (start us, length us, event | category | flops | bytes accessed | tf_op | source)
XLA Modules:
  0.0 162.1 jit_solution(9653462262775382261)
XLA Ops:
  2.8 2.7 %collective-permute-start.1 = (bf16[1,128,128]{2,1,0:T(8,128)(2,1)S(1)}, bf16[1,128,128]{2,1,0:T(8,128)(2,1)S(1)}, u32[]{:S(2)}, u32[]{:S(2)}) collective-permute-start(bf16[1,128,128]{2,1,0:T(8,128)(2,1)S(1)} %bitcast.25), channel_id=1, source_target_pairs={{0,8},{2,10},{4,12},{6,14},{8,0},{10,2},{12,4},{14,6},{16,24},{18,... | collective-permute-start | bytes 98312 | tf_op jit(solution)/shard_map/ppermute | solution.py:49
  5.5 2.6 %collective-permute-start.2 = (bf16[1,128,128]{2,1,0:T(8,128)(2,1)S(1)}, bf16[1,128,128]{2,1,0:T(8,128)(2,1)S(1)}, u32[]{:S(2)}, u32[]{:S(2)}) collective-permute-start(bf16[1,128,128]{2,1,0:T(8,128)(2,1)S(1)} %bitcast.26), channel_id=1, source_target_pairs={{0,16},{2,18},{4,20},{6,22},{8,24},{10,26},{12,28},{14,30},{16,0},... | collective-permute-start | bytes 98312 | tf_op jit(solution)/shard_map/ppermute | solution.py:49
  10.1 2.8 %tables.1 = (f32[2048,128]{1,0:T(8,128)S(1)}, f32[2048,128]{1,0:T(8,128)S(1)}, bf16[2048,128]{1,0:T(8,128)(2,1)S(1)}, bf16[1024,128]{1,0:T(8,128)(2,1)S(1)}, s32[4,4]{1,0:T(4,128)S(1)}) custom-call(s32[2]{0:T(128)S(1)} %pad_add_fusion.where.refs_0_.refs_5_, s32[1,2048]{1,0:T(1,128)S(1)} %copy-done, s32[1,2048]{1,0:T(1,128)S(1)} %copy-done.1, ...), custom_call_target="tpu_custom_call" | custom-call | flops 3000000000 | bytes 4194304 | tf_op jit(solution)/shard_map/tables/pallas_call | solution.py:501
  17.3 2.3 %collective-permute-done.4.refs_2_ = bf16[4,128,128]{2,1,0:T(8,128)(2,1)S(1)} collective-permute-done((bf16[4,128,128]{2,1,0:T(8,128)(2,1)S(1)}, bf16[4,128,128]{2,1,0:T(8,128)(2,1)S(1)}, u32[]{:S(2)}, u32[]{:S(2)}) %collective-permute-start.4) | collective-permute-done | bytes 131104 | tf_op jit(solution)/shard_map/ppermute | solution.py:49
  19.6 3.5 %collective-permute-done.5.refs_3_ = bf16[4,128,128]{2,1,0:T(8,128)(2,1)S(1)} collective-permute-done((bf16[4,128,128]{2,1,0:T(8,128)(2,1)S(1)}, bf16[4,128,128]{2,1,0:T(8,128)(2,1)S(1)}, u32[]{:S(2)}, u32[]{:S(2)}) %collective-permute-start.5) | collective-permute-done | bytes 131104 | tf_op jit(solution)/shard_map/ppermute | solution.py:49
  23.6 1.6 send_chunk.3
  25.5 3.5 %collective-permute-start.12 = (bf16[1,336,128]{2,1,0:T(8,128)(2,1)S(1)}, bf16[1,336,128]{2,1,0:T(8,128)(2,1)S(1)}, u32[]{:S(2)}, u32[]{:S(2)}) collective-permute-start(bf16[1,336,128]{2,1,0:T(8,128)(2,1)S(1)} %bitcast.22), channel_id=1, source_target_pairs={{0,16},{2,18},{4,20},{6,22},{8,24},{10,26},{12,28},{14,30},{16,0},... | collective-permute-start | bytes 258056 | tf_op jit(solution)/shard_map/ppermute | solution.py:49
  29.7 7.9 %project.1 = (bf16[6,1024,128]{2,1,0:T(8,128)(2,1)S(1)}, bf16[6,2048,128]{2,1,0:T(8,128)(2,1)S(1)}, bf16[6,2048,128]{2,1,0:T(8,128)(2,1)S(1)}, bf16[6,64,2048]{2...) custom-call(bf16[1024,384]{1,0:T(8,128)(2,1)} %bitcast.32, ...), custom_call_target="tpu_custom_call" | custom-call | flops 8999999488 | bytes 16777216 | tf_op jit(solution)/shard_map/project/pallas_call | solution.py:598
  39.2 2.1 %collective-permute-start.16 = (bf16[4,336,128]{2,1,0:T(8,128)(2,1)S(1)}, bf16[4,336,128]{2,1,0:T(8,128)(2,1)S(1)}, u32[]{:S(2)}, u32[]{:S(2)}) collective-permute-start(bf16[4,336,128]{2,1,0:T(8,128)(2,1)S(1)} %join.3.refs_0_.refs_1_), channel_id=1, source_target_pairs={{0,6},{2,4},{4,2},{6,0},{8,14},{10,12},{12,10},{14,8},{16,22},{18,... | collective-permute-start | bytes 1032200 | tf_op jit(solution)/shard_map/ppermute | solution.py:49
  41.2 17.6 %attend.1 = (bf16[1024,384]{1,0:T(8,128)(2,1)S(1)}, f32[1024,384]{1,0:T(8,128)S(1)}, bf16[6,1024,128]{2,1,0:T(8,128)(2,1)S(1)}) custom-call(s32[4,4]{1,0:T(4,128)S(1)} %get-tuple-element.112.ranges, bf16[6,1024,128]{2,1,0:T(8,128)(2,1)S(1)} %get-tuple-element.117.qa, bf16[6,2048,128]{2,1,0:T(8,128)(2,1)S(1)} %get-tuple-element.118.ka, ...), custom_call_target="tpu_custom_call" | custom-call | flops 17999998976 | bytes 12582912 | tf_op jit(solution)/shard_map/attend/pallas_call | solution.py:674
  61.7 15.7 %feed.1 = (bf16[1024,384]{1,0:T(8,128)(2,1)}, f32[1024,384]{1,0:T(8,128)S(1)}, bf16[6,1024,128]{2,1,0:T(8,128)(2,1)S(1)}, f32[8,336,128]{2,1,0:T(8,128)S(1)}, bf...) custom-call(bf16[1024,384]{1,0:T(8,128)(2,1)} %bitcast.33, ...), custom_call_target="tpu_custom_call" | custom-call | flops 14000000000 | bytes 16777216 | tf_op jit(solution)/shard_map/feed/pallas_call | solution.py:928
  79.0 2.0 %collective-permute-start.23 = (bf16[8,336,128]{2,1,0:T(8,128)(2,1)S(1)}, bf16[8,336,128]{2,1,0:T(8,128)(2,1)S(1)}, u32[]{:S(2)}, u32[]{:S(2)}) collective-permute-start(bf16[8,336,128]{2,1,0:T(8,128)(2,1)S(1)} %get-tuple-element.136), channel_id=1, source_target_pairs={{0,6},{2,4},{4,2},{6,0},{8,14},{10,12},{12,10},{14,8},{16,22},{18,... | collective-permute-start | bytes 2064392 | tf_op jit(solution)/shard_map/ppermute | solution.py:49
  82.4 23.9 %attend_back.1 = (f32[6,64,1024]{2,1,0:T(8,128)S(1)}, f32[6,2048,128]{2,1,0:T(8,128)S(1)}, bf16[6,1024,128]{2,1,0:T(8,128)(2,1)S(1)}) custom-call(s32[4,4]{1,0:T(4,128)S(1)} %get-tuple-element.112.ranges, bf16[6,1024,128]{2,1,0:T(8,128)(2,1)S(1)} %copy-done.4, bf16[6,2048,128]{2,1,0:T(8,128)(2,1)S(1)} %get-tuple-element.118.ka, ...), custom_call_target="tpu_custom_call" | custom-call | flops 33999998976 | bytes 8388608 | tf_op jit(solution)/shard_map/attend_back/pallas_call | solution.py:736
  106.2 3.8 %project_back.2 = (f32[1024,384]{1,0:T(8,128)S(1)}, f32[384,384]{1,0:T(8,128)S(1)}) custom-call(bf16[1024,384]{1,0:T(8,128)(2,1)} %bitcast.34, f32[2048,128]{1,0:T(8,128)S(1)} %get-tuple-element.113.cosine, f32[2048,128]{1,0:T(8,128)S(1)} %get-tuple-element.114.sine, bf16[384,1152]{1,0:T(8,128)(2,1)S(1)} %get-tuple-element.127.w, ...), custom_call_target="tpu_custom_call" | custom-call | flops 4000000000 | bytes 8388608 | tf_op jit(solution)/shard_map/project_back/pallas_call | solution.py:1041
  111.8 2.5 %collective-permute-done.25.refs_1_ = bf16[4,336,128]{2,1,0:T(8,128)(2,1)S(1)} collective-permute-done((bf16[4,336,128]{2,1,0:T(8,128)(2,1)S(1)}, bf16[4,336,128]{2,1,0:T(8,128)(2,1)S(1)}, u32[]{:S(2)}, u32[]{:S(2)}) %collective-permute-start.25) | collective-permute-done | bytes 344096 | tf_op jit(solution)/shard_map/ppermute | solution.py:53
  115.2 3.8 %collective-permute-start.27 = (bf16[1,336,128]{2,1,0:T(8,128)(2,1)S(1)}, bf16[1,336,128]{2,1,0:T(8,128)(2,1)S(1)}, u32[]{:S(2)}, u32[]{:S(2)}) collective-permute-start(bf16[1,336,128]{2,1,0:T(8,128)(2,1)S(1)} %get-tuple-element.152), channel_id=1, source_target_pairs={{0,16},{2,18},{4,20},{6,22},{8,24},{10,26},{12,28},{14,30},{16,0},... | collective-permute-start | bytes 258056 | tf_op jit(solution)/shard_map/ppermute | solution.py:49
  119.4 5.8 %project_back.3 = (bf16[1024,384]{1,0:T(8,128)(2,1)}, f32[16,120,128]{2,1,0:T(8,128)S(1)}, bf16[16,120,128]{2,1,0:T(8,128)(2,1)S(1)}) custom-call(bf16[1024,384]{1,0:T(8,128)(2,1)} %bitcast.35, f32[2048,128]{1,0:T(8,128)S(1)} %get-tuple-element.113.cosine, f32[2048,128]{1,0:T(8,128)S(1)} %get-tuple-element.114.sine, ...), custom_call_target="tpu_custom_call" | custom-call | flops 4000000000 | bytes 8388608 | tf_op jit(solution)/shard_map/project_back/pallas_call | solution.py:1041
  132.6 2.6 %collective-permute-done.30.refs_1_ = bf16[4,120,128]{2,1,0:T(8,128)(2,1)S(1)} collective-permute-done((bf16[4,120,128]{2,1,0:T(8,128)(2,1)S(1)}, bf16[4,120,128]{2,1,0:T(8,128)(2,1)S(1)}, u32[]{:S(2)}, u32[]{:S(2)}) %collective-permute-start.30) | collective-permute-done | bytes 122912 | tf_op jit(solution)/shard_map/ppermute | solution.py:49
  135.2 2.8 %collective-permute-done.31.refs_2_ = bf16[4,120,128]{2,1,0:T(8,128)(2,1)S(1)} collective-permute-done((bf16[4,120,128]{2,1,0:T(8,128)(2,1)S(1)}, bf16[4,120,128]{2,1,0:T(8,128)(2,1)S(1)}, u32[]{:S(2)}, u32[]{:S(2)}) %collective-permute-start.31) | collective-permute-done | bytes 122912 | tf_op jit(solution)/shard_map/ppermute | solution.py:49
  138.6 1.7 %collective-permute-start.33 = (bf16[1,120,128]{2,1,0:T(8,128)(2,1)S(1)}, bf16[1,120,128]{2,1,0:T(8,128)(2,1)S(1)}, u32[]{:S(2)}, u32[]{:S(2)}) collective-permute-start(bf16[1,120,128]{2,1,0:T(8,128)(2,1)S(1)} %get-tuple-element.163), channel_id=1, source_target_pairs={{0,8},{2,10},{4,12},{6,14},{8,0},{10,2},{12,4},{14,6},{16,24},{18,... | collective-permute-start | bytes 92168 | tf_op jit(solution)/shard_map/ppermute | solution.py:49
  143.0 2.5 %collective-permute-done.34.refs_2_ = bf16[1,120,128]{2,1,0:T(8,128)(2,1)S(1)} collective-permute-done((bf16[1,120,128]{2,1,0:T(8,128)(2,1)S(1)}, bf16[1,120,128]{2,1,0:T(8,128)(2,1)S(1)}, u32[]{:S(2)}, u32[]{:S(2)}) %collective-permute-start.34) | collective-permute-done | bytes 30752 | tf_op jit(solution)/shard_map/ppermute | solution.py:49
  145.6 2.0 %collective-permute-done.35.refs_3_ = bf16[1,120,128]{2,1,0:T(8,128)(2,1)S(1)} collective-permute-done((bf16[1,120,128]{2,1,0:T(8,128)(2,1)S(1)}, bf16[1,120,128]{2,1,0:T(8,128)(2,1)S(1)}, u32[]{:S(2)}, u32[]{:S(2)}) %collective-permute-start.35) | collective-permute-done | bytes 30752 | tf_op jit(solution)/shard_map/ppermute | solution.py:49
  149.6 10.3 %all_to_all.5 = f32[16,1,128]{2,1,0:T(1,128)S(1)} all-to-all(f32[16,1,128]{2,1,0:T(1,128)S(1)} %broadcast_in_dim.25), channel_id=1, replica_groups=mesh['batch'=16,'tm'=2] {'batch'}, dimensions={0} | all-to-all | bytes 16384 | tf_op jit(solution)/shard_map/all_to_all | solution.py:127
  160.0 1.9 %update.1 = (f32[1,1]{1,0:T(1,128)}, f32[24,1152]{1,0:T(8,128)}, f32[24,384]{1,0:T(8,128)}, f32[24,2048]{1,0:T(8,128)}, f32[64,384]{1,0:T(8,128)}, /*index=5*/f3...) custom-call(s32[2]{0:T(128)S(1)} %pad_add_fusion.where.refs_0_.refs_, ...), custom_call_target="tpu_custom_call" | custom-call | tf_op jit(solution)/shard_map/update/pallas_call | solution.py:1153
  (91 shorter events, 33.2 us)
Async XLA Ops:
  0.7 7.4 %collective-permute-start = (bf16[1024,384]{1,0:T(8,128)(2,1)}, bf16[1024,384]{1,0:T(8,128)(2,1)S(1)}, u32[]{:S(2)}, u32[]{:S(2)}) collective-permute-start(bf16[1024,384]{1,0:T(8,128)(2,1)} %bitcast.31), channel_id=1, source_target_pairs={{0,1},{1,0},{2,3},{3,2},{4,5},{5,4},{6,7},{7,6},{8,9},{9,8},{10,11... | collective-permute-start | bytes 2359304 | tf_op jit(solution)/shard_map/ppermute | solution.py:53
  2.8 10.2 %collective-permute-start.1 = (bf16[1,128,128]{2,1,0:T(8,128)(2,1)S(1)}, bf16[1,128,128]{2,1,0:T(8,128)(2,1)S(1)}, u32[]{:S(2)}, u32[]{:S(2)}) collective-permute-start(bf16[1,128,128]{2,1,0:T(8,128)(2,1)S(1)} %bitcast.25), channel_id=1, source_target_pairs={{0,8},{2,10},{4,12},{6,14},{8,0},{10,2},{12,4},{14,6},{16,24},{18,... | collective-permute-start | bytes 98312 | tf_op jit(solution)/shard_map/ppermute | solution.py:49
  5.5 7.6 %collective-permute-start.2 = (bf16[1,128,128]{2,1,0:T(8,128)(2,1)S(1)}, bf16[1,128,128]{2,1,0:T(8,128)(2,1)S(1)}, u32[]{:S(2)}, u32[]{:S(2)}) collective-permute-start(bf16[1,128,128]{2,1,0:T(8,128)(2,1)S(1)} %bitcast.26), channel_id=1, source_target_pairs={{0,16},{2,18},{4,20},{6,22},{8,24},{10,26},{12,28},{14,30},{16,0},... | collective-permute-start | bytes 98312 | tf_op jit(solution)/shard_map/ppermute | solution.py:49
  15.3 7.8 %collective-permute-start.5 = (bf16[4,128,128]{2,1,0:T(8,128)(2,1)S(1)}, bf16[4,128,128]{2,1,0:T(8,128)(2,1)S(1)}, u32[]{:S(2)}, u32[]{:S(2)}) collective-permute-start(bf16[4,128,128]{2,1,0:T(8,128)(2,1)S(1)} %join.2.refs_1_.refs_3_), channel_id=1, source_target_pairs={{0,4},{2,6},{4,0},{6,2},{8,12},{10,14},{12,8},{14,10},{16,20},{18,... | collective-permute-start | bytes 393224 | tf_op jit(solution)/shard_map/ppermute | solution.py:49
  17.3 8.1 %collective-permute-start.7 = (bf16[4,128,128]{2,1,0:T(8,128)(2,1)S(1)}, bf16[4,128,128]{2,1,0:T(8,128)(2,1)S(1)}, u32[]{:S(2)}, u32[]{:S(2)}) collective-permute-start(bf16[4,128,128]{2,1,0:T(8,128)(2,1)S(1)} %join.2.refs_1_.refs_3_), channel_id=1, source_target_pairs={{0,1},{1,0},{2,3},{3,2},{4,5},{5,4},{6,7},{7,6},{8,9},{9,8},{10,11... | collective-permute-start | bytes 393224 | tf_op jit(solution)/shard_map/ppermute | solution.py:53
  19.6 9.3 %collective-permute-start.8 = (bf16[4,128,128]{2,1,0:T(8,128)(2,1)S(1)}, bf16[4,128,128]{2,1,0:T(8,128)(2,1)S(1)}, u32[]{:S(2)}, u32[]{:S(2)}) collective-permute-start(bf16[4,128,128]{2,1,0:T(8,128)(2,1)S(1)} %collective-permute-done.4.refs_2_), channel_id=1, source_target_pairs={{0,1},{1,0},{2,3},{3,2},{4,5},{5,4},{6,7},{7,6},{8,9},{9,8},{10,11... | collective-permute-start | bytes 393224 | tf_op jit(solution)/shard_map/ppermute | solution.py:53
  23.1 6.6 %collective-permute-start.9 = (bf16[4,128,128]{2,1,0:T(8,128)(2,1)S(1)}, bf16[4,128,128]{2,1,0:T(8,128)(2,1)S(1)}, u32[]{:S(2)}, u32[]{:S(2)}) collective-permute-start(bf16[4,128,128]{2,1,0:T(8,128)(2,1)S(1)} %collective-permute-done.5.refs_3_), channel_id=1, source_target_pairs={{0,1},{1,0},{2,3},{3,2},{4,5},{5,4},{6,7},{7,6},{8,9},{9,8},{10,11... | collective-permute-start | bytes 393224 | tf_op jit(solution)/shard_map/ppermute | solution.py:53
  23.1 6.6 %collective-permute-start.10 = (bf16[4,128,128]{2,1,0:T(8,128)(2,1)S(1)}, bf16[4,128,128]{2,1,0:T(8,128)(2,1)S(1)}, u32[]{:S(2)}, u32[]{:S(2)}) collective-permute-start(bf16[4,128,128]{2,1,0:T(8,128)(2,1)S(1)} %collective-permute-done.6.refs_4_), channel_id=1, source_target_pairs={{0,1},{1,0},{2,3},{3,2},{4,5},{5,4},{6,7},{7,6},{8,9},{9,8},{10,11... | collective-permute-start | bytes 393224 | tf_op jit(solution)/shard_map/ppermute | solution.py:53
  25.2 12.4 %collective-permute-start.11 = (bf16[1,336,128]{2,1,0:T(8,128)(2,1)S(1)}, bf16[1,336,128]{2,1,0:T(8,128)(2,1)S(1)}, u32[]{:S(2)}, u32[]{:S(2)}) collective-permute-start(bf16[1,336,128]{2,1,0:T(8,128)(2,1)S(1)} %bitcast.21), channel_id=1, source_target_pairs={{0,8},{2,10},{4,12},{6,14},{8,0},{10,2},{12,4},{14,6},{16,24},{18,... | collective-permute-start | bytes 258056 | tf_op jit(solution)/shard_map/ppermute | solution.py:49
  25.5 12.1 %collective-permute-start.12 = (bf16[1,336,128]{2,1,0:T(8,128)(2,1)S(1)}, bf16[1,336,128]{2,1,0:T(8,128)(2,1)S(1)}, u32[]{:S(2)}, u32[]{:S(2)}) collective-permute-start(bf16[1,336,128]{2,1,0:T(8,128)(2,1)S(1)} %bitcast.22), channel_id=1, source_target_pairs={{0,16},{2,18},{4,20},{6,22},{8,24},{10,26},{12,28},{14,30},{16,0},... | collective-permute-start | bytes 258056 | tf_op jit(solution)/shard_map/ppermute | solution.py:49
  29.0 8.7 %collective-permute-start.13 = (bf16[1,336,128]{2,1,0:T(8,128)(2,1)S(1)}, bf16[1,336,128]{2,1,0:T(8,128)(2,1)S(1)}, u32[]{:S(2)}, u32[]{:S(2)}) collective-permute-start(bf16[1,336,128]{2,1,0:T(8,128)(2,1)S(1)} %bitcast.23), channel_id=1, source_target_pairs={{0,24},{2,26},{4,28},{6,30},{8,16},{10,18},{12,20},{14,22},{16,8},... | collective-permute-start | bytes 258056 | tf_op jit(solution)/shard_map/ppermute | solution.py:49
  37.7 21.2 %collective-permute-start.14 = (bf16[4,336,128]{2,1,0:T(8,128)(2,1)S(1)}, bf16[4,336,128]{2,1,0:T(8,128)(2,1)S(1)}, u32[]{:S(2)}, u32[]{:S(2)}) collective-permute-start(bf16[4,336,128]{2,1,0:T(8,128)(2,1)S(1)} %join.3.refs_0_.refs_1_), channel_id=1, source_target_pairs={{0,2},{2,0},{4,6},{6,4},{8,10},{10,8},{12,14},{14,12},{16,18},{18,... | collective-permute-start | bytes 1032200 | tf_op jit(solution)/shard_map/ppermute | solution.py:49
  37.8 21.0 %collective-permute-start.15 = (bf16[4,336,128]{2,1,0:T(8,128)(2,1)S(1)}, bf16[4,336,128]{2,1,0:T(8,128)(2,1)S(1)}, u32[]{:S(2)}, u32[]{:S(2)}) collective-permute-start(bf16[4,336,128]{2,1,0:T(8,128)(2,1)S(1)} %join.3.refs_0_.refs_1_), channel_id=1, source_target_pairs={{0,4},{2,6},{4,0},{6,2},{8,12},{10,14},{12,8},{14,10},{16,20},{18,... | collective-permute-start | bytes 1032200 | tf_op jit(solution)/shard_map/ppermute | solution.py:49
  39.2 19.7 %collective-permute-start.16 = (bf16[4,336,128]{2,1,0:T(8,128)(2,1)S(1)}, bf16[4,336,128]{2,1,0:T(8,128)(2,1)S(1)}, u32[]{:S(2)}, u32[]{:S(2)}) collective-permute-start(bf16[4,336,128]{2,1,0:T(8,128)(2,1)S(1)} %join.3.refs_0_.refs_1_), channel_id=1, source_target_pairs={{0,6},{2,4},{4,2},{6,0},{8,14},{10,12},{12,10},{14,8},{16,22},{18,... | collective-permute-start | bytes 1032200 | tf_op jit(solution)/shard_map/ppermute | solution.py:49
  41.2 18.7 %collective-permute-start.17 = (bf16[4,336,128]{2,1,0:T(8,128)(2,1)S(1)}, bf16[4,336,128]{2,1,0:T(8,128)(2,1)S(1)}, u32[]{:S(2)}, u32[]{:S(2)}) collective-permute-start(bf16[4,336,128]{2,1,0:T(8,128)(2,1)S(1)} %join.3.refs_0_.refs_1_), channel_id=1, source_target_pairs={{0,1},{1,0},{2,3},{3,2},{4,5},{5,4},{6,7},{7,6},{8,9},{9,8},{10,11... | collective-permute-start | bytes 1032200 | tf_op jit(solution)/shard_map/ppermute | solution.py:53
  77.4 32.7 %collective-permute-start.21 = (bf16[8,336,128]{2,1,0:T(8,128)(2,1)S(1)}, bf16[8,336,128]{2,1,0:T(8,128)(2,1)S(1)}, u32[]{:S(2)}, u32[]{:S(2)}) collective-permute-start(bf16[8,336,128]{2,1,0:T(8,128)(2,1)S(1)} %get-tuple-element.134), channel_id=1, source_target_pairs={{0,2},{2,0},{4,6},{6,4},{8,10},{10,8},{12,14},{14,12},{16,18},{18,... | collective-permute-start | bytes 2064392 | tf_op jit(solution)/shard_map/ppermute | solution.py:49
  77.6 32.5 %collective-permute-start.22 = (bf16[8,336,128]{2,1,0:T(8,128)(2,1)S(1)}, bf16[8,336,128]{2,1,0:T(8,128)(2,1)S(1)}, u32[]{:S(2)}, u32[]{:S(2)}) collective-permute-start(bf16[8,336,128]{2,1,0:T(8,128)(2,1)S(1)} %get-tuple-element.135), channel_id=1, source_target_pairs={{0,4},{2,6},{4,0},{6,2},{8,12},{10,14},{12,8},{14,10},{16,20},{18,... | collective-permute-start | bytes 2064392 | tf_op jit(solution)/shard_map/ppermute | solution.py:49
  79.0 31.4 %collective-permute-start.23 = (bf16[8,336,128]{2,1,0:T(8,128)(2,1)S(1)}, bf16[8,336,128]{2,1,0:T(8,128)(2,1)S(1)}, u32[]{:S(2)}, u32[]{:S(2)}) collective-permute-start(bf16[8,336,128]{2,1,0:T(8,128)(2,1)S(1)} %get-tuple-element.136), channel_id=1, source_target_pairs={{0,6},{2,4},{4,2},{6,0},{8,14},{10,12},{12,10},{14,8},{16,22},{18,... | collective-permute-start | bytes 2064392 | tf_op jit(solution)/shard_map/ppermute | solution.py:49
  110.4 9.0 %collective-permute-start.24 = (bf16[6,1024,128]{2,1,0:T(8,128)(2,1)S(1)}, bf16[6,1024,128]{2,1,0:T(8,128)(2,1)S(1)}, u32[]{:S(2)}, u32[]{:S(2)}) collective-permute-start(bf16[6,1024,128]{2,1,0:T(8,128)(2,1)S(1)} %hold.7), channel_id=1, source_target_pairs={{0,1},{1,0},{2,3},{3,2},{4,5},{5,4},{6,7},{7,6},{8,9},{9,8},{10,11... | collective-permute-start | bytes 4718600 | tf_op jit(solution)/shard_map/ppermute | solution.py:53
  114.9 10.2 %collective-permute-start.26 = (bf16[1,336,128]{2,1,0:T(8,128)(2,1)S(1)}, bf16[1,336,128]{2,1,0:T(8,128)(2,1)S(1)}, u32[]{:S(2)}, u32[]{:S(2)}) collective-permute-start(bf16[1,336,128]{2,1,0:T(8,128)(2,1)S(1)} %get-tuple-element.151), channel_id=1, source_target_pairs={{0,8},{2,10},{4,12},{6,14},{8,0},{10,2},{12,4},{14,6},{16,24},{18,... | collective-permute-start | bytes 258056 | tf_op jit(solution)/shard_map/ppermute | solution.py:49
  115.2 10.7 %collective-permute-start.27 = (bf16[1,336,128]{2,1,0:T(8,128)(2,1)S(1)}, bf16[1,336,128]{2,1,0:T(8,128)(2,1)S(1)}, u32[]{:S(2)}, u32[]{:S(2)}) collective-permute-start(bf16[1,336,128]{2,1,0:T(8,128)(2,1)S(1)} %get-tuple-element.152), channel_id=1, source_target_pairs={{0,16},{2,18},{4,20},{6,22},{8,24},{10,26},{12,28},{14,30},{16,0},... | collective-permute-start | bytes 258056 | tf_op jit(solution)/shard_map/ppermute | solution.py:49
  118.9 6.9 %collective-permute-start.28 = (bf16[1,336,128]{2,1,0:T(8,128)(2,1)S(1)}, bf16[1,336,128]{2,1,0:T(8,128)(2,1)S(1)}, u32[]{:S(2)}, u32[]{:S(2)}) collective-permute-start(bf16[1,336,128]{2,1,0:T(8,128)(2,1)S(1)} %get-tuple-element.153), channel_id=1, source_target_pairs={{0,24},{2,26},{4,28},{6,30},{8,16},{10,18},{12,20},{14,22},{16,8},... | collective-permute-start | bytes 258056 | tf_op jit(solution)/shard_map/ppermute | solution.py:49
  130.2 7.8 %collective-permute-start.31 = (bf16[4,120,128]{2,1,0:T(8,128)(2,1)S(1)}, bf16[4,120,128]{2,1,0:T(8,128)(2,1)S(1)}, u32[]{:S(2)}, u32[]{:S(2)}) collective-permute-start(bf16[4,120,128]{2,1,0:T(8,128)(2,1)S(1)} %get-tuple-element.160), channel_id=1, source_target_pairs={{0,4},{2,6},{4,0},{6,2},{8,12},{10,14},{12,8},{14,10},{16,20},{18,... | collective-permute-start | bytes 368648 | tf_op jit(solution)/shard_map/ppermute | solution.py:49
  132.6 15.6 %collective-permute-start.37 = (f32[336,128]{1,0:T(8,128)S(1)}, f32[336,128]{1,0:T(8,128)S(1)}, u32[]{:S(2)}, u32[]{:S(2)}) collective-permute-start(f32[336,128]{1,0:T(8,128)S(1)} %bitcast.15), channel_id=1, source_target_pairs={{0,1},{1,0},{2,3},{3,2},{4,5},{5,4},{6,7},{7,6},{8,9},{9,8},{10,11... | collective-permute-start | bytes 516104 | tf_op jit(solution)/shard_map/ppermute | solution.py:53
  (19 other events, 64.3 us)

commit v8 on v7

--- a/solution.py
+++ b/solution.py
@@ -68,7 +68,7 @@
 BLOCK = 256
 LANES = 128
 KEEP_LANE = 96
-LIMITS = (12, 20, 12, 38, 12, 20, 12)
+LIMITS = (12, 20, 12, 36, 12, 20, 12)
 WIDE = 512
 NN = (((1,), (0,)), ((), ()))
 NT = (((1,), (1,)), ((), ()))
@@ -446,7 +446,10 @@
 
 
 def tables_kernel(length, where, ids, pads, offsets, *refs):
-    cosine, sine, key_aux, query_aux, ranges = refs[-5:]
+    cosine, sine, key_aux, query_aux, ranges = refs[-9:-4]
+    copies = fetch((ids, pads, offsets), refs[-4:-1], refs[-1])
+    ids, pads, offsets = refs[-4:-1]
+    arrive(copies)
     core = where[0]
     whole = 2 * length
 
@@ -507,12 +510,13 @@
             in_vmem((length, LANES), bf16),
             jax.ShapeDtypeStruct((4, length // BLOCK), jnp.int32),
         ],
-        in_specs=[smem, spec, spec, spec] + [pl.BlockSpec(memory_space=pl.ANY)] * len(waits),
+        in_specs=[smem, HBM, HBM, HBM] + [pl.BlockSpec(memory_space=pl.ANY)] * len(waits),
         out_specs=[spec] * 4 + [smem],
+        scratch_shapes=landing([ids, pads, offsets]),
         compiler_params=limit(LIMITS[0]),
         cost_estimate=cost(3 * 10**9, 4 * 2**20),
         name="tables",
-    )(where, ids, pads, offsets, *waits)
+    )(where, *in_hbm([ids, pads, offsets]), *waits)
 
 
 def project_kernel(fused, own, there, cosine, sine, key_aux, query_aux, *refs):

time: 163 us -> 162 us (level)
  local copies, waits for them, and re-layouts: 3.51 us -> 0.01 us
    unnamed x10 -> x0, local copies, waits for them, and re-layouts: 3.5 us -> none
  transfers between devices with their start and end apart: 38 -> 38, of which waited for: 15 -> 14; matrix products, arithmetic and copies ran while one was open for 0% -> 0% of each run, Pallas kernels for 43% -> 43%
where the time goes in v8:
time: 162 us; the launch traced here: 161 us
  Pallas kernels  89 us (55%)
  starting transfers between devices  35.6 us (22%)
  waiting for transfers between devices  24.1 us (15%)
  blocking collectives  11.3 us (7%)
    ppermute x24, starting transfers between devices, permute_batch(): return lax.ppermute(value, 'batch', [(i, i ^ flip) for i in range(count)])  32.8 us
    pallas_call x1, Pallas kernels, attend_back(): pl.pallas_call(attend_back_kernel, out_shape=[in_vmem((heads, HD, length)...  23.8 us
    ppermute x24, waiting for transfers between devices, permute_batch(): return lax.ppermute(value, 'batch', [(i, i ^ flip) for i in range(count)])  18.4 us
    pallas_call x1, Pallas kernels, attend(): pl.pallas_call(attend_kernel, out_shape=[in_vmem((length, D), bf16), in_v...  17.5 us
    pallas_call x1, Pallas kernels, feed(): pl.pallas_call(partial(feed_kernel, fused), out_shape=out_shape, in_specs...  15.7 us
    all_to_all x1, blocking collectives, sum_batch(): value = lax.all_to_all(value, 'batch', 0, 0, tiled=True)  11.3 us
    pallas_call x2, Pallas kernels, project_back(): pl.pallas_call(partial(project_back_kernel, number, fused), out_shape=out...  9.64 us
    pallas_call x1, Pallas kernels, project(): pl.pallas_call(partial(project_kernel, fused), out_shape=[in_vmem((HEADS,...  7.99 us
  transfers between devices with their start and end apart: 38, of which 14 were waited for; matrix products, arithmetic and copies ran while one was open for 0% of the time, Pallas kernels for 43%

profile of v8, /device:TPU:0, one launch (start us, length us, event | category | flops | bytes accessed | tf_op | source)
XLA Modules:
  0.0 161.3 jit_solution(14159623278448136013)
XLA Ops:
  2.8 2.7 %collective-permute-start.1 = (bf16[1,128,128]{2,1,0:T(8,128)(2,1)S(1)}, bf16[1,128,128]{2,1,0:T(8,128)(2,1)S(1)}, u32[]{:S(2)}, u32[]{:S(2)}) collective-permute-start(bf16[1,128,128]{2,1,0:T(8,128)(2,1)S(1)} %bitcast.25), channel_id=1, source_target_pairs={{0,8},{2,10},{4,12},{6,14},{8,0},{10,2},{12,4},{14,6},{16,24},{18,... | collective-permute-start | bytes 98312 | tf_op jit(solution)/shard_map/ppermute | solution.py:49
  5.5 2.6 %collective-permute-start.2 = (bf16[1,128,128]{2,1,0:T(8,128)(2,1)S(1)}, bf16[1,128,128]{2,1,0:T(8,128)(2,1)S(1)}, u32[]{:S(2)}, u32[]{:S(2)}) collective-permute-start(bf16[1,128,128]{2,1,0:T(8,128)(2,1)S(1)} %bitcast.26), channel_id=1, source_target_pairs={{0,16},{2,18},{4,20},{6,22},{8,24},{10,26},{12,28},{14,30},{16,0},... | collective-permute-start | bytes 98312 | tf_op jit(solution)/shard_map/ppermute | solution.py:49
  8.1 3.6 %tables.1 = (f32[2048,128]{1,0:T(8,128)S(1)}, f32[2048,128]{1,0:T(8,128)S(1)}, bf16[2048,128]{1,0:T(8,128)(2,1)S(1)}, bf16[1024,128]{1,0:T(8,128)(2,1)S(1)}, s32[4,4]{1,0:T(4,128)S(1)}) custom-call(s32[2]{0:T(128)S(1)} %pad_add_fusion.where.refs_0_.refs_5_, s32[1,2048]{1,0:T(1,128)} %ids.1, s32[1,2048]{1,0:T(1,128)} %pads.1, s32[1,2048]{1,0:T(1,128)} %offsets.1, ...), custom_call_target="tpu_custom_call" | custom-call | flops 3000000000 | bytes 4194304 | tf_op jit(solution)/shard_map/tables/pallas_call | solution.py:504
  11.7 2.1 %collective-permute-done.3.refs_3_ = bf16[1,128,128]{2,1,0:T(8,128)(2,1)S(1)} collective-permute-done((bf16[1,128,128]{2,1,0:T(8,128)(2,1)S(1)}, bf16[1,128,128]{2,1,0:T(8,128)(2,1)S(1)}, u32[]{:S(2)}, u32[]{:S(2)}) %collective-permute-start.3) | collective-permute-done | bytes 32800 | tf_op jit(solution)/shard_map/ppermute | solution.py:49
  17.3 2.7 %collective-permute-done.4.refs_2_ = bf16[4,128,128]{2,1,0:T(8,128)(2,1)S(1)} collective-permute-done((bf16[4,128,128]{2,1,0:T(8,128)(2,1)S(1)}, bf16[4,128,128]{2,1,0:T(8,128)(2,1)S(1)}, u32[]{:S(2)}, u32[]{:S(2)}) %collective-permute-start.4) | collective-permute-done | bytes 131104 | tf_op jit(solution)/shard_map/ppermute | solution.py:49
  20.0 2.9 %collective-permute-done.5.refs_3_ = bf16[4,128,128]{2,1,0:T(8,128)(2,1)S(1)} collective-permute-done((bf16[4,128,128]{2,1,0:T(8,128)(2,1)S(1)}, bf16[4,128,128]{2,1,0:T(8,128)(2,1)S(1)}, u32[]{:S(2)}, u32[]{:S(2)}) %collective-permute-start.5) | collective-permute-done | bytes 131104 | tf_op jit(solution)/shard_map/ppermute | solution.py:49
  25.2 2.5 %collective-permute-start.12 = (bf16[1,336,128]{2,1,0:T(8,128)(2,1)S(1)}, bf16[1,336,128]{2,1,0:T(8,128)(2,1)S(1)}, u32[]{:S(2)}, u32[]{:S(2)}) collective-permute-start(bf16[1,336,128]{2,1,0:T(8,128)(2,1)S(1)} %bitcast.22), channel_id=1, source_target_pairs={{0,16},{2,18},{4,20},{6,22},{8,24},{10,26},{12,28},{14,30},{16,0},... | collective-permute-start | bytes 258056 | tf_op jit(solution)/shard_map/ppermute | solution.py:49
  27.6 1.9 %collective-permute-start.13 = (bf16[1,336,128]{2,1,0:T(8,128)(2,1)S(1)}, bf16[1,336,128]{2,1,0:T(8,128)(2,1)S(1)}, u32[]{:S(2)}, u32[]{:S(2)}) collective-permute-start(bf16[1,336,128]{2,1,0:T(8,128)(2,1)S(1)} %bitcast.23), channel_id=1, source_target_pairs={{0,24},{2,26},{4,28},{6,30},{8,16},{10,18},{12,20},{14,22},{16,8},... | collective-permute-start | bytes 258056 | tf_op jit(solution)/shard_map/ppermute | solution.py:49
  29.5 8.0 %project.1 = (bf16[6,1024,128]{2,1,0:T(8,128)(2,1)S(1)}, bf16[6,2048,128]{2,1,0:T(8,128)(2,1)S(1)}, bf16[6,2048,128]{2,1,0:T(8,128)(2,1)S(1)}, bf16[6,64,2048]{2...) custom-call(bf16[1024,384]{1,0:T(8,128)(2,1)} %bitcast.32, ...), custom_call_target="tpu_custom_call" | custom-call | flops 8999999488 | bytes 16777216 | tf_op jit(solution)/shard_map/project/pallas_call | solution.py:602
  38.9 2.3 %collective-permute-start.16 = (bf16[4,336,128]{2,1,0:T(8,128)(2,1)S(1)}, bf16[4,336,128]{2,1,0:T(8,128)(2,1)S(1)}, u32[]{:S(2)}, u32[]{:S(2)}) collective-permute-start(bf16[4,336,128]{2,1,0:T(8,128)(2,1)S(1)} %join.3.refs_0_.refs_1_), channel_id=1, source_target_pairs={{0,6},{2,4},{4,2},{6,0},{8,14},{10,12},{12,10},{14,8},{16,22},{18,... | collective-permute-start | bytes 1032200 | tf_op jit(solution)/shard_map/ppermute | solution.py:49
  41.2 17.5 %attend.1 = (bf16[1024,384]{1,0:T(8,128)(2,1)S(1)}, f32[1024,384]{1,0:T(8,128)S(1)}, bf16[6,1024,128]{2,1,0:T(8,128)(2,1)S(1)}) custom-call(s32[4,4]{1,0:T(4,128)S(1)} %get-tuple-element.112.ranges, bf16[6,1024,128]{2,1,0:T(8,128)(2,1)S(1)} %get-tuple-element.117.qa, bf16[6,2048,128]{2,1,0:T(8,128)(2,1)S(1)} %get-tuple-element.118.ka, ...), custom_call_target="tpu_custom_call" | custom-call | flops 17999998976 | bytes 12582912 | tf_op jit(solution)/shard_map/attend/pallas_call | solution.py:678
  61.5 15.7 %feed.1 = (bf16[1024,384]{1,0:T(8,128)(2,1)}, f32[1024,384]{1,0:T(8,128)S(1)}, bf16[6,1024,128]{2,1,0:T(8,128)(2,1)S(1)}, f32[8,336,128]{2,1,0:T(8,128)S(1)}, bf...) custom-call(bf16[1024,384]{1,0:T(8,128)(2,1)} %bitcast.33, ...), custom_call_target="tpu_custom_call" | custom-call | flops 14000000000 | bytes 16777216 | tf_op jit(solution)/shard_map/feed/pallas_call | solution.py:932
  78.5 2.3 %collective-permute-start.23 = (bf16[8,336,128]{2,1,0:T(8,128)(2,1)S(1)}, bf16[8,336,128]{2,1,0:T(8,128)(2,1)S(1)}, u32[]{:S(2)}, u32[]{:S(2)}) collective-permute-start(bf16[8,336,128]{2,1,0:T(8,128)(2,1)S(1)} %get-tuple-element.136), channel_id=1, source_target_pairs={{0,6},{2,4},{4,2},{6,0},{8,14},{10,12},{12,10},{14,8},{16,22},{18,... | collective-permute-start | bytes 2064392 | tf_op jit(solution)/shard_map/ppermute | solution.py:49
  80.8 23.8 %attend_back.1 = (f32[6,64,1024]{2,1,0:T(8,128)S(1)}, f32[6,2048,128]{2,1,0:T(8,128)S(1)}, bf16[6,1024,128]{2,1,0:T(8,128)(2,1)S(1)}) custom-call(s32[4,4]{1,0:T(4,128)S(1)} %get-tuple-element.112.ranges, bf16[6,1024,128]{2,1,0:T(8,128)(2,1)S(1)} %get-tuple-element.128.qb, bf16[6,2048,128]{2,1,0:T(8,128)(2,1)S(1)} %get-tuple-element.118.ka, ...), custom_call_target="tpu_custom_call" | custom-call | flops 33999998976 | bytes 8388608 | tf_op jit(solution)/shard_map/attend_back/pallas_call | solution.py:740
  104.5 3.9 %project_back.2 = (f32[1024,384]{1,0:T(8,128)S(1)}, f32[384,384]{1,0:T(8,128)S(1)}) custom-call(bf16[1024,384]{1,0:T(8,128)(2,1)} %bitcast.34, f32[2048,128]{1,0:T(8,128)S(1)} %get-tuple-element.113.cosine, f32[2048,128]{1,0:T(8,128)S(1)} %get-tuple-element.114.sine, bf16[384,1152]{1,0:T(8,128)(2,1)S(1)} %get-tuple-element.127.w, ...), custom_call_target="tpu_custom_call" | custom-call | flops 4000000000 | bytes 8388608 | tf_op jit(solution)/shard_map/project_back/pallas_call | solution.py:1045
  111.6 2.5 %collective-permute-done.25.refs_1_ = bf16[4,336,128]{2,1,0:T(8,128)(2,1)S(1)} collective-permute-done((bf16[4,336,128]{2,1,0:T(8,128)(2,1)S(1)}, bf16[4,336,128]{2,1,0:T(8,128)(2,1)S(1)}, u32[]{:S(2)}, u32[]{:S(2)}) %collective-permute-start.25) | collective-permute-done | bytes 344096 | tf_op jit(solution)/shard_map/ppermute | solution.py:53
  114.8 2.8 %collective-permute-start.27 = (bf16[1,336,128]{2,1,0:T(8,128)(2,1)S(1)}, bf16[1,336,128]{2,1,0:T(8,128)(2,1)S(1)}, u32[]{:S(2)}, u32[]{:S(2)}) collective-permute-start(bf16[1,336,128]{2,1,0:T(8,128)(2,1)S(1)} %get-tuple-element.152), channel_id=1, source_target_pairs={{0,16},{2,18},{4,20},{6,22},{8,24},{10,26},{12,28},{14,30},{16,0},... | collective-permute-start | bytes 258056 | tf_op jit(solution)/shard_map/ppermute | solution.py:49
  119.1 5.8 %project_back.3 = (bf16[1024,384]{1,0:T(8,128)(2,1)}, f32[16,120,128]{2,1,0:T(8,128)S(1)}, bf16[16,120,128]{2,1,0:T(8,128)(2,1)S(1)}) custom-call(bf16[1024,384]{1,0:T(8,128)(2,1)} %bitcast.35, f32[2048,128]{1,0:T(8,128)S(1)} %get-tuple-element.113.cosine, f32[2048,128]{1,0:T(8,128)S(1)} %get-tuple-element.114.sine, ...), custom_call_target="tpu_custom_call" | custom-call | flops 4000000000 | bytes 8388608 | tf_op jit(solution)/shard_map/project_back/pallas_call | solution.py:1045
  131.7 2.3 %collective-permute-done.30.refs_1_ = bf16[4,120,128]{2,1,0:T(8,128)(2,1)S(1)} collective-permute-done((bf16[4,120,128]{2,1,0:T(8,128)(2,1)S(1)}, bf16[4,120,128]{2,1,0:T(8,128)(2,1)S(1)}, u32[]{:S(2)}, u32[]{:S(2)}) %collective-permute-start.30) | collective-permute-done | bytes 122912 | tf_op jit(solution)/shard_map/ppermute | solution.py:49
  134.0 3.3 %collective-permute-done.31.refs_2_ = bf16[4,120,128]{2,1,0:T(8,128)(2,1)S(1)} collective-permute-done((bf16[4,120,128]{2,1,0:T(8,128)(2,1)S(1)}, bf16[4,120,128]{2,1,0:T(8,128)(2,1)S(1)}, u32[]{:S(2)}, u32[]{:S(2)}) %collective-permute-start.31) | collective-permute-done | bytes 122912 | tf_op jit(solution)/shard_map/ppermute | solution.py:49
  140.1 2.3 %collective-permute-start.35 = (bf16[1,120,128]{2,1,0:T(8,128)(2,1)S(1)}, bf16[1,120,128]{2,1,0:T(8,128)(2,1)S(1)}, u32[]{:S(2)}, u32[]{:S(2)}) collective-permute-start(bf16[1,120,128]{2,1,0:T(8,128)(2,1)S(1)} %get-tuple-element.165), channel_id=1, source_target_pairs={{0,24},{2,26},{4,28},{6,30},{8,16},{10,18},{12,20},{14,22},{16,8},... | collective-permute-start | bytes 92168 | tf_op jit(solution)/shard_map/ppermute | solution.py:49
  142.4 2.2 %collective-permute-done.34.refs_2_ = bf16[1,120,128]{2,1,0:T(8,128)(2,1)S(1)} collective-permute-done((bf16[1,120,128]{2,1,0:T(8,128)(2,1)S(1)}, bf16[1,120,128]{2,1,0:T(8,128)(2,1)S(1)}, u32[]{:S(2)}, u32[]{:S(2)}) %collective-permute-start.34) | collective-permute-done | bytes 30752 | tf_op jit(solution)/shard_map/ppermute | solution.py:49
  147.9 11.3 %all_to_all.5 = f32[16,1,128]{2,1,0:T(1,128)S(1)} all-to-all(f32[16,1,128]{2,1,0:T(1,128)S(1)} %broadcast_in_dim.25), channel_id=1, replica_groups=mesh['batch'=16,'tm'=2] {'batch'}, dimensions={0} | all-to-all | bytes 16384 | tf_op jit(solution)/shard_map/all_to_all | solution.py:127
  159.2 1.9 %update.1 = (f32[1,1]{1,0:T(1,128)}, f32[24,1152]{1,0:T(8,128)}, f32[24,384]{1,0:T(8,128)}, f32[24,2048]{1,0:T(8,128)}, f32[64,384]{1,0:T(8,128)}, /*index=5*/f3...) custom-call(s32[2]{0:T(128)S(1)} %pad_add_fusion.where.refs_0_.refs_, ...), custom_call_target="tpu_custom_call" | custom-call | tf_op jit(solution)/shard_map/update/pallas_call | solution.py:1157
  (81 shorter events, 31.6 us)
Async XLA Ops:
  0.7 7.4 %collective-permute-start = (bf16[1024,384]{1,0:T(8,128)(2,1)}, bf16[1024,384]{1,0:T(8,128)(2,1)S(1)}, u32[]{:S(2)}, u32[]{:S(2)}) collective-permute-start(bf16[1024,384]{1,0:T(8,128)(2,1)} %bitcast.31), channel_id=1, source_target_pairs={{0,1},{1,0},{2,3},{3,2},{4,5},{5,4},{6,7},{7,6},{8,9},{9,8},{10,11... | collective-permute-start | bytes 2359304 | tf_op jit(solution)/shard_map/ppermute | solution.py:53
  2.8 8.9 %collective-permute-start.1 = (bf16[1,128,128]{2,1,0:T(8,128)(2,1)S(1)}, bf16[1,128,128]{2,1,0:T(8,128)(2,1)S(1)}, u32[]{:S(2)}, u32[]{:S(2)}) collective-permute-start(bf16[1,128,128]{2,1,0:T(8,128)(2,1)S(1)} %bitcast.25), channel_id=1, source_target_pairs={{0,8},{2,10},{4,12},{6,14},{8,0},{10,2},{12,4},{14,6},{16,24},{18,... | collective-permute-start | bytes 98312 | tf_op jit(solution)/shard_map/ppermute | solution.py:49
  15.3 7.6 %collective-permute-start.5 = (bf16[4,128,128]{2,1,0:T(8,128)(2,1)S(1)}, bf16[4,128,128]{2,1,0:T(8,128)(2,1)S(1)}, u32[]{:S(2)}, u32[]{:S(2)}) collective-permute-start(bf16[4,128,128]{2,1,0:T(8,128)(2,1)S(1)} %join.2.refs_1_.refs_3_), channel_id=1, source_target_pairs={{0,4},{2,6},{4,0},{6,2},{8,12},{10,14},{12,8},{14,10},{16,20},{18,... | collective-permute-start | bytes 393224 | tf_op jit(solution)/shard_map/ppermute | solution.py:49
  17.3 7.8 %collective-permute-start.7 = (bf16[4,128,128]{2,1,0:T(8,128)(2,1)S(1)}, bf16[4,128,128]{2,1,0:T(8,128)(2,1)S(1)}, u32[]{:S(2)}, u32[]{:S(2)}) collective-permute-start(bf16[4,128,128]{2,1,0:T(8,128)(2,1)S(1)} %join.2.refs_1_.refs_3_), channel_id=1, source_target_pairs={{0,1},{1,0},{2,3},{3,2},{4,5},{5,4},{6,7},{7,6},{8,9},{9,8},{10,11... | collective-permute-start | bytes 393224 | tf_op jit(solution)/shard_map/ppermute | solution.py:53
  20.0 7.6 %collective-permute-start.8 = (bf16[4,128,128]{2,1,0:T(8,128)(2,1)S(1)}, bf16[4,128,128]{2,1,0:T(8,128)(2,1)S(1)}, u32[]{:S(2)}, u32[]{:S(2)}) collective-permute-start(bf16[4,128,128]{2,1,0:T(8,128)(2,1)S(1)} %collective-permute-done.4.refs_2_), channel_id=1, source_target_pairs={{0,1},{1,0},{2,3},{3,2},{4,5},{5,4},{6,7},{7,6},{8,9},{9,8},{10,11... | collective-permute-start | bytes 393224 | tf_op jit(solution)/shard_map/ppermute | solution.py:53
  22.9 6.6 %collective-permute-start.9 = (bf16[4,128,128]{2,1,0:T(8,128)(2,1)S(1)}, bf16[4,128,128]{2,1,0:T(8,128)(2,1)S(1)}, u32[]{:S(2)}, u32[]{:S(2)}) collective-permute-start(bf16[4,128,128]{2,1,0:T(8,128)(2,1)S(1)} %collective-permute-done.5.refs_3_), channel_id=1, source_target_pairs={{0,1},{1,0},{2,3},{3,2},{4,5},{5,4},{6,7},{7,6},{8,9},{9,8},{10,11... | collective-permute-start | bytes 393224 | tf_op jit(solution)/shard_map/ppermute | solution.py:53
  23.0 6.6 %collective-permute-start.10 = (bf16[4,128,128]{2,1,0:T(8,128)(2,1)S(1)}, bf16[4,128,128]{2,1,0:T(8,128)(2,1)S(1)}, u32[]{:S(2)}, u32[]{:S(2)}) collective-permute-start(bf16[4,128,128]{2,1,0:T(8,128)(2,1)S(1)} %collective-permute-done.6.refs_4_), channel_id=1, source_target_pairs={{0,1},{1,0},{2,3},{3,2},{4,5},{5,4},{6,7},{7,6},{8,9},{9,8},{10,11... | collective-permute-start | bytes 393224 | tf_op jit(solution)/shard_map/ppermute | solution.py:53
  25.1 12.5 %collective-permute-start.11 = (bf16[1,336,128]{2,1,0:T(8,128)(2,1)S(1)}, bf16[1,336,128]{2,1,0:T(8,128)(2,1)S(1)}, u32[]{:S(2)}, u32[]{:S(2)}) collective-permute-start(bf16[1,336,128]{2,1,0:T(8,128)(2,1)S(1)} %bitcast.21), channel_id=1, source_target_pairs={{0,8},{2,10},{4,12},{6,14},{8,0},{10,2},{12,4},{14,6},{16,24},{18,... | collective-permute-start | bytes 258056 | tf_op jit(solution)/shard_map/ppermute | solution.py:49
  25.2 12.4 %collective-permute-start.12 = (bf16[1,336,128]{2,1,0:T(8,128)(2,1)S(1)}, bf16[1,336,128]{2,1,0:T(8,128)(2,1)S(1)}, u32[]{:S(2)}, u32[]{:S(2)}) collective-permute-start(bf16[1,336,128]{2,1,0:T(8,128)(2,1)S(1)} %bitcast.22), channel_id=1, source_target_pairs={{0,16},{2,18},{4,20},{6,22},{8,24},{10,26},{12,28},{14,30},{16,0},... | collective-permute-start | bytes 258056 | tf_op jit(solution)/shard_map/ppermute | solution.py:49
  27.6 9.9 %collective-permute-start.13 = (bf16[1,336,128]{2,1,0:T(8,128)(2,1)S(1)}, bf16[1,336,128]{2,1,0:T(8,128)(2,1)S(1)}, u32[]{:S(2)}, u32[]{:S(2)}) collective-permute-start(bf16[1,336,128]{2,1,0:T(8,128)(2,1)S(1)} %bitcast.23), channel_id=1, source_target_pairs={{0,24},{2,26},{4,28},{6,30},{8,16},{10,18},{12,20},{14,22},{16,8},... | collective-permute-start | bytes 258056 | tf_op jit(solution)/shard_map/ppermute | solution.py:49
  37.6 21.0 %collective-permute-start.14 = (bf16[4,336,128]{2,1,0:T(8,128)(2,1)S(1)}, bf16[4,336,128]{2,1,0:T(8,128)(2,1)S(1)}, u32[]{:S(2)}, u32[]{:S(2)}) collective-permute-start(bf16[4,336,128]{2,1,0:T(8,128)(2,1)S(1)} %join.3.refs_0_.refs_1_), channel_id=1, source_target_pairs={{0,2},{2,0},{4,6},{6,4},{8,10},{10,8},{12,14},{14,12},{16,18},{18,... | collective-permute-start | bytes 1032200 | tf_op jit(solution)/shard_map/ppermute | solution.py:49
  37.7 21.0 %collective-permute-start.15 = (bf16[4,336,128]{2,1,0:T(8,128)(2,1)S(1)}, bf16[4,336,128]{2,1,0:T(8,128)(2,1)S(1)}, u32[]{:S(2)}, u32[]{:S(2)}) collective-permute-start(bf16[4,336,128]{2,1,0:T(8,128)(2,1)S(1)} %join.3.refs_0_.refs_1_), channel_id=1, source_target_pairs={{0,4},{2,6},{4,0},{6,2},{8,12},{10,14},{12,8},{14,10},{16,20},{18,... | collective-permute-start | bytes 1032200 | tf_op jit(solution)/shard_map/ppermute | solution.py:49
  38.9 19.8 %collective-permute-start.16 = (bf16[4,336,128]{2,1,0:T(8,128)(2,1)S(1)}, bf16[4,336,128]{2,1,0:T(8,128)(2,1)S(1)}, u32[]{:S(2)}, u32[]{:S(2)}) collective-permute-start(bf16[4,336,128]{2,1,0:T(8,128)(2,1)S(1)} %join.3.refs_0_.refs_1_), channel_id=1, source_target_pairs={{0,6},{2,4},{4,2},{6,0},{8,14},{10,12},{12,10},{14,8},{16,22},{18,... | collective-permute-start | bytes 1032200 | tf_op jit(solution)/shard_map/ppermute | solution.py:49
  41.2 18.6 %collective-permute-start.17 = (bf16[4,336,128]{2,1,0:T(8,128)(2,1)S(1)}, bf16[4,336,128]{2,1,0:T(8,128)(2,1)S(1)}, u32[]{:S(2)}, u32[]{:S(2)}) collective-permute-start(bf16[4,336,128]{2,1,0:T(8,128)(2,1)S(1)} %join.3.refs_0_.refs_1_), channel_id=1, source_target_pairs={{0,1},{1,0},{2,3},{3,2},{4,5},{5,4},{6,7},{7,6},{8,9},{9,8},{10,11... | collective-permute-start | bytes 1032200 | tf_op jit(solution)/shard_map/ppermute | solution.py:53
  77.2 31.2 %collective-permute-start.21 = (bf16[8,336,128]{2,1,0:T(8,128)(2,1)S(1)}, bf16[8,336,128]{2,1,0:T(8,128)(2,1)S(1)}, u32[]{:S(2)}, u32[]{:S(2)}) collective-permute-start(bf16[8,336,128]{2,1,0:T(8,128)(2,1)S(1)} %get-tuple-element.134), channel_id=1, source_target_pairs={{0,2},{2,0},{4,6},{6,4},{8,10},{10,8},{12,14},{14,12},{16,18},{18,... | collective-permute-start | bytes 2064392 | tf_op jit(solution)/shard_map/ppermute | solution.py:49
  77.3 31.1 %collective-permute-start.22 = (bf16[8,336,128]{2,1,0:T(8,128)(2,1)S(1)}, bf16[8,336,128]{2,1,0:T(8,128)(2,1)S(1)}, u32[]{:S(2)}, u32[]{:S(2)}) collective-permute-start(bf16[8,336,128]{2,1,0:T(8,128)(2,1)S(1)} %get-tuple-element.135), channel_id=1, source_target_pairs={{0,4},{2,6},{4,0},{6,2},{8,12},{10,14},{12,8},{14,10},{16,20},{18,... | collective-permute-start | bytes 2064392 | tf_op jit(solution)/shard_map/ppermute | solution.py:49
  78.5 31.7 %collective-permute-start.23 = (bf16[8,336,128]{2,1,0:T(8,128)(2,1)S(1)}, bf16[8,336,128]{2,1,0:T(8,128)(2,1)S(1)}, u32[]{:S(2)}, u32[]{:S(2)}) collective-permute-start(bf16[8,336,128]{2,1,0:T(8,128)(2,1)S(1)} %get-tuple-element.136), channel_id=1, source_target_pairs={{0,6},{2,4},{4,2},{6,0},{8,14},{10,12},{12,10},{14,8},{16,22},{18,... | collective-permute-start | bytes 2064392 | tf_op jit(solution)/shard_map/ppermute | solution.py:49
  110.2 9.0 %collective-permute-start.24 = (bf16[6,1024,128]{2,1,0:T(8,128)(2,1)S(1)}, bf16[6,1024,128]{2,1,0:T(8,128)(2,1)S(1)}, u32[]{:S(2)}, u32[]{:S(2)}) collective-permute-start(bf16[6,1024,128]{2,1,0:T(8,128)(2,1)S(1)} %hold.7), channel_id=1, source_target_pairs={{0,1},{1,0},{2,3},{3,2},{4,5},{5,4},{6,7},{7,6},{8,9},{9,8},{10,11... | collective-permute-start | bytes 4718600 | tf_op jit(solution)/shard_map/ppermute | solution.py:53
  114.7 10.2 %collective-permute-start.26 = (bf16[1,336,128]{2,1,0:T(8,128)(2,1)S(1)}, bf16[1,336,128]{2,1,0:T(8,128)(2,1)S(1)}, u32[]{:S(2)}, u32[]{:S(2)}) collective-permute-start(bf16[1,336,128]{2,1,0:T(8,128)(2,1)S(1)} %get-tuple-element.151), channel_id=1, source_target_pairs={{0,8},{2,10},{4,12},{6,14},{8,0},{10,2},{12,4},{14,6},{16,24},{18,... | collective-permute-start | bytes 258056 | tf_op jit(solution)/shard_map/ppermute | solution.py:49
  114.8 10.2 %collective-permute-start.27 = (bf16[1,336,128]{2,1,0:T(8,128)(2,1)S(1)}, bf16[1,336,128]{2,1,0:T(8,128)(2,1)S(1)}, u32[]{:S(2)}, u32[]{:S(2)}) collective-permute-start(bf16[1,336,128]{2,1,0:T(8,128)(2,1)S(1)} %get-tuple-element.152), channel_id=1, source_target_pairs={{0,16},{2,18},{4,20},{6,22},{8,24},{10,26},{12,28},{14,30},{16,0},... | collective-permute-start | bytes 258056 | tf_op jit(solution)/shard_map/ppermute | solution.py:49
  117.5 7.4 %collective-permute-start.28 = (bf16[1,336,128]{2,1,0:T(8,128)(2,1)S(1)}, bf16[1,336,128]{2,1,0:T(8,128)(2,1)S(1)}, u32[]{:S(2)}, u32[]{:S(2)}) collective-permute-start(bf16[1,336,128]{2,1,0:T(8,128)(2,1)S(1)} %get-tuple-element.153), channel_id=1, source_target_pairs={{0,24},{2,26},{4,28},{6,30},{8,16},{10,18},{12,20},{14,22},{16,8},... | collective-permute-start | bytes 258056 | tf_op jit(solution)/shard_map/ppermute | solution.py:49
  129.5 7.8 %collective-permute-start.31 = (bf16[4,120,128]{2,1,0:T(8,128)(2,1)S(1)}, bf16[4,120,128]{2,1,0:T(8,128)(2,1)S(1)}, u32[]{:S(2)}, u32[]{:S(2)}) collective-permute-start(bf16[4,120,128]{2,1,0:T(8,128)(2,1)S(1)} %get-tuple-element.160), channel_id=1, source_target_pairs={{0,4},{2,6},{4,0},{6,2},{8,12},{10,14},{12,8},{14,10},{16,20},{18,... | collective-permute-start | bytes 368648 | tf_op jit(solution)/shard_map/ppermute | solution.py:49
  130.5 6.8 %collective-permute-start.32 = (bf16[4,120,128]{2,1,0:T(8,128)(2,1)S(1)}, bf16[4,120,128]{2,1,0:T(8,128)(2,1)S(1)}, u32[]{:S(2)}, u32[]{:S(2)}) collective-permute-start(bf16[4,120,128]{2,1,0:T(8,128)(2,1)S(1)} %get-tuple-element.161), channel_id=1, source_target_pairs={{0,6},{2,4},{4,2},{6,0},{8,14},{10,12},{12,10},{14,8},{16,22},{18,... | collective-permute-start | bytes 368648 | tf_op jit(solution)/shard_map/ppermute | solution.py:49
  131.7 14.7 %collective-permute-start.37 = (f32[336,128]{1,0:T(8,128)S(1)}, f32[336,128]{1,0:T(8,128)S(1)}, u32[]{:S(2)}, u32[]{:S(2)}) collective-permute-start(f32[336,128]{1,0:T(8,128)S(1)} %bitcast.15), channel_id=1, source_target_pairs={{0,1},{1,0},{2,3},{3,2},{4,5},{5,4},{6,7},{7,6},{8,9},{9,8},{10,11... | collective-permute-start | bytes 516104 | tf_op jit(solution)/shard_map/ppermute | solution.py:53
  (14 other events, 57.4 us)

commit v9 on v8

--- a/solution.py
+++ b/solution.py
@@ -226,7 +226,7 @@
     )(where, *items, *waits)
 
 
-def scatter_parts(where, parts, count, groups, waits=None):
+def scatter_parts(where, parts, count, groups, waits=None, before_sum=()):
     for n, (low, width) in enumerate(groups):
         got = [permute_batch(item, k << low, count) for k, item in enumerate(parts) if k]
         if waits and n == 0:
@@ -235,7 +235,7 @@
         if n + 1 < len(groups):
             fan = 1 << groups[n + 1][1]
             split = (parts[0].shape[0] // fan, fan, 1, 1, groups[n + 1][0])
-        parts = combine(where, [parts[0], *got], split)
+        parts = combine(where, [parts[0], *got], split, () if n else before_sum)
     return parts[0]
 
 
@@ -1308,8 +1308,8 @@
         brought = bring([*masters, *firsts, *seconds])
         masters, firsts, seconds = brought[:5], brought[5:10], brought[10:]
         waits = brought[:1]
-    parts = combine(where, [kept, swap_tm(given)], (left, fan, 1, 1, 0), waits)
-    first_sum = scatter_parts(where, parts, count, groups).reshape(-1, LANES)
+    parts = combine(where, [kept, swap_tm(given)], (left, fan, 1, 1, 0))
+    first_sum = scatter_parts(where, parts, count, groups, None, waits).reshape(-1, LANES)
     sums = (first_sum, swap_tm(first_sum), second_sum, swap_tm(second_sum))
     total = sum_batch(squares(sums), count)
     if fuse_in:

time: 162 us -> 162 us (level)
  no operation moved by 1% of the time
where the time goes in v9:
time: 162 us; the launch traced here: 161 us
  Pallas kernels  88.9 us (55%)
  starting transfers between devices  35.6 us (22%)
  waiting for transfers between devices  24.5 us (15%)
  blocking collectives  11 us (7%)
    ppermute x24, starting transfers between devices, permute_batch(): return lax.ppermute(value, 'batch', [(i, i ^ flip) for i in range(count)])  32.8 us
    pallas_call x1, Pallas kernels, attend_back(): pl.pallas_call(attend_back_kernel, out_shape=[in_vmem((heads, HD, length)...  23.8 us
    pallas_call x1, Pallas kernels, attend(): pl.pallas_call(attend_kernel, out_shape=[in_vmem((length, D), bf16), in_v...  17.5 us
    ppermute x24, waiting for transfers between devices, permute_batch(): return lax.ppermute(value, 'batch', [(i, i ^ flip) for i in range(count)])  17.2 us
    pallas_call x1, Pallas kernels, feed(): pl.pallas_call(partial(feed_kernel, fused), out_shape=out_shape, in_specs...  15.7 us
    all_to_all x1, blocking collectives, sum_batch(): value = lax.all_to_all(value, 'batch', 0, 0, tiled=True)  11 us
    pallas_call x2, Pallas kernels, project_back(): pl.pallas_call(partial(project_back_kernel, number, fused), out_shape=out...  9.64 us
    pallas_call x1, Pallas kernels, project(): pl.pallas_call(partial(project_kernel, fused), out_shape=[in_vmem((HEADS,...  7.99 us
  transfers between devices with their start and end apart: 38, of which 14 were waited for; matrix products, arithmetic and copies ran while one was open for 0% of the time, Pallas kernels for 43%

profile of v9, /device:TPU:0, one launch (start us, length us, event | category | flops | bytes accessed | tf_op | source)
XLA Modules:
  0.0 161.3 jit_solution(11382330284557032020)
XLA Ops:
  2.8 2.7 %collective-permute-start.1 = (bf16[1,128,128]{2,1,0:T(8,128)(2,1)S(1)}, bf16[1,128,128]{2,1,0:T(8,128)(2,1)S(1)}, u32[]{:S(2)}, u32[]{:S(2)}) collective-permute-start(bf16[1,128,128]{2,1,0:T(8,128)(2,1)S(1)} %bitcast.25), channel_id=1, source_target_pairs={{0,8},{2,10},{4,12},{6,14},{8,0},{10,2},{12,4},{14,6},{16,24},{18,... | collective-permute-start | bytes 98312 | tf_op jit(solution)/shard_map/ppermute | solution.py:49
  5.5 2.6 %collective-permute-start.2 = (bf16[1,128,128]{2,1,0:T(8,128)(2,1)S(1)}, bf16[1,128,128]{2,1,0:T(8,128)(2,1)S(1)}, u32[]{:S(2)}, u32[]{:S(2)}) collective-permute-start(bf16[1,128,128]{2,1,0:T(8,128)(2,1)S(1)} %bitcast.26), channel_id=1, source_target_pairs={{0,16},{2,18},{4,20},{6,22},{8,24},{10,26},{12,28},{14,30},{16,0},... | collective-permute-start | bytes 98312 | tf_op jit(solution)/shard_map/ppermute | solution.py:49
  8.1 3.6 %tables.1 = (f32[2048,128]{1,0:T(8,128)S(1)}, f32[2048,128]{1,0:T(8,128)S(1)}, bf16[2048,128]{1,0:T(8,128)(2,1)S(1)}, bf16[1024,128]{1,0:T(8,128)(2,1)S(1)}, s32[4,4]{1,0:T(4,128)S(1)}) custom-call(s32[2]{0:T(128)S(1)} %pad_add_fusion.where.refs_0_.refs_5_, s32[1,2048]{1,0:T(1,128)} %ids.1, s32[1,2048]{1,0:T(1,128)} %pads.1, s32[1,2048]{1,0:T(1,128)} %offsets.1, ...), custom_call_target="tpu_custom_call" | custom-call | flops 3000000000 | bytes 4194304 | tf_op jit(solution)/shard_map/tables/pallas_call | solution.py:504
  11.7 2.1 %collective-permute-done.3.refs_3_ = bf16[1,128,128]{2,1,0:T(8,128)(2,1)S(1)} collective-permute-done((bf16[1,128,128]{2,1,0:T(8,128)(2,1)S(1)}, bf16[1,128,128]{2,1,0:T(8,128)(2,1)S(1)}, u32[]{:S(2)}, u32[]{:S(2)}) %collective-permute-start.3) | collective-permute-done | bytes 32800 | tf_op jit(solution)/shard_map/ppermute | solution.py:49
  17.3 2.7 %collective-permute-done.4.refs_2_ = bf16[4,128,128]{2,1,0:T(8,128)(2,1)S(1)} collective-permute-done((bf16[4,128,128]{2,1,0:T(8,128)(2,1)S(1)}, bf16[4,128,128]{2,1,0:T(8,128)(2,1)S(1)}, u32[]{:S(2)}, u32[]{:S(2)}) %collective-permute-start.4) | collective-permute-done | bytes 131104 | tf_op jit(solution)/shard_map/ppermute | solution.py:49
  20.0 2.9 %collective-permute-done.5.refs_3_ = bf16[4,128,128]{2,1,0:T(8,128)(2,1)S(1)} collective-permute-done((bf16[4,128,128]{2,1,0:T(8,128)(2,1)S(1)}, bf16[4,128,128]{2,1,0:T(8,128)(2,1)S(1)}, u32[]{:S(2)}, u32[]{:S(2)}) %collective-permute-start.5) | collective-permute-done | bytes 131104 | tf_op jit(solution)/shard_map/ppermute | solution.py:49
  25.2 2.5 %collective-permute-start.12 = (bf16[1,336,128]{2,1,0:T(8,128)(2,1)S(1)}, bf16[1,336,128]{2,1,0:T(8,128)(2,1)S(1)}, u32[]{:S(2)}, u32[]{:S(2)}) collective-permute-start(bf16[1,336,128]{2,1,0:T(8,128)(2,1)S(1)} %bitcast.22), channel_id=1, source_target_pairs={{0,16},{2,18},{4,20},{6,22},{8,24},{10,26},{12,28},{14,30},{16,0},... | collective-permute-start | bytes 258056 | tf_op jit(solution)/shard_map/ppermute | solution.py:49
  27.6 1.9 %collective-permute-start.13 = (bf16[1,336,128]{2,1,0:T(8,128)(2,1)S(1)}, bf16[1,336,128]{2,1,0:T(8,128)(2,1)S(1)}, u32[]{:S(2)}, u32[]{:S(2)}) collective-permute-start(bf16[1,336,128]{2,1,0:T(8,128)(2,1)S(1)} %bitcast.23), channel_id=1, source_target_pairs={{0,24},{2,26},{4,28},{6,30},{8,16},{10,18},{12,20},{14,22},{16,8},... | collective-permute-start | bytes 258056 | tf_op jit(solution)/shard_map/ppermute | solution.py:49
  29.5 8.0 %project.1 = (bf16[6,1024,128]{2,1,0:T(8,128)(2,1)S(1)}, bf16[6,2048,128]{2,1,0:T(8,128)(2,1)S(1)}, bf16[6,2048,128]{2,1,0:T(8,128)(2,1)S(1)}, bf16[6,64,2048]{2...) custom-call(bf16[1024,384]{1,0:T(8,128)(2,1)} %bitcast.32, ...), custom_call_target="tpu_custom_call" | custom-call | flops 8999999488 | bytes 16777216 | tf_op jit(solution)/shard_map/project/pallas_call | solution.py:602
  38.9 2.3 %collective-permute-start.16 = (bf16[4,336,128]{2,1,0:T(8,128)(2,1)S(1)}, bf16[4,336,128]{2,1,0:T(8,128)(2,1)S(1)}, u32[]{:S(2)}, u32[]{:S(2)}) collective-permute-start(bf16[4,336,128]{2,1,0:T(8,128)(2,1)S(1)} %join.3.refs_0_.refs_1_), channel_id=1, source_target_pairs={{0,6},{2,4},{4,2},{6,0},{8,14},{10,12},{12,10},{14,8},{16,22},{18,... | collective-permute-start | bytes 1032200 | tf_op jit(solution)/shard_map/ppermute | solution.py:49
  41.2 17.5 %attend.1 = (bf16[1024,384]{1,0:T(8,128)(2,1)S(1)}, f32[1024,384]{1,0:T(8,128)S(1)}, bf16[6,1024,128]{2,1,0:T(8,128)(2,1)S(1)}) custom-call(s32[4,4]{1,0:T(4,128)S(1)} %get-tuple-element.112.ranges, bf16[6,1024,128]{2,1,0:T(8,128)(2,1)S(1)} %get-tuple-element.117.qa, bf16[6,2048,128]{2,1,0:T(8,128)(2,1)S(1)} %get-tuple-element.118.ka, ...), custom_call_target="tpu_custom_call" | custom-call | flops 17999998976 | bytes 12582912 | tf_op jit(solution)/shard_map/attend/pallas_call | solution.py:678
  61.5 15.7 %feed.1 = (bf16[1024,384]{1,0:T(8,128)(2,1)}, f32[1024,384]{1,0:T(8,128)S(1)}, bf16[6,1024,128]{2,1,0:T(8,128)(2,1)S(1)}, f32[8,336,128]{2,1,0:T(8,128)S(1)}, bf...) custom-call(bf16[1024,384]{1,0:T(8,128)(2,1)} %bitcast.33, ...), custom_call_target="tpu_custom_call" | custom-call | flops 14000000000 | bytes 16777216 | tf_op jit(solution)/shard_map/feed/pallas_call | solution.py:932
  78.5 2.3 %collective-permute-start.23 = (bf16[8,336,128]{2,1,0:T(8,128)(2,1)S(1)}, bf16[8,336,128]{2,1,0:T(8,128)(2,1)S(1)}, u32[]{:S(2)}, u32[]{:S(2)}) collective-permute-start(bf16[8,336,128]{2,1,0:T(8,128)(2,1)S(1)} %get-tuple-element.136), channel_id=1, source_target_pairs={{0,6},{2,4},{4,2},{6,0},{8,14},{10,12},{12,10},{14,8},{16,22},{18,... | collective-permute-start | bytes 2064392 | tf_op jit(solution)/shard_map/ppermute | solution.py:49
  80.8 23.8 %attend_back.1 = (f32[6,64,1024]{2,1,0:T(8,128)S(1)}, f32[6,2048,128]{2,1,0:T(8,128)S(1)}, bf16[6,1024,128]{2,1,0:T(8,128)(2,1)S(1)}) custom-call(s32[4,4]{1,0:T(4,128)S(1)} %get-tuple-element.112.ranges, bf16[6,1024,128]{2,1,0:T(8,128)(2,1)S(1)} %get-tuple-element.128.qb, bf16[6,2048,128]{2,1,0:T(8,128)(2,1)S(1)} %get-tuple-element.118.ka, ...), custom_call_target="tpu_custom_call" | custom-call | flops 33999998976 | bytes 8388608 | tf_op jit(solution)/shard_map/attend_back/pallas_call | solution.py:740
  104.5 3.9 %project_back.2 = (f32[1024,384]{1,0:T(8,128)S(1)}, f32[384,384]{1,0:T(8,128)S(1)}) custom-call(bf16[1024,384]{1,0:T(8,128)(2,1)} %bitcast.34, f32[2048,128]{1,0:T(8,128)S(1)} %get-tuple-element.113.cosine, f32[2048,128]{1,0:T(8,128)S(1)} %get-tuple-element.114.sine, bf16[384,1152]{1,0:T(8,128)(2,1)S(1)} %get-tuple-element.127.w, ...), custom_call_target="tpu_custom_call" | custom-call | flops 4000000000 | bytes 8388608 | tf_op jit(solution)/shard_map/project_back/pallas_call | solution.py:1045
  111.6 2.5 %collective-permute-done.25.refs_1_ = bf16[4,336,128]{2,1,0:T(8,128)(2,1)S(1)} collective-permute-done((bf16[4,336,128]{2,1,0:T(8,128)(2,1)S(1)}, bf16[4,336,128]{2,1,0:T(8,128)(2,1)S(1)}, u32[]{:S(2)}, u32[]{:S(2)}) %collective-permute-start.25) | collective-permute-done | bytes 344096 | tf_op jit(solution)/shard_map/ppermute | solution.py:53
  114.8 2.8 %collective-permute-start.27 = (bf16[1,336,128]{2,1,0:T(8,128)(2,1)S(1)}, bf16[1,336,128]{2,1,0:T(8,128)(2,1)S(1)}, u32[]{:S(2)}, u32[]{:S(2)}) collective-permute-start(bf16[1,336,128]{2,1,0:T(8,128)(2,1)S(1)} %get-tuple-element.152), channel_id=1, source_target_pairs={{0,16},{2,18},{4,20},{6,22},{8,24},{10,26},{12,28},{14,30},{16,0},... | collective-permute-start | bytes 258056 | tf_op jit(solution)/shard_map/ppermute | solution.py:49
  119.1 5.8 %project_back.3 = (bf16[1024,384]{1,0:T(8,128)(2,1)}, f32[16,120,128]{2,1,0:T(8,128)S(1)}, bf16[16,120,128]{2,1,0:T(8,128)(2,1)S(1)}) custom-call(bf16[1024,384]{1,0:T(8,128)(2,1)} %bitcast.35, f32[2048,128]{1,0:T(8,128)S(1)} %get-tuple-element.113.cosine, f32[2048,128]{1,0:T(8,128)S(1)} %get-tuple-element.114.sine, ...), custom_call_target="tpu_custom_call" | custom-call | flops 4000000000 | bytes 8388608 | tf_op jit(solution)/shard_map/project_back/pallas_call | solution.py:1045
  125.6 1.9 %collective-permute-done.29.refs_1_ = bf16[16,120,128]{2,1,0:T(8,128)(2,1)S(1)} collective-permute-done((bf16[16,120,128]{2,1,0:T(8,128)(2,1)S(1)}, bf16[16,120,128]{2,1,0:T(8,128)(2,1)S(1)}, u32[]{:S(2)}, u32[]{:S(2)}) %collective-permute-start.29) | collective-permute-done | bytes 491552 | tf_op jit(solution)/shard_map/ppermute | solution.py:53
  134.0 3.3 %collective-permute-done.31.refs_2_ = bf16[4,120,128]{2,1,0:T(8,128)(2,1)S(1)} collective-permute-done((bf16[4,120,128]{2,1,0:T(8,128)(2,1)S(1)}, bf16[4,120,128]{2,1,0:T(8,128)(2,1)S(1)}, u32[]{:S(2)}, u32[]{:S(2)}) %collective-permute-start.31) | collective-permute-done | bytes 122912 | tf_op jit(solution)/shard_map/ppermute | solution.py:49
  140.4 1.9 %collective-permute-start.35 = (bf16[1,120,128]{2,1,0:T(8,128)(2,1)S(1)}, bf16[1,120,128]{2,1,0:T(8,128)(2,1)S(1)}, u32[]{:S(2)}, u32[]{:S(2)}) collective-permute-start(bf16[1,120,128]{2,1,0:T(8,128)(2,1)S(1)} %get-tuple-element.165), channel_id=1, source_target_pairs={{0,24},{2,26},{4,28},{6,30},{8,16},{10,18},{12,20},{14,22},{16,8},... | collective-permute-start | bytes 92168 | tf_op jit(solution)/shard_map/ppermute | solution.py:49
  142.3 2.2 %collective-permute-done.34.refs_2_ = bf16[1,120,128]{2,1,0:T(8,128)(2,1)S(1)} collective-permute-done((bf16[1,120,128]{2,1,0:T(8,128)(2,1)S(1)}, bf16[1,120,128]{2,1,0:T(8,128)(2,1)S(1)}, u32[]{:S(2)}, u32[]{:S(2)}) %collective-permute-start.34) | collective-permute-done | bytes 30752 | tf_op jit(solution)/shard_map/ppermute | solution.py:49
  148.2 11.0 %all_to_all.5 = f32[16,1,128]{2,1,0:T(1,128)S(1)} all-to-all(f32[16,1,128]{2,1,0:T(1,128)S(1)} %broadcast_in_dim.25), channel_id=1, replica_groups=mesh['batch'=16,'tm'=2] {'batch'}, dimensions={0} | all-to-all | bytes 16384 | tf_op jit(solution)/shard_map/all_to_all | solution.py:127
  159.2 1.9 %update.1 = (f32[1,1]{1,0:T(1,128)}, f32[24,1152]{1,0:T(8,128)}, f32[24,384]{1,0:T(8,128)}, f32[24,2048]{1,0:T(8,128)}, f32[64,384]{1,0:T(8,128)}, /*index=5*/f3...) custom-call(s32[2]{0:T(128)S(1)} %pad_add_fusion.where.refs_0_.refs_, ...), custom_call_target="tpu_custom_call" | custom-call | tf_op jit(solution)/shard_map/update/pallas_call | solution.py:1157
  (81 shorter events, 32.8 us)
Async XLA Ops:
  0.7 7.4 %collective-permute-start = (bf16[1024,384]{1,0:T(8,128)(2,1)}, bf16[1024,384]{1,0:T(8,128)(2,1)S(1)}, u32[]{:S(2)}, u32[]{:S(2)}) collective-permute-start(bf16[1024,384]{1,0:T(8,128)(2,1)} %bitcast.31), channel_id=1, source_target_pairs={{0,1},{1,0},{2,3},{3,2},{4,5},{5,4},{6,7},{7,6},{8,9},{9,8},{10,11... | collective-permute-start | bytes 2359304 | tf_op jit(solution)/shard_map/ppermute | solution.py:53
  2.8 8.9 %collective-permute-start.1 = (bf16[1,128,128]{2,1,0:T(8,128)(2,1)S(1)}, bf16[1,128,128]{2,1,0:T(8,128)(2,1)S(1)}, u32[]{:S(2)}, u32[]{:S(2)}) collective-permute-start(bf16[1,128,128]{2,1,0:T(8,128)(2,1)S(1)} %bitcast.25), channel_id=1, source_target_pairs={{0,8},{2,10},{4,12},{6,14},{8,0},{10,2},{12,4},{14,6},{16,24},{18,... | collective-permute-start | bytes 98312 | tf_op jit(solution)/shard_map/ppermute | solution.py:49
  15.3 7.6 %collective-permute-start.5 = (bf16[4,128,128]{2,1,0:T(8,128)(2,1)S(1)}, bf16[4,128,128]{2,1,0:T(8,128)(2,1)S(1)}, u32[]{:S(2)}, u32[]{:S(2)}) collective-permute-start(bf16[4,128,128]{2,1,0:T(8,128)(2,1)S(1)} %join.2.refs_1_.refs_3_), channel_id=1, source_target_pairs={{0,4},{2,6},{4,0},{6,2},{8,12},{10,14},{12,8},{14,10},{16,20},{18,... | collective-permute-start | bytes 393224 | tf_op jit(solution)/shard_map/ppermute | solution.py:49
  17.3 7.8 %collective-permute-start.7 = (bf16[4,128,128]{2,1,0:T(8,128)(2,1)S(1)}, bf16[4,128,128]{2,1,0:T(8,128)(2,1)S(1)}, u32[]{:S(2)}, u32[]{:S(2)}) collective-permute-start(bf16[4,128,128]{2,1,0:T(8,128)(2,1)S(1)} %join.2.refs_1_.refs_3_), channel_id=1, source_target_pairs={{0,1},{1,0},{2,3},{3,2},{4,5},{5,4},{6,7},{7,6},{8,9},{9,8},{10,11... | collective-permute-start | bytes 393224 | tf_op jit(solution)/shard_map/ppermute | solution.py:53
  20.0 7.6 %collective-permute-start.8 = (bf16[4,128,128]{2,1,0:T(8,128)(2,1)S(1)}, bf16[4,128,128]{2,1,0:T(8,128)(2,1)S(1)}, u32[]{:S(2)}, u32[]{:S(2)}) collective-permute-start(bf16[4,128,128]{2,1,0:T(8,128)(2,1)S(1)} %collective-permute-done.4.refs_2_), channel_id=1, source_target_pairs={{0,1},{1,0},{2,3},{3,2},{4,5},{5,4},{6,7},{7,6},{8,9},{9,8},{10,11... | collective-permute-start | bytes 393224 | tf_op jit(solution)/shard_map/ppermute | solution.py:53
  22.9 6.6 %collective-permute-start.9 = (bf16[4,128,128]{2,1,0:T(8,128)(2,1)S(1)}, bf16[4,128,128]{2,1,0:T(8,128)(2,1)S(1)}, u32[]{:S(2)}, u32[]{:S(2)}) collective-permute-start(bf16[4,128,128]{2,1,0:T(8,128)(2,1)S(1)} %collective-permute-done.5.refs_3_), channel_id=1, source_target_pairs={{0,1},{1,0},{2,3},{3,2},{4,5},{5,4},{6,7},{7,6},{8,9},{9,8},{10,11... | collective-permute-start | bytes 393224 | tf_op jit(solution)/shard_map/ppermute | solution.py:53
  23.0 6.6 %collective-permute-start.10 = (bf16[4,128,128]{2,1,0:T(8,128)(2,1)S(1)}, bf16[4,128,128]{2,1,0:T(8,128)(2,1)S(1)}, u32[]{:S(2)}, u32[]{:S(2)}) collective-permute-start(bf16[4,128,128]{2,1,0:T(8,128)(2,1)S(1)} %collective-permute-done.6.refs_4_), channel_id=1, source_target_pairs={{0,1},{1,0},{2,3},{3,2},{4,5},{5,4},{6,7},{7,6},{8,9},{9,8},{10,11... | collective-permute-start | bytes 393224 | tf_op jit(solution)/shard_map/ppermute | solution.py:53
  25.1 12.5 %collective-permute-start.11 = (bf16[1,336,128]{2,1,0:T(8,128)(2,1)S(1)}, bf16[1,336,128]{2,1,0:T(8,128)(2,1)S(1)}, u32[]{:S(2)}, u32[]{:S(2)}) collective-permute-start(bf16[1,336,128]{2,1,0:T(8,128)(2,1)S(1)} %bitcast.21), channel_id=1, source_target_pairs={{0,8},{2,10},{4,12},{6,14},{8,0},{10,2},{12,4},{14,6},{16,24},{18,... | collective-permute-start | bytes 258056 | tf_op jit(solution)/shard_map/ppermute | solution.py:49
  25.2 12.4 %collective-permute-start.12 = (bf16[1,336,128]{2,1,0:T(8,128)(2,1)S(1)}, bf16[1,336,128]{2,1,0:T(8,128)(2,1)S(1)}, u32[]{:S(2)}, u32[]{:S(2)}) collective-permute-start(bf16[1,336,128]{2,1,0:T(8,128)(2,1)S(1)} %bitcast.22), channel_id=1, source_target_pairs={{0,16},{2,18},{4,20},{6,22},{8,24},{10,26},{12,28},{14,30},{16,0},... | collective-permute-start | bytes 258056 | tf_op jit(solution)/shard_map/ppermute | solution.py:49
  27.6 9.9 %collective-permute-start.13 = (bf16[1,336,128]{2,1,0:T(8,128)(2,1)S(1)}, bf16[1,336,128]{2,1,0:T(8,128)(2,1)S(1)}, u32[]{:S(2)}, u32[]{:S(2)}) collective-permute-start(bf16[1,336,128]{2,1,0:T(8,128)(2,1)S(1)} %bitcast.23), channel_id=1, source_target_pairs={{0,24},{2,26},{4,28},{6,30},{8,16},{10,18},{12,20},{14,22},{16,8},... | collective-permute-start | bytes 258056 | tf_op jit(solution)/shard_map/ppermute | solution.py:49
  37.6 21.0 %collective-permute-start.14 = (bf16[4,336,128]{2,1,0:T(8,128)(2,1)S(1)}, bf16[4,336,128]{2,1,0:T(8,128)(2,1)S(1)}, u32[]{:S(2)}, u32[]{:S(2)}) collective-permute-start(bf16[4,336,128]{2,1,0:T(8,128)(2,1)S(1)} %join.3.refs_0_.refs_1_), channel_id=1, source_target_pairs={{0,2},{2,0},{4,6},{6,4},{8,10},{10,8},{12,14},{14,12},{16,18},{18,... | collective-permute-start | bytes 1032200 | tf_op jit(solution)/shard_map/ppermute | solution.py:49
  37.7 21.0 %collective-permute-start.15 = (bf16[4,336,128]{2,1,0:T(8,128)(2,1)S(1)}, bf16[4,336,128]{2,1,0:T(8,128)(2,1)S(1)}, u32[]{:S(2)}, u32[]{:S(2)}) collective-permute-start(bf16[4,336,128]{2,1,0:T(8,128)(2,1)S(1)} %join.3.refs_0_.refs_1_), channel_id=1, source_target_pairs={{0,4},{2,6},{4,0},{6,2},{8,12},{10,14},{12,8},{14,10},{16,20},{18,... | collective-permute-start | bytes 1032200 | tf_op jit(solution)/shard_map/ppermute | solution.py:49
  38.9 19.8 %collective-permute-start.16 = (bf16[4,336,128]{2,1,0:T(8,128)(2,1)S(1)}, bf16[4,336,128]{2,1,0:T(8,128)(2,1)S(1)}, u32[]{:S(2)}, u32[]{:S(2)}) collective-permute-start(bf16[4,336,128]{2,1,0:T(8,128)(2,1)S(1)} %join.3.refs_0_.refs_1_), channel_id=1, source_target_pairs={{0,6},{2,4},{4,2},{6,0},{8,14},{10,12},{12,10},{14,8},{16,22},{18,... | collective-permute-start | bytes 1032200 | tf_op jit(solution)/shard_map/ppermute | solution.py:49
  41.2 18.6 %collective-permute-start.17 = (bf16[4,336,128]{2,1,0:T(8,128)(2,1)S(1)}, bf16[4,336,128]{2,1,0:T(8,128)(2,1)S(1)}, u32[]{:S(2)}, u32[]{:S(2)}) collective-permute-start(bf16[4,336,128]{2,1,0:T(8,128)(2,1)S(1)} %join.3.refs_0_.refs_1_), channel_id=1, source_target_pairs={{0,1},{1,0},{2,3},{3,2},{4,5},{5,4},{6,7},{7,6},{8,9},{9,8},{10,11... | collective-permute-start | bytes 1032200 | tf_op jit(solution)/shard_map/ppermute | solution.py:53
  77.2 31.2 %collective-permute-start.21 = (bf16[8,336,128]{2,1,0:T(8,128)(2,1)S(1)}, bf16[8,336,128]{2,1,0:T(8,128)(2,1)S(1)}, u32[]{:S(2)}, u32[]{:S(2)}) collective-permute-start(bf16[8,336,128]{2,1,0:T(8,128)(2,1)S(1)} %get-tuple-element.134), channel_id=1, source_target_pairs={{0,2},{2,0},{4,6},{6,4},{8,10},{10,8},{12,14},{14,12},{16,18},{18,... | collective-permute-start | bytes 2064392 | tf_op jit(solution)/shard_map/ppermute | solution.py:49
  77.3 31.2 %collective-permute-start.22 = (bf16[8,336,128]{2,1,0:T(8,128)(2,1)S(1)}, bf16[8,336,128]{2,1,0:T(8,128)(2,1)S(1)}, u32[]{:S(2)}, u32[]{:S(2)}) collective-permute-start(bf16[8,336,128]{2,1,0:T(8,128)(2,1)S(1)} %get-tuple-element.135), channel_id=1, source_target_pairs={{0,4},{2,6},{4,0},{6,2},{8,12},{10,14},{12,8},{14,10},{16,20},{18,... | collective-permute-start | bytes 2064392 | tf_op jit(solution)/shard_map/ppermute | solution.py:49
  78.5 31.7 %collective-permute-start.23 = (bf16[8,336,128]{2,1,0:T(8,128)(2,1)S(1)}, bf16[8,336,128]{2,1,0:T(8,128)(2,1)S(1)}, u32[]{:S(2)}, u32[]{:S(2)}) collective-permute-start(bf16[8,336,128]{2,1,0:T(8,128)(2,1)S(1)} %get-tuple-element.136), channel_id=1, source_target_pairs={{0,6},{2,4},{4,2},{6,0},{8,14},{10,12},{12,10},{14,8},{16,22},{18,... | collective-permute-start | bytes 2064392 | tf_op jit(solution)/shard_map/ppermute | solution.py:49
  110.2 9.0 %collective-permute-start.24 = (bf16[6,1024,128]{2,1,0:T(8,128)(2,1)S(1)}, bf16[6,1024,128]{2,1,0:T(8,128)(2,1)S(1)}, u32[]{:S(2)}, u32[]{:S(2)}) collective-permute-start(bf16[6,1024,128]{2,1,0:T(8,128)(2,1)S(1)} %hold.7), channel_id=1, source_target_pairs={{0,1},{1,0},{2,3},{3,2},{4,5},{5,4},{6,7},{7,6},{8,9},{9,8},{10,11... | collective-permute-start | bytes 4718600 | tf_op jit(solution)/shard_map/ppermute | solution.py:53
  114.7 10.2 %collective-permute-start.26 = (bf16[1,336,128]{2,1,0:T(8,128)(2,1)S(1)}, bf16[1,336,128]{2,1,0:T(8,128)(2,1)S(1)}, u32[]{:S(2)}, u32[]{:S(2)}) collective-permute-start(bf16[1,336,128]{2,1,0:T(8,128)(2,1)S(1)} %get-tuple-element.151), channel_id=1, source_target_pairs={{0,8},{2,10},{4,12},{6,14},{8,0},{10,2},{12,4},{14,6},{16,24},{18,... | collective-permute-start | bytes 258056 | tf_op jit(solution)/shard_map/ppermute | solution.py:49
  114.8 10.2 %collective-permute-start.27 = (bf16[1,336,128]{2,1,0:T(8,128)(2,1)S(1)}, bf16[1,336,128]{2,1,0:T(8,128)(2,1)S(1)}, u32[]{:S(2)}, u32[]{:S(2)}) collective-permute-start(bf16[1,336,128]{2,1,0:T(8,128)(2,1)S(1)} %get-tuple-element.152), channel_id=1, source_target_pairs={{0,16},{2,18},{4,20},{6,22},{8,24},{10,26},{12,28},{14,30},{16,0},... | collective-permute-start | bytes 258056 | tf_op jit(solution)/shard_map/ppermute | solution.py:49
  117.5 7.4 %collective-permute-start.28 = (bf16[1,336,128]{2,1,0:T(8,128)(2,1)S(1)}, bf16[1,336,128]{2,1,0:T(8,128)(2,1)S(1)}, u32[]{:S(2)}, u32[]{:S(2)}) collective-permute-start(bf16[1,336,128]{2,1,0:T(8,128)(2,1)S(1)} %get-tuple-element.153), channel_id=1, source_target_pairs={{0,24},{2,26},{4,28},{6,30},{8,16},{10,18},{12,20},{14,22},{16,8},... | collective-permute-start | bytes 258056 | tf_op jit(solution)/shard_map/ppermute | solution.py:49
  129.5 7.7 %collective-permute-start.31 = (bf16[4,120,128]{2,1,0:T(8,128)(2,1)S(1)}, bf16[4,120,128]{2,1,0:T(8,128)(2,1)S(1)}, u32[]{:S(2)}, u32[]{:S(2)}) collective-permute-start(bf16[4,120,128]{2,1,0:T(8,128)(2,1)S(1)} %get-tuple-element.159), channel_id=1, source_target_pairs={{0,4},{2,6},{4,0},{6,2},{8,12},{10,14},{12,8},{14,10},{16,20},{18,... | collective-permute-start | bytes 368648 | tf_op jit(solution)/shard_map/ppermute | solution.py:49
  130.5 6.7 %collective-permute-start.32 = (bf16[4,120,128]{2,1,0:T(8,128)(2,1)S(1)}, bf16[4,120,128]{2,1,0:T(8,128)(2,1)S(1)}, u32[]{:S(2)}, u32[]{:S(2)}) collective-permute-start(bf16[4,120,128]{2,1,0:T(8,128)(2,1)S(1)} %get-tuple-element.160), channel_id=1, source_target_pairs={{0,6},{2,4},{4,2},{6,0},{8,14},{10,12},{12,10},{14,8},{16,22},{18,... | collective-permute-start | bytes 368648 | tf_op jit(solution)/shard_map/ppermute | solution.py:49
  131.7 15.0 %collective-permute-start.37 = (f32[336,128]{1,0:T(8,128)S(1)}, f32[336,128]{1,0:T(8,128)S(1)}, u32[]{:S(2)}, u32[]{:S(2)}) collective-permute-start(f32[336,128]{1,0:T(8,128)S(1)} %bitcast.15), channel_id=1, source_target_pairs={{0,1},{1,0},{2,3},{3,2},{4,5},{5,4},{6,7},{7,6},{8,9},{9,8},{10,11... | collective-permute-start | bytes 516104 | tf_op jit(solution)/shard_map/ppermute | solution.py:53
  (14 other events, 57.4 us)
